TPU v7x, 32 devices: a whole 2x2x4 slice. The times are simulated.
32 devices in a mesh: grp: 2 (over y), space: 4 (over z), tm: 4 (over x, core).
Axes of the slice: x: 2, y: 2, z: 4, core: 2. Of those that a mesh axis runs over, the one named last changes fastest.
Arguments:
- snapshots: bfloat16 [128, 512, 1024], P(('grp', 'tm'), None, 'space'), parts along dimension 0, may hold values from -100 to 100
- entry_weight: float32 [2048], P(('grp', 'space')), parts along dimension 0, may hold values from 0.3 to 9
- freq_index: int32 [256], replicated, may hold values from 0 to 256, as said below
Outputs:
- energy_map: float32 [512, 1024], P(('grp', 'tm'), 'space'), parts along dimension 0
- filters: float32 [512, 2, 64, 64], P(('grp', 'tm')), parts along dimension 0
There are 2 independent parts, one for each index of `grp`. A program takes and returns all parts, laid end to end along the dimension named above; an argument that names none is the same for every part. Nothing has to cross between parts.
Inputs may be any that keep to these rules, and one draw needn't show every extreme that they name: `freq_index`: distinct and increasing; 0 and 256 are always retained.
All inputs are finite; a program needn't handle non-finite values.
Results may differ from a plain program's by a relative error of at most 0.0019.
Values may be sent and summed in bfloat16 or wider, within the bound.
No kernel may reach another device: no remote copies, remote signals or barrier semaphores. Data moves between devices by JAX's collectives and lax.ppermute only.
A program may use at most 128 MiB of HBM per device.

v0:
```python
import math

import jax
import jax.numpy as jnp
from jax import lax
from jax.sharding import PartitionSpec as P


def dft_table(freq_index, length):
    times = jnp.arange(length, dtype=jnp.int32)
    phase = freq_index[:, None] * times[None, :] % length
    angle = 2.0 * math.pi / length * phase.astype(jnp.float32)
    window = 0.5 - 0.5 * jnp.cos(2.0 * math.pi / length * times.astype(jnp.float32))
    norm = math.sqrt(0.375 * length)
    rows = jnp.stack([window * jnp.cos(angle), -window * jnp.sin(angle)], axis=1) / norm
    return rows.reshape(2 * freq_index.shape[0], length).astype(jnp.bfloat16)


def solve_filters(gram_rows, blocks):
    grams = jnp.transpose(gram_rows, (1, 2, 0, 3))
    real_gram = grams[:, 0]
    imag_gram = grams[:, 1]
    eye = jnp.eye(blocks, dtype=jnp.float32)
    shift = jnp.trace(real_gram, axis1=1, axis2=2) / blocks
    shifted = real_gram + shift[:, None, None] * eye
    system = jnp.concatenate(
        [jnp.concatenate([shifted, -imag_gram], 2), jnp.concatenate([imag_gram, shifted], 2)], 1
    )
    factor = jnp.linalg.cholesky(system)
    solved = jax.scipy.linalg.cho_solve((factor, True), jnp.concatenate([real_gram, imag_gram], 1))
    filters = jnp.stack([solved[:, :blocks], solved[:, blocks:]], 1)
    wide = lax.optimization_barrier(filters.astype(jnp.bfloat16)).astype(jnp.float32)
    highest = lax.Precision.HIGHEST
    real_h = jnp.einsum("fbc,fcd->fbd", real_gram, wide[:, 0], precision=highest) - jnp.einsum(
        "fbc,fcd->fbd", imag_gram, wide[:, 1], precision=highest
    )
    imag_h = jnp.einsum("fbc,fcd->fbd", real_gram, wide[:, 1], precision=highest) + jnp.einsum(
        "fbc,fcd->fbd", imag_gram, wide[:, 0], precision=highest
    )
    total = blocks * jnp.sum(wide[:, 0] * real_h + wide[:, 1] * imag_h, axis=(1, 2))
    return (filters, total)


def on_device(snapshots, entry_weight, freq_index):
    groups = lax.axis_size("tm")
    blocks_here, length, entries = snapshots.shape
    retained = freq_index.shape[0]
    table = dft_table(freq_index, length)
    root = jnp.sqrt(entry_weight)
    spectra = jnp.einsum("kt,bts->bks", table, snapshots, preferred_element_type=jnp.float32)
    spectra = (spectra * root[None, None, :]).astype(jnp.bfloat16)
    spectra = spectra.reshape(blocks_here, groups, retained // groups, 2, entries)
    items = lax.all_to_all(spectra, "tm", split_axis=1, concat_axis=0, tiled=True)
    count = items.shape[2]
    total_blocks = items.shape[0]
    stacked = items.reshape(total_blocks, count, 2 * entries)
    turned = jnp.concatenate([stacked[..., entries:], -stacked[..., :entries]], axis=-1)
    paired = jnp.stack([stacked, turned], axis=0)
    gram = (
        jnp.einsum("bfs,kcfs->bfkc", stacked, paired, preferred_element_type=jnp.float32)
        / total_blocks
    )
    merged, gram = (stacked, gram)
    blocks = merged.shape[0]
    share = lax.psum_scatter(gram, "space", scatter_dimension=1, tiled=True)
    own_filters, own_total = solve_filters(share, blocks)
    filters, total_gram = (
        lax.all_gather(own_filters, "space", axis=0, tiled=True),
        lax.all_gather(own_total, "space", axis=0, tiled=True),
    )
    rounded = lax.optimization_barrier(filters.astype(jnp.bfloat16))
    part_one = jnp.einsum("bfs,fbc->fcs", merged, rounded[:, 0], preferred_element_type=jnp.float32)
    part_two = jnp.einsum("bfs,fbc->fcs", merged, rounded[:, 1], preferred_element_type=jnp.float32)
    real_part = part_one[..., :entries] - part_two[..., entries:]
    imag_part = part_two[..., :entries] + part_one[..., entries:]
    energy = jnp.sum(real_part * real_part + imag_part * imag_part, axis=1)
    total = lax.psum(jnp.sum(energy, axis=1), "space")
    state_count = entries * lax.axis_size("space")
    energy_map = state_count * energy / total[:, None]
    return (energy_map, filters)


def solution(mesh):
    in_specs = (P(("grp", "tm"), None, "space"), P(("grp", "space")), P())
    out_specs = (P(("grp", "tm"), "space"), P(("grp", "tm"), None, None, None))
    return jax.shard_map(
        on_device, mesh=mesh, in_specs=in_specs, out_specs=out_specs, check_vma=False
    )
```

profile of v0, /device:TPU:0, one launch (start us, length us, event | category | flops | bytes accessed | tf_op | source)
XLA Modules:
  0.0 639.8 jit_solution(17517460697980622918)
XLA Ops:
  7.2 0.0 reduce-scatter.4.cloned.1.call-start
  7.3 0.7 sqrt.3
  7.9 2.8 cosine_multiply_fusion
  10.8 0.1 fusion.13
  10.9 0.5 copy.38
  11.5 0.2 reshape.190
  11.7 6.6 %fusion.2 = bf16[16,512,256]{2,1,0:T(8,128)(2,1)} fusion(f32[256]{0:T(256)S(1)} %sqrt.3, bf16[512,512,1]{1,0,2:T(8,128)(2,1)S(1)} %reshape.190, bf16[16,512,256]{2,1,0:T(8,128)(2,1)} %param.3), kind=kOutput, calls=%fused_computation.4 | convolution fusion | flops 2151677952 | bytes 8913920 | tf_op jit(solution)/shard_map/kt,bts->bks/dot_general | solution.py:50
  18.2 7.2 %reshape.188 = bf16[16,4,64,2,256]{4,3,2,1,0:T(2,128)(2,1)} reshape(bf16[16,512,256]{2,1,0:T(8,128)(2,1)} %fusion.2) | data formatting | bytes 8388608 | tf_op jit(solution)/shard_map/reshape | solution.py:52
  25.4 5.8 copy.39
  31.2 52.4 %all_to_all.15 = bf16[16,4,64,2,256]{4,3,2,0,1:T(2,128)(2,1)} all-to-all(bf16[16,4,64,2,256]{4,3,2,0,1:T(2,128)(2,1)S(1)} %copy.39), channel_id=1, replica_groups=mesh['grp'=2,'space'=4,'tm'=4] {'tm'}, dimensions={1} | all-to-all | bytes 8388608 | tf_op jit(solution)/shard_map/all_to_all | solution.py:53
  83.7 7.6 %reshape.194 = bf16[64,64,512]{2,1,0:T(8,128)(2,1)} reshape(bf16[4,16,1,64,2,256]{5,4,3,1,0,2:T(2,128)(2,1)} %bitcast.64) | data formatting | bytes 8388608 | tf_op jit(solution)/shard_map/reshape | solution.py:56
  91.2 7.6 %reshape.193 = bf16[1,64,64,512]{3,2,1,0:T(8,128)(2,1)} reshape(bf16[4,16,1,64,2,256]{5,4,3,1,0,2:T(2,128)(2,1)} %bitcast.65) | data formatting | bytes 8388608 | tf_op jit(solution)/shard_map/stack;reshape | solution.py:58
  98.8 0.0 copy-start
  98.9 4.7 copy.51
  103.5 0.0 copy-done
  103.5 2.3 copy.52
  105.9 0.3 fusion.36
  106.2 0.4 maximum_bitcast_fusion
  106.6 6.9 %broadcast_multiply_fusion = f32[64,2,64,64]{3,2,1,0:T(8,128)} fusion(bf16[64,64,512]{2,1,0:T(8,128)(2,1)S(1)} %copy-done, bf16[1,64,64,512]{3,1,2,0:T(8,128)(2,1)S(1)} %maximum_bitcast_fusion, bf16[1,64,64,512]{3,1,2,0:T(8,128)(2,1)S(1)} %copy.51), kind=kOutput, calls=%fused_computation.13 | convolution fusion | flops 541589504 | bytes 14680064 | tf_op jit(solution)/shard_map/bfs,kcfs->bfkc/dot_general | solution.py:60
  113.5 4.8 reshape.195
  118.3 0.0 reduce-scatter.4.cloned.1.call-update
  118.3 0.3 all-gather.2.cloned.1.call-start
  118.6 44.8 %reduce-scatter.4.cloned.1.call-done = f32[16,8192]{1,0:T(8,128)} async-done(((f32[64,8192]{1,0:T(8,128)}), f32[16,8192]{1,0:T(8,128)}) %reduce-scatter.4.cloned.1.call-update) | async-done | bytes 524304
  163.4 1.5 reshape.196
  164.8 0.1 copy_bitcast_fusion
  164.9 0.1 slice_bitcast_fusion.7
  165.0 0.2 fusion.31
  165.2 0.1 multiply_add_fusion
  165.3 1.3 maximum_maximum_fusion
  166.7 1.6 copy.44
  168.2 1.3 fusion.18
  169.6 188.3 %custom-call.11 = f32[16,128,128]{2,1,0:T(8,128)S(1)} custom-call(f32[16,128,128]{2,1,0:T(8,128)} %fusion.18), custom_call_target="Cholesky" | custom-call | tf_op jit(solution)/shard_map/jit(cholesky)/cholesky | solution.py:29
  357.9 0.1 select_reduce_fusion
  358.0 0.1 compare_reduce_fusion
  358.1 0.2 select_bitcast_fusion
  358.3 157.4 %custom-call.12 = f32[16,1,128,128]{2,3,1,0:T(8,128)S(1)} custom-call(f32[16,1,128,128]{3,2,1,0:T(8,128)S(1)} %select_bitcast_fusion), custom_call_target="InvertDiagBlocksLowerTriangular" | custom-call | tf_op jit(solution)/shard_map/jit(_cho_solve)/vmap()/triangular_solve | solution.py:30
  515.7 1.1 fusion.16
  516.8 2.1 fusion.14
  518.9 0.2 slice_bitcast_fusion.5
  519.1 1.1 pad_maximum_fusion.1
  520.2 0.0 all-gather.2.cloned.1.call-update
  520.2 80.3 %all-gather.2.cloned.1.call-done = f32[64,2,64,64]{2,3,0,1:T(8,128)} async-done(((f32[16,2,64,64]{2,3,0,1:T(8,128)}), f32[64,2,64,64]{2,3,0,1:T(8,128)}) %all-gather.2.cloned.1.call-update) | async-done | bytes 2097168 | tf_op jit(solution)/shard_map/all_gather | solution.py:68
  600.5 0.0 copy-start.1
  600.5 2.8 convert_element_type.55
  603.3 0.6 copy-done.1
  603.9 5.5 fusion.11
  609.4 5.8 fusion.12
  615.2 2.0 fusion.35
  617.1 9.0 %psum.7 = f32[64]{0:T(128)S(1)} all-reduce(f32[64]{0:T(128)S(1)} %get-tuple-element.12), channel_id=1, replica_groups=mesh['grp'=2,'space'=4,'tm'=4] {'space'}, use_global_device_ids=true, to_apply=%region_6.7 | all-reduce | flops 64 | bytes 512 | tf_op jit(solution)/shard_map/psum | solution.py:77
  626.1 0.7 multiply_divide_fusion
  626.8 5.6 copy.47
  (6 shorter events, 0.1 us)
Async XLA Ops:
  7.2 156.2 %reduce-scatter.4.cloned.1.call-start = ((), (), s32[]{:S(2)}) async-start(), calls=%async_computation.3 | async-start | bytes 2621440
  98.8 4.7 copy-start
  118.3 482.2 %all-gather.2.cloned.1.call-start = ((), (), s32[]{:S(2)}) async-start(), calls=%async_computation.2 | async-start | bytes 5242880 | tf_op jit(solution)/shard_map/all_gather | solution.py:68
  600.5 3.4 copy-start.1
Sparse Core Ops, SparseCore 0:
  118.4 44.9 reduce-scatter.3
  520.4 80.0 all-gather.1
where the time goes:
time: 647 us; the launch traced here: 640 us
  other arithmetic  359 us (55%)
  waiting for transfers between devices  125 us (19%)
  blocking collectives  61.4 us (9%)
  local copies, waits for them, and re-layouts  50.9 us (8%)
  matrix products  27.9 us (4%)
  between operations  14.7 us (2%)
    another operation x4, other arithmetic, solve_filters(): factor = jnp.linalg.cholesky(system)  189 us
    another operation x3, other arithmetic, solve_filters(): jax.scipy.linalg.cho_solve((factor, True), jnp.concatenate([real_gram, im...  158 us
    all_gather x1, waiting for transfers between devices, on_device(): lax.all_gather(own_filters, 'space', axis=0, tiled=True)  80.3 us
    all_to_all x1, blocking collectives, on_device(): lax.all_to_all(spectra, 'tm', split_axis=1, concat_axis=0, tiled=True)  52.4 us
    unnamed x3, waiting for transfers between devices  44.8 us
    reshape x2, local copies, waits for them, and re-layouts, on_device(): spectra.reshape(blocks_here, groups, retained // groups, 2, entries)  13 us
  transfers between devices with their start and end apart: 2, of which 2 were waited for; matrix products, arithmetic and copies ran while one was open for 0% of the time, Pallas kernels for 0%

commit v1 on v0

v1 whole, which is shorter than its diff:
```python
import functools
import math

import jax
import jax.numpy as jnp
from jax import lax
from jax.experimental import pallas as pl
from jax.experimental.pallas import tpu as pltpu
from jax.sharding import PartitionSpec as P

F32 = jnp.float32
BF16 = jnp.bfloat16
VMEM_LIMIT = 30 * 1024 * 1024
DIRECT_LIMIT = 8
LANES = 128


def params(**kwargs):
    return pltpu.CompilerParams(vmem_limit_bytes=VMEM_LIMIT, **kwargs)


def whole_spec():
    return pl.BlockSpec(memory_space=pltpu.VMEM)


def dot(a, b):
    return lax.dot_general(a, b, (((1,), (0,)), ((), ())), preferred_element_type=F32)


def cos_sin(phase, length):
    quarter = length // 4
    eighth = length // 8
    shifted = phase + eighth
    low = (shifted & (quarter - 1)) - eighth
    quadrant = (shifted // quarter) & 3
    x = low.astype(F32) * F32(2.0 * math.pi / length)
    x2 = x * x
    cos = F32(1 / 40320)
    for c in (-1 / 720, 1 / 24, -0.5, 1.0):
        cos = cos * x2 + F32(c)
    sin = F32(1 / 362880)
    for c in (-1 / 5040, 1 / 120, -1 / 6, 1.0):
        sin = sin * x2 + F32(c)
    sin = sin * x
    odd = (quadrant & 1) == 1
    c0 = jnp.where(odd, sin, cos)
    s0 = jnp.where(odd, cos, sin)
    c1 = jnp.where((quadrant == 1) | (quadrant == 2), -c0, c0)
    s1 = jnp.where(quadrant >= 2, -s0, s0)
    return c1, s1


def transform_kernel(peers, count, first, step_blocks, freq_ref, root_ref, snap_ref, *refs):
    outs, (table, wide) = refs[:peers], refs[peers:]
    me = lax.axis_index("tm")
    length = snap_ref.shape[1]
    entries = snap_ref.shape[2]
    rows = peers * count
    per_peer = freq_ref.shape[0] // peers
    step = pl.program_id(0)

    @pl.when(step == 0)
    def _():
        times = lax.broadcasted_iota(jnp.int32, (8, length), 1)
        sub = lax.broadcasted_iota(jnp.int32, (8, length), 0)
        window = 0.5 - 0.5 * cos_sin(times, length)[0]
        scaled = window / F32(math.sqrt(0.375 * length))

        def eight(group):
            base = group * 8
            peer = base // count
            start = jnp.bitwise_xor(me, peer) * per_peer + first + (base - peer * count)
            k = jnp.zeros((8, length), jnp.int32)
            for i in range(8):
                k = jnp.where(sub == i, freq_ref[start + i], k)
            cos, sin = cos_sin((k * times) & (length - 1), length)
            return scaled * cos, -(scaled * sin)

        for pair in range(rows // 16):
            re0, im0 = eight(2 * pair)
            re1, im1 = eight(2 * pair + 1)
            table[16 * pair : 16 * pair + 16, :] = jnp.concatenate([re0, re1], 0).astype(BF16)
            table[rows + 16 * pair : rows + 16 * pair + 16, :] = jnp.concatenate(
                [im0, im1], 0
            ).astype(BF16)

    root = jnp.sqrt(root_ref[...])
    blocks = outs[0].shape[1]
    tiles = entries // LANES
    for i in range(step_blocks):
        spec = dot(table[...], snap_ref[i]) * root
        b = step * step_blocks + i
        for tile in range(tiles):
            lanes = slice(tile * LANES, (tile + 1) * LANES)
            wide[tile, pl.ds(b, rows, stride=blocks), :] = spec[:rows, lanes]
            wide[tiles + tile, pl.ds(b, rows, stride=blocks), :] = spec[rows:, lanes]

    @pl.when(step == pl.num_programs(0) - 1)
    def _():
        for peer in range(peers):
            for j in range(count):
                at = (peer * count + j) * blocks
                for tile in range(2 * tiles):
                    lanes = slice(tile * LANES, (tile + 1) * LANES)
                    outs[peer][j, :, lanes] = wide[tile, at : at + blocks, :].astype(BF16)


def transform(snapshots, weight, freq_index, peers, count, first):
    blocks, length, entries = snapshots.shape
    step_blocks = 4
    return pl.pallas_call(
        functools.partial(transform_kernel, peers, count, first, step_blocks),
        grid=(blocks // step_blocks,),
        in_specs=[
            pl.BlockSpec(memory_space=pltpu.SMEM),
            pl.BlockSpec((1, entries), lambda b: (0, 0)),
            pl.BlockSpec((step_blocks, length, entries), lambda b: (b, 0, 0)),
        ],
        out_specs=[pl.BlockSpec((count, blocks, 2 * entries), lambda b: (0, 0, 0))] * peers,
        out_shape=[jax.ShapeDtypeStruct((count, blocks, 2 * entries), BF16)] * peers,
        scratch_shapes=[
            pltpu.VMEM((2 * peers * count, length), BF16),
            pltpu.VMEM((2 * entries // LANES, peers * count * blocks, LANES), F32),
        ],
        compiler_params=params(),
        cost_estimate=pl.CostEstimate(
            flops=4 * peers * count * length * entries * blocks,
            bytes_accessed=2 * blocks * length * entries + 4 * peers * count * blocks * entries,
            transcendentals=0,
        ),
        name="transform",
    )(freq_index, weight, snapshots)


def lane_low(shape, half):
    return lax.broadcasted_iota(jnp.int32, shape, 1) < half


def swap(x):
    return pltpu.roll(x, x.shape[1] // 2, 1)


def pack(compact):
    half = compact.shape[0]
    both = compact + swap(compact)
    low = lane_low((half // 2, 2 * half), half)
    return jnp.where(low, both[: half // 2], both[half // 2 :])


def unpack(packed):
    rows, half = packed.shape[0], packed.shape[1] // 2
    low = lane_low(packed.shape, half)
    other = swap(packed)
    both = jnp.concatenate(
        [jnp.where(low, packed, other), jnp.where(low, other, packed)], 0
    )
    turned = jnp.transpose(jnp.concatenate([both, both], 0))[:half]
    low = lane_low(both.shape, half)
    return 0.5 * jnp.where(low, both + turned, both - turned)


def full(compact):
    half = compact.shape[0]
    turned = swap(compact)
    low = lane_low(compact.shape, half)
    return jnp.concatenate([compact, jnp.where(low, -turned, turned)], 0)


def slot_owner(direct, slot):
    return jnp.bitwise_xor(lax.axis_index("space"), slot) if direct else slot


def gram_kernel(peers, slots, direct, *refs):
    pieces, merged, grams = refs[:peers], refs[peers], refs[peers + 1 :]
    me = lax.axis_index("tm")
    here = pieces[0].shape[1]
    entries = pieces[0].shape[2] // 2
    blocks = here * peers
    per_slot = pieces[0].shape[0] // slots
    stage = None
    if here % 16:
        grams, stage = grams[:-1], grams[-1]
    low = lane_low((blocks, 2 * blocks), blocks)
    for slot in range(slots):
        owner = slot_owner(direct, slot)
        for i in range(per_slot):
            f = owner * per_slot + i
            if stage is None:
                for peer in range(peers):
                    start = pl.multiple_of(jnp.bitwise_xor(me, peer) * here, here)
                    merged[f, pl.ds(start, here), :] = pieces[peer][f]
                z = merged[f]
            else:
                for peer in range(peers):
                    start = pl.multiple_of(jnp.bitwise_xor(me, peer) * here, here)
                    stage[pl.ds(start, here), :] = pieces[peer][f].astype(F32)
                z = stage[...].astype(BF16)
                merged[f] = z
            w = jnp.concatenate([z[:, :entries], z[:, entries:]], 0)
            s = lax.dot_general(w, w, (((1,), (1,)), ((), ())), preferred_element_type=F32)
            s = s * F32(1.0 / blocks)
            top, bottom = s[:blocks], swap(s[blocks:])
            compact = jnp.where(low, top + bottom, top - bottom)
            if direct:
                grams[slot][i] = pack(compact)
            else:
                grams[0][f] = pack(compact)


def gram(pieces, slots, direct):
    peers = len(pieces)
    count, here, width = pieces[0].shape
    blocks = here * peers
    if direct:
        shapes = [(count // slots, blocks // 2, 2 * blocks)] * slots
    else:
        shapes = [(count, blocks // 2, 2 * blocks)]
    out = pl.pallas_call(
        functools.partial(gram_kernel, peers, slots, direct),
        in_specs=[whole_spec()] * peers,
        out_specs=[whole_spec()] * (1 + len(shapes)),
        out_shape=[jax.ShapeDtypeStruct((count, blocks, width), BF16)]
        + [jax.ShapeDtypeStruct(s, F32) for s in shapes],
        scratch_shapes=[pltpu.VMEM((blocks, width), F32)] if here % 16 else [],
        compiler_params=params(),
        cost_estimate=pl.CostEstimate(
            flops=4 * count * blocks * blocks * width,
            bytes_accessed=4 * count * blocks * width + 4 * count * blocks * blocks,
            transcendentals=0,
        ),
        name="gram",
    )(*pieces)
    return out[0], out[1:]


def split(x):
    high = x.astype(BF16)
    return high, (x - high.astype(F32)).astype(BF16)


def each(fn, *lists):
    return [fn(*items) for items in zip(*lists)]


def solve_kernel(parts, *refs):
    ins, out = refs[:parts], refs[parts]
    number, half_rows, width = ins[0].shape
    half = width // 2
    shape = (half, width)
    row = lax.broadcasted_iota(jnp.int32, shape, 0)
    lane = lax.broadcasted_iota(jnp.int32, shape, 1)
    eye = jnp.where(row == lane, F32(1), F32(0))

    def load(i):
        total = ins[0][i]
        for r in ins[1:]:
            total = total + r[i]
        return unpack(total)

    grams = [load(i) for i in range(number)]
    shift = each(lambda g: jnp.sum(g * eye, keepdims=True) * F32(1.0 / half), grams)
    system = each(lambda g, m: g / m + eye, grams, shift)
    parts_a = each(lambda a: split(full(a)), system)
    high = [p[0] for p in parts_a]
    both = parts_a

    low_end, high_end = 1.0, float(half + 1)
    mid, radius = (high_end + low_end) / 2, (high_end - low_end) / 2
    ratio = mid / radius
    t = 2 * ratio * ratio - 1
    scale = 2.0 / (radius * radius * t)
    x = each(lambda a: F32(scale) * (F32(2 * mid) * eye - a), system)
    for kind in ("one", "one", "one", "two", "last"):
        xb = each(lambda v: v.astype(BF16), x)
        if kind == "one":
            residual = each(lambda v, a: eye - dot(v, a), xb, high)
        else:
            residual = each(lambda v, a: eye - (dot(v, a[0]) + dot(v, a[1])), xb, both)
        xw = each(lambda v: v.astype(F32), xb)
        xf = each(lambda v: full(v).astype(BF16), xw)
        step = each(lambda r, v: dot(r.astype(BF16), v), residual, xf)
        if kind == "last":
            factor = 1.0
        else:
            t_next = 2 * t * t - 1
            factor = 2 * t * t / t_next
            t = t_next
        x = each(lambda v, s: F32(factor) * (v + s), xw, step)
    packed = each(lambda v: pack(eye - v), x)
    for i in range(number):
        out[i * half_rows : (i + 1) * half_rows, :] = packed[i]
    filters = each(unpack, packed)
    rounded = each(lambda c: c.astype(BF16), filters)
    turned = each(lambda c: full(c.astype(F32)).astype(BF16), rounded)
    split_g = each(split, grams)
    moved = each(lambda g, c: dot(g[0], c) + dot(g[1], c), split_g, turned)
    energy = each(
        lambda c, h: jnp.sum(c.astype(F32) * h, keepdims=True) * F32(half), rounded, moved
    )
    tail = out.shape[0] - number * half_rows
    line = lax.broadcasted_iota(jnp.int32, (tail, width), 0)
    totals = jnp.ones((tail, width), F32)
    for i in range(number):
        totals = jnp.where(line == i, energy[i], totals)
    out[number * half_rows :, :] = totals


def tail_rows(number):
    return -(-number // 8) * 8


def solve(parts):
    number, half_rows, width = parts[0].shape
    rows = number * half_rows + tail_rows(number)
    return pl.pallas_call(
        functools.partial(solve_kernel, len(parts)),
        in_specs=[whole_spec()] * len(parts),
        out_specs=whole_spec(),
        out_shape=jax.ShapeDtypeStruct((rows, width), F32),
        compiler_params=params(),
        cost_estimate=pl.CostEstimate(
            flops=40 * number * width * width * width,
            bytes_accessed=4 * number * half_rows * width * (len(parts) + 1),
            transcendentals=0,
        ),
        name="filters",
    )(*parts)


def energy_kernel(slots, direct, carried, merged, *refs):
    pieces, refs = refs[: len(refs) - 2 - carried], refs[len(refs) - 2 - carried :]
    energies, filters = refs[-2:]
    count, blocks, width = merged.shape
    entries = width // 2
    per_slot = count // slots
    half_rows = blocks // 2
    states = entries * lax.axis_size("space")
    for slot in range(slots):
        owner = slot_owner(direct, slot)
        piece = pieces[slot] if direct else pieces[0].at[slot]
        for i in range(per_slot):
            f = owner * per_slot + i
            compact = unpack(piece[i * half_rows : (i + 1) * half_rows, :])
            filters[f, 0] = compact[:, :blocks]
            filters[f, 1] = compact[:, blocks:]
            wide = compact.astype(BF16).astype(F32)
            both = full(wide).astype(BF16)
            z = merged[f]
            w = jnp.concatenate([z[:, :entries], z[:, entries:]], 0)
            r = dot(both, w)
            energy = jnp.sum(r * r, axis=0, keepdims=True)
            at = per_slot * half_rows + i
            total = piece[at : at + 1, 0:1]
            energies[pl.ds(f, 1), :] = energy * (F32(states) / total)


def filtered(merged, pieces, slots, direct, carry, owned, first):
    count, blocks, width = merged.shape
    entries = width // 2
    carried = 0 if carry is None else 2
    args = [merged, *pieces] + ([] if carry is None else list(carry))
    fixed = 1 + len(pieces)
    index = first // count
    out = pl.pallas_call(
        functools.partial(energy_kernel, slots, direct, carried),
        grid=(1,),
        in_specs=[whole_spec()] * fixed + [pl.BlockSpec(memory_space=pl.ANY)] * carried,
        out_specs=[
            pl.BlockSpec((count, entries), lambda g: (index, 0)),
            pl.BlockSpec((count, 2, blocks, blocks), lambda g: (index, 0, 0, 0)),
        ],
        out_shape=[
            jax.ShapeDtypeStruct((owned, entries), F32),
            jax.ShapeDtypeStruct((owned, 2, blocks, blocks), F32),
        ],
        input_output_aliases={fixed: 0, fixed + 1: 1} if carried else {},
        compiler_params=params(),
        cost_estimate=pl.CostEstimate(
            flops=4 * count * blocks * blocks * width,
            bytes_accessed=2 * count * blocks * width + 24 * count * blocks * blocks,
            transcendentals=0,
        ),
        name="energy",
    )(*args)
    return out


def exchange(arrays, axis):
    size = lax.axis_size(axis)
    got = [arrays[0]]
    for offset in range(1, size):
        pairs = [(i, i ^ offset) for i in range(size)]
        got.append(lax.ppermute(arrays[offset], axis, pairs))
    return got


def on_device(snapshots, entry_weight, freq_index):
    peers = lax.axis_size("tm")
    slots = lax.axis_size("space")
    retained = freq_index.shape[0]
    owned = retained // peers
    direct = slots <= DIRECT_LIMIT
    chunks = 4
    while chunks > 1 and (owned // chunks) % max(slots, 8):
        chunks //= 2
    count = owned // chunks
    weight = entry_weight.reshape(1, -1)
    carry = None
    for c in range(chunks):
        first = c * count
        sent = transform(snapshots, weight, freq_index, peers, count, first)
        merged, grams = gram(exchange(sent, "tm"), slots, direct)
        if direct:
            parts = exchange(grams, "space")
        else:
            parts = [lax.psum_scatter(grams[0], "space", scatter_dimension=0, tiled=True)]
        own = solve(parts)
        if direct:
            pieces = exchange([own] * slots, "space")
        else:
            pieces = [lax.all_gather(own, "space", axis=0, tiled=False)]
        carry = filtered(merged, pieces, slots, direct, carry, owned, first)
    return (carry[0], carry[1])


def solution(mesh):
    in_specs = (P(("grp", "tm"), None, "space"), P(("grp", "space")), P())
    out_specs = (P(("grp", "tm"), "space"), P(("grp", "tm"), None, None, None))
    return jax.shard_map(
        on_device, mesh=mesh, in_specs=in_specs, out_specs=out_specs, check_vma=False
    )
```

time: 647 us -> 110 us (0.17); the launches traced: 640 us -> 110 us
  other arithmetic: 359 us -> 0 us
  waiting for transfers between devices: 125 us -> 22.1 us
  blocking collectives: 61.4 us -> 0 us
  starting transfers between devices: 0.29 us -> 49.5 us
  local copies, waits for them, and re-layouts: 50.9 us -> 3.54 us
  Pallas kernels: 0 us -> 34.3 us
  matrix products: 27.9 us -> 0 us
  between operations: 14.7 us -> 0.87 us
    another operation x9 -> x0, other arithmetic: 348 us -> none  [the longest x4 189 us: solve_filters(): factor = jnp.linalg.cholesky(system)]
    all_gather x1 -> x0, waiting for transfers between devices: 80.3 us -> none  [on_device(): lax.all_gather(own_filters, 'space', axis=0, tiled=True)]
    all_to_all x1 -> x0, blocking collectives: 52.4 us -> none  [on_device(): lax.all_to_all(spectra, 'tm', split_axis=1, concat_axis=0, tiled=True)]
    ppermute x0 -> x36, starting transfers between devices: none -> 49.5 us  [exchange(): got.append(lax.ppermute(arrays[offset], axis, pairs))]
    unnamed x3 -> x0, waiting for transfers between devices: 44.8 us -> none
    pallas_call x0 -> x16, Pallas kernels: none -> 34.3 us  [the longest x4 11.6 us: filtered(): pl.pallas_call(functools.partial(energy_kernel, slots, direct, carried),...]
    dot_general x4 -> x0, matrix products: 24.7 us -> none  [the longest x1 6.91 us: on_device(): jnp.einsum('bfs,kcfs->bfkc', stacked, paired, preferred_element_type=jnp....]
    reshape x4 -> x0, local copies, waits for them, and re-layouts: 22.9 us -> none  [the longest x2 13 us: on_device(): spectra.reshape(blocks_here, groups, retained // groups, 2, entries)]
  transfers between devices with their start and end apart: 2 -> 36, of which waited for: 2 -> 7; matrix products, arithmetic and copies ran while one was open for 0% -> 0% of each run, Pallas kernels for 0% -> 26%
where the time goes in v1:
time: 110 us
  starting transfers between devices  49.5 us (45%)
  Pallas kernels  34.3 us (31%)
  waiting for transfers between devices  22.1 us (20%)
  local copies, waits for them, and re-layouts  3.54 us (3%)
    ppermute x36, starting transfers between devices, exchange(): got.append(lax.ppermute(arrays[offset], axis, pairs))  49.5 us
    ppermute x36, waiting for transfers between devices, exchange(): got.append(lax.ppermute(arrays[offset], axis, pairs))  22.1 us
    pallas_call x4, Pallas kernels, filtered(): pl.pallas_call(functools.partial(energy_kernel, slots, direct, carried),...  11.6 us
    pallas_call x4, Pallas kernels, transform(): pl.pallas_call(functools.partial(transform_kernel, peers, count, first, s...  10.7 us
    pallas_call x4, Pallas kernels, solve(): pl.pallas_call(functools.partial(solve_kernel, len(parts)), in_specs=[who...  9.51 us
    unnamed x6, local copies, waits for them, and re-layouts  3.54 us
    pallas_call x4, Pallas kernels, gram(): pl.pallas_call(functools.partial(gram_kernel, peers, slots, direct), in_s...  2.4 us
  transfers between devices with their start and end apart: 36, of which 7 were waited for; matrix products, arithmetic and copies ran while one was open for 0% of the time, Pallas kernels for 26%

profile of v1, /device:TPU:0, one launch (start us, length us, event | category | flops | bytes accessed | tf_op | source)
XLA Modules:
  0.0 110.3 jit_solution(11701698080729388009)
XLA Ops:
  0.6 2.2 %copy-done = bf16[16,512,256]{2,1,0:T(8,128)(2,1)S(1)} copy-done((bf16[16,512,256]{2,1,0:T(8,128)(2,1)S(1)}, bf16[16,512,256]{2,1,0:T(8,128)(2,1)}, u32[]{:S(2)}) %copy-start) | copy-done | bytes 4194328
  2.8 0.7 copy-done.1
  3.5 0.7 copy-done.2
  4.2 2.6 %transform.7 = (bf16[16,16,512]{2,1,0:T(8,128)(2,1)S(1)}, bf16[16,16,512]{2,1,0:T(8,128)(2,1)S(1)}, bf16[16,16,512]{2,1,0:T(8,128)(2,1)S(1)}, bf16[16,16,512]{2,1,0:T(8,128)(2,1)S(1)}) custom-call(s32[256]{0:T(256)S(1)} %copy-done.1, f32[1,256]{1,0:T(1,128)S(1)} %bitcast.1, bf16[16,512,256]{2,1,0:T(8,128)(2,1)S(1)} %copy-done), custom_call_target="tpu_custom_call" | custom-call | flops 536870912 | bytes 5242880 | tf_op jit(solution)/shard_map/transform/pallas_call | solution.py:111
  6.8 0.5 collective-permute-start.27
  7.3 2.6 %collective-permute-start.28 = (bf16[16,16,512]{2,1,0:T(8,128)(2,1)S(1)}, bf16[16,16,512]{2,1,0:T(8,128)(2,1)S(1)}, u32[]{:S(2)}, u32[]{:S(2)}) collective-permute-start(bf16[16,16,512]{2,1,0:T(8,128)(2,1)S(1)} %get-tuple-element.73), channel_id=1, source_target_pairs={{0,2},{1,3},{2,0},{3,1},{4,6},{5,7},{6,4},{7,5},{8,10},{9,11},{10,... | collective-permute-start | bytes 786440 | tf_op jit(solution)/shard_map/ppermute | solution.py:393
  9.9 0.1 collective-permute-start.29
  10.0 2.6 %transform.6 = (bf16[16,16,512]{2,1,0:T(8,128)(2,1)S(1)}, bf16[16,16,512]{2,1,0:T(8,128)(2,1)S(1)}, bf16[16,16,512]{2,1,0:T(8,128)(2,1)S(1)}, bf16[16,16,512]{2,1,0:T(8,128)(2,1)S(1)}) custom-call(s32[256]{0:T(256)S(1)} %copy-done.1, f32[1,256]{1,0:T(1,128)S(1)} %bitcast.2, bf16[16,512,256]{2,1,0:T(8,128)(2,1)S(1)} %copy-done), custom_call_target="tpu_custom_call" | custom-call | flops 536870912 | bytes 5242880 | tf_op jit(solution)/shard_map/transform/pallas_call | solution.py:111
  12.6 0.2 collective-permute-start.18
  12.8 1.9 %collective-permute-start.19 = (bf16[16,16,512]{2,1,0:T(8,128)(2,1)S(1)}, bf16[16,16,512]{2,1,0:T(8,128)(2,1)S(1)}, u32[]{:S(2)}, u32[]{:S(2)}) collective-permute-start(bf16[16,16,512]{2,1,0:T(8,128)(2,1)S(1)} %get-tuple-element.64), channel_id=1, source_target_pairs={{0,2},{1,3},{2,0},{3,1},{4,6},{5,7},{6,4},{7,5},{8,10},{9,11},{10,... | collective-permute-start | bytes 786440 | tf_op jit(solution)/shard_map/ppermute | solution.py:393
  14.8 0.0 collective-permute-done.27.refs_1_
  14.8 0.0 collective-permute-start.20
  14.8 2.6 %transform.5 = (bf16[16,16,512]{2,1,0:T(8,128)(2,1)S(1)}, bf16[16,16,512]{2,1,0:T(8,128)(2,1)S(1)}, bf16[16,16,512]{2,1,0:T(8,128)(2,1)S(1)}, bf16[16,16,512]{2,1,0:T(8,128)(2,1)S(1)}) custom-call(s32[256]{0:T(256)S(1)} %copy-done.1, f32[1,256]{1,0:T(1,128)S(1)} %bitcast.3, bf16[16,512,256]{2,1,0:T(8,128)(2,1)S(1)} %copy-done), custom_call_target="tpu_custom_call" | custom-call | flops 536870912 | bytes 5242880 | tf_op jit(solution)/shard_map/transform/pallas_call | solution.py:111
  17.4 1.6 %collective-permute-start.10 = (bf16[16,16,512]{2,1,0:T(8,128)(2,1)S(1)}, bf16[16,16,512]{2,1,0:T(8,128)(2,1)S(1)}, u32[]{:S(2)}, u32[]{:S(2)}) collective-permute-start(bf16[16,16,512]{2,1,0:T(8,128)(2,1)S(1)} %get-tuple-element.55), channel_id=1, source_target_pairs={{0,2},{1,3},{2,0},{3,1},{4,6},{5,7},{6,4},{7,5},{8,10},{9,11},{10,... | collective-permute-start | bytes 786440 | tf_op jit(solution)/shard_map/ppermute | solution.py:393
  19.0 3.1 %collective-permute-done.29.refs_3_ = bf16[16,16,512]{2,1,0:T(8,128)(2,1)S(1)} collective-permute-done((bf16[16,16,512]{2,1,0:T(8,128)(2,1)S(1)}, bf16[16,16,512]{2,1,0:T(8,128)(2,1)S(1)}, u32[]{:S(2)}, u32[]{:S(2)}) %collective-permute-start.29) | collective-permute-done | bytes 262176 | tf_op jit(solution)/shard_map/ppermute | solution.py:393
  22.2 1.9 %collective-permute-start.11 = (bf16[16,16,512]{2,1,0:T(8,128)(2,1)S(1)}, bf16[16,16,512]{2,1,0:T(8,128)(2,1)S(1)}, u32[]{:S(2)}, u32[]{:S(2)}) collective-permute-start(bf16[16,16,512]{2,1,0:T(8,128)(2,1)S(1)} %get-tuple-element.56), channel_id=1, source_target_pairs={{0,3},{1,2},{2,1},{3,0},{4,7},{5,6},{6,5},{7,4},{8,11},{9,10},{10,... | collective-permute-start | bytes 786440 | tf_op jit(solution)/shard_map/ppermute | solution.py:393
  24.1 2.8 %transform.4 = (bf16[16,16,512]{2,1,0:T(8,128)(2,1)S(1)}, bf16[16,16,512]{2,1,0:T(8,128)(2,1)S(1)}, bf16[16,16,512]{2,1,0:T(8,128)(2,1)S(1)}, bf16[16,16,512]{2,1,0:T(8,128)(2,1)S(1)}) custom-call(s32[256]{0:T(256)S(1)} %copy-done.1, f32[1,256]{1,0:T(1,128)S(1)} %bitcast.4, bf16[16,512,256]{2,1,0:T(8,128)(2,1)S(1)} %copy-done), custom_call_target="tpu_custom_call" | custom-call | flops 536870912 | bytes 5242880 | tf_op jit(solution)/shard_map/transform/pallas_call | solution.py:111
  26.9 0.1 collective-permute-start.9
  27.0 1.3 %collective-permute-done.19.refs_2_ = bf16[16,16,512]{2,1,0:T(8,128)(2,1)S(1)} collective-permute-done((bf16[16,16,512]{2,1,0:T(8,128)(2,1)S(1)}, bf16[16,16,512]{2,1,0:T(8,128)(2,1)S(1)}, u32[]{:S(2)}, u32[]{:S(2)}) %collective-permute-start.19) | collective-permute-done | bytes 262176 | tf_op jit(solution)/shard_map/ppermute | solution.py:393
  28.3 0.0 collective-permute-start
  28.3 5.1 %collective-permute-done.20.refs_3_ = bf16[16,16,512]{2,1,0:T(8,128)(2,1)S(1)} collective-permute-done((bf16[16,16,512]{2,1,0:T(8,128)(2,1)S(1)}, bf16[16,16,512]{2,1,0:T(8,128)(2,1)S(1)}, u32[]{:S(2)}, u32[]{:S(2)}) %collective-permute-start.20) | collective-permute-done | bytes 262176 | tf_op jit(solution)/shard_map/ppermute | solution.py:393
  33.4 1.6 %collective-permute-start.1 = (bf16[16,16,512]{2,1,0:T(8,128)(2,1)S(1)}, bf16[16,16,512]{2,1,0:T(8,128)(2,1)S(1)}, u32[]{:S(2)}, u32[]{:S(2)}) collective-permute-start(bf16[16,16,512]{2,1,0:T(8,128)(2,1)S(1)} %get-tuple-element.46), channel_id=1, source_target_pairs={{0,2},{1,3},{2,0},{3,1},{4,6},{5,7},{6,4},{7,5},{8,10},{9,11},{10,... | collective-permute-start | bytes 786440 | tf_op jit(solution)/shard_map/ppermute | solution.py:393
  35.0 4.6 %collective-permute-done.10.refs_2_ = bf16[16,16,512]{2,1,0:T(8,128)(2,1)S(1)} collective-permute-done((bf16[16,16,512]{2,1,0:T(8,128)(2,1)S(1)}, bf16[16,16,512]{2,1,0:T(8,128)(2,1)S(1)}, u32[]{:S(2)}, u32[]{:S(2)}) %collective-permute-start.10) | collective-permute-done | bytes 262176 | tf_op jit(solution)/shard_map/ppermute | solution.py:393
  39.5 0.8 collective-permute-start.2
  40.3 0.6 gram.7
  40.9 3.7 %collective-permute-done.11.refs_3_ = bf16[16,16,512]{2,1,0:T(8,128)(2,1)S(1)} collective-permute-done((bf16[16,16,512]{2,1,0:T(8,128)(2,1)S(1)}, bf16[16,16,512]{2,1,0:T(8,128)(2,1)S(1)}, u32[]{:S(2)}, u32[]{:S(2)}) %collective-permute-start.11) | collective-permute-done | bytes 262176 | tf_op jit(solution)/shard_map/ppermute | solution.py:393
  44.6 1.7 %collective-permute-start.30 = (f32[4,32,128]{2,1,0:T(8,128)S(1)}, f32[4,32,128]{2,1,0:T(8,128)S(1)}, u32[]{:S(2)}, u32[]{:S(2)}) collective-permute-start(f32[4,32,128]{2,1,0:T(8,128)S(1)} %get-tuple-element.77), channel_id=1, source_target_pairs={{0,4},{4,0},{8,12},{12,8},{1,5},{5,1},{9,13},{13,9},{2,6},{6,2},{1... | collective-permute-start | bytes 196616 | tf_op jit(solution)/shard_map/ppermute | solution.py:393
  46.3 0.0 collective-permute-done.9.refs_1_
  46.3 2.6 %collective-permute-start.31 = (f32[4,32,128]{2,1,0:T(8,128)S(1)}, f32[4,32,128]{2,1,0:T(8,128)S(1)}, u32[]{:S(2)}, u32[]{:S(2)}) collective-permute-start(f32[4,32,128]{2,1,0:T(8,128)S(1)} %get-tuple-element.78), channel_id=1, source_target_pairs={{0,8},{4,12},{8,0},{12,4},{1,9},{5,13},{9,1},{13,5},{2,10},{6,14},... | collective-permute-start | bytes 196616 | tf_op jit(solution)/shard_map/ppermute | solution.py:393
  48.9 0.0 collective-permute-done.refs_1_
  48.9 0.1 collective-permute-start.32
  49.0 0.6 gram.6
  49.6 1.1 %collective-permute-done.1.refs_2_ = bf16[16,16,512]{2,1,0:T(8,128)(2,1)S(1)} collective-permute-done((bf16[16,16,512]{2,1,0:T(8,128)(2,1)S(1)}, bf16[16,16,512]{2,1,0:T(8,128)(2,1)S(1)}, u32[]{:S(2)}, u32[]{:S(2)}) %collective-permute-start.1) | collective-permute-done | bytes 262176 | tf_op jit(solution)/shard_map/ppermute | solution.py:393
  50.8 2.0 %collective-permute-start.21 = (f32[4,32,128]{2,1,0:T(8,128)S(1)}, f32[4,32,128]{2,1,0:T(8,128)S(1)}, u32[]{:S(2)}, u32[]{:S(2)}) collective-permute-start(f32[4,32,128]{2,1,0:T(8,128)S(1)} %get-tuple-element.68), channel_id=1, source_target_pairs={{0,4},{4,0},{8,12},{12,8},{1,5},{5,1},{9,13},{13,9},{2,6},{6,2},{1... | collective-permute-start | bytes 196616 | tf_op jit(solution)/shard_map/ppermute | solution.py:393
  52.8 3.1 %collective-permute-done.2.refs_3_ = bf16[16,16,512]{2,1,0:T(8,128)(2,1)S(1)} collective-permute-done((bf16[16,16,512]{2,1,0:T(8,128)(2,1)S(1)}, bf16[16,16,512]{2,1,0:T(8,128)(2,1)S(1)}, u32[]{:S(2)}, u32[]{:S(2)}) %collective-permute-start.2) | collective-permute-done | bytes 262176 | tf_op jit(solution)/shard_map/ppermute | solution.py:393
  55.9 2.7 %collective-permute-start.22 = (f32[4,32,128]{2,1,0:T(8,128)S(1)}, f32[4,32,128]{2,1,0:T(8,128)S(1)}, u32[]{:S(2)}, u32[]{:S(2)}) collective-permute-start(f32[4,32,128]{2,1,0:T(8,128)S(1)} %get-tuple-element.69), channel_id=1, source_target_pairs={{0,8},{4,12},{8,0},{12,4},{1,9},{5,13},{9,1},{13,5},{2,10},{6,14},... | collective-permute-start | bytes 196616 | tf_op jit(solution)/shard_map/ppermute | solution.py:393
  58.5 1.3 %collective-permute-start.23 = (f32[4,32,128]{2,1,0:T(8,128)S(1)}, f32[4,32,128]{2,1,0:T(8,128)S(1)}, u32[]{:S(2)}, u32[]{:S(2)}) collective-permute-start(f32[4,32,128]{2,1,0:T(8,128)S(1)} %get-tuple-element.70), channel_id=1, source_target_pairs={{0,12},{4,8},{8,4},{12,0},{1,13},{5,9},{9,5},{13,1},{2,14},{6,10},... | collective-permute-start | bytes 196616 | tf_op jit(solution)/shard_map/ppermute | solution.py:393
  59.9 0.6 gram.5
  60.5 0.3 collective-permute-start.12
  60.8 2.8 %collective-permute-start.13 = (f32[4,32,128]{2,1,0:T(8,128)S(1)}, f32[4,32,128]{2,1,0:T(8,128)S(1)}, u32[]{:S(2)}, u32[]{:S(2)}) collective-permute-start(f32[4,32,128]{2,1,0:T(8,128)S(1)} %get-tuple-element.60), channel_id=1, source_target_pairs={{0,8},{4,12},{8,0},{12,4},{1,9},{5,13},{9,1},{13,5},{2,10},{6,14},... | collective-permute-start | bytes 196616 | tf_op jit(solution)/shard_map/ppermute | solution.py:393
  63.6 1.3 %collective-permute-start.14 = (f32[4,32,128]{2,1,0:T(8,128)S(1)}, f32[4,32,128]{2,1,0:T(8,128)S(1)}, u32[]{:S(2)}, u32[]{:S(2)}) collective-permute-start(f32[4,32,128]{2,1,0:T(8,128)S(1)} %get-tuple-element.61), channel_id=1, source_target_pairs={{0,12},{4,8},{8,4},{12,0},{1,13},{5,9},{9,5},{13,1},{2,14},{6,10},... | collective-permute-start | bytes 196616 | tf_op jit(solution)/shard_map/ppermute | solution.py:393
  65.0 0.6 gram.4
  65.6 0.1 collective-permute-start.3
  65.7 5.2 %collective-permute-start.4 = (f32[4,32,128]{2,1,0:T(8,128)S(1)}, f32[4,32,128]{2,1,0:T(8,128)S(1)}, u32[]{:S(2)}, u32[]{:S(2)}) collective-permute-start(f32[4,32,128]{2,1,0:T(8,128)S(1)} %get-tuple-element.51), channel_id=1, source_target_pairs={{0,8},{4,12},{8,0},{12,4},{1,9},{5,13},{9,1},{13,5},{2,10},{6,14},... | collective-permute-start | bytes 196616 | tf_op jit(solution)/shard_map/ppermute | solution.py:393
  70.8 2.4 %filters.7.refs_0_ = f32[136,128]{1,0:T(8,128)S(1)} custom-call(f32[4,32,128]{2,1,0:T(8,128)S(1)} %get-tuple-element.76.refs_0_, f32[4,32,128]{2,1,0:T(8,128)S(1)} %collective-permute-done.30.refs_1_, f32[4,32,128]{2,1,0:T(8,128)S(1)} %collective-permute-done.31.refs_2_, f32[4,32,128]{2,1,0:T(8,128)S(1)} %collective-permute-done.32.refs_3_), custom_call_target="tpu_custom_call" | custom-call | flops 335544320 | bytes 327680 | tf_op jit(solution)/shard_map/filters/pallas_call | solution.py:315
  73.2 0.1 collective-permute-start.33
  73.3 1.0 collective-permute-start.34
  74.3 3.4 %collective-permute-start.5 = (f32[4,32,128]{2,1,0:T(8,128)S(1)}, f32[4,32,128]{2,1,0:T(8,128)S(1)}, u32[]{:S(2)}, u32[]{:S(2)}) collective-permute-start(f32[4,32,128]{2,1,0:T(8,128)S(1)} %get-tuple-element.52), channel_id=1, source_target_pairs={{0,12},{4,8},{8,4},{12,0},{1,13},{5,9},{9,5},{13,1},{2,14},{6,10},... | collective-permute-start | bytes 196616 | tf_op jit(solution)/shard_map/ppermute | solution.py:393
  77.7 2.4 %filters.6.refs_0_ = f32[136,128]{1,0:T(8,128)S(1)} custom-call(f32[4,32,128]{2,1,0:T(8,128)S(1)} %get-tuple-element.67.refs_0_, f32[4,32,128]{2,1,0:T(8,128)S(1)} %collective-permute-done.21.refs_1_, f32[4,32,128]{2,1,0:T(8,128)S(1)} %collective-permute-done.22.refs_2_, f32[4,32,128]{2,1,0:T(8,128)S(1)} %collective-permute-done.23.refs_3_), custom_call_target="tpu_custom_call" | custom-call | flops 335544320 | bytes 327680 | tf_op jit(solution)/shard_map/filters/pallas_call | solution.py:315
  80.1 0.5 collective-permute-start.35
  80.6 2.4 %filters.5.refs_0_ = f32[136,128]{1,0:T(8,128)S(1)} custom-call(f32[4,32,128]{2,1,0:T(8,128)S(1)} %get-tuple-element.58.refs_0_, f32[4,32,128]{2,1,0:T(8,128)S(1)} %collective-permute-done.12.refs_1_, f32[4,32,128]{2,1,0:T(8,128)S(1)} %collective-permute-done.13.refs_2_, f32[4,32,128]{2,1,0:T(8,128)S(1)} %collective-permute-done.14.refs_3_), custom_call_target="tpu_custom_call" | custom-call | flops 335544320 | bytes 327680 | tf_op jit(solution)/shard_map/filters/pallas_call | solution.py:315
  83.0 4.0 %collective-permute-start.25 = (f32[136,128]{1,0:T(8,128)S(1)}, f32[136,128]{1,0:T(8,128)S(1)}, u32[]{:S(2)}, u32[]{:S(2)}) collective-permute-start(f32[136,128]{1,0:T(8,128)S(1)} %filters.6.refs_0_), channel_id=1, source_target_pairs={{0,8},{4,12},{8,0},{12,4},{1,9},{5,13},{9,1},{13,5},{2,10},{6,14},... | collective-permute-start | bytes 208904 | tf_op jit(solution)/shard_map/ppermute | solution.py:393
  87.0 0.4 collective-permute-start.26
  87.4 0.2 collective-permute-start.15
  87.7 3.7 %collective-permute-start.16 = (f32[136,128]{1,0:T(8,128)S(1)}, f32[136,128]{1,0:T(8,128)S(1)}, u32[]{:S(2)}, u32[]{:S(2)}) collective-permute-start(f32[136,128]{1,0:T(8,128)S(1)} %filters.5.refs_0_), channel_id=1, source_target_pairs={{0,8},{4,12},{8,0},{12,4},{1,9},{5,13},{9,1},{13,5},{2,10},{6,14},... | collective-permute-start | bytes 208904 | tf_op jit(solution)/shard_map/ppermute | solution.py:393
  91.4 0.4 collective-permute-start.17
  91.8 2.4 %filters.4.refs_0_ = f32[136,128]{1,0:T(8,128)S(1)} custom-call(f32[4,32,128]{2,1,0:T(8,128)S(1)} %get-tuple-element.49.refs_0_, f32[4,32,128]{2,1,0:T(8,128)S(1)} %collective-permute-done.3.refs_1_, f32[4,32,128]{2,1,0:T(8,128)S(1)} %collective-permute-done.4.refs_2_, f32[4,32,128]{2,1,0:T(8,128)S(1)} %collective-permute-done.5.refs_3_), custom_call_target="tpu_custom_call" | custom-call | flops 335544320 | bytes 327680 | tf_op jit(solution)/shard_map/filters/pallas_call | solution.py:315
  94.2 0.3 collective-permute-start.6
  94.5 3.8 %collective-permute-start.7 = (f32[136,128]{1,0:T(8,128)S(1)}, f32[136,128]{1,0:T(8,128)S(1)}, u32[]{:S(2)}, u32[]{:S(2)}) collective-permute-start(f32[136,128]{1,0:T(8,128)S(1)} %filters.4.refs_0_), channel_id=1, source_target_pairs={{0,8},{4,12},{8,0},{12,4},{1,9},{5,13},{9,1},{13,5},{2,10},{6,14},... | collective-permute-start | bytes 208904 | tf_op jit(solution)/shard_map/ppermute | solution.py:393
  98.3 0.4 collective-permute-start.8
  98.7 2.9 %energy.4 = (f32[64,256]{1,0:T(8,128)}, f32[64,2,64,64]{3,2,1,0:T(8,128)}) custom-call(bf16[16,64,512]{2,1,0:T(8,128)(2,1)S(1)} %get-tuple-element.75.merged, f32[136,128]{1,0:T(8,128)S(1)} %filters.7.refs_0_, f32[136,128]{1,0:T(8,128)S(1)} %collective-permute-done.33.refs_1_, f32[136,128]{1,0:T(8,128)S(1)} %collective-permute-done.34.refs_2_, ...), custom_call_target="tpu_custom_call" | custom-call | flops 134217728 | bytes 2621440 | tf_op jit(solution)/shard_map/energy/pallas_call | solution.py:364
  101.6 2.9 %energy.5 = (f32[64,256]{1,0:T(8,128)}, f32[64,2,64,64]{3,2,1,0:T(8,128)}) custom-call(bf16[16,64,512]{2,1,0:T(8,128)(2,1)S(1)} %get-tuple-element.66.merged, f32[136,128]{1,0:T(8,128)S(1)} %filters.6.refs_0_, f32[136,128]{1,0:T(8,128)S(1)} %collective-permute-done.24.refs_1_, ...), custom_call_target="tpu_custom_call", output_to_operand_aliasing={{0}: (5, {}), {1}: (6, {})} | custom-call | flops 134217728 | bytes 2621440 | tf_op jit(solution)/shard_map/energy/pallas_call | solution.py:364
  104.5 2.9 %energy.6 = (f32[64,256]{1,0:T(8,128)}, f32[64,2,64,64]{3,2,1,0:T(8,128)}) custom-call(bf16[16,64,512]{2,1,0:T(8,128)(2,1)S(1)} %get-tuple-element.57.merged, f32[136,128]{1,0:T(8,128)S(1)} %filters.5.refs_0_, f32[136,128]{1,0:T(8,128)S(1)} %collective-permute-done.15.refs_1_, ...), custom_call_target="tpu_custom_call", output_to_operand_aliasing={{0}: (5, {}), {1}: (6, {})} | custom-call | flops 134217728 | bytes 2621440 | tf_op jit(solution)/shard_map/energy/pallas_call | solution.py:364
  107.4 2.9 %energy.7 = (f32[64,256]{1,0:T(8,128)}, f32[64,2,64,64]{3,2,1,0:T(8,128)}) custom-call(bf16[16,64,512]{2,1,0:T(8,128)(2,1)S(1)} %get-tuple-element.48.merged, f32[136,128]{1,0:T(8,128)S(1)} %filters.4.refs_0_, f32[136,128]{1,0:T(8,128)S(1)} %collective-permute-done.6.refs_1_, ...), custom_call_target="tpu_custom_call", output_to_operand_aliasing={{0}: (5, {}), {1}: (6, {})} | custom-call | flops 134217728 | bytes 2621440 | tf_op jit(solution)/shard_map/energy/pallas_call | solution.py:364
  (30 shorter events, 0.1 us)
Async XLA Ops:
  0.6 2.2 %copy-start = (bf16[16,512,256]{2,1,0:T(8,128)(2,1)S(1)}, bf16[16,512,256]{2,1,0:T(8,128)(2,1)}, u32[]{:S(2)}) copy-start(bf16[16,512,256]{2,1,0:T(8,128)(2,1)} %snap_ref.7) | copy-start | bytes 12582916
  2.8 0.7 copy-start.1
  3.5 0.7 copy-start.2
  6.8 7.9 %collective-permute-start.27 = (bf16[16,16,512]{2,1,0:T(8,128)(2,1)S(1)}, bf16[16,16,512]{2,1,0:T(8,128)(2,1)S(1)}, u32[]{:S(2)}, u32[]{:S(2)}) collective-permute-start(bf16[16,16,512]{2,1,0:T(8,128)(2,1)S(1)} %get-tuple-element.72), channel_id=1, source_target_pairs={{0,1},{1,0},{2,3},{3,2},{4,5},{5,4},{6,7},{7,6},{8,9},{9,8},{10,11... | collective-permute-start | bytes 786440 | tf_op jit(solution)/shard_map/ppermute | solution.py:393
  7.3 10.1 %collective-permute-start.28 = (bf16[16,16,512]{2,1,0:T(8,128)(2,1)S(1)}, bf16[16,16,512]{2,1,0:T(8,128)(2,1)S(1)}, u32[]{:S(2)}, u32[]{:S(2)}) collective-permute-start(bf16[16,16,512]{2,1,0:T(8,128)(2,1)S(1)} %get-tuple-element.73), channel_id=1, source_target_pairs={{0,2},{1,3},{2,0},{3,1},{4,6},{5,7},{6,4},{7,5},{8,10},{9,11},{10,... | collective-permute-start | bytes 786440 | tf_op jit(solution)/shard_map/ppermute | solution.py:393
  9.9 12.3 %collective-permute-start.29 = (bf16[16,16,512]{2,1,0:T(8,128)(2,1)S(1)}, bf16[16,16,512]{2,1,0:T(8,128)(2,1)S(1)}, u32[]{:S(2)}, u32[]{:S(2)}) collective-permute-start(bf16[16,16,512]{2,1,0:T(8,128)(2,1)S(1)} %get-tuple-element.74), channel_id=1, source_target_pairs={{0,3},{1,2},{2,1},{3,0},{4,7},{5,6},{6,5},{7,4},{8,11},{9,10},{10,... | collective-permute-start | bytes 786440 | tf_op jit(solution)/shard_map/ppermute | solution.py:393
  12.6 14.3 %collective-permute-start.18 = (bf16[16,16,512]{2,1,0:T(8,128)(2,1)S(1)}, bf16[16,16,512]{2,1,0:T(8,128)(2,1)S(1)}, u32[]{:S(2)}, u32[]{:S(2)}) collective-permute-start(bf16[16,16,512]{2,1,0:T(8,128)(2,1)S(1)} %get-tuple-element.63), channel_id=1, source_target_pairs={{0,1},{1,0},{2,3},{3,2},{4,5},{5,4},{6,7},{7,6},{8,9},{9,8},{10,11... | collective-permute-start | bytes 786440 | tf_op jit(solution)/shard_map/ppermute | solution.py:393
  12.8 15.5 %collective-permute-start.19 = (bf16[16,16,512]{2,1,0:T(8,128)(2,1)S(1)}, bf16[16,16,512]{2,1,0:T(8,128)(2,1)S(1)}, u32[]{:S(2)}, u32[]{:S(2)}) collective-permute-start(bf16[16,16,512]{2,1,0:T(8,128)(2,1)S(1)} %get-tuple-element.64), channel_id=1, source_target_pairs={{0,2},{1,3},{2,0},{3,1},{4,6},{5,7},{6,4},{7,5},{8,10},{9,11},{10,... | collective-permute-start | bytes 786440 | tf_op jit(solution)/shard_map/ppermute | solution.py:393
  14.8 18.6 %collective-permute-start.20 = (bf16[16,16,512]{2,1,0:T(8,128)(2,1)S(1)}, bf16[16,16,512]{2,1,0:T(8,128)(2,1)S(1)}, u32[]{:S(2)}, u32[]{:S(2)}) collective-permute-start(bf16[16,16,512]{2,1,0:T(8,128)(2,1)S(1)} %get-tuple-element.65), channel_id=1, source_target_pairs={{0,3},{1,2},{2,1},{3,0},{4,7},{5,6},{6,5},{7,4},{8,11},{9,10},{10,... | collective-permute-start | bytes 786440 | tf_op jit(solution)/shard_map/ppermute | solution.py:393
  17.4 22.1 %collective-permute-start.10 = (bf16[16,16,512]{2,1,0:T(8,128)(2,1)S(1)}, bf16[16,16,512]{2,1,0:T(8,128)(2,1)S(1)}, u32[]{:S(2)}, u32[]{:S(2)}) collective-permute-start(bf16[16,16,512]{2,1,0:T(8,128)(2,1)S(1)} %get-tuple-element.55), channel_id=1, source_target_pairs={{0,2},{1,3},{2,0},{3,1},{4,6},{5,7},{6,4},{7,5},{8,10},{9,11},{10,... | collective-permute-start | bytes 786440 | tf_op jit(solution)/shard_map/ppermute | solution.py:393
  22.2 22.5 %collective-permute-start.11 = (bf16[16,16,512]{2,1,0:T(8,128)(2,1)S(1)}, bf16[16,16,512]{2,1,0:T(8,128)(2,1)S(1)}, u32[]{:S(2)}, u32[]{:S(2)}) collective-permute-start(bf16[16,16,512]{2,1,0:T(8,128)(2,1)S(1)} %get-tuple-element.56), channel_id=1, source_target_pairs={{0,3},{1,2},{2,1},{3,0},{4,7},{5,6},{6,5},{7,4},{8,11},{9,10},{10,... | collective-permute-start | bytes 786440 | tf_op jit(solution)/shard_map/ppermute | solution.py:393
  26.9 19.4 %collective-permute-start.9 = (bf16[16,16,512]{2,1,0:T(8,128)(2,1)S(1)}, bf16[16,16,512]{2,1,0:T(8,128)(2,1)S(1)}, u32[]{:S(2)}, u32[]{:S(2)}) collective-permute-start(bf16[16,16,512]{2,1,0:T(8,128)(2,1)S(1)} %get-tuple-element.54), channel_id=1, source_target_pairs={{0,1},{1,0},{2,3},{3,2},{4,5},{5,4},{6,7},{7,6},{8,9},{9,8},{10,11... | collective-permute-start | bytes 786440 | tf_op jit(solution)/shard_map/ppermute | solution.py:393
  28.3 20.6 %collective-permute-start = (bf16[16,16,512]{2,1,0:T(8,128)(2,1)S(1)}, bf16[16,16,512]{2,1,0:T(8,128)(2,1)S(1)}, u32[]{:S(2)}, u32[]{:S(2)}) collective-permute-start(bf16[16,16,512]{2,1,0:T(8,128)(2,1)S(1)} %get-tuple-element.45), channel_id=1, source_target_pairs={{0,1},{1,0},{2,3},{3,2},{4,5},{5,4},{6,7},{7,6},{8,9},{9,8},{10,11... | collective-permute-start | bytes 786440 | tf_op jit(solution)/shard_map/ppermute | solution.py:393
  33.4 17.4 %collective-permute-start.1 = (bf16[16,16,512]{2,1,0:T(8,128)(2,1)S(1)}, bf16[16,16,512]{2,1,0:T(8,128)(2,1)S(1)}, u32[]{:S(2)}, u32[]{:S(2)}) collective-permute-start(bf16[16,16,512]{2,1,0:T(8,128)(2,1)S(1)} %get-tuple-element.46), channel_id=1, source_target_pairs={{0,2},{1,3},{2,0},{3,1},{4,6},{5,7},{6,4},{7,5},{8,10},{9,11},{10,... | collective-permute-start | bytes 786440 | tf_op jit(solution)/shard_map/ppermute | solution.py:393
  39.5 16.3 %collective-permute-start.2 = (bf16[16,16,512]{2,1,0:T(8,128)(2,1)S(1)}, bf16[16,16,512]{2,1,0:T(8,128)(2,1)S(1)}, u32[]{:S(2)}, u32[]{:S(2)}) collective-permute-start(bf16[16,16,512]{2,1,0:T(8,128)(2,1)S(1)} %get-tuple-element.47), channel_id=1, source_target_pairs={{0,3},{1,2},{2,1},{3,0},{4,7},{5,6},{6,5},{7,4},{8,11},{9,10},{10,... | collective-permute-start | bytes 786440 | tf_op jit(solution)/shard_map/ppermute | solution.py:393
  44.6 13.9 %collective-permute-start.30 = (f32[4,32,128]{2,1,0:T(8,128)S(1)}, f32[4,32,128]{2,1,0:T(8,128)S(1)}, u32[]{:S(2)}, u32[]{:S(2)}) collective-permute-start(f32[4,32,128]{2,1,0:T(8,128)S(1)} %get-tuple-element.77), channel_id=1, source_target_pairs={{0,4},{4,0},{8,12},{12,8},{1,5},{5,1},{9,13},{13,9},{2,6},{6,2},{1... | collective-permute-start | bytes 196616 | tf_op jit(solution)/shard_map/ppermute | solution.py:393
  46.3 14.2 %collective-permute-start.31 = (f32[4,32,128]{2,1,0:T(8,128)S(1)}, f32[4,32,128]{2,1,0:T(8,128)S(1)}, u32[]{:S(2)}, u32[]{:S(2)}) collective-permute-start(f32[4,32,128]{2,1,0:T(8,128)S(1)} %get-tuple-element.78), channel_id=1, source_target_pairs={{0,8},{4,12},{8,0},{12,4},{1,9},{5,13},{9,1},{13,5},{2,10},{6,14},... | collective-permute-start | bytes 196616 | tf_op jit(solution)/shard_map/ppermute | solution.py:393
  48.9 11.9 %collective-permute-start.32 = (f32[4,32,128]{2,1,0:T(8,128)S(1)}, f32[4,32,128]{2,1,0:T(8,128)S(1)}, u32[]{:S(2)}, u32[]{:S(2)}) collective-permute-start(f32[4,32,128]{2,1,0:T(8,128)S(1)} %get-tuple-element.79), channel_id=1, source_target_pairs={{0,12},{4,8},{8,4},{12,0},{1,13},{5,9},{9,5},{13,1},{2,14},{6,10},... | collective-permute-start | bytes 196616 | tf_op jit(solution)/shard_map/ppermute | solution.py:393
  50.8 12.8 %collective-permute-start.21 = (f32[4,32,128]{2,1,0:T(8,128)S(1)}, f32[4,32,128]{2,1,0:T(8,128)S(1)}, u32[]{:S(2)}, u32[]{:S(2)}) collective-permute-start(f32[4,32,128]{2,1,0:T(8,128)S(1)} %get-tuple-element.68), channel_id=1, source_target_pairs={{0,4},{4,0},{8,12},{12,8},{1,5},{5,1},{9,13},{13,9},{2,6},{6,2},{1... | collective-permute-start | bytes 196616 | tf_op jit(solution)/shard_map/ppermute | solution.py:393
  55.9 9.7 %collective-permute-start.22 = (f32[4,32,128]{2,1,0:T(8,128)S(1)}, f32[4,32,128]{2,1,0:T(8,128)S(1)}, u32[]{:S(2)}, u32[]{:S(2)}) collective-permute-start(f32[4,32,128]{2,1,0:T(8,128)S(1)} %get-tuple-element.69), channel_id=1, source_target_pairs={{0,8},{4,12},{8,0},{12,4},{1,9},{5,13},{9,1},{13,5},{2,10},{6,14},... | collective-permute-start | bytes 196616 | tf_op jit(solution)/shard_map/ppermute | solution.py:393
  58.5 7.1 %collective-permute-start.23 = (f32[4,32,128]{2,1,0:T(8,128)S(1)}, f32[4,32,128]{2,1,0:T(8,128)S(1)}, u32[]{:S(2)}, u32[]{:S(2)}) collective-permute-start(f32[4,32,128]{2,1,0:T(8,128)S(1)} %get-tuple-element.70), channel_id=1, source_target_pairs={{0,12},{4,8},{8,4},{12,0},{1,13},{5,9},{9,5},{13,1},{2,14},{6,10},... | collective-permute-start | bytes 196616 | tf_op jit(solution)/shard_map/ppermute | solution.py:393
  60.5 12.7 %collective-permute-start.12 = (f32[4,32,128]{2,1,0:T(8,128)S(1)}, f32[4,32,128]{2,1,0:T(8,128)S(1)}, u32[]{:S(2)}, u32[]{:S(2)}) collective-permute-start(f32[4,32,128]{2,1,0:T(8,128)S(1)} %get-tuple-element.59), channel_id=1, source_target_pairs={{0,4},{4,0},{8,12},{12,8},{1,5},{5,1},{9,13},{13,9},{2,6},{6,2},{1... | collective-permute-start | bytes 196616 | tf_op jit(solution)/shard_map/ppermute | solution.py:393
  60.8 12.5 %collective-permute-start.13 = (f32[4,32,128]{2,1,0:T(8,128)S(1)}, f32[4,32,128]{2,1,0:T(8,128)S(1)}, u32[]{:S(2)}, u32[]{:S(2)}) collective-permute-start(f32[4,32,128]{2,1,0:T(8,128)S(1)} %get-tuple-element.60), channel_id=1, source_target_pairs={{0,8},{4,12},{8,0},{12,4},{1,9},{5,13},{9,1},{13,5},{2,10},{6,14},... | collective-permute-start | bytes 196616 | tf_op jit(solution)/shard_map/ppermute | solution.py:393
  63.6 10.7 %collective-permute-start.14 = (f32[4,32,128]{2,1,0:T(8,128)S(1)}, f32[4,32,128]{2,1,0:T(8,128)S(1)}, u32[]{:S(2)}, u32[]{:S(2)}) collective-permute-start(f32[4,32,128]{2,1,0:T(8,128)S(1)} %get-tuple-element.61), channel_id=1, source_target_pairs={{0,12},{4,8},{8,4},{12,0},{1,13},{5,9},{9,5},{13,1},{2,14},{6,10},... | collective-permute-start | bytes 196616 | tf_op jit(solution)/shard_map/ppermute | solution.py:393
  65.6 14.5 %collective-permute-start.3 = (f32[4,32,128]{2,1,0:T(8,128)S(1)}, f32[4,32,128]{2,1,0:T(8,128)S(1)}, u32[]{:S(2)}, u32[]{:S(2)}) collective-permute-start(f32[4,32,128]{2,1,0:T(8,128)S(1)} %get-tuple-element.50), channel_id=1, source_target_pairs={{0,4},{4,0},{8,12},{12,8},{1,5},{5,1},{9,13},{13,9},{2,6},{6,2},{1... | collective-permute-start | bytes 196616 | tf_op jit(solution)/shard_map/ppermute | solution.py:393
  65.7 14.9 %collective-permute-start.4 = (f32[4,32,128]{2,1,0:T(8,128)S(1)}, f32[4,32,128]{2,1,0:T(8,128)S(1)}, u32[]{:S(2)}, u32[]{:S(2)}) collective-permute-start(f32[4,32,128]{2,1,0:T(8,128)S(1)} %get-tuple-element.51), channel_id=1, source_target_pairs={{0,8},{4,12},{8,0},{12,4},{1,9},{5,13},{9,1},{13,5},{2,10},{6,14},... | collective-permute-start | bytes 196616 | tf_op jit(solution)/shard_map/ppermute | solution.py:393
  73.2 13.8 %collective-permute-start.33 = (f32[136,128]{1,0:T(8,128)S(1)}, f32[136,128]{1,0:T(8,128)S(1)}, u32[]{:S(2)}, u32[]{:S(2)}) collective-permute-start(f32[136,128]{1,0:T(8,128)S(1)} %filters.7.refs_0_), channel_id=1, source_target_pairs={{0,4},{4,0},{8,12},{12,8},{1,5},{5,1},{9,13},{13,9},{2,6},{6,2},{1... | collective-permute-start | bytes 208904 | tf_op jit(solution)/shard_map/ppermute | solution.py:393
  73.3 14.1 %collective-permute-start.34 = (f32[136,128]{1,0:T(8,128)S(1)}, f32[136,128]{1,0:T(8,128)S(1)}, u32[]{:S(2)}, u32[]{:S(2)}) collective-permute-start(f32[136,128]{1,0:T(8,128)S(1)} %filters.7.refs_0_), channel_id=1, source_target_pairs={{0,8},{4,12},{8,0},{12,4},{1,9},{5,13},{9,1},{13,5},{2,10},{6,14},... | collective-permute-start | bytes 208904 | tf_op jit(solution)/shard_map/ppermute | solution.py:393
  74.3 8.7 %collective-permute-start.5 = (f32[4,32,128]{2,1,0:T(8,128)S(1)}, f32[4,32,128]{2,1,0:T(8,128)S(1)}, u32[]{:S(2)}, u32[]{:S(2)}) collective-permute-start(f32[4,32,128]{2,1,0:T(8,128)S(1)} %get-tuple-element.52), channel_id=1, source_target_pairs={{0,12},{4,8},{8,4},{12,0},{1,13},{5,9},{9,5},{13,1},{2,14},{6,10},... | collective-permute-start | bytes 196616 | tf_op jit(solution)/shard_map/ppermute | solution.py:393
  80.1 7.6 %collective-permute-start.35 = (f32[136,128]{1,0:T(8,128)S(1)}, f32[136,128]{1,0:T(8,128)S(1)}, u32[]{:S(2)}, u32[]{:S(2)}) collective-permute-start(f32[136,128]{1,0:T(8,128)S(1)} %filters.7.refs_0_), channel_id=1, source_target_pairs={{0,12},{4,8},{8,4},{12,0},{1,13},{5,9},{9,5},{13,1},{2,14},{6,10},... | collective-permute-start | bytes 208904 | tf_op jit(solution)/shard_map/ppermute | solution.py:393
  80.6 10.8 %collective-permute-start.24 = (f32[136,128]{1,0:T(8,128)S(1)}, f32[136,128]{1,0:T(8,128)S(1)}, u32[]{:S(2)}, u32[]{:S(2)}) collective-permute-start(f32[136,128]{1,0:T(8,128)S(1)} %filters.6.refs_0_), channel_id=1, source_target_pairs={{0,4},{4,0},{8,12},{12,8},{1,5},{5,1},{9,13},{13,9},{2,6},{6,2},{1... | collective-permute-start | bytes 208904 | tf_op jit(solution)/shard_map/ppermute | solution.py:393
  83.0 11.2 %collective-permute-start.25 = (f32[136,128]{1,0:T(8,128)S(1)}, f32[136,128]{1,0:T(8,128)S(1)}, u32[]{:S(2)}, u32[]{:S(2)}) collective-permute-start(f32[136,128]{1,0:T(8,128)S(1)} %filters.6.refs_0_), channel_id=1, source_target_pairs={{0,8},{4,12},{8,0},{12,4},{1,9},{5,13},{9,1},{13,5},{2,10},{6,14},... | collective-permute-start | bytes 208904 | tf_op jit(solution)/shard_map/ppermute | solution.py:393
  87.0 7.5 %collective-permute-start.26 = (f32[136,128]{1,0:T(8,128)S(1)}, f32[136,128]{1,0:T(8,128)S(1)}, u32[]{:S(2)}, u32[]{:S(2)}) collective-permute-start(f32[136,128]{1,0:T(8,128)S(1)} %filters.6.refs_0_), channel_id=1, source_target_pairs={{0,12},{4,8},{8,4},{12,0},{1,13},{5,9},{9,5},{13,1},{2,14},{6,10},... | collective-permute-start | bytes 208904 | tf_op jit(solution)/shard_map/ppermute | solution.py:393
  87.4 10.8 %collective-permute-start.15 = (f32[136,128]{1,0:T(8,128)S(1)}, f32[136,128]{1,0:T(8,128)S(1)}, u32[]{:S(2)}, u32[]{:S(2)}) collective-permute-start(f32[136,128]{1,0:T(8,128)S(1)} %filters.5.refs_0_), channel_id=1, source_target_pairs={{0,4},{4,0},{8,12},{12,8},{1,5},{5,1},{9,13},{13,9},{2,6},{6,2},{1... | collective-permute-start | bytes 208904 | tf_op jit(solution)/shard_map/ppermute | solution.py:393
  87.7 16.8 %collective-permute-start.16 = (f32[136,128]{1,0:T(8,128)S(1)}, f32[136,128]{1,0:T(8,128)S(1)}, u32[]{:S(2)}, u32[]{:S(2)}) collective-permute-start(f32[136,128]{1,0:T(8,128)S(1)} %filters.5.refs_0_), channel_id=1, source_target_pairs={{0,8},{4,12},{8,0},{12,4},{1,9},{5,13},{9,1},{13,5},{2,10},{6,14},... | collective-permute-start | bytes 208904 | tf_op jit(solution)/shard_map/ppermute | solution.py:393
  91.4 13.1 %collective-permute-start.17 = (f32[136,128]{1,0:T(8,128)S(1)}, f32[136,128]{1,0:T(8,128)S(1)}, u32[]{:S(2)}, u32[]{:S(2)}) collective-permute-start(f32[136,128]{1,0:T(8,128)S(1)} %filters.5.refs_0_), channel_id=1, source_target_pairs={{0,12},{4,8},{8,4},{12,0},{1,13},{5,9},{9,5},{13,1},{2,14},{6,10},... | collective-permute-start | bytes 208904 | tf_op jit(solution)/shard_map/ppermute | solution.py:393
  94.2 13.2 %collective-permute-start.6 = (f32[136,128]{1,0:T(8,128)S(1)}, f32[136,128]{1,0:T(8,128)S(1)}, u32[]{:S(2)}, u32[]{:S(2)}) collective-permute-start(f32[136,128]{1,0:T(8,128)S(1)} %filters.4.refs_0_), channel_id=1, source_target_pairs={{0,4},{4,0},{8,12},{12,8},{1,5},{5,1},{9,13},{13,9},{2,6},{6,2},{1... | collective-permute-start | bytes 208904 | tf_op jit(solution)/shard_map/ppermute | solution.py:393
  94.5 12.9 %collective-permute-start.7 = (f32[136,128]{1,0:T(8,128)S(1)}, f32[136,128]{1,0:T(8,128)S(1)}, u32[]{:S(2)}, u32[]{:S(2)}) collective-permute-start(f32[136,128]{1,0:T(8,128)S(1)} %filters.4.refs_0_), channel_id=1, source_target_pairs={{0,8},{4,12},{8,0},{12,4},{1,9},{5,13},{9,1},{13,5},{2,10},{6,14},... | collective-permute-start | bytes 208904 | tf_op jit(solution)/shard_map/ppermute | solution.py:393
  98.3 9.1 %collective-permute-start.8 = (f32[136,128]{1,0:T(8,128)S(1)}, f32[136,128]{1,0:T(8,128)S(1)}, u32[]{:S(2)}, u32[]{:S(2)}) collective-permute-start(f32[136,128]{1,0:T(8,128)S(1)} %filters.4.refs_0_), channel_id=1, source_target_pairs={{0,12},{4,8},{8,4},{12,0},{1,13},{5,9},{9,5},{13,1},{2,14},{6,10},... | collective-permute-start | bytes 208904 | tf_op jit(solution)/shard_map/ppermute | solution.py:393

commit v2 on v1

--- a/solution.py
+++ b/solution.py
@@ -21,6 +21,21 @@
 
 def whole_spec():
     return pl.BlockSpec(memory_space=pltpu.VMEM)
+
+
+TOKEN = jax.ShapeDtypeStruct((8, LANES), F32)
+
+
+def light():
+    return pl.CostEstimate(flops=1024, bytes_accessed=1024, transcendentals=0)
+
+
+def in_hbm(x):
+    return pltpu.with_memory_space_constraint(x, pltpu.HBM)
+
+
+def any_spec():
+    return pl.BlockSpec(memory_space=pl.ANY)
 
 
 def dot(a, b):
@@ -50,86 +65,94 @@
     return c1, s1
 
 
-def transform_kernel(peers, count, first, step_blocks, freq_ref, root_ref, snap_ref, *refs):
-    outs, (table, wide) = refs[:peers], refs[peers:]
+def transform_kernel(peers, count, first, group, *refs):
+    freq_hbm, weight_hbm, snap_hbm = refs[:3]
+    outs, token = refs[-peers - 8 : -8], refs[-8]
+    freq, weight, snap, table, wide, small_sem, snap_sem = refs[-7:]
+    blocks, length, entries = snap.shape
+    steps = blocks // group
+    get_freq = pltpu.make_async_copy(freq_hbm, freq, small_sem.at[0])
+    get_weight = pltpu.make_async_copy(weight_hbm, weight, small_sem.at[1])
+    get_snap = [
+        pltpu.make_async_copy(
+            snap_hbm.at[pl.ds(i * group, group)], snap.at[pl.ds(i * group, group)], snap_sem.at[i]
+        )
+        for i in range(steps)
+    ]
+    token[...] = jnp.zeros_like(token)
+    get_freq.start()
+    for get in get_snap:
+        get.start()
+    get_weight.start()
+
     me = lax.axis_index("tm")
-    length = snap_ref.shape[1]
-    entries = snap_ref.shape[2]
     rows = peers * count
-    per_peer = freq_ref.shape[0] // peers
-    step = pl.program_id(0)
-
-    @pl.when(step == 0)
-    def _():
-        times = lax.broadcasted_iota(jnp.int32, (8, length), 1)
-        sub = lax.broadcasted_iota(jnp.int32, (8, length), 0)
-        window = 0.5 - 0.5 * cos_sin(times, length)[0]
-        scaled = window / F32(math.sqrt(0.375 * length))
-
-        def eight(group):
-            base = group * 8
-            peer = base // count
-            start = jnp.bitwise_xor(me, peer) * per_peer + first + (base - peer * count)
-            k = jnp.zeros((8, length), jnp.int32)
-            for i in range(8):
-                k = jnp.where(sub == i, freq_ref[start + i], k)
-            cos, sin = cos_sin((k * times) & (length - 1), length)
-            return scaled * cos, -(scaled * sin)
-
-        for pair in range(rows // 16):
-            re0, im0 = eight(2 * pair)
-            re1, im1 = eight(2 * pair + 1)
-            table[16 * pair : 16 * pair + 16, :] = jnp.concatenate([re0, re1], 0).astype(BF16)
-            table[rows + 16 * pair : rows + 16 * pair + 16, :] = jnp.concatenate(
-                [im0, im1], 0
-            ).astype(BF16)
-
-    root = jnp.sqrt(root_ref[...])
-    blocks = outs[0].shape[1]
+    per_peer = freq.shape[0] // peers
+    times = lax.broadcasted_iota(jnp.int32, (8, length), 1)
+    sub = lax.broadcasted_iota(jnp.int32, (8, length), 0)
+    window = 0.5 - 0.5 * cos_sin(times, length)[0]
+    scaled = window / F32(math.sqrt(0.375 * length))
+    get_freq.wait()
+
+    def eight(index):
+        base = index * 8
+        peer = base // count
+        start = jnp.bitwise_xor(me, peer) * per_peer + first + (base - peer * count)
+        k = jnp.zeros((8, length), jnp.int32)
+        for i in range(8):
+            k = jnp.where(sub == i, freq[start + i], k)
+        cos, sin = cos_sin((k * times) & (length - 1), length)
+        return scaled * cos, -(scaled * sin)
+
+    for pair in range(rows // 16):
+        re0, im0 = eight(2 * pair)
+        re1, im1 = eight(2 * pair + 1)
+        table[16 * pair : 16 * pair + 16, :] = jnp.concatenate([re0, re1], 0).astype(BF16)
+        table[rows + 16 * pair : rows + 16 * pair + 16, :] = jnp.concatenate(
+            [im0, im1], 0
+        ).astype(BF16)
+
+    get_weight.wait()
+    root = jnp.sqrt(weight[...])
     tiles = entries // LANES
-    for i in range(step_blocks):
-        spec = dot(table[...], snap_ref[i]) * root
-        b = step * step_blocks + i
-        for tile in range(tiles):
-            lanes = slice(tile * LANES, (tile + 1) * LANES)
-            wide[tile, pl.ds(b, rows, stride=blocks), :] = spec[:rows, lanes]
-            wide[tiles + tile, pl.ds(b, rows, stride=blocks), :] = spec[rows:, lanes]
-
-    @pl.when(step == pl.num_programs(0) - 1)
-    def _():
-        for peer in range(peers):
-            for j in range(count):
-                at = (peer * count + j) * blocks
-                for tile in range(2 * tiles):
-                    lanes = slice(tile * LANES, (tile + 1) * LANES)
-                    outs[peer][j, :, lanes] = wide[tile, at : at + blocks, :].astype(BF16)
-
-
-def transform(snapshots, weight, freq_index, peers, count, first):
+    for step in range(steps):
+        get_snap[step].wait()
+        for b in range(step * group, (step + 1) * group):
+            spec = dot(table[...], snap[b]) * root
+            for tile in range(tiles):
+                lanes = slice(tile * LANES, (tile + 1) * LANES)
+                wide[tile, pl.ds(b, rows, stride=blocks), :] = spec[:rows, lanes]
+                wide[tiles + tile, pl.ds(b, rows, stride=blocks), :] = spec[rows:, lanes]
+    for peer in range(peers):
+        for j in range(count):
+            at = (peer * count + j) * blocks
+            for tile in range(2 * tiles):
+                lanes = slice(tile * LANES, (tile + 1) * LANES)
+                outs[peer][j, :, lanes] = wide[tile, at : at + blocks, :].astype(BF16)
+
+
+def transform(snapshots, weight, freq_index, peers, count, first, after):
     blocks, length, entries = snapshots.shape
-    step_blocks = 4
+    group = min(blocks, 4)
+    hbm = pl.BlockSpec(memory_space=pltpu.HBM)
     return pl.pallas_call(
-        functools.partial(transform_kernel, peers, count, first, step_blocks),
-        grid=(blocks // step_blocks,),
-        in_specs=[
-            pl.BlockSpec(memory_space=pltpu.SMEM),
-            pl.BlockSpec((1, entries), lambda b: (0, 0)),
-            pl.BlockSpec((step_blocks, length, entries), lambda b: (b, 0, 0)),
-        ],
-        out_specs=[pl.BlockSpec((count, blocks, 2 * entries), lambda b: (0, 0, 0))] * peers,
-        out_shape=[jax.ShapeDtypeStruct((count, blocks, 2 * entries), BF16)] * peers,
+        functools.partial(transform_kernel, peers, count, first, group),
+        in_specs=[hbm] * 3 + [any_spec()] * len(after),
+        out_specs=[whole_spec()] * (peers + 1),
+        out_shape=[jax.ShapeDtypeStruct((count, blocks, 2 * entries), BF16)] * peers + [TOKEN],
         scratch_shapes=[
+            pltpu.SMEM(freq_index.shape, jnp.int32),
+            pltpu.VMEM(weight.shape, F32),
+            pltpu.VMEM(snapshots.shape, BF16),
             pltpu.VMEM((2 * peers * count, length), BF16),
             pltpu.VMEM((2 * entries // LANES, peers * count * blocks, LANES), F32),
+            pltpu.SemaphoreType.DMA((2,)),
+            pltpu.SemaphoreType.DMA((blocks // group,)),
         ],
         compiler_params=params(),
-        cost_estimate=pl.CostEstimate(
-            flops=4 * peers * count * length * entries * blocks,
-            bytes_accessed=2 * blocks * length * entries + 4 * peers * count * blocks * entries,
-            transcendentals=0,
-        ),
+        cost_estimate=light(),
         name="transform",
-    )(freq_index, weight, snapshots)
+    )(in_hbm(freq_index), in_hbm(weight), in_hbm(snapshots), *after)
 
 
 def lane_low(shape, half):
@@ -170,8 +193,10 @@
     return jnp.bitwise_xor(lax.axis_index("space"), slot) if direct else slot
 
 
-def gram_kernel(peers, slots, direct, *refs):
-    pieces, merged, grams = refs[:peers], refs[peers], refs[peers + 1 :]
+def gram_kernel(peers, slots, direct, after, *refs):
+    pieces, refs = refs[:peers], refs[peers + after :]
+    merged, token, grams = refs[0], refs[1], refs[2:]
+    token[...] = jnp.zeros_like(token)
     me = lax.axis_index("tm")
     here = pieces[0].shape[1]
     entries = pieces[0].shape[2] // 2
@@ -207,7 +232,7 @@
                 grams[0][f] = pack(compact)
 
 
-def gram(pieces, slots, direct):
+def gram(pieces, slots, direct, after):
     peers = len(pieces)
     count, here, width = pieces[0].shape
     blocks = here * peers
@@ -216,21 +241,17 @@
     else:
         shapes = [(count, blocks // 2, 2 * blocks)]
     out = pl.pallas_call(
-        functools.partial(gram_kernel, peers, slots, direct),
-        in_specs=[whole_spec()] * peers,
-        out_specs=[whole_spec()] * (1 + len(shapes)),
-        out_shape=[jax.ShapeDtypeStruct((count, blocks, width), BF16)]
+        functools.partial(gram_kernel, peers, slots, direct, len(after)),
+        in_specs=[whole_spec()] * peers + [any_spec()] * len(after),
+        out_specs=[whole_spec()] * (2 + len(shapes)),
+        out_shape=[jax.ShapeDtypeStruct((count, blocks, width), BF16), TOKEN]
         + [jax.ShapeDtypeStruct(s, F32) for s in shapes],
         scratch_shapes=[pltpu.VMEM((blocks, width), F32)] if here % 16 else [],
         compiler_params=params(),
-        cost_estimate=pl.CostEstimate(
-            flops=4 * count * blocks * blocks * width,
-            bytes_accessed=4 * count * blocks * width + 4 * count * blocks * blocks,
-            transcendentals=0,
-        ),
+        cost_estimate=light(),
         name="gram",
-    )(*pieces)
-    return out[0], out[1:]
+    )(*pieces, *after)
+    return out[0], out[2:], out[1]
 
 
 def split(x):
@@ -243,7 +264,8 @@
 
 
 def solve_kernel(parts, *refs):
-    ins, out = refs[:parts], refs[parts]
+    ins, out, token = refs[:parts], refs[-2], refs[-1]
+    token[...] = jnp.zeros_like(token)
     number, half_rows, width = ins[0].shape
     half = width // 2
     shape = (half, width)
@@ -309,32 +331,30 @@
     return -(-number // 8) * 8
 
 
-def solve(parts):
+def solve(parts, after):
     number, half_rows, width = parts[0].shape
     rows = number * half_rows + tail_rows(number)
     return pl.pallas_call(
         functools.partial(solve_kernel, len(parts)),
-        in_specs=[whole_spec()] * len(parts),
-        out_specs=whole_spec(),
-        out_shape=jax.ShapeDtypeStruct((rows, width), F32),
+        in_specs=[whole_spec()] * len(parts) + [any_spec()] * len(after),
+        out_specs=[whole_spec()] * 2,
+        out_shape=[jax.ShapeDtypeStruct((rows, width), F32), TOKEN],
         compiler_params=params(),
-        cost_estimate=pl.CostEstimate(
-            flops=40 * number * width * width * width,
-            bytes_accessed=4 * number * half_rows * width * (len(parts) + 1),
-            transcendentals=0,
-        ),
+        cost_estimate=light(),
         name="filters",
-    )(*parts)
-
-
-def energy_kernel(slots, direct, carried, merged, *refs):
-    pieces, refs = refs[: len(refs) - 2 - carried], refs[len(refs) - 2 - carried :]
-    energies, filters = refs[-2:]
+    )(*parts, *after)
+
+
+def energy_kernel(slots, direct, number, first, merged, *refs):
+    pieces = refs[:number]
+    energies_out, filters_out, token, energies, filters, energies_sem, filters_sem = refs[-7:]
+    token[...] = jnp.zeros_like(token)
     count, blocks, width = merged.shape
     entries = width // 2
     per_slot = count // slots
     half_rows = blocks // 2
     states = entries * lax.axis_size("space")
+    puts = []
     for slot in range(slots):
         owner = slot_owner(direct, slot)
         piece = pieces[slot] if direct else pieces[0].at[slot]
@@ -352,37 +372,49 @@
             at = per_slot * half_rows + i
             total = piece[at : at + 1, 0:1]
             energies[pl.ds(f, 1), :] = energy * (F32(states) / total)
-
-
-def filtered(merged, pieces, slots, direct, carry, owned, first):
+        put = pltpu.make_async_copy(
+            filters.at[pl.ds(owner * per_slot, per_slot)],
+            filters_out.at[pl.ds(first + owner * per_slot, per_slot)],
+            filters_sem.at[slot],
+        )
+        put.start()
+        puts.append(put)
+    put = pltpu.make_async_copy(
+        energies, energies_out.at[pl.ds(first, count)], energies_sem.at[0]
+    )
+    put.start()
+    for p in [*puts, put]:
+        p.wait()
+
+
+def filtered(merged, pieces, slots, direct, carry, owned, first, after):
     count, blocks, width = merged.shape
     entries = width // 2
-    carried = 0 if carry is None else 2
-    args = [merged, *pieces] + ([] if carry is None else list(carry))
     fixed = 1 + len(pieces)
-    index = first // count
-    out = pl.pallas_call(
-        functools.partial(energy_kernel, slots, direct, carried),
-        grid=(1,),
-        in_specs=[whole_spec()] * fixed + [pl.BlockSpec(memory_space=pl.ANY)] * carried,
-        out_specs=[
-            pl.BlockSpec((count, entries), lambda g: (index, 0)),
-            pl.BlockSpec((count, 2, blocks, blocks), lambda g: (index, 0, 0, 0)),
-        ],
+    args = [merged, *pieces] + ([] if carry is None else list(carry)) + list(after)
+    hbm = pl.BlockSpec(memory_space=pltpu.HBM)
+    return pl.pallas_call(
+        functools.partial(energy_kernel, slots, direct, len(pieces), first),
+        in_specs=[whole_spec()] * fixed
+        + ([] if carry is None else [hbm] * 2)
+        + [any_spec()] * len(after),
+        out_specs=[hbm] * 2 + [whole_spec()],
         out_shape=[
             jax.ShapeDtypeStruct((owned, entries), F32),
             jax.ShapeDtypeStruct((owned, 2, blocks, blocks), F32),
+            TOKEN,
         ],
-        input_output_aliases={fixed: 0, fixed + 1: 1} if carried else {},
+        input_output_aliases={} if carry is None else {fixed: 0, fixed + 1: 1},
+        scratch_shapes=[
+            pltpu.VMEM((count, entries), F32),
+            pltpu.VMEM((count, 2, blocks, blocks), F32),
+            pltpu.SemaphoreType.DMA((1,)),
+            pltpu.SemaphoreType.DMA((slots,)),
+        ],
         compiler_params=params(),
-        cost_estimate=pl.CostEstimate(
-            flops=4 * count * blocks * blocks * width,
-            bytes_accessed=2 * count * blocks * width + 24 * count * blocks * blocks,
-            transcendentals=0,
-        ),
+        cost_estimate=light(),
         name="energy",
     )(*args)
-    return out
 
 
 def exchange(arrays, axis):
@@ -394,32 +426,69 @@
     return got
 
 
+def plan(owned, slots):
+    unit = max(slots, 8)
+    if owned % unit or owned // unit < 8:
+        return [owned]
+    return [owned // 4] * 4
+
+
+def order(chunks):
+    if chunks != 4:
+        return [(stage, c) for c in range(chunks) for stage in "TGFE"]
+    steps = "T0 T1 G0 T2 G1 F0 T3 G2 F1 E0 F2 E1 G3 E2 F3 E3"
+    return [(step[0], int(step[1:])) for step in steps.split()]
+
+
 def on_device(snapshots, entry_weight, freq_index):
     peers = lax.axis_size("tm")
     slots = lax.axis_size("space")
-    retained = freq_index.shape[0]
-    owned = retained // peers
-    direct = slots <= DIRECT_LIMIT
-    chunks = 4
-    while chunks > 1 and (owned // chunks) % max(slots, 8):
-        chunks //= 2
-    count = owned // chunks
+    owned = freq_index.shape[0] // peers
+    sizes = plan(owned, slots)
+    starts = [sum(sizes[:c]) for c in range(len(sizes))]
+    chunks = len(sizes)
+    direct = [False] * chunks
     weight = entry_weight.reshape(1, -1)
+    sent, merged, parts, pieces = {}, {}, {}, {}
     carry = None
-    for c in range(chunks):
-        first = c * count
-        sent = transform(snapshots, weight, freq_index, peers, count, first)
-        merged, grams = gram(exchange(sent, "tm"), slots, direct)
-        if direct:
-            parts = exchange(grams, "space")
+    token = []
+
+    def do_transform(c):
+        nonlocal token
+        out = transform(snapshots, weight, freq_index, peers, sizes[c], starts[c], token)
+        token = [out[peers]]
+        sent[c] = exchange(out[:peers], "tm")
+        if c + 1 < chunks:
+            token.append(sent[c][1])
+
+    def do_gram(c):
+        nonlocal token
+        merged[c], grams, done = gram(sent[c], slots, direct[c], token)
+        token = [done]
+        if direct[c]:
+            parts[c] = exchange(grams, "space")
         else:
-            parts = [lax.psum_scatter(grams[0], "space", scatter_dimension=0, tiled=True)]
-        own = solve(parts)
-        if direct:
-            pieces = exchange([own] * slots, "space")
+            parts[c] = [lax.psum_scatter(grams[0], "space", scatter_dimension=0, tiled=True)]
+
+    def do_solve(c):
+        nonlocal token
+        own, done = solve(parts[c], token)
+        token = [done]
+        if direct[c]:
+            pieces[c] = exchange([own] * slots, "space")
         else:
-            pieces = [lax.all_gather(own, "space", axis=0, tiled=False)]
-        carry = filtered(merged, pieces, slots, direct, carry, owned, first)
+            pieces[c] = [lax.all_gather(own, "space", axis=0, tiled=False)]
+
+    def do_energy(c):
+        nonlocal token, carry
+        *carry, done = filtered(
+            merged[c], pieces[c], slots, direct[c], carry, owned, starts[c], token
+        )
+        token = [done]
+
+    stages = {"T": do_transform, "G": do_gram, "F": do_solve, "E": do_energy}
+    for stage, c in order(chunks):
+        stages[stage](c)
     return (carry[0], carry[1])
 
 

time: 110 us -> 156 us (1.42)
  blocking collectives: 0 us -> 58.5 us
  starting transfers between devices: 49.5 us -> 10.1 us
  between operations: 0.87 us -> 14 us
  Pallas kernels: 34.3 us -> 41.8 us
  local copies, waits for them, and re-layouts: 3.54 us -> 10.4 us
    all_gather x0 -> x4, blocking collectives: none -> 58.5 us  [do_solve(): pieces[c] = [lax.all_gather(own, 'space', axis=0, tiled=False)]]
    ppermute x36 -> x12, starting transfers between devices: 49.5 us -> 9.96 us  [exchange(): got.append(lax.ppermute(arrays[offset], axis, pairs))]
    ppermute x36 -> x12, waiting for transfers between devices: 22.1 us -> 13.6 us  [exchange(): got.append(lax.ppermute(arrays[offset], axis, pairs))]
    reduce_scatter x0 -> x4, waiting for transfers between devices: none -> 7.62 us  [do_gram(): lax.psum_scatter(grams[0], 'space', scatter_dimension=0, tiled=True)]
    pallas_call x12, Pallas kernels: 24.8 us -> 32.3 us  [the longest x4 14.9 us: transform(): pl.pallas_call(functools.partial(transform_kernel, peers, count, first, g...]
    unnamed x6 -> x40, local copies, waits for them, and re-layouts: 3.54 us -> 10.4 us
  transfers between devices with their start and end apart: 36 -> 16, of which waited for: 7 -> 7; matrix products, arithmetic and copies ran while one was open for 0% -> 0% of each run, Pallas kernels for 26% -> 18%
where the time goes in v2:
time: 156 us
  blocking collectives  58.5 us (38%)
  Pallas kernels  41.8 us (27%)
  waiting for transfers between devices  21.3 us (14%)
  between operations  14 us (9%)
  local copies, waits for them, and re-layouts  10.4 us (7%)
  starting transfers between devices  10.1 us (6%)
    all_gather x4, blocking collectives, do_solve(): pieces[c] = [lax.all_gather(own, 'space', axis=0, tiled=False)]  58.5 us
    pallas_call x4, Pallas kernels, transform(): pl.pallas_call(functools.partial(transform_kernel, peers, count, first, g...  14.9 us
    ppermute x12, waiting for transfers between devices, exchange(): got.append(lax.ppermute(arrays[offset], axis, pairs))  13.6 us
    pallas_call x4, Pallas kernels, filtered(): pl.pallas_call(functools.partial(energy_kernel, slots, direct, len(pieces...  11.4 us
    unnamed x40, local copies, waits for them, and re-layouts  10.4 us
    ppermute x12, starting transfers between devices, exchange(): got.append(lax.ppermute(arrays[offset], axis, pairs))  9.96 us
    pallas_call x4, Pallas kernels, solve(): pl.pallas_call(functools.partial(solve_kernel, len(parts)), in_specs=[who...  9.48 us
    reduce_scatter x4, waiting for transfers between devices, do_gram(): lax.psum_scatter(grams[0], 'space', scatter_dimension=0, tiled=True)  7.62 us
  transfers between devices with their start and end apart: 16, of which 7 were waited for; matrix products, arithmetic and copies ran while one was open for 0% of the time, Pallas kernels for 18%

profile of v2, /device:TPU:0, one launch (start us, length us, event | category | flops | bytes accessed | tf_op | source)
XLA Modules:
  0.0 156.0 jit_solution(715720176215928555)
XLA Ops:
  7.2 0.0 reduce-scatter.5.cloned.1.call-start
  7.2 3.7 %transform.4 = (bf16[16,16,512]{2,1,0:T(8,128)(2,1)S(1)}, bf16[16,16,512]{2,1,0:T(8,128)(2,1)S(1)}, bf16[16,16,512]{2,1,0:T(8,128)(2,1)S(1)}, bf16[16,16,512]{2,1,0:T(8,128)(2,1)S(1)}, f32[8,128]{1,0:T(8,128)S(1)}) custom-call(s32[256]{0:T(256)} %refs_0_.7, f32[1,256]{1,0:T(1,128)} %bitcast.9, bf16[16,512,256]{2,1,0:T(8,128)(2,1)} %refs_2_.7), custom_call_target="tpu_custom_call" | custom-call | flops 1024 | bytes 1024 | tf_op jit(solution)/shard_map/transform/pallas_call | solution.py:138
  11.0 0.5 collective-permute-start
  11.5 2.6 %collective-permute-start.1 = (bf16[16,16,512]{2,1,0:T(8,128)(2,1)S(1)}, bf16[16,16,512]{2,1,0:T(8,128)(2,1)S(1)}, u32[]{:S(2)}, u32[]{:S(2)}) collective-permute-start(bf16[16,16,512]{2,1,0:T(8,128)(2,1)S(1)} %get-tuple-element.55), channel_id=1, source_target_pairs={{0,2},{1,3},{2,0},{3,1},{4,6},{5,7},{6,4},{7,5},{8,10},{9,11},{10,... | collective-permute-start | bytes 786440 | tf_op jit(solution)/shard_map/ppermute | solution.py:425
  14.0 0.1 collective-permute-start.2
  14.1 0.0 collective-permute-done.refs_4_.refs_1_
  14.1 3.7 %transform.5 = (bf16[16,16,512]{2,1,0:T(8,128)(2,1)S(1)}, bf16[16,16,512]{2,1,0:T(8,128)(2,1)S(1)}, bf16[16,16,512]{2,1,0:T(8,128)(2,1)S(1)}, bf16[16,16,512]{2,1,0:T(8,128)(2,1)S(1)}, f32[8,128]{1,0:T(8,128)S(1)}) custom-call(s32[256]{0:T(256)} %refs_0_.7, f32[1,256]{1,0:T(1,128)} %bitcast.10, bf16[16,512,256]{2,1,0:T(8,128)(2,1)} %refs_2_.7, ...), custom_call_target="tpu_custom_call" | custom-call | flops 1024 | bytes 1024 | tf_op jit(solution)/shard_map/transform/pallas_call | solution.py:138
  17.8 0.2 collective-permute-start.3
  18.1 3.1 %collective-permute-done.1.refs_2_ = bf16[16,16,512]{2,1,0:T(8,128)(2,1)S(1)} collective-permute-done((bf16[16,16,512]{2,1,0:T(8,128)(2,1)S(1)}, bf16[16,16,512]{2,1,0:T(8,128)(2,1)S(1)}, u32[]{:S(2)}, u32[]{:S(2)}) %collective-permute-start.1) | collective-permute-done | bytes 262176 | tf_op jit(solution)/shard_map/ppermute | solution.py:425
  21.2 5.1 %collective-permute-done.2.refs_3_ = bf16[16,16,512]{2,1,0:T(8,128)(2,1)S(1)} collective-permute-done((bf16[16,16,512]{2,1,0:T(8,128)(2,1)S(1)}, bf16[16,16,512]{2,1,0:T(8,128)(2,1)S(1)}, u32[]{:S(2)}, u32[]{:S(2)}) %collective-permute-start.2) | collective-permute-done | bytes 262176 | tf_op jit(solution)/shard_map/ppermute | solution.py:425
  26.3 0.0 collective-permute-done.3.refs_5_.refs_1_
  26.3 1.4 gram.4
  27.7 0.0 reduce-scatter.5.cloned.1.call-update
  27.7 0.0 reduce-scatter.7.cloned.1.call-start
  27.7 1.6 %collective-permute-start.4 = (bf16[16,16,512]{2,1,0:T(8,128)(2,1)S(1)}, bf16[16,16,512]{2,1,0:T(8,128)(2,1)S(1)}, u32[]{:S(2)}, u32[]{:S(2)}) collective-permute-start(bf16[16,16,512]{2,1,0:T(8,128)(2,1)S(1)} %get-tuple-element.62), channel_id=1, source_target_pairs={{0,2},{1,3},{2,0},{3,1},{4,6},{5,7},{6,4},{7,5},{8,10},{9,11},{10,... | collective-permute-start | bytes 786440 | tf_op jit(solution)/shard_map/ppermute | solution.py:425
  29.4 0.0 collective-permute-start.5
  29.4 3.7 %transform.6 = (bf16[16,16,512]{2,1,0:T(8,128)(2,1)S(1)}, bf16[16,16,512]{2,1,0:T(8,128)(2,1)S(1)}, bf16[16,16,512]{2,1,0:T(8,128)(2,1)S(1)}, bf16[16,16,512]{2,1,0:T(8,128)(2,1)S(1)}, f32[8,128]{1,0:T(8,128)S(1)}) custom-call(s32[256]{0:T(256)} %refs_0_.7, f32[1,256]{1,0:T(1,128)} %bitcast.11, bf16[16,512,256]{2,1,0:T(8,128)(2,1)} %refs_2_.7, ...), custom_call_target="tpu_custom_call" | custom-call | flops 1024 | bytes 1024 | tf_op jit(solution)/shard_map/transform/pallas_call | solution.py:138
  33.2 0.7 copy-done.5
  33.9 0.7 copy-done.18
  34.6 0.7 copy-done.19
  35.3 0.6 collective-permute-start.6
  35.9 1.1 collective-permute-done.4.refs_2_
  37.0 4.0 %collective-permute-done.5.refs_3_ = bf16[16,16,512]{2,1,0:T(8,128)(2,1)S(1)} collective-permute-done((bf16[16,16,512]{2,1,0:T(8,128)(2,1)S(1)}, bf16[16,16,512]{2,1,0:T(8,128)(2,1)S(1)}, u32[]{:S(2)}, u32[]{:S(2)}) %collective-permute-start.5) | collective-permute-done | bytes 262176 | tf_op jit(solution)/shard_map/ppermute | solution.py:425
  41.0 0.0 collective-permute-done.6.refs_5_.refs_1_
  41.0 1.4 gram.5
  42.4 0.0 reduce-scatter.7.cloned.1.call-update
  42.4 0.0 reduce-scatter.9.cloned.1.call-start
  42.5 1.9 %collective-permute-start.10 = (bf16[16,16,512]{2,1,0:T(8,128)(2,1)}, bf16[16,16,512]{2,1,0:T(8,128)(2,1)S(1)}, u32[]{:S(2)}, u32[]{:S(2)}) collective-permute-start(bf16[16,16,512]{2,1,0:T(8,128)(2,1)} %copy-done.19), channel_id=1, source_target_pairs={{0,2},{1,3},{2,0},{3,1},{4,6},{5,7},{6,4},{7,5},{8,10},{9,11},{10,... | collective-permute-start | bytes 786440 | tf_op jit(solution)/shard_map/ppermute | solution.py:425
  44.4 0.6 collective-permute-start.11
  44.9 3.9 %reduce-scatter.5.cloned.1.call-done.refs_0_ = f32[4,32,128]{2,1,0:T(8,128)} async-done(((f32[16,32,128]{2,1,0:T(8,128)}), f32[4,32,128]{2,1,0:T(8,128)}) %reduce-scatter.5.cloned.1.call-update) | async-done | bytes 65552 | tf_op jit(solution)/shard_map/reduce_scatter | solution.py:471
  48.9 0.9 copy-done.12
  49.8 2.4 %filters.4 = (f32[136,128]{1,0:T(8,128)S(1)}, f32[8,128]{1,0:T(8,128)S(1)}) custom-call(f32[4,32,128]{2,1,0:T(8,128)S(1)} %copy-done.12, f32[8,128]{1,0:T(8,128)S(1)} %get-tuple-element.67.refs_1_), custom_call_target="tpu_custom_call" | custom-call | flops 1024 | bytes 1024 | tf_op jit(solution)/shard_map/filters/pallas_call | solution.py:337
  52.1 3.7 %transform.7 = (bf16[16,16,512]{2,1,0:T(8,128)(2,1)S(1)}, bf16[16,16,512]{2,1,0:T(8,128)(2,1)S(1)}, bf16[16,16,512]{2,1,0:T(8,128)(2,1)S(1)}, bf16[16,16,512]{2,1,0:T(8,128)(2,1)S(1)}, f32[8,128]{1,0:T(8,128)S(1)}) custom-call(s32[256]{0:T(256)} %refs_0_.7, f32[1,256]{1,0:T(1,128)} %bitcast.12, bf16[16,512,256]{2,1,0:T(8,128)(2,1)} %refs_2_.7, ...), custom_call_target="tpu_custom_call" | custom-call | flops 1024 | bytes 1024 | tf_op jit(solution)/shard_map/transform/pallas_call | solution.py:138
  55.9 0.7 copy-done.3
  56.6 0.0 copy-start.7
  56.6 0.7 copy-done.7
  57.3 0.2 collective-permute-done.11.refs_3_
  57.6 0.7 copy-done.9
  58.3 0.9 copy-done.8
  59.2 0.9 copy-done.10
  60.2 0.7 gram.6
  60.9 0.7 copy-done.2
  61.6 0.0 reduce-scatter.9.cloned.1.call-update
  61.6 0.0 reduce-scatter.11.cloned.1.call-start
  61.7 0.2 collective-permute-start.7
  61.9 1.6 %collective-permute-start.8 = (bf16[16,16,512]{2,1,0:T(8,128)(2,1)}, bf16[16,16,512]{2,1,0:T(8,128)(2,1)}, u32[]{:S(2)}, u32[]{:S(2)}) collective-permute-start(bf16[16,16,512]{2,1,0:T(8,128)(2,1)} %copy-done.16), channel_id=1, source_target_pairs={{0,2},{1,3},{2,0},{3,1},{4,6},{5,7},{6,4},{7,5},{8,10},{9,11},{10,... | collective-permute-start | bytes 786440 | tf_op jit(solution)/shard_map/ppermute | solution.py:425
  63.5 0.1 collective-permute-start.9
  63.6 14.4 %all-gather.1 = f32[544,128]{1,0:T(8,128)S(1)} all-gather(f32[136,128]{1,0:T(8,128)S(1)} %get-tuple-element.82), channel_id=3, replica_groups=mesh['grp'=2,'space'=4,'tm'=4] {'space'}, dimensions={0}, use_global_device_ids=true | all-gather | bytes 348160 | tf_op jit(solution)/shard_map/all_gather | solution.py:480
  78.1 0.8 copy-done.11
  78.9 2.4 %filters.5 = (f32[136,128]{1,0:T(8,128)S(1)}, f32[8,128]{1,0:T(8,128)S(1)}) custom-call(f32[4,32,128]{2,1,0:T(8,128)S(1)} %copy-done.11, f32[8,128]{1,0:T(8,128)S(1)} %get-tuple-element.79.refs_1_), custom_call_target="tpu_custom_call" | custom-call | flops 1024 | bytes 1024 | tf_op jit(solution)/shard_map/filters/pallas_call | solution.py:337
  81.3 2.7 %energy.4 = (f32[64,256]{1,0:T(8,128)}, f32[64,2,64,64]{3,2,1,0:T(8,128)}, f32[8,128]{1,0:T(8,128)S(1)}) custom-call(bf16[16,64,512]{2,1,0:T(8,128)(2,1)S(1)} %get-tuple-element.81.merged, f32[4,136,128]{2,1,0:T(8,128)S(1)} %bitcast.8, f32[8,128]{1,0:T(8,128)S(1)} %get-tuple-element.83.refs_1_), custom_call_target="tpu_custom_call" | custom-call | flops 1024 | bytes 1024 | tf_op jit(solution)/shard_map/energy/pallas_call | solution.py:396
  84.0 15.1 %all-gather = f32[544,128]{1,0:T(8,128)S(1)} all-gather(f32[136,128]{1,0:T(8,128)S(1)} %get-tuple-element.80), channel_id=2, replica_groups=mesh['grp'=2,'space'=4,'tm'=4] {'space'}, dimensions={0}, use_global_device_ids=true | all-gather | bytes 348160 | tf_op jit(solution)/shard_map/all_gather | solution.py:480
  99.1 0.8 copy-done.13
  99.9 2.4 %filters.6 = (f32[136,128]{1,0:T(8,128)S(1)}, f32[8,128]{1,0:T(8,128)S(1)}) custom-call(f32[4,32,128]{2,1,0:T(8,128)S(1)} %copy-done.13, f32[8,128]{1,0:T(8,128)S(1)} %get-tuple-element.87.refs_1_), custom_call_target="tpu_custom_call" | custom-call | flops 1024 | bytes 1024 | tf_op jit(solution)/shard_map/filters/pallas_call | solution.py:337
  102.3 2.7 %energy.5 = (f32[64,256]{1,0:T(8,128)}, f32[64,2,64,64]{3,2,1,0:T(8,128)}, f32[8,128]{1,0:T(8,128)S(1)}) custom-call(bf16[16,64,512]{2,1,0:T(8,128)(2,1)S(1)} %get-tuple-element.73.merged, f32[4,136,128]{2,1,0:T(8,128)S(1)} %bitcast.5, f32[64,256]{1,0:T(8,128)} %get-tuple-element.84.refs_1_, ...), custom_call_target="tpu_custom_call", output_to_operand_aliasing={{0}: (2, {}), {1}: (3, {})} | custom-call | flops 1024 | bytes 1024 | tf_op jit(solution)/shard_map/energy/pallas_call | solution.py:396
  105.1 2.5 %gram.7 = (bf16[16,64,512]{2,1,0:T(8,128)(2,1)S(1)}, f32[8,128]{1,0:T(8,128)S(1)}, f32[16,32,128]{2,1,0:T(8,128)}) custom-call(bf16[16,16,512]{2,1,0:T(8,128)(2,1)S(1)} %copy-done.4, bf16[16,16,512]{2,1,0:T(8,128)(2,1)} %collective-permute-done.7.refs_1_, bf16[16,16,512]{2,1,0:T(8,128)(2,1)} %collective-permute-done.8.refs_2_, ...), custom_call_target="tpu_custom_call" | custom-call | flops 1024 | bytes 1024 | tf_op jit(solution)/shard_map/gram/pallas_call | solution.py:243
  107.6 0.0 reduce-scatter.11.cloned.1.call-update
  107.6 15.0 %all-gather.2 = f32[544,128]{1,0:T(8,128)S(1)} all-gather(f32[136,128]{1,0:T(8,128)S(1)} %get-tuple-element.93), channel_id=4, replica_groups=mesh['grp'=2,'space'=4,'tm'=4] {'space'}, dimensions={0}, use_global_device_ids=true | all-gather | bytes 348160 | tf_op jit(solution)/shard_map/all_gather | solution.py:480
  122.6 2.7 %energy.6 = (f32[64,256]{1,0:T(8,128)}, f32[64,2,64,64]{3,2,1,0:T(8,128)}, f32[8,128]{1,0:T(8,128)S(1)}) custom-call(bf16[16,64,512]{2,1,0:T(8,128)(2,1)S(1)} %get-tuple-element.92.merged, f32[4,136,128]{2,1,0:T(8,128)S(1)} %bitcast.7, f32[64,256]{1,0:T(8,128)} %get-tuple-element.94.refs_1_, ...), custom_call_target="tpu_custom_call", output_to_operand_aliasing={{0}: (2, {}), {1}: (3, {})} | custom-call | flops 1024 | bytes 1024 | tf_op jit(solution)/shard_map/energy/pallas_call | solution.py:396
  125.3 3.7 %reduce-scatter.11.cloned.1.call-done.refs_0_ = f32[4,32,128]{2,1,0:T(8,128)} async-done(((f32[16,32,128]{2,1,0:T(8,128)}), f32[4,32,128]{2,1,0:T(8,128)}) %reduce-scatter.11.cloned.1.call-update) | async-done | bytes 65552 | tf_op jit(solution)/shard_map/reduce_scatter | solution.py:471
  129.0 0.8 copy-done.14
  129.8 2.4 %filters.7 = (f32[136,128]{1,0:T(8,128)S(1)}, f32[8,128]{1,0:T(8,128)S(1)}) custom-call(f32[4,32,128]{2,1,0:T(8,128)S(1)} %copy-done.14, f32[8,128]{1,0:T(8,128)S(1)} %get-tuple-element.97.refs_1_), custom_call_target="tpu_custom_call" | custom-call | flops 1024 | bytes 1024 | tf_op jit(solution)/shard_map/filters/pallas_call | solution.py:337
  132.2 14.0 %all-gather.3 = f32[544,128]{1,0:T(8,128)S(1)} all-gather(f32[136,128]{1,0:T(8,128)S(1)} %get-tuple-element.98), channel_id=5, replica_groups=mesh['grp'=2,'space'=4,'tm'=4] {'space'}, dimensions={0}, use_global_device_ids=true | all-gather | bytes 348160 | tf_op jit(solution)/shard_map/all_gather | solution.py:480
  146.2 3.3 %energy.7 = (f32[64,256]{1,0:T(8,128)}, f32[64,2,64,64]{3,2,1,0:T(8,128)}, f32[8,128]{1,0:T(8,128)}) custom-call(bf16[16,64,512]{2,1,0:T(8,128)(2,1)S(1)} %get-tuple-element.90.merged, f32[4,136,128]{2,1,0:T(8,128)S(1)} %bitcast.6, f32[64,256]{1,0:T(8,128)} %get-tuple-element.99.refs_1_, ...), custom_call_target="tpu_custom_call", output_to_operand_aliasing={{0}: (2, {}), {1}: (3, {})} | custom-call | flops 1024 | bytes 1024 | tf_op jit(solution)/shard_map/energy/pallas_call | solution.py:396
  (32 shorter events, 0.1 us)
Async XLA Ops:
  7.2 41.7 %reduce-scatter.5.cloned.1.call-start = ((), (), s32[]{:S(2)}) async-start(), calls=%async_computation.4 | async-start | bytes 327680 | tf_op jit(solution)/shard_map/reduce_scatter | solution.py:471
  11.0 3.2 %collective-permute-start = (bf16[16,16,512]{2,1,0:T(8,128)(2,1)S(1)}, bf16[16,16,512]{2,1,0:T(8,128)(2,1)S(1)}, u32[]{:S(2)}, u32[]{:S(2)}) collective-permute-start(bf16[16,16,512]{2,1,0:T(8,128)(2,1)S(1)} %get-tuple-element.54), channel_id=1, source_target_pairs={{0,1},{1,0},{2,3},{3,2},{4,5},{5,4},{6,7},{7,6},{8,9},{9,8},{10,11... | collective-permute-start | bytes 786440 | tf_op jit(solution)/shard_map/ppermute | solution.py:425
  11.5 9.7 %collective-permute-start.1 = (bf16[16,16,512]{2,1,0:T(8,128)(2,1)S(1)}, bf16[16,16,512]{2,1,0:T(8,128)(2,1)S(1)}, u32[]{:S(2)}, u32[]{:S(2)}) collective-permute-start(bf16[16,16,512]{2,1,0:T(8,128)(2,1)S(1)} %get-tuple-element.55), channel_id=1, source_target_pairs={{0,2},{1,3},{2,0},{3,1},{4,6},{5,7},{6,4},{7,5},{8,10},{9,11},{10,... | collective-permute-start | bytes 786440 | tf_op jit(solution)/shard_map/ppermute | solution.py:425
  14.0 12.3 %collective-permute-start.2 = (bf16[16,16,512]{2,1,0:T(8,128)(2,1)S(1)}, bf16[16,16,512]{2,1,0:T(8,128)(2,1)S(1)}, u32[]{:S(2)}, u32[]{:S(2)}) collective-permute-start(bf16[16,16,512]{2,1,0:T(8,128)(2,1)S(1)} %get-tuple-element.56), channel_id=1, source_target_pairs={{0,3},{1,2},{2,1},{3,0},{4,7},{5,6},{6,5},{7,4},{8,11},{9,10},{10,... | collective-permute-start | bytes 786440 | tf_op jit(solution)/shard_map/ppermute | solution.py:425
  17.8 8.4 %collective-permute-start.3 = (bf16[16,16,512]{2,1,0:T(8,128)(2,1)S(1)}, bf16[16,16,512]{2,1,0:T(8,128)(2,1)S(1)}, u32[]{:S(2)}, u32[]{:S(2)}) collective-permute-start(bf16[16,16,512]{2,1,0:T(8,128)(2,1)S(1)} %get-tuple-element.59), channel_id=1, source_target_pairs={{0,1},{1,0},{2,3},{3,2},{4,5},{5,4},{6,7},{7,6},{8,9},{9,8},{10,11... | collective-permute-start | bytes 786440 | tf_op jit(solution)/shard_map/ppermute | solution.py:425
  27.7 50.4 %reduce-scatter.7.cloned.1.call-start = ((), (), s32[]{:S(2)}) async-start(), calls=%async_computation.5 | async-start | bytes 327680 | tf_op jit(solution)/shard_map/reduce_scatter | solution.py:471
  27.7 9.2 %collective-permute-start.4 = (bf16[16,16,512]{2,1,0:T(8,128)(2,1)S(1)}, bf16[16,16,512]{2,1,0:T(8,128)(2,1)S(1)}, u32[]{:S(2)}, u32[]{:S(2)}) collective-permute-start(bf16[16,16,512]{2,1,0:T(8,128)(2,1)S(1)} %get-tuple-element.62), channel_id=1, source_target_pairs={{0,2},{1,3},{2,0},{3,1},{4,6},{5,7},{6,4},{7,5},{8,10},{9,11},{10,... | collective-permute-start | bytes 786440 | tf_op jit(solution)/shard_map/ppermute | solution.py:425
  29.4 11.6 %collective-permute-start.5 = (bf16[16,16,512]{2,1,0:T(8,128)(2,1)S(1)}, bf16[16,16,512]{2,1,0:T(8,128)(2,1)S(1)}, u32[]{:S(2)}, u32[]{:S(2)}) collective-permute-start(bf16[16,16,512]{2,1,0:T(8,128)(2,1)S(1)} %get-tuple-element.63), channel_id=1, source_target_pairs={{0,3},{1,2},{2,1},{3,0},{4,7},{5,6},{6,5},{7,4},{8,11},{9,10},{10,... | collective-permute-start | bytes 786440 | tf_op jit(solution)/shard_map/ppermute | solution.py:425
  33.1 0.7 copy-start.5
  33.9 0.7 copy-start.18
  34.6 0.7 copy-start.19
  35.3 5.7 %collective-permute-start.6 = (bf16[16,16,512]{2,1,0:T(8,128)(2,1)S(1)}, bf16[16,16,512]{2,1,0:T(8,128)(2,1)S(1)}, u32[]{:S(2)}, u32[]{:S(2)}) collective-permute-start(bf16[16,16,512]{2,1,0:T(8,128)(2,1)S(1)} %get-tuple-element.66), channel_id=1, source_target_pairs={{0,1},{1,0},{2,3},{3,2},{4,5},{5,4},{6,7},{7,6},{8,9},{9,8},{10,11... | collective-permute-start | bytes 786440 | tf_op jit(solution)/shard_map/ppermute | solution.py:425
  41.0 1.4 copy-start
  42.4 15.9 %copy-start.1 = (bf16[16,16,512]{2,1,0:T(8,128)(2,1)S(1)}, bf16[16,16,512]{2,1,0:T(8,128)(2,1)}, u32[]{:S(2)}) copy-start(bf16[16,16,512]{2,1,0:T(8,128)(2,1)} %copy-done) | copy-start | bytes 786436
  42.4 56.7 %reduce-scatter.9.cloned.1.call-start = ((), (), s32[]{:S(2)}) async-start(), calls=%async_computation.6 | async-start | bytes 327680 | tf_op jit(solution)/shard_map/reduce_scatter | solution.py:471
  42.5 14.1 %collective-permute-start.10 = (bf16[16,16,512]{2,1,0:T(8,128)(2,1)}, bf16[16,16,512]{2,1,0:T(8,128)(2,1)S(1)}, u32[]{:S(2)}, u32[]{:S(2)}) collective-permute-start(bf16[16,16,512]{2,1,0:T(8,128)(2,1)} %copy-done.19), channel_id=1, source_target_pairs={{0,2},{1,3},{2,0},{3,1},{4,6},{5,7},{6,4},{7,5},{8,10},{9,11},{10,... | collective-permute-start | bytes 786440 | tf_op jit(solution)/shard_map/ppermute | solution.py:425
  44.4 13.2 %collective-permute-start.11 = (bf16[16,16,512]{2,1,0:T(8,128)(2,1)}, bf16[16,16,512]{2,1,0:T(8,128)(2,1)S(1)}, u32[]{:S(2)}, u32[]{:S(2)}) collective-permute-start(bf16[16,16,512]{2,1,0:T(8,128)(2,1)} %copy-done.18), channel_id=1, source_target_pairs={{0,3},{1,2},{2,1},{3,0},{4,7},{5,6},{6,5},{7,4},{8,11},{9,10},{10,... | collective-permute-start | bytes 786440 | tf_op jit(solution)/shard_map/ppermute | solution.py:425
  48.9 9.4 %copy-start.6 = (bf16[16,16,512]{2,1,0:T(8,128)(2,1)S(1)}, bf16[16,16,512]{2,1,0:T(8,128)(2,1)}, u32[]{:S(2)}) copy-start(bf16[16,16,512]{2,1,0:T(8,128)(2,1)} %copy-done.5) | copy-start | bytes 786436
  48.9 0.9 copy-start.12
  55.9 0.7 copy-start.3
  56.6 1.7 %copy-start.16 = (bf16[16,16,512]{2,1,0:T(8,128)(2,1)}, bf16[16,16,512]{2,1,0:T(8,128)(2,1)S(1)}, u32[]{:S(2)}) copy-start(bf16[16,16,512]{2,1,0:T(8,128)(2,1)S(1)} %get-tuple-element.71) | copy-start | bytes 786436
  56.6 1.7 %copy-start.17 = (bf16[16,16,512]{2,1,0:T(8,128)(2,1)}, bf16[16,16,512]{2,1,0:T(8,128)(2,1)S(1)}, u32[]{:S(2)}) copy-start(bf16[16,16,512]{2,1,0:T(8,128)(2,1)S(1)} %get-tuple-element.70) | copy-start | bytes 786436
  56.6 4.3 %copy-start.15 = (bf16[16,16,512]{2,1,0:T(8,128)(2,1)}, bf16[16,16,512]{2,1,0:T(8,128)(2,1)S(1)}, u32[]{:S(2)}) copy-start(bf16[16,16,512]{2,1,0:T(8,128)(2,1)S(1)} %get-tuple-element.72) | copy-start | bytes 786436
  56.6 0.7 copy-start.7
  57.6 0.7 copy-start.9
  58.3 1.0 copy-start.8
  59.2 0.9 copy-start.10
  60.9 0.7 copy-start.2
  61.6 67.3 %reduce-scatter.11.cloned.1.call-start = ((), (), s32[]{:S(2)}) async-start(), calls=%async_computation.7 | async-start | bytes 327680 | tf_op jit(solution)/shard_map/reduce_scatter | solution.py:471
  61.7 43.4 %collective-permute-start.7 = (bf16[16,16,512]{2,1,0:T(8,128)(2,1)}, bf16[16,16,512]{2,1,0:T(8,128)(2,1)}, u32[]{:S(2)}, u32[]{:S(2)}) collective-permute-start(bf16[16,16,512]{2,1,0:T(8,128)(2,1)} %copy-done.17), channel_id=1, source_target_pairs={{0,1},{1,0},{2,3},{3,2},{4,5},{5,4},{6,7},{7,6},{8,9},{9,8},{10,11... | collective-permute-start | bytes 786440 | tf_op jit(solution)/shard_map/ppermute | solution.py:425
  61.9 43.2 %collective-permute-start.8 = (bf16[16,16,512]{2,1,0:T(8,128)(2,1)}, bf16[16,16,512]{2,1,0:T(8,128)(2,1)}, u32[]{:S(2)}, u32[]{:S(2)}) collective-permute-start(bf16[16,16,512]{2,1,0:T(8,128)(2,1)} %copy-done.16), channel_id=1, source_target_pairs={{0,2},{1,3},{2,0},{3,1},{4,6},{5,7},{6,4},{7,5},{8,10},{9,11},{10,... | collective-permute-start | bytes 786440 | tf_op jit(solution)/shard_map/ppermute | solution.py:425
  63.5 41.6 %collective-permute-start.9 = (bf16[16,16,512]{2,1,0:T(8,128)(2,1)}, bf16[16,16,512]{2,1,0:T(8,128)(2,1)}, u32[]{:S(2)}, u32[]{:S(2)}) collective-permute-start(bf16[16,16,512]{2,1,0:T(8,128)(2,1)} %copy-done.15), channel_id=1, source_target_pairs={{0,3},{1,2},{2,1},{3,0},{4,7},{5,6},{6,5},{7,4},{8,11},{9,10},{10,... | collective-permute-start | bytes 786440 | tf_op jit(solution)/shard_map/ppermute | solution.py:425
  78.1 0.8 copy-start.11
  84.0 21.0 %copy-start.4 = (bf16[16,16,512]{2,1,0:T(8,128)(2,1)S(1)}, bf16[16,16,512]{2,1,0:T(8,128)(2,1)}, u32[]{:S(2)}) copy-start(bf16[16,16,512]{2,1,0:T(8,128)(2,1)} %copy-done.3) | copy-start | bytes 786436
  99.1 0.8 copy-start.13
  129.0 0.8 copy-start.14
Sparse Core Ops, SparseCore 0:
  27.8 21.0 reduce-scatter.4
  51.2 17.8 reduce-scatter.6
  71.4 18.0 reduce-scatter.8
  107.7 21.2 reduce-scatter.10

commit v3 on v2

--- a/solution.py
+++ b/solution.py
@@ -11,7 +11,6 @@
 F32 = jnp.float32
 BF16 = jnp.bfloat16
 VMEM_LIMIT = 30 * 1024 * 1024
-DIRECT_LIMIT = 8
 LANES = 128
 
 
@@ -65,9 +64,9 @@
     return c1, s1
 
 
-def transform_kernel(peers, count, first, group, *refs):
+def transform_kernel(peers, parts, group, *refs):
     freq_hbm, weight_hbm, snap_hbm = refs[:3]
-    outs, token = refs[-peers - 8 : -8], refs[-8]
+    outs, token = refs[-peers * len(parts) - 8 : -8], refs[-8]
     freq, weight, snap, table, wide, small_sem, snap_sem = refs[-7:]
     blocks, length, entries = snap.shape
     steps = blocks // group
@@ -86,7 +85,13 @@
     get_weight.start()
 
     me = lax.axis_index("tm")
-    rows = peers * count
+    groups = [
+        (peer, first + j)
+        for first, count in parts
+        for peer in range(peers)
+        for j in range(0, count, 8)
+    ]
+    rows = 8 * len(groups)
     per_peer = freq.shape[0] // peers
     times = lax.broadcasted_iota(jnp.int32, (8, length), 1)
     sub = lax.broadcasted_iota(jnp.int32, (8, length), 0)
@@ -95,9 +100,8 @@
     get_freq.wait()
 
     def eight(index):
-        base = index * 8
-        peer = base // count
-        start = jnp.bitwise_xor(me, peer) * per_peer + first + (base - peer * count)
+        peer, offset = groups[index]
+        start = jnp.bitwise_xor(me, peer) * per_peer + offset
         k = jnp.zeros((8, length), jnp.int32)
         for i in range(8):
             k = jnp.where(sub == i, freq[start + i], k)
@@ -123,29 +127,36 @@
                 lanes = slice(tile * LANES, (tile + 1) * LANES)
                 wide[tile, pl.ds(b, rows, stride=blocks), :] = spec[:rows, lanes]
                 wide[tiles + tile, pl.ds(b, rows, stride=blocks), :] = spec[rows:, lanes]
-    for peer in range(peers):
-        for j in range(count):
-            at = (peer * count + j) * blocks
+    at = 0
+    for out in outs:
+        for j in range(out.shape[0]):
             for tile in range(2 * tiles):
                 lanes = slice(tile * LANES, (tile + 1) * LANES)
-                outs[peer][j, :, lanes] = wide[tile, at : at + blocks, :].astype(BF16)
-
-
-def transform(snapshots, weight, freq_index, peers, count, first, after):
+                out[j, :, lanes] = wide[tile, at : at + blocks, :].astype(BF16)
+            at += blocks
+
+
+def transform(snapshots, weight, freq_index, peers, parts, after):
     blocks, length, entries = snapshots.shape
     group = min(blocks, 4)
+    total = peers * sum(count for _, count in parts)
+    shapes = [
+        jax.ShapeDtypeStruct((count, blocks, 2 * entries), BF16)
+        for _, count in parts
+        for _ in range(peers)
+    ]
     hbm = pl.BlockSpec(memory_space=pltpu.HBM)
-    return pl.pallas_call(
-        functools.partial(transform_kernel, peers, count, first, group),
+    out = pl.pallas_call(
+        functools.partial(transform_kernel, peers, parts, group),
         in_specs=[hbm] * 3 + [any_spec()] * len(after),
-        out_specs=[whole_spec()] * (peers + 1),
-        out_shape=[jax.ShapeDtypeStruct((count, blocks, 2 * entries), BF16)] * peers + [TOKEN],
+        out_specs=[whole_spec()] * (len(shapes) + 1),
+        out_shape=shapes + [TOKEN],
         scratch_shapes=[
             pltpu.SMEM(freq_index.shape, jnp.int32),
             pltpu.VMEM(weight.shape, F32),
             pltpu.VMEM(snapshots.shape, BF16),
-            pltpu.VMEM((2 * peers * count, length), BF16),
-            pltpu.VMEM((2 * entries // LANES, peers * count * blocks, LANES), F32),
+            pltpu.VMEM((2 * total, length), BF16),
+            pltpu.VMEM((2 * entries // LANES, total * blocks, LANES), F32),
             pltpu.SemaphoreType.DMA((2,)),
             pltpu.SemaphoreType.DMA((blocks // group,)),
         ],
@@ -153,6 +164,7 @@
         cost_estimate=light(),
         name="transform",
     )(in_hbm(freq_index), in_hbm(weight), in_hbm(snapshots), *after)
+    return [out[i * peers : (i + 1) * peers] for i in range(len(parts))], out[-1]
 
 
 def lane_low(shape, half):
@@ -177,7 +189,9 @@
     both = jnp.concatenate(
         [jnp.where(low, packed, other), jnp.where(low, other, packed)], 0
     )
-    turned = jnp.transpose(jnp.concatenate([both, both], 0))[:half]
+    turned = jnp.transpose(jnp.concatenate([packed, packed], 0))
+    turned = jnp.where(lane_low((half, half), rows), turned[:half], turned[half:])
+    turned = jnp.concatenate([turned, turned], 1)
     low = lane_low(both.shape, half)
     return 0.5 * jnp.where(low, both + turned, both - turned)
 
@@ -190,7 +204,7 @@
 
 
 def slot_owner(direct, slot):
-    return jnp.bitwise_xor(lax.axis_index("space"), slot) if direct else slot
+    return jnp.bitwise_xor(lax.axis_index("space") & 1, slot) if direct else slot
 
 
 def gram_kernel(peers, slots, direct, after, *refs):
@@ -252,6 +266,24 @@
         name="gram",
     )(*pieces, *after)
     return out[0], out[2:], out[1]
+
+
+def add_kernel(one, two, *refs):
+    out, token = refs[-2:]
+    token[...] = jnp.zeros_like(token)
+    out[...] = one[...] + two[...]
+
+
+def add(one, two, after):
+    return pl.pallas_call(
+        add_kernel,
+        in_specs=[whole_spec()] * 2 + [any_spec()] * len(after),
+        out_specs=[whole_spec()] * 2,
+        out_shape=[jax.ShapeDtypeStruct(one.shape, F32), TOKEN],
+        compiler_params=params(),
+        cost_estimate=light(),
+        name="add",
+    )(one, two, *after)
 
 
 def split(x):
@@ -358,20 +390,24 @@
     for slot in range(slots):
         owner = slot_owner(direct, slot)
         piece = pieces[slot] if direct else pieces[0].at[slot]
-        for i in range(per_slot):
-            f = owner * per_slot + i
-            compact = unpack(piece[i * half_rows : (i + 1) * half_rows, :])
-            filters[f, 0] = compact[:, :blocks]
-            filters[f, 1] = compact[:, blocks:]
-            wide = compact.astype(BF16).astype(F32)
-            both = full(wide).astype(BF16)
-            z = merged[f]
-            w = jnp.concatenate([z[:, :entries], z[:, entries:]], 0)
-            r = dot(both, w)
-            energy = jnp.sum(r * r, axis=0, keepdims=True)
-            at = per_slot * half_rows + i
-            total = piece[at : at + 1, 0:1]
-            energies[pl.ds(f, 1), :] = energy * (F32(states) / total)
+        for begin in range(0, per_slot, 4):
+            some = range(begin, min(begin + 4, per_slot))
+            at = [owner * per_slot + i for i in some]
+            packed = [piece[i * half_rows : (i + 1) * half_rows, :] for i in some]
+            tail = per_slot * half_rows
+            total = [piece[tail + i : tail + i + 1, 0:1] for i in some]
+            z = [merged[f] for f in at]
+            compact = each(unpack, packed)
+            both = each(lambda c: full(c.astype(BF16).astype(F32)).astype(BF16), compact)
+            w = each(lambda v: jnp.concatenate([v[:, :entries], v[:, entries:]], 0), z)
+            r = each(dot, both, w)
+            energy = each(
+                lambda v, t: jnp.sum(v * v, axis=0, keepdims=True) * (F32(states) / t), r, total
+            )
+            for f, c, e in zip(at, compact, energy):
+                filters[f, 0] = c[:, :blocks]
+                filters[f, 1] = c[:, blocks:]
+                energies[pl.ds(f, 1), :] = e
         put = pltpu.make_async_copy(
             filters.at[pl.ds(owner * per_slot, per_slot)],
             filters_out.at[pl.ds(first + owner * per_slot, per_slot)],
@@ -427,67 +463,81 @@
 
 
 def plan(owned, slots):
-    unit = max(slots, 8)
-    if owned % unit or owned // unit < 8:
-        return [owned]
-    return [owned // 4] * 4
-
-
-def order(chunks):
-    if chunks != 4:
-        return [(stage, c) for c in range(chunks) for stage in "TGFE"]
-    steps = "T0 T1 G0 T2 G1 F0 T3 G2 F1 E0 F2 E1 G3 E2 F3 E3"
-    return [(step[0], int(step[1:])) for step in steps.split()]
+    if slots != 4 or owned != 64:
+        return [owned], (("T", 0), ("G", 0), ("F", 0), ("E", 0))
+    return SIZES, ORDER
+
+
+SIZES = [24, 24, 16]
+ORDER = (
+    ("T", 0), ("T", 1), ("G", 0), ("A", 0), ("G", 1), ("F", 0), ("A", 1), ("E", 0),
+    ("G", 2), ("A", 2), ("F", 1), ("E", 1), ("F", 2), ("E", 2),
+)
+
+
+def permute(x, axis, offset):
+    pairs = [(i, i ^ offset) for i in range(lax.axis_size(axis))]
+    return lax.ppermute(x, axis, pairs)
 
 
 def on_device(snapshots, entry_weight, freq_index):
     peers = lax.axis_size("tm")
     slots = lax.axis_size("space")
     owned = freq_index.shape[0] // peers
-    sizes = plan(owned, slots)
+    sizes, order = plan(owned, slots)
     starts = [sum(sizes[:c]) for c in range(len(sizes))]
-    chunks = len(sizes)
-    direct = [False] * chunks
+    paired = slots == 4
+    halves = 2 if paired else slots
     weight = entry_weight.reshape(1, -1)
-    sent, merged, parts, pieces = {}, {}, {}, {}
+    sent, merged, grams, parts, pieces = {}, {}, {}, {}, {}
     carry = None
     token = []
 
     def do_transform(c):
         nonlocal token
-        out = transform(snapshots, weight, freq_index, peers, sizes[c], starts[c], token)
-        token = [out[peers]]
-        sent[c] = exchange(out[:peers], "tm")
-        if c + 1 < chunks:
-            token.append(sent[c][1])
+        chunks = [0] if c == 0 else range(1, len(sizes))
+        out, done = transform(
+            snapshots, weight, freq_index, peers, [(starts[k], sizes[k]) for k in chunks], token
+        )
+        token = [done]
+        for k, pieces_out in zip(chunks, out):
+            sent[k] = [pieces_out[0]] + [
+                permute(pieces_out[offset], "tm", offset) for offset in range(1, peers)
+            ]
 
     def do_gram(c):
         nonlocal token
-        merged[c], grams, done = gram(sent[c], slots, direct[c], token)
+        merged[c], grams[c], done = gram(sent[c], halves, paired, token)
         token = [done]
-        if direct[c]:
-            parts[c] = exchange(grams, "space")
+        if paired:
+            grams[c] = [grams[c][0], permute(grams[c][1], "space", 1)]
         else:
-            parts[c] = [lax.psum_scatter(grams[0], "space", scatter_dimension=0, tiled=True)]
+            parts[c] = [lax.psum_scatter(grams[c][0], "space", scatter_dimension=0, tiled=True)]
+
+    def do_add(c):
+        nonlocal token
+        half, done = add(*grams[c], token)
+        token = [done]
+        parts[c] = [half, permute(half, "space", 2)]
 
     def do_solve(c):
         nonlocal token
         own, done = solve(parts[c], token)
         token = [done]
-        if direct[c]:
-            pieces[c] = exchange([own] * slots, "space")
+        if paired:
+            pieces[c] = [own, permute(own, "space", 1)]
         else:
             pieces[c] = [lax.all_gather(own, "space", axis=0, tiled=False)]
 
     def do_energy(c):
         nonlocal token, carry
         *carry, done = filtered(
-            merged[c], pieces[c], slots, direct[c], carry, owned, starts[c], token
+            merged[c], pieces[c], halves, paired, carry, owned, starts[c], token
         )
         token = [done]
 
-    stages = {"T": do_transform, "G": do_gram, "F": do_solve, "E": do_energy}
-    for stage, c in order(chunks):
+    stages = {"T": do_transform, "G": do_gram, "A": do_add, "F": do_solve, "E": do_energy}
+    for stage, c in order:
         stages[stage](c)
     return (carry[0], carry[1])
 

time: 156 us -> 93.1 us (0.60)
  blocking collectives: 58.5 us -> 0 us
  waiting for transfers between devices: 21.3 us -> 40.9 us
  between operations: 14 us -> 0.96 us
  Pallas kernels: 41.8 us -> 29.7 us
  starting transfers between devices: 10.1 us -> 21.4 us
  local copies, waits for them, and re-layouts: 10.4 us -> 0 us
    all_gather x4 -> x0, blocking collectives: 58.5 us -> none  [do_solve(): pieces[c] = [lax.all_gather(own, 'space', axis=0, tiled=False)]]
    ppermute x12 -> x18, waiting for transfers between devices: 13.6 us -> 40.9 us  [permute(): return lax.ppermute(x, axis, pairs)]
    ppermute x12 -> x18, starting transfers between devices: 9.96 us -> 21.4 us  [permute(): return lax.ppermute(x, axis, pairs)]
    unnamed x40 -> x0, local copies, waits for them, and re-layouts: 10.4 us -> none
    reduce_scatter x4 -> x0, waiting for transfers between devices: 7.62 us -> none  [do_gram(): lax.psum_scatter(grams[0], 'space', scatter_dimension=0, tiled=True)]
    pallas_call x4 -> x5, Pallas kernels: 14.9 us -> 9.84 us  [the longest x2 9.78 us: transform(): pl.pallas_call(functools.partial(transform_kernel, peers, parts, group),...]
    pallas_call x4 -> x3, Pallas kernels: 5.92 us -> 2.14 us  [gram(): pl.pallas_call(functools.partial(gram_kernel, peers, slots, direct, len(a...]
    pallas_call x4 -> x3, Pallas kernels: 11.4 us -> 8.03 us  [filtered(): pl.pallas_call(functools.partial(energy_kernel, slots, direct, len(pieces...]
  transfers between devices with their start and end apart: 16 -> 18, of which waited for: 7 -> 9; matrix products, arithmetic and copies ran while one was open for 0% -> 0% of each run, Pallas kernels for 18% -> 18%
where the time goes in v3:
time: 93.1 us; the launch traced here: 92.9 us
  waiting for transfers between devices  40.9 us (44%)
  Pallas kernels  29.7 us (32%)
  starting transfers between devices  21.4 us (23%)
  between operations  0.96 us (1%)
    ppermute x18, waiting for transfers between devices, permute(): return lax.ppermute(x, axis, pairs)  40.9 us
    ppermute x18, starting transfers between devices, permute(): return lax.ppermute(x, axis, pairs)  21.4 us
    pallas_call x2, Pallas kernels, transform(): pl.pallas_call(functools.partial(transform_kernel, peers, parts, group),...  9.78 us
    pallas_call x3, Pallas kernels, solve(): pl.pallas_call(functools.partial(solve_kernel, len(parts)), in_specs=[who...  9.67 us
    pallas_call x3, Pallas kernels, filtered(): pl.pallas_call(functools.partial(energy_kernel, slots, direct, len(pieces...  8.03 us
    pallas_call x3, Pallas kernels, gram(): pl.pallas_call(functools.partial(gram_kernel, peers, slots, direct, len(a...  2.14 us
  transfers between devices with their start and end apart: 18, of which 9 were waited for; matrix products, arithmetic and copies ran while one was open for 0% of the time, Pallas kernels for 18%

profile of v3, /device:TPU:0, one launch (start us, length us, event | category | flops | bytes accessed | tf_op | source)
XLA Modules:
  0.0 92.9 jit_solution(3134321010249937021)
XLA Ops:
  0.6 4.3 %transform.2 = (bf16[24,16,512]{2,1,0:T(8,128)(2,1)S(1)}, bf16[24,16,512]{2,1,0:T(8,128)(2,1)S(1)}, bf16[24,16,512]{2,1,0:T(8,128)(2,1)S(1)}, bf16[24,16,512]{2,1,0:T(8,128)(2,1)S(1)}, f32[8,128]{1,0:T(8,128)S(1)}) custom-call(s32[256]{0:T(256)} %refs_0_.3, f32[1,256]{1,0:T(1,128)} %bitcast.1, bf16[16,512,256]{2,1,0:T(8,128)(2,1)} %refs_2_.3), custom_call_target="tpu_custom_call" | custom-call | flops 1024 | bytes 1024 | tf_op jit(solution)/shard_map/transform/pallas_call | solution.py:149
  4.9 0.5 collective-permute-start.3
  5.5 2.6 %collective-permute-start.4 = (bf16[24,16,512]{2,1,0:T(8,128)(2,1)S(1)}, bf16[24,16,512]{2,1,0:T(8,128)(2,1)S(1)}, u32[]{:S(2)}, u32[]{:S(2)}) collective-permute-start(bf16[24,16,512]{2,1,0:T(8,128)(2,1)S(1)} %get-tuple-element.55), channel_id=1, source_target_pairs={{0,2},{1,3},{2,0},{3,1},{4,6},{5,7},{6,4},{7,5},{8,10},{9,11},{10,... | collective-permute-start | bytes 1179656 | tf_op jit(solution)/shard_map/ppermute | solution.py:480
  8.0 0.1 collective-permute-start.5
  8.1 5.5 %transform.3 = (bf16[24,16,512]{2,1,0:T(8,128)(2,1)S(1)}, bf16[24,16,512]{2,1,0:T(8,128)(2,1)S(1)}, bf16[24,16,512]{2,1,0:T(8,128)(2,1)S(1)}, bf16[24,16,512]{2,...) custom-call(s32[256]{0:T(256)} %refs_0_.3, ...), custom_call_target="tpu_custom_call" | custom-call | flops 1024 | bytes 1024 | tf_op jit(solution)/shard_map/transform/pallas_call | solution.py:149
  13.6 1.7 %collective-permute-start.10 = (bf16[24,16,512]{2,1,0:T(8,128)(2,1)S(1)}, bf16[24,16,512]{2,1,0:T(8,128)(2,1)S(1)}, u32[]{:S(2)}, u32[]{:S(2)}) collective-permute-start(bf16[24,16,512]{2,1,0:T(8,128)(2,1)S(1)} %get-tuple-element.66), channel_id=1, source_target_pairs={{0,3},{1,2},{2,1},{3,0},{4,7},{5,6},{6,5},{7,4},{8,11},{9,10},{10,... | collective-permute-start | bytes 1179656 | tf_op jit(solution)/shard_map/ppermute | solution.py:480
  15.3 0.2 collective-permute-start.8
  15.5 0.0 collective-permute-done.3.refs_1_
  15.5 0.3 collective-permute-start.9
  15.8 2.2 %collective-permute-done.4.refs_2_ = bf16[24,16,512]{2,1,0:T(8,128)(2,1)S(1)} collective-permute-done((bf16[24,16,512]{2,1,0:T(8,128)(2,1)S(1)}, bf16[24,16,512]{2,1,0:T(8,128)(2,1)S(1)}, u32[]{:S(2)}, u32[]{:S(2)}) %collective-permute-start.4) | collective-permute-done | bytes 393248 | tf_op jit(solution)/shard_map/ppermute | solution.py:480
  18.0 7.9 %collective-permute-done.5.refs_3_ = bf16[24,16,512]{2,1,0:T(8,128)(2,1)S(1)} collective-permute-done((bf16[24,16,512]{2,1,0:T(8,128)(2,1)S(1)}, bf16[24,16,512]{2,1,0:T(8,128)(2,1)S(1)}, u32[]{:S(2)}, u32[]{:S(2)}) %collective-permute-start.5) | collective-permute-done | bytes 393248 | tf_op jit(solution)/shard_map/ppermute | solution.py:480
  25.9 0.8 gram.3
  26.7 1.7 %collective-permute-start.6 = (f32[12,32,128]{2,1,0:T(8,128)S(1)}, f32[12,32,128]{2,1,0:T(8,128)S(1)}, u32[]{:S(2)}, u32[]{:S(2)}) collective-permute-start(f32[12,32,128]{2,1,0:T(8,128)S(1)} %get-tuple-element.60), channel_id=1, source_target_pairs={{0,4},{4,0},{8,12},{12,8},{1,5},{5,1},{9,13},{13,9},{2,6},{6,2},{1... | collective-permute-start | bytes 589832 | tf_op jit(solution)/shard_map/ppermute | solution.py:480
  28.4 6.1 %collective-permute-done.6.two = f32[12,32,128]{2,1,0:T(8,128)S(1)} collective-permute-done((f32[12,32,128]{2,1,0:T(8,128)S(1)}, f32[12,32,128]{2,1,0:T(8,128)S(1)}, u32[]{:S(2)}, u32[]{:S(2)}) %collective-permute-start.6) | collective-permute-done | bytes 196640 | tf_op jit(solution)/shard_map/ppermute | solution.py:480
  34.5 2.7 %collective-permute-start.7 = (f32[12,32,128]{2,1,0:T(8,128)S(1)}, f32[12,32,128]{2,1,0:T(8,128)S(1)}, u32[]{:S(2)}, u32[]{:S(2)}) collective-permute-start(f32[12,32,128]{2,1,0:T(8,128)S(1)} %get-tuple-element.62.refs_0_), channel_id=1, source_target_pairs={{0,8},{4,12},{8,0},{12,4},{1,9},{5,13},{9,1},{13,5},{2,10},{6,14},... | collective-permute-start | bytes 589832 | tf_op jit(solution)/shard_map/ppermute | solution.py:480
  37.2 0.0 collective-permute-start
  37.2 0.0 collective-permute-done.10.refs_3_
  37.2 1.5 %collective-permute-start.1 = (bf16[16,16,512]{2,1,0:T(8,128)(2,1)S(1)}, bf16[16,16,512]{2,1,0:T(8,128)(2,1)S(1)}, u32[]{:S(2)}, u32[]{:S(2)}) collective-permute-start(bf16[16,16,512]{2,1,0:T(8,128)(2,1)S(1)} %get-tuple-element.51), channel_id=1, source_target_pairs={{0,2},{1,3},{2,0},{3,1},{4,6},{5,7},{6,4},{7,5},{8,10},{9,11},{10,... | collective-permute-start | bytes 786440 | tf_op jit(solution)/shard_map/ppermute | solution.py:480
  38.7 0.0 collective-permute-done.8.refs_1_
  38.7 0.3 collective-permute-start.2
  39.1 4.2 %collective-permute-done.9.refs_2_ = bf16[24,16,512]{2,1,0:T(8,128)(2,1)S(1)} collective-permute-done((bf16[24,16,512]{2,1,0:T(8,128)(2,1)S(1)}, bf16[24,16,512]{2,1,0:T(8,128)(2,1)S(1)}, u32[]{:S(2)}, u32[]{:S(2)}) %collective-permute-start.9) | collective-permute-done | bytes 393248 | tf_op jit(solution)/shard_map/ppermute | solution.py:480
  43.3 0.8 gram.4
  44.0 2.1 %collective-permute-start.12 = (f32[12,32,128]{2,1,0:T(8,128)S(1)}, f32[12,32,128]{2,1,0:T(8,128)S(1)}, u32[]{:S(2)}, u32[]{:S(2)}) collective-permute-start(f32[12,32,128]{2,1,0:T(8,128)S(1)} %get-tuple-element.71), channel_id=1, source_target_pairs={{0,4},{4,0},{8,12},{12,8},{1,5},{5,1},{9,13},{13,9},{2,6},{6,2},{1... | collective-permute-start | bytes 589832 | tf_op jit(solution)/shard_map/ppermute | solution.py:480
  46.1 0.5 collective-permute-done.7.refs_1_
  46.6 3.4 %filters.3 = (f32[400,128]{1,0:T(8,128)S(1)}, f32[8,128]{1,0:T(8,128)S(1)}) custom-call(f32[12,32,128]{2,1,0:T(8,128)S(1)} %get-tuple-element.62.refs_0_, f32[12,32,128]{2,1,0:T(8,128)S(1)} %collective-permute-done.7.refs_1_, f32[8,128]{1,0:T(8,128)S(1)} %get-tuple-element.68.refs_2_), custom_call_target="tpu_custom_call" | custom-call | flops 1024 | bytes 1024 | tf_op jit(solution)/shard_map/filters/pallas_call | solution.py:369
  50.0 0.8 collective-permute-start.11
  50.8 0.0 collective-permute-done.12.two
  50.8 3.5 %collective-permute-start.15 = (f32[12,32,128]{2,1,0:T(8,128)S(1)}, f32[12,32,128]{2,1,0:T(8,128)S(1)}, u32[]{:S(2)}, u32[]{:S(2)}) collective-permute-start(f32[12,32,128]{2,1,0:T(8,128)S(1)} %get-tuple-element.81.refs_0_), channel_id=1, source_target_pairs={{0,8},{4,12},{8,0},{12,4},{1,9},{5,13},{9,1},{13,5},{2,10},{6,14},... | collective-permute-start | bytes 589832 | tf_op jit(solution)/shard_map/ppermute | solution.py:480
  54.3 6.1 %collective-permute-done.11.refs_1_ = f32[400,128]{1,0:T(8,128)S(1)} collective-permute-done((f32[400,128]{1,0:T(8,128)S(1)}, f32[400,128]{1,0:T(8,128)S(1)}, u32[]{:S(2)}, u32[]{:S(2)}) %collective-permute-start.11) | collective-permute-done | bytes 204832 | tf_op jit(solution)/shard_map/ppermute | solution.py:480
  60.4 2.8 %energy.3 = (f32[64,256]{1,0:T(8,128)}, f32[64,2,64,64]{3,2,1,0:T(8,128)}, f32[8,128]{1,0:T(8,128)S(1)}) custom-call(bf16[24,64,512]{2,1,0:T(8,128)(2,1)S(1)} %get-tuple-element.58.merged, f32[400,128]{1,0:T(8,128)S(1)} %get-tuple-element.69.refs_0_, f32[400,128]{1,0:T(8,128)S(1)} %collective-permute-done.11.refs_1_, f32[8,128]{1,0:T(8,128)S(1)} %get-tuple-element.73.refs_2_), custom_call_target="tpu_custom_call" | custom-call | flops 1024 | bytes 1024 | tf_op jit(solution)/shard_map/energy/pallas_call | solution.py:432
  63.2 0.0 collective-permute-done.refs_1_
  63.2 0.0 collective-permute-done.1.refs_2_
  63.2 0.0 collective-permute-done.2.refs_3_
  63.2 0.6 gram.5
  63.9 0.1 collective-permute-start.13
  63.9 5.0 %collective-permute-done.13.two = f32[8,32,128]{2,1,0:T(8,128)S(1)} collective-permute-done((f32[8,32,128]{2,1,0:T(8,128)S(1)}, f32[8,32,128]{2,1,0:T(8,128)S(1)}, u32[]{:S(2)}, u32[]{:S(2)}) %collective-permute-start.13) | collective-permute-done | bytes 131104 | tf_op jit(solution)/shard_map/ppermute | solution.py:480
  68.9 0.0 collective-permute-done.15.refs_1_
  68.9 3.4 %filters.4 = (f32[400,128]{1,0:T(8,128)S(1)}, f32[8,128]{1,0:T(8,128)S(1)}) custom-call(f32[12,32,128]{2,1,0:T(8,128)S(1)} %get-tuple-element.81.refs_0_, f32[12,32,128]{2,1,0:T(8,128)S(1)} %collective-permute-done.15.refs_1_, f32[8,128]{1,0:T(8,128)S(1)} %get-tuple-element.82.refs_2_), custom_call_target="tpu_custom_call" | custom-call | flops 1024 | bytes 1024 | tf_op jit(solution)/shard_map/filters/pallas_call | solution.py:369
  72.3 0.1 collective-permute-start.16
  72.4 3.2 %collective-permute-start.14 = (f32[8,32,128]{2,1,0:T(8,128)S(1)}, f32[8,32,128]{2,1,0:T(8,128)S(1)}, u32[]{:S(2)}, u32[]{:S(2)}) collective-permute-start(f32[8,32,128]{2,1,0:T(8,128)S(1)} %get-tuple-element.79.refs_0_), channel_id=1, source_target_pairs={{0,8},{4,12},{8,0},{12,4},{1,9},{5,13},{9,1},{13,5},{2,10},{6,14},... | collective-permute-start | bytes 393224 | tf_op jit(solution)/shard_map/ppermute | solution.py:480
  75.6 4.0 %collective-permute-done.16.refs_1_ = f32[400,128]{1,0:T(8,128)S(1)} collective-permute-done((f32[400,128]{1,0:T(8,128)S(1)}, f32[400,128]{1,0:T(8,128)S(1)}, u32[]{:S(2)}, u32[]{:S(2)}) %collective-permute-start.16) | collective-permute-done | bytes 204832 | tf_op jit(solution)/shard_map/ppermute | solution.py:480
  79.6 2.6 %energy.4 = (f32[64,256]{1,0:T(8,128)}, f32[64,2,64,64]{3,2,1,0:T(8,128)}, f32[8,128]{1,0:T(8,128)S(1)}) custom-call(bf16[24,64,512]{2,1,0:T(8,128)(2,1)S(1)} %get-tuple-element.80.merged, f32[400,128]{1,0:T(8,128)S(1)} %get-tuple-element.83.refs_0_, f32[400,128]{1,0:T(8,128)S(1)} %collective-permute-done.16.refs_1_, ...), custom_call_target="tpu_custom_call", output_to_operand_aliasing={{0}: (3, {}), {1}: (4, {})} | custom-call | flops 1024 | bytes 1024 | tf_op jit(solution)/shard_map/energy/pallas_call | solution.py:432
  82.2 0.0 collective-permute-done.14.refs_1_
  82.2 2.8 %filters.5 = (f32[264,128]{1,0:T(8,128)S(1)}, f32[8,128]{1,0:T(8,128)S(1)}) custom-call(f32[8,32,128]{2,1,0:T(8,128)S(1)} %get-tuple-element.79.refs_0_, f32[8,32,128]{2,1,0:T(8,128)S(1)} %collective-permute-done.14.refs_1_, f32[8,128]{1,0:T(8,128)S(1)} %get-tuple-element.87.refs_2_), custom_call_target="tpu_custom_call" | custom-call | flops 1024 | bytes 1024 | tf_op jit(solution)/shard_map/filters/pallas_call | solution.py:369
  85.1 0.1 collective-permute-start.17
  85.2 5.0 %collective-permute-done.17.refs_1_ = f32[264,128]{1,0:T(8,128)S(1)} collective-permute-done((f32[264,128]{1,0:T(8,128)S(1)}, f32[264,128]{1,0:T(8,128)S(1)}, u32[]{:S(2)}, u32[]{:S(2)}) %collective-permute-start.17) | collective-permute-done | bytes 135200 | tf_op jit(solution)/shard_map/ppermute | solution.py:480
  90.2 2.6 %energy.5 = (f32[64,256]{1,0:T(8,128)}, f32[64,2,64,64]{3,2,1,0:T(8,128)}, f32[8,128]{1,0:T(8,128)}) custom-call(bf16[16,64,512]{2,1,0:T(8,128)(2,1)S(1)} %get-tuple-element.75.merged, f32[264,128]{1,0:T(8,128)S(1)} %get-tuple-element.88.refs_0_, f32[264,128]{1,0:T(8,128)S(1)} %collective-permute-done.17.refs_1_, ...), custom_call_target="tpu_custom_call", output_to_operand_aliasing={{0}: (3, {}), {1}: (4, {})} | custom-call | flops 1024 | bytes 1024 | tf_op jit(solution)/shard_map/energy/pallas_call | solution.py:432
  (3 shorter events, 0.1 us)
Async XLA Ops:
  4.9 10.6 %collective-permute-start.3 = (bf16[24,16,512]{2,1,0:T(8,128)(2,1)S(1)}, bf16[24,16,512]{2,1,0:T(8,128)(2,1)S(1)}, u32[]{:S(2)}, u32[]{:S(2)}) collective-permute-start(bf16[24,16,512]{2,1,0:T(8,128)(2,1)S(1)} %get-tuple-element.54), channel_id=1, source_target_pairs={{0,1},{1,0},{2,3},{3,2},{4,5},{5,4},{6,7},{7,6},{8,9},{9,8},{10,11... | collective-permute-start | bytes 1179656 | tf_op jit(solution)/shard_map/ppermute | solution.py:480
  5.5 12.5 %collective-permute-start.4 = (bf16[24,16,512]{2,1,0:T(8,128)(2,1)S(1)}, bf16[24,16,512]{2,1,0:T(8,128)(2,1)S(1)}, u32[]{:S(2)}, u32[]{:S(2)}) collective-permute-start(bf16[24,16,512]{2,1,0:T(8,128)(2,1)S(1)} %get-tuple-element.55), channel_id=1, source_target_pairs={{0,2},{1,3},{2,0},{3,1},{4,6},{5,7},{6,4},{7,5},{8,10},{9,11},{10,... | collective-permute-start | bytes 1179656 | tf_op jit(solution)/shard_map/ppermute | solution.py:480
  8.0 17.9 %collective-permute-start.5 = (bf16[24,16,512]{2,1,0:T(8,128)(2,1)S(1)}, bf16[24,16,512]{2,1,0:T(8,128)(2,1)S(1)}, u32[]{:S(2)}, u32[]{:S(2)}) collective-permute-start(bf16[24,16,512]{2,1,0:T(8,128)(2,1)S(1)} %get-tuple-element.56), channel_id=1, source_target_pairs={{0,3},{1,2},{2,1},{3,0},{4,7},{5,6},{6,5},{7,4},{8,11},{9,10},{10,... | collective-permute-start | bytes 1179656 | tf_op jit(solution)/shard_map/ppermute | solution.py:480
  13.6 23.6 %collective-permute-start.10 = (bf16[24,16,512]{2,1,0:T(8,128)(2,1)S(1)}, bf16[24,16,512]{2,1,0:T(8,128)(2,1)S(1)}, u32[]{:S(2)}, u32[]{:S(2)}) collective-permute-start(bf16[24,16,512]{2,1,0:T(8,128)(2,1)S(1)} %get-tuple-element.66), channel_id=1, source_target_pairs={{0,3},{1,2},{2,1},{3,0},{4,7},{5,6},{6,5},{7,4},{8,11},{9,10},{10,... | collective-permute-start | bytes 1179656 | tf_op jit(solution)/shard_map/ppermute | solution.py:480
  15.3 23.4 %collective-permute-start.8 = (bf16[24,16,512]{2,1,0:T(8,128)(2,1)S(1)}, bf16[24,16,512]{2,1,0:T(8,128)(2,1)S(1)}, u32[]{:S(2)}, u32[]{:S(2)}) collective-permute-start(bf16[24,16,512]{2,1,0:T(8,128)(2,1)S(1)} %get-tuple-element.64), channel_id=1, source_target_pairs={{0,1},{1,0},{2,3},{3,2},{4,5},{5,4},{6,7},{7,6},{8,9},{9,8},{10,11... | collective-permute-start | bytes 1179656 | tf_op jit(solution)/shard_map/ppermute | solution.py:480
  15.5 27.8 %collective-permute-start.9 = (bf16[24,16,512]{2,1,0:T(8,128)(2,1)S(1)}, bf16[24,16,512]{2,1,0:T(8,128)(2,1)S(1)}, u32[]{:S(2)}, u32[]{:S(2)}) collective-permute-start(bf16[24,16,512]{2,1,0:T(8,128)(2,1)S(1)} %get-tuple-element.65), channel_id=1, source_target_pairs={{0,2},{1,3},{2,0},{3,1},{4,6},{5,7},{6,4},{7,5},{8,10},{9,11},{10,... | collective-permute-start | bytes 1179656 | tf_op jit(solution)/shard_map/ppermute | solution.py:480
  26.7 7.8 %collective-permute-start.6 = (f32[12,32,128]{2,1,0:T(8,128)S(1)}, f32[12,32,128]{2,1,0:T(8,128)S(1)}, u32[]{:S(2)}, u32[]{:S(2)}) collective-permute-start(f32[12,32,128]{2,1,0:T(8,128)S(1)} %get-tuple-element.60), channel_id=1, source_target_pairs={{0,4},{4,0},{8,12},{12,8},{1,5},{5,1},{9,13},{13,9},{2,6},{6,2},{1... | collective-permute-start | bytes 589832 | tf_op jit(solution)/shard_map/ppermute | solution.py:480
  34.5 12.1 %collective-permute-start.7 = (f32[12,32,128]{2,1,0:T(8,128)S(1)}, f32[12,32,128]{2,1,0:T(8,128)S(1)}, u32[]{:S(2)}, u32[]{:S(2)}) collective-permute-start(f32[12,32,128]{2,1,0:T(8,128)S(1)} %get-tuple-element.62.refs_0_), channel_id=1, source_target_pairs={{0,8},{4,12},{8,0},{12,4},{1,9},{5,13},{9,1},{13,5},{2,10},{6,14},... | collective-permute-start | bytes 589832 | tf_op jit(solution)/shard_map/ppermute | solution.py:480
  37.2 26.0 %collective-permute-start = (bf16[16,16,512]{2,1,0:T(8,128)(2,1)S(1)}, bf16[16,16,512]{2,1,0:T(8,128)(2,1)S(1)}, u32[]{:S(2)}, u32[]{:S(2)}) collective-permute-start(bf16[16,16,512]{2,1,0:T(8,128)(2,1)S(1)} %get-tuple-element.50), channel_id=1, source_target_pairs={{0,1},{1,0},{2,3},{3,2},{4,5},{5,4},{6,7},{7,6},{8,9},{9,8},{10,11... | collective-permute-start | bytes 786440 | tf_op jit(solution)/shard_map/ppermute | solution.py:480
  37.2 26.0 %collective-permute-start.1 = (bf16[16,16,512]{2,1,0:T(8,128)(2,1)S(1)}, bf16[16,16,512]{2,1,0:T(8,128)(2,1)S(1)}, u32[]{:S(2)}, u32[]{:S(2)}) collective-permute-start(bf16[16,16,512]{2,1,0:T(8,128)(2,1)S(1)} %get-tuple-element.51), channel_id=1, source_target_pairs={{0,2},{1,3},{2,0},{3,1},{4,6},{5,7},{6,4},{7,5},{8,10},{9,11},{10,... | collective-permute-start | bytes 786440 | tf_op jit(solution)/shard_map/ppermute | solution.py:480
  38.7 24.5 %collective-permute-start.2 = (bf16[16,16,512]{2,1,0:T(8,128)(2,1)S(1)}, bf16[16,16,512]{2,1,0:T(8,128)(2,1)S(1)}, u32[]{:S(2)}, u32[]{:S(2)}) collective-permute-start(bf16[16,16,512]{2,1,0:T(8,128)(2,1)S(1)} %get-tuple-element.52), channel_id=1, source_target_pairs={{0,3},{1,2},{2,1},{3,0},{4,7},{5,6},{6,5},{7,4},{8,11},{9,10},{10,... | collective-permute-start | bytes 786440 | tf_op jit(solution)/shard_map/ppermute | solution.py:480
  44.0 6.8 %collective-permute-start.12 = (f32[12,32,128]{2,1,0:T(8,128)S(1)}, f32[12,32,128]{2,1,0:T(8,128)S(1)}, u32[]{:S(2)}, u32[]{:S(2)}) collective-permute-start(f32[12,32,128]{2,1,0:T(8,128)S(1)} %get-tuple-element.71), channel_id=1, source_target_pairs={{0,4},{4,0},{8,12},{12,8},{1,5},{5,1},{9,13},{13,9},{2,6},{6,2},{1... | collective-permute-start | bytes 589832 | tf_op jit(solution)/shard_map/ppermute | solution.py:480
  50.0 10.4 %collective-permute-start.11 = (f32[400,128]{1,0:T(8,128)S(1)}, f32[400,128]{1,0:T(8,128)S(1)}, u32[]{:S(2)}, u32[]{:S(2)}) collective-permute-start(f32[400,128]{1,0:T(8,128)S(1)} %get-tuple-element.69.refs_0_), channel_id=1, source_target_pairs={{0,4},{4,0},{8,12},{12,8},{1,5},{5,1},{9,13},{13,9},{2,6},{6,2},{1... | collective-permute-start | bytes 614408 | tf_op jit(solution)/shard_map/ppermute | solution.py:480
  50.8 18.1 %collective-permute-start.15 = (f32[12,32,128]{2,1,0:T(8,128)S(1)}, f32[12,32,128]{2,1,0:T(8,128)S(1)}, u32[]{:S(2)}, u32[]{:S(2)}) collective-permute-start(f32[12,32,128]{2,1,0:T(8,128)S(1)} %get-tuple-element.81.refs_0_), channel_id=1, source_target_pairs={{0,8},{4,12},{8,0},{12,4},{1,9},{5,13},{9,1},{13,5},{2,10},{6,14},... | collective-permute-start | bytes 589832 | tf_op jit(solution)/shard_map/ppermute | solution.py:480
  63.9 5.0 %collective-permute-start.13 = (f32[8,32,128]{2,1,0:T(8,128)S(1)}, f32[8,32,128]{2,1,0:T(8,128)S(1)}, u32[]{:S(2)}, u32[]{:S(2)}) collective-permute-start(f32[8,32,128]{2,1,0:T(8,128)S(1)} %get-tuple-element.77), channel_id=1, source_target_pairs={{0,4},{4,0},{8,12},{12,8},{1,5},{5,1},{9,13},{13,9},{2,6},{6,2},{1... | collective-permute-start | bytes 393224 | tf_op jit(solution)/shard_map/ppermute | solution.py:480
  72.3 7.2 %collective-permute-start.16 = (f32[400,128]{1,0:T(8,128)S(1)}, f32[400,128]{1,0:T(8,128)S(1)}, u32[]{:S(2)}, u32[]{:S(2)}) collective-permute-start(f32[400,128]{1,0:T(8,128)S(1)} %get-tuple-element.83.refs_0_), channel_id=1, source_target_pairs={{0,4},{4,0},{8,12},{12,8},{1,5},{5,1},{9,13},{13,9},{2,6},{6,2},{1... | collective-permute-start | bytes 614408 | tf_op jit(solution)/shard_map/ppermute | solution.py:480
  72.4 9.8 %collective-permute-start.14 = (f32[8,32,128]{2,1,0:T(8,128)S(1)}, f32[8,32,128]{2,1,0:T(8,128)S(1)}, u32[]{:S(2)}, u32[]{:S(2)}) collective-permute-start(f32[8,32,128]{2,1,0:T(8,128)S(1)} %get-tuple-element.79.refs_0_), channel_id=1, source_target_pairs={{0,8},{4,12},{8,0},{12,4},{1,9},{5,13},{9,1},{13,5},{2,10},{6,14},... | collective-permute-start | bytes 393224 | tf_op jit(solution)/shard_map/ppermute | solution.py:480
  85.1 5.1 %collective-permute-start.17 = (f32[264,128]{1,0:T(8,128)S(1)}, f32[264,128]{1,0:T(8,128)S(1)}, u32[]{:S(2)}, u32[]{:S(2)}) collective-permute-start(f32[264,128]{1,0:T(8,128)S(1)} %get-tuple-element.88.refs_0_), channel_id=1, source_target_pairs={{0,4},{4,0},{8,12},{12,8},{1,5},{5,1},{9,13},{13,9},{2,6},{6,2},{1... | collective-permute-start | bytes 405512 | tf_op jit(solution)/shard_map/ppermute | solution.py:480

commit v4 on v3

--- a/solution.py
+++ b/solution.py
@@ -314,32 +314,33 @@
     grams = [load(i) for i in range(number)]
     shift = each(lambda g: jnp.sum(g * eye, keepdims=True) * F32(1.0 / half), grams)
     system = each(lambda g, m: g / m + eye, grams, shift)
-    parts_a = each(lambda a: split(full(a)), system)
-    high = [p[0] for p in parts_a]
-    both = parts_a
+    both = each(lambda a: split(full(a)), system)
 
     low_end, high_end = 1.0, float(half + 1)
     mid, radius = (high_end + low_end) / 2, (high_end - low_end) / 2
     ratio = mid / radius
     t = 2 * ratio * ratio - 1
     scale = 2.0 / (radius * radius * t)
-    x = each(lambda a: F32(scale) * (F32(2 * mid) * eye - a), system)
-    for kind in ("one", "one", "one", "two", "last"):
+    x = each(lambda a: (F32(scale) * (F32(2 * mid) * eye - a)).astype(BF16), system)
+    p = each(lambda v, a: eye - (dot(v, a[0]) + dot(v, a[1])), x, both)
+    x = each(lambda v: v.astype(F32), x)
+    for _ in range(3):
+        t_next = 2 * t * t - 1
+        c = F32(2 * t * t / t_next)
+        pf = each(lambda q: full(q).astype(BF16), p)
+        xp = each(lambda v, q: jnp.concatenate([v, q], 0).astype(BF16), x, p)
+        moved = each(dot, xp, pf)
+        x = each(lambda v, m: c * (v + m[:half]), x, moved)
+        p = each(lambda m: c * m[half:] - F32(1 / t_next) * eye, moved)
+        t = t_next
+    for kind in ("scaled", "last"):
         xb = each(lambda v: v.astype(BF16), x)
-        if kind == "one":
-            residual = each(lambda v, a: eye - dot(v, a), xb, high)
-        else:
-            residual = each(lambda v, a: eye - (dot(v, a[0]) + dot(v, a[1])), xb, both)
         xw = each(lambda v: v.astype(F32), xb)
         xf = each(lambda v: full(v).astype(BF16), xw)
+        residual = each(lambda v, a: eye - (dot(v, a[0]) + dot(v, a[1])), xb, both)
         step = each(lambda r, v: dot(r.astype(BF16), v), residual, xf)
-        if kind == "last":
-            factor = 1.0
-        else:
-            t_next = 2 * t * t - 1
-            factor = 2 * t * t / t_next
-            t = t_next
-        x = each(lambda v, s: F32(factor) * (v + s), xw, step)
+        factor = 1.0 if kind == "last" else 2 * t * t / (2 * t * t - 1)
+        x = each(lambda v, m: F32(factor) * (v + m), xw, step)
     packed = each(lambda v: pack(eye - v), x)
     for i in range(number):
         out[i * half_rows : (i + 1) * half_rows, :] = packed[i]
@@ -408,13 +409,13 @@
                 filters[f, 0] = c[:, :blocks]
                 filters[f, 1] = c[:, blocks:]
                 energies[pl.ds(f, 1), :] = e
-        put = pltpu.make_async_copy(
-            filters.at[pl.ds(owner * per_slot, per_slot)],
-            filters_out.at[pl.ds(first + owner * per_slot, per_slot)],
-            filters_sem.at[slot],
-        )
-        put.start()
-        puts.append(put)
+            put = pltpu.make_async_copy(
+                filters.at[pl.ds(at[0], len(at))],
+                filters_out.at[pl.ds(first + at[0], len(at))],
+                filters_sem.at[len(puts)],
+            )
+            put.start()
+            puts.append(put)
     put = pltpu.make_async_copy(
         energies, energies_out.at[pl.ds(first, count)], energies_sem.at[0]
     )
@@ -445,7 +446,7 @@
             pltpu.VMEM((count, entries), F32),
             pltpu.VMEM((count, 2, blocks, blocks), F32),
             pltpu.SemaphoreType.DMA((1,)),
-            pltpu.SemaphoreType.DMA((slots,)),
+            pltpu.SemaphoreType.DMA((slots * -(-(count // slots) // 4),)),
         ],
         compiler_params=params(),
         cost_estimate=light(),
@@ -470,8 +471,8 @@
 
 SIZES = [24, 24, 16]
 ORDER = (
-    ("T", 0), ("T", 1), ("G", 0), ("A", 0), ("G", 1), ("F", 0), ("A", 1), ("E", 0),
-    ("G", 2), ("A", 2), ("F", 1), ("E", 1), ("F", 2), ("E", 2),
+    ("T", 0), ("T", 1), ("G", 0), ("A", 0), ("G", 1), ("F", 0), ("A", 1), ("G", 2),
+    ("E", 0), ("A", 2), ("F", 1), ("F", 2), ("E", 1), ("E", 2),
 )
 
 

time: 93.1 us -> 83.6 us (0.90)
  waiting for transfers between devices: 40.9 us -> 29 us
  starting transfers between devices: 21.4 us -> 23.4 us
    ppermute x18, waiting for transfers between devices: 40.9 us -> 29 us  [permute(): return lax.ppermute(x, axis, pairs)]
    ppermute x18, starting transfers between devices: 21.4 us -> 23.4 us  [permute(): return lax.ppermute(x, axis, pairs)]
  transfers between devices with their start and end apart: 18 -> 18, of which waited for: 9 -> 10; matrix products, arithmetic and copies ran while one was open for 0% -> 0% of each run, Pallas kernels for 18% -> 28%
where the time goes in v4:
time: 83.6 us; the launch traced here: 83.4 us
  Pallas kernels  30.1 us (36%)
  waiting for transfers between devices  29 us (35%)
  starting transfers between devices  23.4 us (28%)
  between operations  0.91 us (1%)
    ppermute x18, waiting for transfers between devices, permute(): return lax.ppermute(x, axis, pairs)  29 us
    ppermute x18, starting transfers between devices, permute(): return lax.ppermute(x, axis, pairs)  23.4 us
    pallas_call x3, Pallas kernels, solve(): pl.pallas_call(functools.partial(solve_kernel, len(parts)), in_specs=[who...  10.4 us
    pallas_call x2, Pallas kernels, transform(): pl.pallas_call(functools.partial(transform_kernel, peers, parts, group),...  9.78 us
    pallas_call x3, Pallas kernels, filtered(): pl.pallas_call(functools.partial(energy_kernel, slots, direct, len(pieces...  7.78 us
    pallas_call x3, Pallas kernels, gram(): pl.pallas_call(functools.partial(gram_kernel, peers, slots, direct, len(a...  2.14 us
  transfers between devices with their start and end apart: 18, of which 10 were waited for; matrix products, arithmetic and copies ran while one was open for 0% of the time, Pallas kernels for 28%

profile of v4, /device:TPU:0, one launch (start us, length us, event | category | flops | bytes accessed | tf_op | source)
XLA Modules:
  0.0 83.4 jit_solution(16505303774681422812)
XLA Ops:
  0.6 4.3 %transform.2 = (bf16[24,16,512]{2,1,0:T(8,128)(2,1)S(1)}, bf16[24,16,512]{2,1,0:T(8,128)(2,1)S(1)}, bf16[24,16,512]{2,1,0:T(8,128)(2,1)S(1)}, bf16[24,16,512]{2,1,0:T(8,128)(2,1)S(1)}, f32[8,128]{1,0:T(8,128)S(1)}) custom-call(s32[256]{0:T(256)} %refs_0_.3, f32[1,256]{1,0:T(1,128)} %bitcast.1, bf16[16,512,256]{2,1,0:T(8,128)(2,1)} %refs_2_.3), custom_call_target="tpu_custom_call" | custom-call | flops 1024 | bytes 1024 | tf_op jit(solution)/shard_map/transform/pallas_call | solution.py:149
  4.9 0.5 collective-permute-start.6
  5.5 2.6 %collective-permute-start.7 = (bf16[24,16,512]{2,1,0:T(8,128)(2,1)S(1)}, bf16[24,16,512]{2,1,0:T(8,128)(2,1)S(1)}, u32[]{:S(2)}, u32[]{:S(2)}) collective-permute-start(bf16[24,16,512]{2,1,0:T(8,128)(2,1)S(1)} %get-tuple-element.59), channel_id=1, source_target_pairs={{0,2},{1,3},{2,0},{3,1},{4,6},{5,7},{6,4},{7,5},{8,10},{9,11},{10,... | collective-permute-start | bytes 1179656 | tf_op jit(solution)/shard_map/ppermute | solution.py:481
  8.0 0.1 collective-permute-start.8
  8.1 5.5 %transform.3 = (bf16[24,16,512]{2,1,0:T(8,128)(2,1)S(1)}, bf16[24,16,512]{2,1,0:T(8,128)(2,1)S(1)}, bf16[24,16,512]{2,1,0:T(8,128)(2,1)S(1)}, bf16[24,16,512]{2,...) custom-call(s32[256]{0:T(256)} %refs_0_.3, ...), custom_call_target="tpu_custom_call" | custom-call | flops 1024 | bytes 1024 | tf_op jit(solution)/shard_map/transform/pallas_call | solution.py:149
  13.6 0.2 collective-permute-start.3
  13.8 1.9 %collective-permute-start.4 = (bf16[24,16,512]{2,1,0:T(8,128)(2,1)S(1)}, bf16[24,16,512]{2,1,0:T(8,128)(2,1)S(1)}, u32[]{:S(2)}, u32[]{:S(2)}) collective-permute-start(bf16[24,16,512]{2,1,0:T(8,128)(2,1)S(1)} %get-tuple-element.55), channel_id=1, source_target_pairs={{0,2},{1,3},{2,0},{3,1},{4,6},{5,7},{6,4},{7,5},{8,10},{9,11},{10,... | collective-permute-start | bytes 1179656 | tf_op jit(solution)/shard_map/ppermute | solution.py:481
  15.7 0.0 collective-permute-done.6.refs_1_
  15.7 0.0 collective-permute-start.5
  15.7 2.3 %collective-permute-done.7.refs_2_ = bf16[24,16,512]{2,1,0:T(8,128)(2,1)S(1)} collective-permute-done((bf16[24,16,512]{2,1,0:T(8,128)(2,1)S(1)}, bf16[24,16,512]{2,1,0:T(8,128)(2,1)S(1)}, u32[]{:S(2)}, u32[]{:S(2)}) %collective-permute-start.7) | collective-permute-done | bytes 393248 | tf_op jit(solution)/shard_map/ppermute | solution.py:481
  18.0 7.9 %collective-permute-done.8.refs_3_ = bf16[24,16,512]{2,1,0:T(8,128)(2,1)S(1)} collective-permute-done((bf16[24,16,512]{2,1,0:T(8,128)(2,1)S(1)}, bf16[24,16,512]{2,1,0:T(8,128)(2,1)S(1)}, u32[]{:S(2)}, u32[]{:S(2)}) %collective-permute-start.8) | collective-permute-done | bytes 393248 | tf_op jit(solution)/shard_map/ppermute | solution.py:481
  25.9 0.8 gram.3
  26.7 1.7 %collective-permute-start.9 = (f32[12,32,128]{2,1,0:T(8,128)S(1)}, f32[12,32,128]{2,1,0:T(8,128)S(1)}, u32[]{:S(2)}, u32[]{:S(2)}) collective-permute-start(f32[12,32,128]{2,1,0:T(8,128)S(1)} %get-tuple-element.63), channel_id=1, source_target_pairs={{0,4},{4,0},{8,12},{12,8},{1,5},{5,1},{9,13},{13,9},{2,6},{6,2},{1... | collective-permute-start | bytes 589832 | tf_op jit(solution)/shard_map/ppermute | solution.py:481
  28.4 5.8 %collective-permute-done.9.two = f32[12,32,128]{2,1,0:T(8,128)S(1)} collective-permute-done((f32[12,32,128]{2,1,0:T(8,128)S(1)}, f32[12,32,128]{2,1,0:T(8,128)S(1)}, u32[]{:S(2)}, u32[]{:S(2)}) %collective-permute-start.9) | collective-permute-done | bytes 196640 | tf_op jit(solution)/shard_map/ppermute | solution.py:481
  34.2 2.8 %collective-permute-start.11 = (f32[12,32,128]{2,1,0:T(8,128)S(1)}, f32[12,32,128]{2,1,0:T(8,128)S(1)}, u32[]{:S(2)}, u32[]{:S(2)}) collective-permute-start(f32[12,32,128]{2,1,0:T(8,128)S(1)} %get-tuple-element.68.refs_0_), channel_id=1, source_target_pairs={{0,8},{4,12},{8,0},{12,4},{1,9},{5,13},{9,1},{13,5},{2,10},{6,14},... | collective-permute-start | bytes 589832 | tf_op jit(solution)/shard_map/ppermute | solution.py:481
  37.0 0.0 collective-permute-start
  37.0 0.0 collective-permute-done.3.refs_1_
  37.0 1.5 %collective-permute-start.1 = (bf16[16,16,512]{2,1,0:T(8,128)(2,1)S(1)}, bf16[16,16,512]{2,1,0:T(8,128)(2,1)S(1)}, u32[]{:S(2)}, u32[]{:S(2)}) collective-permute-start(bf16[16,16,512]{2,1,0:T(8,128)(2,1)S(1)} %get-tuple-element.51), channel_id=1, source_target_pairs={{0,2},{1,3},{2,0},{3,1},{4,6},{5,7},{6,4},{7,5},{8,10},{9,11},{10,... | collective-permute-start | bytes 786440 | tf_op jit(solution)/shard_map/ppermute | solution.py:481
  38.5 0.0 collective-permute-done.4.refs_2_
  38.5 0.3 collective-permute-start.2
  38.9 3.9 %collective-permute-done.5.refs_3_ = bf16[24,16,512]{2,1,0:T(8,128)(2,1)S(1)} collective-permute-done((bf16[24,16,512]{2,1,0:T(8,128)(2,1)S(1)}, bf16[24,16,512]{2,1,0:T(8,128)(2,1)S(1)}, u32[]{:S(2)}, u32[]{:S(2)}) %collective-permute-start.5) | collective-permute-done | bytes 393248 | tf_op jit(solution)/shard_map/ppermute | solution.py:481
  42.7 0.8 gram.4
  43.5 1.7 %collective-permute-start.10 = (f32[12,32,128]{2,1,0:T(8,128)S(1)}, f32[12,32,128]{2,1,0:T(8,128)S(1)}, u32[]{:S(2)}, u32[]{:S(2)}) collective-permute-start(f32[12,32,128]{2,1,0:T(8,128)S(1)} %get-tuple-element.67), channel_id=1, source_target_pairs={{0,4},{4,0},{8,12},{12,8},{1,5},{5,1},{9,13},{13,9},{2,6},{6,2},{1... | collective-permute-start | bytes 589832 | tf_op jit(solution)/shard_map/ppermute | solution.py:481
  45.2 0.9 %collective-permute-done.11.refs_1_ = f32[12,32,128]{2,1,0:T(8,128)S(1)} collective-permute-done((f32[12,32,128]{2,1,0:T(8,128)S(1)}, f32[12,32,128]{2,1,0:T(8,128)S(1)}, u32[]{:S(2)}, u32[]{:S(2)}) %collective-permute-start.11) | collective-permute-done | bytes 196640 | tf_op jit(solution)/shard_map/ppermute | solution.py:481
  46.1 3.7 %filters.3 = (f32[400,128]{1,0:T(8,128)S(1)}, f32[8,128]{1,0:T(8,128)S(1)}) custom-call(f32[12,32,128]{2,1,0:T(8,128)S(1)} %get-tuple-element.68.refs_0_, f32[12,32,128]{2,1,0:T(8,128)S(1)} %collective-permute-done.11.refs_1_, f32[8,128]{1,0:T(8,128)S(1)} %get-tuple-element.69.refs_2_), custom_call_target="tpu_custom_call" | custom-call | flops 1024 | bytes 1024 | tf_op jit(solution)/shard_map/filters/pallas_call | solution.py:370
  49.8 0.8 collective-permute-start.13
  50.6 0.4 collective-permute-done.10.two
  51.0 3.0 %collective-permute-start.15 = (f32[12,32,128]{2,1,0:T(8,128)S(1)}, f32[12,32,128]{2,1,0:T(8,128)S(1)}, u32[]{:S(2)}, u32[]{:S(2)}) collective-permute-start(f32[12,32,128]{2,1,0:T(8,128)S(1)} %get-tuple-element.80.refs_0_), channel_id=1, source_target_pairs={{0,8},{4,12},{8,0},{12,4},{1,9},{5,13},{9,1},{13,5},{2,10},{6,14},... | collective-permute-start | bytes 589832 | tf_op jit(solution)/shard_map/ppermute | solution.py:481
  54.1 0.0 collective-permute-done.refs_1_
  54.1 0.0 collective-permute-done.1.refs_2_
  54.1 0.0 collective-permute-done.2.refs_3_
  54.1 0.6 gram.5
  54.7 1.6 %collective-permute-start.12 = (f32[8,32,128]{2,1,0:T(8,128)S(1)}, f32[8,32,128]{2,1,0:T(8,128)S(1)}, u32[]{:S(2)}, u32[]{:S(2)}) collective-permute-start(f32[8,32,128]{2,1,0:T(8,128)S(1)} %get-tuple-element.74), channel_id=1, source_target_pairs={{0,4},{4,0},{8,12},{12,8},{1,5},{5,1},{9,13},{13,9},{2,6},{6,2},{1... | collective-permute-start | bytes 393224 | tf_op jit(solution)/shard_map/ppermute | solution.py:481
  56.3 5.4 %collective-permute-done.13.refs_1_ = f32[400,128]{1,0:T(8,128)S(1)} collective-permute-done((f32[400,128]{1,0:T(8,128)S(1)}, f32[400,128]{1,0:T(8,128)S(1)}, u32[]{:S(2)}, u32[]{:S(2)}) %collective-permute-start.13) | collective-permute-done | bytes 204832 | tf_op jit(solution)/shard_map/ppermute | solution.py:481
  61.7 2.7 %energy.3 = (f32[64,256]{1,0:T(8,128)}, f32[64,2,64,64]{3,2,1,0:T(8,128)}, f32[8,128]{1,0:T(8,128)S(1)}) custom-call(bf16[24,64,512]{2,1,0:T(8,128)(2,1)S(1)} %get-tuple-element.75.merged, f32[400,128]{1,0:T(8,128)S(1)} %get-tuple-element.76.refs_0_, f32[400,128]{1,0:T(8,128)S(1)} %collective-permute-done.13.refs_1_, f32[8,128]{1,0:T(8,128)S(1)} %get-tuple-element.77.refs_2_), custom_call_target="tpu_custom_call" | custom-call | flops 1024 | bytes 1024 | tf_op jit(solution)/shard_map/energy/pallas_call | solution.py:433
  64.4 0.0 collective-permute-done.12.two
  64.4 2.0 %collective-permute-start.14 = (f32[8,32,128]{2,1,0:T(8,128)S(1)}, f32[8,32,128]{2,1,0:T(8,128)S(1)}, u32[]{:S(2)}, u32[]{:S(2)}) collective-permute-start(f32[8,32,128]{2,1,0:T(8,128)S(1)} %get-tuple-element.79.refs_0_), channel_id=1, source_target_pairs={{0,8},{4,12},{8,0},{12,4},{1,9},{5,13},{9,1},{13,5},{2,10},{6,14},... | collective-permute-start | bytes 393224 | tf_op jit(solution)/shard_map/ppermute | solution.py:481
  66.4 0.0 collective-permute-done.15.refs_1_
  66.4 3.7 %filters.4 = (f32[400,128]{1,0:T(8,128)S(1)}, f32[8,128]{1,0:T(8,128)S(1)}) custom-call(f32[12,32,128]{2,1,0:T(8,128)S(1)} %get-tuple-element.80.refs_0_, f32[12,32,128]{2,1,0:T(8,128)S(1)} %collective-permute-done.15.refs_1_, f32[8,128]{1,0:T(8,128)S(1)} %get-tuple-element.81.refs_2_), custom_call_target="tpu_custom_call" | custom-call | flops 1024 | bytes 1024 | tf_op jit(solution)/shard_map/filters/pallas_call | solution.py:370
  70.1 1.9 %collective-permute-start.17 = (f32[400,128]{1,0:T(8,128)S(1)}, f32[400,128]{1,0:T(8,128)S(1)}, u32[]{:S(2)}, u32[]{:S(2)}) collective-permute-start(f32[400,128]{1,0:T(8,128)S(1)} %get-tuple-element.85.refs_0_), channel_id=1, source_target_pairs={{0,4},{4,0},{8,12},{12,8},{1,5},{5,1},{9,13},{13,9},{2,6},{6,2},{1... | collective-permute-start | bytes 614408 | tf_op jit(solution)/shard_map/ppermute | solution.py:481
  72.0 0.6 collective-permute-done.14.refs_1_
  72.6 3.0 %filters.5 = (f32[264,128]{1,0:T(8,128)S(1)}, f32[8,128]{1,0:T(8,128)S(1)}) custom-call(f32[8,32,128]{2,1,0:T(8,128)S(1)} %get-tuple-element.79.refs_0_, f32[8,32,128]{2,1,0:T(8,128)S(1)} %collective-permute-done.14.refs_1_, f32[8,128]{1,0:T(8,128)S(1)} %get-tuple-element.82.refs_2_), custom_call_target="tpu_custom_call" | custom-call | flops 1024 | bytes 1024 | tf_op jit(solution)/shard_map/filters/pallas_call | solution.py:370
  75.6 0.7 collective-permute-start.16
  76.3 0.7 collective-permute-done.17.refs_1_
  77.0 2.5 %energy.4 = (f32[64,256]{1,0:T(8,128)}, f32[64,2,64,64]{3,2,1,0:T(8,128)}, f32[8,128]{1,0:T(8,128)S(1)}) custom-call(bf16[24,64,512]{2,1,0:T(8,128)(2,1)S(1)} %get-tuple-element.84.merged, f32[400,128]{1,0:T(8,128)S(1)} %get-tuple-element.85.refs_0_, f32[400,128]{1,0:T(8,128)S(1)} %collective-permute-done.17.refs_1_, ...), custom_call_target="tpu_custom_call", output_to_operand_aliasing={{0}: (3, {}), {1}: (4, {})} | custom-call | flops 1024 | bytes 1024 | tf_op jit(solution)/shard_map/energy/pallas_call | solution.py:433
  79.5 1.2 %collective-permute-done.16.refs_1_ = f32[264,128]{1,0:T(8,128)S(1)} collective-permute-done((f32[264,128]{1,0:T(8,128)S(1)}, f32[264,128]{1,0:T(8,128)S(1)}, u32[]{:S(2)}, u32[]{:S(2)}) %collective-permute-start.16) | collective-permute-done | bytes 135200 | tf_op jit(solution)/shard_map/ppermute | solution.py:481
  80.7 2.6 %energy.5 = (f32[64,256]{1,0:T(8,128)}, f32[64,2,64,64]{3,2,1,0:T(8,128)}, f32[8,128]{1,0:T(8,128)}) custom-call(bf16[16,64,512]{2,1,0:T(8,128)(2,1)S(1)} %get-tuple-element.72.merged, f32[264,128]{1,0:T(8,128)S(1)} %get-tuple-element.83.refs_0_, f32[264,128]{1,0:T(8,128)S(1)} %collective-permute-done.16.refs_1_, ...), custom_call_target="tpu_custom_call", output_to_operand_aliasing={{0}: (3, {}), {1}: (4, {})} | custom-call | flops 1024 | bytes 1024 | tf_op jit(solution)/shard_map/energy/pallas_call | solution.py:433
  (3 shorter events, 0.1 us)
Async XLA Ops:
  4.9 10.8 %collective-permute-start.6 = (bf16[24,16,512]{2,1,0:T(8,128)(2,1)S(1)}, bf16[24,16,512]{2,1,0:T(8,128)(2,1)S(1)}, u32[]{:S(2)}, u32[]{:S(2)}) collective-permute-start(bf16[24,16,512]{2,1,0:T(8,128)(2,1)S(1)} %get-tuple-element.58), channel_id=1, source_target_pairs={{0,1},{1,0},{2,3},{3,2},{4,5},{5,4},{6,7},{7,6},{8,9},{9,8},{10,11... | collective-permute-start | bytes 1179656 | tf_op jit(solution)/shard_map/ppermute | solution.py:481
  5.5 12.5 %collective-permute-start.7 = (bf16[24,16,512]{2,1,0:T(8,128)(2,1)S(1)}, bf16[24,16,512]{2,1,0:T(8,128)(2,1)S(1)}, u32[]{:S(2)}, u32[]{:S(2)}) collective-permute-start(bf16[24,16,512]{2,1,0:T(8,128)(2,1)S(1)} %get-tuple-element.59), channel_id=1, source_target_pairs={{0,2},{1,3},{2,0},{3,1},{4,6},{5,7},{6,4},{7,5},{8,10},{9,11},{10,... | collective-permute-start | bytes 1179656 | tf_op jit(solution)/shard_map/ppermute | solution.py:481
  8.0 17.9 %collective-permute-start.8 = (bf16[24,16,512]{2,1,0:T(8,128)(2,1)S(1)}, bf16[24,16,512]{2,1,0:T(8,128)(2,1)S(1)}, u32[]{:S(2)}, u32[]{:S(2)}) collective-permute-start(bf16[24,16,512]{2,1,0:T(8,128)(2,1)S(1)} %get-tuple-element.60), channel_id=1, source_target_pairs={{0,3},{1,2},{2,1},{3,0},{4,7},{5,6},{6,5},{7,4},{8,11},{9,10},{10,... | collective-permute-start | bytes 1179656 | tf_op jit(solution)/shard_map/ppermute | solution.py:481
  13.6 23.4 %collective-permute-start.3 = (bf16[24,16,512]{2,1,0:T(8,128)(2,1)S(1)}, bf16[24,16,512]{2,1,0:T(8,128)(2,1)S(1)}, u32[]{:S(2)}, u32[]{:S(2)}) collective-permute-start(bf16[24,16,512]{2,1,0:T(8,128)(2,1)S(1)} %get-tuple-element.54), channel_id=1, source_target_pairs={{0,1},{1,0},{2,3},{3,2},{4,5},{5,4},{6,7},{7,6},{8,9},{9,8},{10,11... | collective-permute-start | bytes 1179656 | tf_op jit(solution)/shard_map/ppermute | solution.py:481
  13.8 24.7 %collective-permute-start.4 = (bf16[24,16,512]{2,1,0:T(8,128)(2,1)S(1)}, bf16[24,16,512]{2,1,0:T(8,128)(2,1)S(1)}, u32[]{:S(2)}, u32[]{:S(2)}) collective-permute-start(bf16[24,16,512]{2,1,0:T(8,128)(2,1)S(1)} %get-tuple-element.55), channel_id=1, source_target_pairs={{0,2},{1,3},{2,0},{3,1},{4,6},{5,7},{6,4},{7,5},{8,10},{9,11},{10,... | collective-permute-start | bytes 1179656 | tf_op jit(solution)/shard_map/ppermute | solution.py:481
  15.7 27.0 %collective-permute-start.5 = (bf16[24,16,512]{2,1,0:T(8,128)(2,1)S(1)}, bf16[24,16,512]{2,1,0:T(8,128)(2,1)S(1)}, u32[]{:S(2)}, u32[]{:S(2)}) collective-permute-start(bf16[24,16,512]{2,1,0:T(8,128)(2,1)S(1)} %get-tuple-element.56), channel_id=1, source_target_pairs={{0,3},{1,2},{2,1},{3,0},{4,7},{5,6},{6,5},{7,4},{8,11},{9,10},{10,... | collective-permute-start | bytes 1179656 | tf_op jit(solution)/shard_map/ppermute | solution.py:481
  26.7 7.5 %collective-permute-start.9 = (f32[12,32,128]{2,1,0:T(8,128)S(1)}, f32[12,32,128]{2,1,0:T(8,128)S(1)}, u32[]{:S(2)}, u32[]{:S(2)}) collective-permute-start(f32[12,32,128]{2,1,0:T(8,128)S(1)} %get-tuple-element.63), channel_id=1, source_target_pairs={{0,4},{4,0},{8,12},{12,8},{1,5},{5,1},{9,13},{13,9},{2,6},{6,2},{1... | collective-permute-start | bytes 589832 | tf_op jit(solution)/shard_map/ppermute | solution.py:481
  34.2 12.0 %collective-permute-start.11 = (f32[12,32,128]{2,1,0:T(8,128)S(1)}, f32[12,32,128]{2,1,0:T(8,128)S(1)}, u32[]{:S(2)}, u32[]{:S(2)}) collective-permute-start(f32[12,32,128]{2,1,0:T(8,128)S(1)} %get-tuple-element.68.refs_0_), channel_id=1, source_target_pairs={{0,8},{4,12},{8,0},{12,4},{1,9},{5,13},{9,1},{13,5},{2,10},{6,14},... | collective-permute-start | bytes 589832 | tf_op jit(solution)/shard_map/ppermute | solution.py:481
  37.0 17.1 %collective-permute-start = (bf16[16,16,512]{2,1,0:T(8,128)(2,1)S(1)}, bf16[16,16,512]{2,1,0:T(8,128)(2,1)S(1)}, u32[]{:S(2)}, u32[]{:S(2)}) collective-permute-start(bf16[16,16,512]{2,1,0:T(8,128)(2,1)S(1)} %get-tuple-element.50), channel_id=1, source_target_pairs={{0,1},{1,0},{2,3},{3,2},{4,5},{5,4},{6,7},{7,6},{8,9},{9,8},{10,11... | collective-permute-start | bytes 786440 | tf_op jit(solution)/shard_map/ppermute | solution.py:481
  37.0 17.1 %collective-permute-start.1 = (bf16[16,16,512]{2,1,0:T(8,128)(2,1)S(1)}, bf16[16,16,512]{2,1,0:T(8,128)(2,1)S(1)}, u32[]{:S(2)}, u32[]{:S(2)}) collective-permute-start(bf16[16,16,512]{2,1,0:T(8,128)(2,1)S(1)} %get-tuple-element.51), channel_id=1, source_target_pairs={{0,2},{1,3},{2,0},{3,1},{4,6},{5,7},{6,4},{7,5},{8,10},{9,11},{10,... | collective-permute-start | bytes 786440 | tf_op jit(solution)/shard_map/ppermute | solution.py:481
  38.5 15.6 %collective-permute-start.2 = (bf16[16,16,512]{2,1,0:T(8,128)(2,1)S(1)}, bf16[16,16,512]{2,1,0:T(8,128)(2,1)S(1)}, u32[]{:S(2)}, u32[]{:S(2)}) collective-permute-start(bf16[16,16,512]{2,1,0:T(8,128)(2,1)S(1)} %get-tuple-element.52), channel_id=1, source_target_pairs={{0,3},{1,2},{2,1},{3,0},{4,7},{5,6},{6,5},{7,4},{8,11},{9,10},{10,... | collective-permute-start | bytes 786440 | tf_op jit(solution)/shard_map/ppermute | solution.py:481
  43.5 7.5 %collective-permute-start.10 = (f32[12,32,128]{2,1,0:T(8,128)S(1)}, f32[12,32,128]{2,1,0:T(8,128)S(1)}, u32[]{:S(2)}, u32[]{:S(2)}) collective-permute-start(f32[12,32,128]{2,1,0:T(8,128)S(1)} %get-tuple-element.67), channel_id=1, source_target_pairs={{0,4},{4,0},{8,12},{12,8},{1,5},{5,1},{9,13},{13,9},{2,6},{6,2},{1... | collective-permute-start | bytes 589832 | tf_op jit(solution)/shard_map/ppermute | solution.py:481
  49.8 11.9 %collective-permute-start.13 = (f32[400,128]{1,0:T(8,128)S(1)}, f32[400,128]{1,0:T(8,128)S(1)}, u32[]{:S(2)}, u32[]{:S(2)}) collective-permute-start(f32[400,128]{1,0:T(8,128)S(1)} %get-tuple-element.76.refs_0_), channel_id=1, source_target_pairs={{0,4},{4,0},{8,12},{12,8},{1,5},{5,1},{9,13},{13,9},{2,6},{6,2},{1... | collective-permute-start | bytes 614408 | tf_op jit(solution)/shard_map/ppermute | solution.py:481
  51.0 15.4 %collective-permute-start.15 = (f32[12,32,128]{2,1,0:T(8,128)S(1)}, f32[12,32,128]{2,1,0:T(8,128)S(1)}, u32[]{:S(2)}, u32[]{:S(2)}) collective-permute-start(f32[12,32,128]{2,1,0:T(8,128)S(1)} %get-tuple-element.80.refs_0_), channel_id=1, source_target_pairs={{0,8},{4,12},{8,0},{12,4},{1,9},{5,13},{9,1},{13,5},{2,10},{6,14},... | collective-permute-start | bytes 589832 | tf_op jit(solution)/shard_map/ppermute | solution.py:481
  54.7 9.6 %collective-permute-start.12 = (f32[8,32,128]{2,1,0:T(8,128)S(1)}, f32[8,32,128]{2,1,0:T(8,128)S(1)}, u32[]{:S(2)}, u32[]{:S(2)}) collective-permute-start(f32[8,32,128]{2,1,0:T(8,128)S(1)} %get-tuple-element.74), channel_id=1, source_target_pairs={{0,4},{4,0},{8,12},{12,8},{1,5},{5,1},{9,13},{13,9},{2,6},{6,2},{1... | collective-permute-start | bytes 393224 | tf_op jit(solution)/shard_map/ppermute | solution.py:481
  64.4 8.2 %collective-permute-start.14 = (f32[8,32,128]{2,1,0:T(8,128)S(1)}, f32[8,32,128]{2,1,0:T(8,128)S(1)}, u32[]{:S(2)}, u32[]{:S(2)}) collective-permute-start(f32[8,32,128]{2,1,0:T(8,128)S(1)} %get-tuple-element.79.refs_0_), channel_id=1, source_target_pairs={{0,8},{4,12},{8,0},{12,4},{1,9},{5,13},{9,1},{13,5},{2,10},{6,14},... | collective-permute-start | bytes 393224 | tf_op jit(solution)/shard_map/ppermute | solution.py:481
  70.1 6.8 %collective-permute-start.17 = (f32[400,128]{1,0:T(8,128)S(1)}, f32[400,128]{1,0:T(8,128)S(1)}, u32[]{:S(2)}, u32[]{:S(2)}) collective-permute-start(f32[400,128]{1,0:T(8,128)S(1)} %get-tuple-element.85.refs_0_), channel_id=1, source_target_pairs={{0,4},{4,0},{8,12},{12,8},{1,5},{5,1},{9,13},{13,9},{2,6},{6,2},{1... | collective-permute-start | bytes 614408 | tf_op jit(solution)/shard_map/ppermute | solution.py:481
  75.6 5.1 %collective-permute-start.16 = (f32[264,128]{1,0:T(8,128)S(1)}, f32[264,128]{1,0:T(8,128)S(1)}, u32[]{:S(2)}, u32[]{:S(2)}) collective-permute-start(f32[264,128]{1,0:T(8,128)S(1)} %get-tuple-element.83.refs_0_), channel_id=1, source_target_pairs={{0,4},{4,0},{8,12},{12,8},{1,5},{5,1},{9,13},{13,9},{2,6},{6,2},{1... | collective-permute-start | bytes 405512 | tf_op jit(solution)/shard_map/ppermute | solution.py:481

commit v5 on v4

--- a/solution.py
+++ b/solution.py
@@ -119,21 +119,32 @@
     get_weight.wait()
     root = jnp.sqrt(weight[...])
     tiles = entries // LANES
+
     for step in range(steps):
         get_snap[step].wait()
-        for b in range(step * group, (step + 1) * group):
+
+        def block(i, _):
+            b = step * group + i
             spec = dot(table[...], snap[b]) * root
             for tile in range(tiles):
                 lanes = slice(tile * LANES, (tile + 1) * LANES)
                 wide[tile, pl.ds(b, rows, stride=blocks), :] = spec[:rows, lanes]
                 wide[tiles + tile, pl.ds(b, rows, stride=blocks), :] = spec[rows:, lanes]
-    at = 0
+            return 0
+
+        lax.fori_loop(0, group, block, 0)
+    base = 0
     for out in outs:
-        for j in range(out.shape[0]):
+
+        def row(j, _):
+            at = pl.multiple_of(base + j * blocks, blocks)
             for tile in range(2 * tiles):
                 lanes = slice(tile * LANES, (tile + 1) * LANES)
-                out[j, :, lanes] = wide[tile, at : at + blocks, :].astype(BF16)
-            at += blocks
+                out[j, :, lanes] = wide[tile, pl.ds(at, blocks), :].astype(BF16)
+            return 0
+
+        lax.fori_loop(0, out.shape[0], row, 0, unroll=4)
+        base += out.shape[0] * blocks
 
 
 def transform(snapshots, weight, freq_index, peers, parts, after):
@@ -387,16 +398,21 @@
     per_slot = count // slots
     half_rows = blocks // 2
     states = entries * lax.axis_size("space")
-    puts = []
+    group = 4 if per_slot % 4 == 0 else 1
+    tail = per_slot * half_rows
     for slot in range(slots):
         owner = slot_owner(direct, slot)
         piece = pieces[slot] if direct else pieces[0].at[slot]
-        for begin in range(0, per_slot, 4):
-            some = range(begin, min(begin + 4, per_slot))
-            at = [owner * per_slot + i for i in some]
-            packed = [piece[i * half_rows : (i + 1) * half_rows, :] for i in some]
-            tail = per_slot * half_rows
-            total = [piece[tail + i : tail + i + 1, 0:1] for i in some]
+
+        def some(step, _):
+            begin = step * group
+            base = owner * per_slot + begin
+            at = [base + i for i in range(group)]
+            packed = [
+                piece[pl.ds(pl.multiple_of((begin + i) * half_rows, half_rows), half_rows), :]
+                for i in range(group)
+            ]
+            total = [piece[pl.ds(tail + begin + i, 1), :][:, 0:1] for i in range(group)]
             z = [merged[f] for f in at]
             compact = each(unpack, packed)
             both = each(lambda c: full(c.astype(BF16).astype(F32)).astype(BF16), compact)
@@ -409,19 +425,22 @@
                 filters[f, 0] = c[:, :blocks]
                 filters[f, 1] = c[:, blocks:]
                 energies[pl.ds(f, 1), :] = e
-            put = pltpu.make_async_copy(
-                filters.at[pl.ds(at[0], len(at))],
-                filters_out.at[pl.ds(first + at[0], len(at))],
-                filters_sem.at[len(puts)],
-            )
-            put.start()
-            puts.append(put)
+            pltpu.make_async_copy(
+                filters.at[pl.ds(base, group)],
+                filters_out.at[pl.ds(first + base, group)],
+                filters_sem.at[0],
+            ).start()
+            return 0
+
+        lax.fori_loop(0, per_slot // group, some, 0)
     put = pltpu.make_async_copy(
         energies, energies_out.at[pl.ds(first, count)], energies_sem.at[0]
     )
     put.start()
-    for p in [*puts, put]:
-        p.wait()
+    pltpu.make_async_copy(
+        filters, filters_out.at[pl.ds(first, count)], filters_sem.at[0]
+    ).wait()
+    put.wait()
 
 
 def filtered(merged, pieces, slots, direct, carry, owned, first, after):
@@ -446,7 +465,7 @@
             pltpu.VMEM((count, entries), F32),
             pltpu.VMEM((count, 2, blocks, blocks), F32),
             pltpu.SemaphoreType.DMA((1,)),
-            pltpu.SemaphoreType.DMA((slots * -(-(count // slots) // 4),)),
+            pltpu.SemaphoreType.DMA((1,)),
         ],
         compiler_params=params(),
         cost_estimate=light(),

time: 83.6 us -> 86.2 us (1.031)
  Pallas kernels: 30.1 us -> 36.9 us
  waiting for transfers between devices: 29 us -> 25.8 us
  starting transfers between devices: 23.4 us -> 22.5 us
    pallas_call x2, Pallas kernels: 9.78 us -> 14.2 us  [transform(): pl.pallas_call(functools.partial(transform_kernel, peers, parts, group),...]
    ppermute x18, waiting for transfers between devices: 29 us -> 25.8 us  [permute(): return lax.ppermute(x, axis, pairs)]
    pallas_call x3, Pallas kernels: 7.78 us -> 10.1 us  [filtered(): pl.pallas_call(functools.partial(energy_kernel, slots, direct, len(pieces...]
    ppermute x18, starting transfers between devices: 23.4 us -> 22.5 us  [permute(): return lax.ppermute(x, axis, pairs)]
  transfers between devices with their start and end apart: 18 -> 18, of which waited for: 10 -> 9; matrix products, arithmetic and copies ran while one was open for 0% -> 0% of each run, Pallas kernels for 28% -> 32%
where the time goes in v5:
time: 86.2 us; the launch traced here: 86.1 us
  Pallas kernels  36.9 us (43%)
  waiting for transfers between devices  25.8 us (30%)
  starting transfers between devices  22.5 us (26%)
  between operations  0.91 us (1%)
    ppermute x18, waiting for transfers between devices, permute(): return lax.ppermute(x, axis, pairs)  25.8 us
    ppermute x18, starting transfers between devices, permute(): return lax.ppermute(x, axis, pairs)  22.5 us
    pallas_call x2, Pallas kernels, transform(): pl.pallas_call(functools.partial(transform_kernel, peers, parts, group),...  14.2 us
    pallas_call x3, Pallas kernels, solve(): pl.pallas_call(functools.partial(solve_kernel, len(parts)), in_specs=[who...  10.4 us
    pallas_call x3, Pallas kernels, filtered(): pl.pallas_call(functools.partial(energy_kernel, slots, direct, len(pieces...  10.1 us
    pallas_call x3, Pallas kernels, gram(): pl.pallas_call(functools.partial(gram_kernel, peers, slots, direct, len(a...  2.13 us
  transfers between devices with their start and end apart: 18, of which 9 were waited for; matrix products, arithmetic and copies ran while one was open for 0% of the time, Pallas kernels for 32%

profile of v5, /device:TPU:0, one launch (start us, length us, event | category | flops | bytes accessed | tf_op | source)
XLA Modules:
  0.0 86.1 jit_solution(3004717839867012175)
XLA Ops:
  0.6 6.4 %transform.2 = (bf16[24,16,512]{2,1,0:T(8,128)(2,1)S(1)}, bf16[24,16,512]{2,1,0:T(8,128)(2,1)S(1)}, bf16[24,16,512]{2,1,0:T(8,128)(2,1)S(1)}, bf16[24,16,512]{2,1,0:T(8,128)(2,1)S(1)}, f32[8,128]{1,0:T(8,128)S(1)}) custom-call(s32[256]{0:T(256)} %refs_0_.3, f32[1,256]{1,0:T(1,128)} %bitcast.1, bf16[16,512,256]{2,1,0:T(8,128)(2,1)} %refs_2_.3), custom_call_target="tpu_custom_call" | custom-call | flops 1024 | bytes 1024 | tf_op jit(solution)/shard_map/transform/pallas_call | solution.py:160
  7.1 0.5 collective-permute-start.6
  7.6 2.6 %collective-permute-start.7 = (bf16[24,16,512]{2,1,0:T(8,128)(2,1)S(1)}, bf16[24,16,512]{2,1,0:T(8,128)(2,1)S(1)}, u32[]{:S(2)}, u32[]{:S(2)}) collective-permute-start(bf16[24,16,512]{2,1,0:T(8,128)(2,1)S(1)} %get-tuple-element.59), channel_id=1, source_target_pairs={{0,2},{1,3},{2,0},{3,1},{4,6},{5,7},{6,4},{7,5},{8,10},{9,11},{10,... | collective-permute-start | bytes 1179656 | tf_op jit(solution)/shard_map/ppermute | solution.py:500
  10.2 0.1 collective-permute-start.8
  10.2 7.8 %transform.3 = (bf16[24,16,512]{2,1,0:T(8,128)(2,1)S(1)}, bf16[24,16,512]{2,1,0:T(8,128)(2,1)S(1)}, bf16[24,16,512]{2,1,0:T(8,128)(2,1)S(1)}, bf16[24,16,512]{2,...) custom-call(s32[256]{0:T(256)} %refs_0_.3, ...), custom_call_target="tpu_custom_call" | custom-call | flops 1024 | bytes 1024 | tf_op jit(solution)/shard_map/transform/pallas_call | solution.py:160
  18.0 0.2 collective-permute-start.3
  18.2 1.9 %collective-permute-start.4 = (bf16[24,16,512]{2,1,0:T(8,128)(2,1)S(1)}, bf16[24,16,512]{2,1,0:T(8,128)(2,1)S(1)}, u32[]{:S(2)}, u32[]{:S(2)}) collective-permute-start(bf16[24,16,512]{2,1,0:T(8,128)(2,1)S(1)} %get-tuple-element.55), channel_id=1, source_target_pairs={{0,2},{1,3},{2,0},{3,1},{4,6},{5,7},{6,4},{7,5},{8,10},{9,11},{10,... | collective-permute-start | bytes 1179656 | tf_op jit(solution)/shard_map/ppermute | solution.py:500
  20.2 0.0 collective-permute-done.6.refs_1_
  20.2 0.0 collective-permute-start.5
  20.2 0.0 collective-permute-done.7.refs_2_
  20.2 7.9 %collective-permute-done.8.refs_3_ = bf16[24,16,512]{2,1,0:T(8,128)(2,1)S(1)} collective-permute-done((bf16[24,16,512]{2,1,0:T(8,128)(2,1)S(1)}, bf16[24,16,512]{2,1,0:T(8,128)(2,1)S(1)}, u32[]{:S(2)}, u32[]{:S(2)}) %collective-permute-start.8) | collective-permute-done | bytes 393248 | tf_op jit(solution)/shard_map/ppermute | solution.py:500
  28.0 0.8 gram.3
  28.8 1.7 %collective-permute-start.9 = (f32[12,32,128]{2,1,0:T(8,128)S(1)}, f32[12,32,128]{2,1,0:T(8,128)S(1)}, u32[]{:S(2)}, u32[]{:S(2)}) collective-permute-start(f32[12,32,128]{2,1,0:T(8,128)S(1)} %get-tuple-element.63), channel_id=1, source_target_pairs={{0,4},{4,0},{8,12},{12,8},{1,5},{5,1},{9,13},{13,9},{2,6},{6,2},{1... | collective-permute-start | bytes 589832 | tf_op jit(solution)/shard_map/ppermute | solution.py:500
  30.5 5.8 %collective-permute-done.9.two = f32[12,32,128]{2,1,0:T(8,128)S(1)} collective-permute-done((f32[12,32,128]{2,1,0:T(8,128)S(1)}, f32[12,32,128]{2,1,0:T(8,128)S(1)}, u32[]{:S(2)}, u32[]{:S(2)}) %collective-permute-start.9) | collective-permute-done | bytes 196640 | tf_op jit(solution)/shard_map/ppermute | solution.py:500
  36.3 2.8 %collective-permute-start.11 = (f32[12,32,128]{2,1,0:T(8,128)S(1)}, f32[12,32,128]{2,1,0:T(8,128)S(1)}, u32[]{:S(2)}, u32[]{:S(2)}) collective-permute-start(f32[12,32,128]{2,1,0:T(8,128)S(1)} %get-tuple-element.68.refs_0_), channel_id=1, source_target_pairs={{0,8},{4,12},{8,0},{12,4},{1,9},{5,13},{9,1},{13,5},{2,10},{6,14},... | collective-permute-start | bytes 589832 | tf_op jit(solution)/shard_map/ppermute | solution.py:500
  39.1 0.0 collective-permute-start
  39.1 0.0 collective-permute-done.3.refs_1_
  39.2 1.5 %collective-permute-start.1 = (bf16[16,16,512]{2,1,0:T(8,128)(2,1)S(1)}, bf16[16,16,512]{2,1,0:T(8,128)(2,1)S(1)}, u32[]{:S(2)}, u32[]{:S(2)}) collective-permute-start(bf16[16,16,512]{2,1,0:T(8,128)(2,1)S(1)} %get-tuple-element.51), channel_id=1, source_target_pairs={{0,2},{1,3},{2,0},{3,1},{4,6},{5,7},{6,4},{7,5},{8,10},{9,11},{10,... | collective-permute-start | bytes 786440 | tf_op jit(solution)/shard_map/ppermute | solution.py:500
  40.7 0.0 collective-permute-done.4.refs_2_
  40.7 0.3 collective-permute-start.2
  41.0 3.9 %collective-permute-done.5.refs_3_ = bf16[24,16,512]{2,1,0:T(8,128)(2,1)S(1)} collective-permute-done((bf16[24,16,512]{2,1,0:T(8,128)(2,1)S(1)}, bf16[24,16,512]{2,1,0:T(8,128)(2,1)S(1)}, u32[]{:S(2)}, u32[]{:S(2)}) %collective-permute-start.5) | collective-permute-done | bytes 393248 | tf_op jit(solution)/shard_map/ppermute | solution.py:500
  44.9 0.8 gram.4
  45.7 1.7 %collective-permute-start.10 = (f32[12,32,128]{2,1,0:T(8,128)S(1)}, f32[12,32,128]{2,1,0:T(8,128)S(1)}, u32[]{:S(2)}, u32[]{:S(2)}) collective-permute-start(f32[12,32,128]{2,1,0:T(8,128)S(1)} %get-tuple-element.67), channel_id=1, source_target_pairs={{0,4},{4,0},{8,12},{12,8},{1,5},{5,1},{9,13},{13,9},{2,6},{6,2},{1... | collective-permute-start | bytes 589832 | tf_op jit(solution)/shard_map/ppermute | solution.py:500
  47.4 0.9 %collective-permute-done.11.refs_1_ = f32[12,32,128]{2,1,0:T(8,128)S(1)} collective-permute-done((f32[12,32,128]{2,1,0:T(8,128)S(1)}, f32[12,32,128]{2,1,0:T(8,128)S(1)}, u32[]{:S(2)}, u32[]{:S(2)}) %collective-permute-start.11) | collective-permute-done | bytes 196640 | tf_op jit(solution)/shard_map/ppermute | solution.py:500
  48.3 3.7 %filters.3 = (f32[400,128]{1,0:T(8,128)S(1)}, f32[8,128]{1,0:T(8,128)S(1)}) custom-call(f32[12,32,128]{2,1,0:T(8,128)S(1)} %get-tuple-element.68.refs_0_, f32[12,32,128]{2,1,0:T(8,128)S(1)} %collective-permute-done.11.refs_1_, f32[8,128]{1,0:T(8,128)S(1)} %get-tuple-element.69.refs_2_), custom_call_target="tpu_custom_call" | custom-call | flops 1024 | bytes 1024 | tf_op jit(solution)/shard_map/filters/pallas_call | solution.py:381
  52.0 0.8 collective-permute-start.13
  52.8 0.4 collective-permute-done.10.two
  53.2 3.0 %collective-permute-start.15 = (f32[12,32,128]{2,1,0:T(8,128)S(1)}, f32[12,32,128]{2,1,0:T(8,128)S(1)}, u32[]{:S(2)}, u32[]{:S(2)}) collective-permute-start(f32[12,32,128]{2,1,0:T(8,128)S(1)} %get-tuple-element.80.refs_0_), channel_id=1, source_target_pairs={{0,8},{4,12},{8,0},{12,4},{1,9},{5,13},{9,1},{13,5},{2,10},{6,14},... | collective-permute-start | bytes 589832 | tf_op jit(solution)/shard_map/ppermute | solution.py:500
  56.2 0.0 collective-permute-done.refs_1_
  56.2 0.0 collective-permute-done.1.refs_2_
  56.2 0.0 collective-permute-done.2.refs_3_
  56.3 0.6 gram.5
  56.9 1.6 %collective-permute-start.12 = (f32[8,32,128]{2,1,0:T(8,128)S(1)}, f32[8,32,128]{2,1,0:T(8,128)S(1)}, u32[]{:S(2)}, u32[]{:S(2)}) collective-permute-start(f32[8,32,128]{2,1,0:T(8,128)S(1)} %get-tuple-element.74), channel_id=1, source_target_pairs={{0,4},{4,0},{8,12},{12,8},{1,5},{5,1},{9,13},{13,9},{2,6},{6,2},{1... | collective-permute-start | bytes 393224 | tf_op jit(solution)/shard_map/ppermute | solution.py:500
  58.5 5.4 %collective-permute-done.13.refs_1_ = f32[400,128]{1,0:T(8,128)S(1)} collective-permute-done((f32[400,128]{1,0:T(8,128)S(1)}, f32[400,128]{1,0:T(8,128)S(1)}, u32[]{:S(2)}, u32[]{:S(2)}) %collective-permute-start.13) | collective-permute-done | bytes 204832 | tf_op jit(solution)/shard_map/ppermute | solution.py:500
  63.9 3.6 %energy.3 = (f32[64,256]{1,0:T(8,128)}, f32[64,2,64,64]{3,2,1,0:T(8,128)}, f32[8,128]{1,0:T(8,128)S(1)}) custom-call(bf16[24,64,512]{2,1,0:T(8,128)(2,1)S(1)} %get-tuple-element.75.merged, f32[400,128]{1,0:T(8,128)S(1)} %get-tuple-element.76.refs_0_, f32[400,128]{1,0:T(8,128)S(1)} %collective-permute-done.13.refs_1_, f32[8,128]{1,0:T(8,128)S(1)} %get-tuple-element.77.refs_2_), custom_call_target="tpu_custom_call" | custom-call | flops 1024 | bytes 1024 | tf_op jit(solution)/shard_map/energy/pallas_call | solution.py:452
  67.4 0.0 collective-permute-done.12.two
  67.5 1.1 %collective-permute-start.14 = (f32[8,32,128]{2,1,0:T(8,128)S(1)}, f32[8,32,128]{2,1,0:T(8,128)S(1)}, u32[]{:S(2)}, u32[]{:S(2)}) collective-permute-start(f32[8,32,128]{2,1,0:T(8,128)S(1)} %get-tuple-element.79.refs_0_), channel_id=1, source_target_pairs={{0,8},{4,12},{8,0},{12,4},{1,9},{5,13},{9,1},{13,5},{2,10},{6,14},... | collective-permute-start | bytes 393224 | tf_op jit(solution)/shard_map/ppermute | solution.py:500
  68.6 0.0 collective-permute-done.15.refs_1_
  68.6 3.7 %filters.4 = (f32[400,128]{1,0:T(8,128)S(1)}, f32[8,128]{1,0:T(8,128)S(1)}) custom-call(f32[12,32,128]{2,1,0:T(8,128)S(1)} %get-tuple-element.80.refs_0_, f32[12,32,128]{2,1,0:T(8,128)S(1)} %collective-permute-done.15.refs_1_, f32[8,128]{1,0:T(8,128)S(1)} %get-tuple-element.81.refs_2_), custom_call_target="tpu_custom_call" | custom-call | flops 1024 | bytes 1024 | tf_op jit(solution)/shard_map/filters/pallas_call | solution.py:381
  72.3 1.9 %collective-permute-start.17 = (f32[400,128]{1,0:T(8,128)S(1)}, f32[400,128]{1,0:T(8,128)S(1)}, u32[]{:S(2)}, u32[]{:S(2)}) collective-permute-start(f32[400,128]{1,0:T(8,128)S(1)} %get-tuple-element.85.refs_0_), channel_id=1, source_target_pairs={{0,4},{4,0},{8,12},{12,8},{1,5},{5,1},{9,13},{13,9},{2,6},{6,2},{1... | collective-permute-start | bytes 614408 | tf_op jit(solution)/shard_map/ppermute | solution.py:500
  74.2 0.6 collective-permute-done.14.refs_1_
  74.7 3.0 %filters.5 = (f32[264,128]{1,0:T(8,128)S(1)}, f32[8,128]{1,0:T(8,128)S(1)}) custom-call(f32[8,32,128]{2,1,0:T(8,128)S(1)} %get-tuple-element.79.refs_0_, f32[8,32,128]{2,1,0:T(8,128)S(1)} %collective-permute-done.14.refs_1_, f32[8,128]{1,0:T(8,128)S(1)} %get-tuple-element.82.refs_2_), custom_call_target="tpu_custom_call" | custom-call | flops 1024 | bytes 1024 | tf_op jit(solution)/shard_map/filters/pallas_call | solution.py:381
  77.8 0.7 collective-permute-start.16
  78.4 0.7 collective-permute-done.17.refs_1_
  79.1 3.4 %energy.4 = (f32[64,256]{1,0:T(8,128)}, f32[64,2,64,64]{3,2,1,0:T(8,128)}, f32[8,128]{1,0:T(8,128)S(1)}) custom-call(bf16[24,64,512]{2,1,0:T(8,128)(2,1)S(1)} %get-tuple-element.84.merged, f32[400,128]{1,0:T(8,128)S(1)} %get-tuple-element.85.refs_0_, f32[400,128]{1,0:T(8,128)S(1)} %collective-permute-done.17.refs_1_, ...), custom_call_target="tpu_custom_call", output_to_operand_aliasing={{0}: (3, {}), {1}: (4, {})} | custom-call | flops 1024 | bytes 1024 | tf_op jit(solution)/shard_map/energy/pallas_call | solution.py:452
  82.5 0.3 collective-permute-done.16.refs_1_
  82.8 3.1 %energy.5 = (f32[64,256]{1,0:T(8,128)}, f32[64,2,64,64]{3,2,1,0:T(8,128)}, f32[8,128]{1,0:T(8,128)}) custom-call(bf16[16,64,512]{2,1,0:T(8,128)(2,1)S(1)} %get-tuple-element.72.merged, f32[264,128]{1,0:T(8,128)S(1)} %get-tuple-element.83.refs_0_, f32[264,128]{1,0:T(8,128)S(1)} %collective-permute-done.16.refs_1_, ...), custom_call_target="tpu_custom_call", output_to_operand_aliasing={{0}: (3, {}), {1}: (4, {})} | custom-call | flops 1024 | bytes 1024 | tf_op jit(solution)/shard_map/energy/pallas_call | solution.py:452
  (3 shorter events, 0.1 us)
Async XLA Ops:
  7.1 13.1 %collective-permute-start.6 = (bf16[24,16,512]{2,1,0:T(8,128)(2,1)S(1)}, bf16[24,16,512]{2,1,0:T(8,128)(2,1)S(1)}, u32[]{:S(2)}, u32[]{:S(2)}) collective-permute-start(bf16[24,16,512]{2,1,0:T(8,128)(2,1)S(1)} %get-tuple-element.58), channel_id=1, source_target_pairs={{0,1},{1,0},{2,3},{3,2},{4,5},{5,4},{6,7},{7,6},{8,9},{9,8},{10,11... | collective-permute-start | bytes 1179656 | tf_op jit(solution)/shard_map/ppermute | solution.py:500
  7.6 12.6 %collective-permute-start.7 = (bf16[24,16,512]{2,1,0:T(8,128)(2,1)S(1)}, bf16[24,16,512]{2,1,0:T(8,128)(2,1)S(1)}, u32[]{:S(2)}, u32[]{:S(2)}) collective-permute-start(bf16[24,16,512]{2,1,0:T(8,128)(2,1)S(1)} %get-tuple-element.59), channel_id=1, source_target_pairs={{0,2},{1,3},{2,0},{3,1},{4,6},{5,7},{6,4},{7,5},{8,10},{9,11},{10,... | collective-permute-start | bytes 1179656 | tf_op jit(solution)/shard_map/ppermute | solution.py:500
  10.2 17.9 %collective-permute-start.8 = (bf16[24,16,512]{2,1,0:T(8,128)(2,1)S(1)}, bf16[24,16,512]{2,1,0:T(8,128)(2,1)S(1)}, u32[]{:S(2)}, u32[]{:S(2)}) collective-permute-start(bf16[24,16,512]{2,1,0:T(8,128)(2,1)S(1)} %get-tuple-element.60), channel_id=1, source_target_pairs={{0,3},{1,2},{2,1},{3,0},{4,7},{5,6},{6,5},{7,4},{8,11},{9,10},{10,... | collective-permute-start | bytes 1179656 | tf_op jit(solution)/shard_map/ppermute | solution.py:500
  18.0 21.1 %collective-permute-start.3 = (bf16[24,16,512]{2,1,0:T(8,128)(2,1)S(1)}, bf16[24,16,512]{2,1,0:T(8,128)(2,1)S(1)}, u32[]{:S(2)}, u32[]{:S(2)}) collective-permute-start(bf16[24,16,512]{2,1,0:T(8,128)(2,1)S(1)} %get-tuple-element.54), channel_id=1, source_target_pairs={{0,1},{1,0},{2,3},{3,2},{4,5},{5,4},{6,7},{7,6},{8,9},{9,8},{10,11... | collective-permute-start | bytes 1179656 | tf_op jit(solution)/shard_map/ppermute | solution.py:500
  18.2 22.4 %collective-permute-start.4 = (bf16[24,16,512]{2,1,0:T(8,128)(2,1)S(1)}, bf16[24,16,512]{2,1,0:T(8,128)(2,1)S(1)}, u32[]{:S(2)}, u32[]{:S(2)}) collective-permute-start(bf16[24,16,512]{2,1,0:T(8,128)(2,1)S(1)} %get-tuple-element.55), channel_id=1, source_target_pairs={{0,2},{1,3},{2,0},{3,1},{4,6},{5,7},{6,4},{7,5},{8,10},{9,11},{10,... | collective-permute-start | bytes 1179656 | tf_op jit(solution)/shard_map/ppermute | solution.py:500
  20.2 24.7 %collective-permute-start.5 = (bf16[24,16,512]{2,1,0:T(8,128)(2,1)S(1)}, bf16[24,16,512]{2,1,0:T(8,128)(2,1)S(1)}, u32[]{:S(2)}, u32[]{:S(2)}) collective-permute-start(bf16[24,16,512]{2,1,0:T(8,128)(2,1)S(1)} %get-tuple-element.56), channel_id=1, source_target_pairs={{0,3},{1,2},{2,1},{3,0},{4,7},{5,6},{6,5},{7,4},{8,11},{9,10},{10,... | collective-permute-start | bytes 1179656 | tf_op jit(solution)/shard_map/ppermute | solution.py:500
  28.8 7.5 %collective-permute-start.9 = (f32[12,32,128]{2,1,0:T(8,128)S(1)}, f32[12,32,128]{2,1,0:T(8,128)S(1)}, u32[]{:S(2)}, u32[]{:S(2)}) collective-permute-start(f32[12,32,128]{2,1,0:T(8,128)S(1)} %get-tuple-element.63), channel_id=1, source_target_pairs={{0,4},{4,0},{8,12},{12,8},{1,5},{5,1},{9,13},{13,9},{2,6},{6,2},{1... | collective-permute-start | bytes 589832 | tf_op jit(solution)/shard_map/ppermute | solution.py:500
  36.3 12.0 %collective-permute-start.11 = (f32[12,32,128]{2,1,0:T(8,128)S(1)}, f32[12,32,128]{2,1,0:T(8,128)S(1)}, u32[]{:S(2)}, u32[]{:S(2)}) collective-permute-start(f32[12,32,128]{2,1,0:T(8,128)S(1)} %get-tuple-element.68.refs_0_), channel_id=1, source_target_pairs={{0,8},{4,12},{8,0},{12,4},{1,9},{5,13},{9,1},{13,5},{2,10},{6,14},... | collective-permute-start | bytes 589832 | tf_op jit(solution)/shard_map/ppermute | solution.py:500
  39.1 17.1 %collective-permute-start = (bf16[16,16,512]{2,1,0:T(8,128)(2,1)S(1)}, bf16[16,16,512]{2,1,0:T(8,128)(2,1)S(1)}, u32[]{:S(2)}, u32[]{:S(2)}) collective-permute-start(bf16[16,16,512]{2,1,0:T(8,128)(2,1)S(1)} %get-tuple-element.50), channel_id=1, source_target_pairs={{0,1},{1,0},{2,3},{3,2},{4,5},{5,4},{6,7},{7,6},{8,9},{9,8},{10,11... | collective-permute-start | bytes 786440 | tf_op jit(solution)/shard_map/ppermute | solution.py:500
  39.2 17.1 %collective-permute-start.1 = (bf16[16,16,512]{2,1,0:T(8,128)(2,1)S(1)}, bf16[16,16,512]{2,1,0:T(8,128)(2,1)S(1)}, u32[]{:S(2)}, u32[]{:S(2)}) collective-permute-start(bf16[16,16,512]{2,1,0:T(8,128)(2,1)S(1)} %get-tuple-element.51), channel_id=1, source_target_pairs={{0,2},{1,3},{2,0},{3,1},{4,6},{5,7},{6,4},{7,5},{8,10},{9,11},{10,... | collective-permute-start | bytes 786440 | tf_op jit(solution)/shard_map/ppermute | solution.py:500
  40.7 15.6 %collective-permute-start.2 = (bf16[16,16,512]{2,1,0:T(8,128)(2,1)S(1)}, bf16[16,16,512]{2,1,0:T(8,128)(2,1)S(1)}, u32[]{:S(2)}, u32[]{:S(2)}) collective-permute-start(bf16[16,16,512]{2,1,0:T(8,128)(2,1)S(1)} %get-tuple-element.52), channel_id=1, source_target_pairs={{0,3},{1,2},{2,1},{3,0},{4,7},{5,6},{6,5},{7,4},{8,11},{9,10},{10,... | collective-permute-start | bytes 786440 | tf_op jit(solution)/shard_map/ppermute | solution.py:500
  45.7 7.5 %collective-permute-start.10 = (f32[12,32,128]{2,1,0:T(8,128)S(1)}, f32[12,32,128]{2,1,0:T(8,128)S(1)}, u32[]{:S(2)}, u32[]{:S(2)}) collective-permute-start(f32[12,32,128]{2,1,0:T(8,128)S(1)} %get-tuple-element.67), channel_id=1, source_target_pairs={{0,4},{4,0},{8,12},{12,8},{1,5},{5,1},{9,13},{13,9},{2,6},{6,2},{1... | collective-permute-start | bytes 589832 | tf_op jit(solution)/shard_map/ppermute | solution.py:500
  52.0 11.9 %collective-permute-start.13 = (f32[400,128]{1,0:T(8,128)S(1)}, f32[400,128]{1,0:T(8,128)S(1)}, u32[]{:S(2)}, u32[]{:S(2)}) collective-permute-start(f32[400,128]{1,0:T(8,128)S(1)} %get-tuple-element.76.refs_0_), channel_id=1, source_target_pairs={{0,4},{4,0},{8,12},{12,8},{1,5},{5,1},{9,13},{13,9},{2,6},{6,2},{1... | collective-permute-start | bytes 614408 | tf_op jit(solution)/shard_map/ppermute | solution.py:500
  53.2 15.4 %collective-permute-start.15 = (f32[12,32,128]{2,1,0:T(8,128)S(1)}, f32[12,32,128]{2,1,0:T(8,128)S(1)}, u32[]{:S(2)}, u32[]{:S(2)}) collective-permute-start(f32[12,32,128]{2,1,0:T(8,128)S(1)} %get-tuple-element.80.refs_0_), channel_id=1, source_target_pairs={{0,8},{4,12},{8,0},{12,4},{1,9},{5,13},{9,1},{13,5},{2,10},{6,14},... | collective-permute-start | bytes 589832 | tf_op jit(solution)/shard_map/ppermute | solution.py:500
  56.9 10.6 %collective-permute-start.12 = (f32[8,32,128]{2,1,0:T(8,128)S(1)}, f32[8,32,128]{2,1,0:T(8,128)S(1)}, u32[]{:S(2)}, u32[]{:S(2)}) collective-permute-start(f32[8,32,128]{2,1,0:T(8,128)S(1)} %get-tuple-element.74), channel_id=1, source_target_pairs={{0,4},{4,0},{8,12},{12,8},{1,5},{5,1},{9,13},{13,9},{2,6},{6,2},{1... | collective-permute-start | bytes 393224 | tf_op jit(solution)/shard_map/ppermute | solution.py:500
  67.5 7.2 %collective-permute-start.14 = (f32[8,32,128]{2,1,0:T(8,128)S(1)}, f32[8,32,128]{2,1,0:T(8,128)S(1)}, u32[]{:S(2)}, u32[]{:S(2)}) collective-permute-start(f32[8,32,128]{2,1,0:T(8,128)S(1)} %get-tuple-element.79.refs_0_), channel_id=1, source_target_pairs={{0,8},{4,12},{8,0},{12,4},{1,9},{5,13},{9,1},{13,5},{2,10},{6,14},... | collective-permute-start | bytes 393224 | tf_op jit(solution)/shard_map/ppermute | solution.py:500
  72.3 6.8 %collective-permute-start.17 = (f32[400,128]{1,0:T(8,128)S(1)}, f32[400,128]{1,0:T(8,128)S(1)}, u32[]{:S(2)}, u32[]{:S(2)}) collective-permute-start(f32[400,128]{1,0:T(8,128)S(1)} %get-tuple-element.85.refs_0_), channel_id=1, source_target_pairs={{0,4},{4,0},{8,12},{12,8},{1,5},{5,1},{9,13},{13,9},{2,6},{6,2},{1... | collective-permute-start | bytes 614408 | tf_op jit(solution)/shard_map/ppermute | solution.py:500
  77.8 5.1 %collective-permute-start.16 = (f32[264,128]{1,0:T(8,128)S(1)}, f32[264,128]{1,0:T(8,128)S(1)}, u32[]{:S(2)}, u32[]{:S(2)}) collective-permute-start(f32[264,128]{1,0:T(8,128)S(1)} %get-tuple-element.83.refs_0_), channel_id=1, source_target_pairs={{0,4},{4,0},{8,12},{12,8},{1,5},{5,1},{9,13},{13,9},{2,6},{6,2},{1... | collective-permute-start | bytes 405512 | tf_op jit(solution)/shard_map/ppermute | solution.py:500

commit v6 on v4

--- a/solution.py
+++ b/solution.py
@@ -182,6 +182,70 @@
     return jnp.where(low, both[: half // 2], both[half // 2 :])
 
 
+LOG_STEPS = 64.0
+TOP = 23169.0
+FINE = float(2**21)
+
+
+def outer(code):
+    scale = jnp.exp2(code * F32(1 / LOG_STEPS))
+    width = code.shape[1]
+    rows = width // 4
+    shape = (rows, width)
+    row = lax.broadcasted_iota(jnp.int32, shape, 0)
+    lane = lax.broadcasted_iota(jnp.int32, shape, 1)
+    first = jnp.sum(jnp.where(lane == row, scale, F32(0)), axis=1, keepdims=True)
+    second = jnp.sum(jnp.where(lane == row + rows, scale, F32(0)), axis=1, keepdims=True)
+    return scale * jnp.where(lane < width // 2, first, second)
+
+
+def encode(packed):
+    rows, width = packed.shape
+    row = lax.broadcasted_iota(jnp.int32, packed.shape, 0)
+    lane = lax.broadcasted_iota(jnp.int32, packed.shape, 1)
+    on = (lane == row) | (lane == row + 3 * rows)
+    diagonal = jnp.sum(jnp.where(on, packed, F32(0)), axis=0, keepdims=True)
+    diagonal = diagonal + pltpu.roll(diagonal, width // 2, 1)
+    logs = jnp.log(jnp.maximum(diagonal, F32(1e-30))) * F32(0.5 * LOG_STEPS / math.log(2.0))
+    code = jnp.ceil(logs)
+    value = jnp.round(packed * (F32(TOP) / outer(code)))
+    return jnp.clip(value, F32(-32767), F32(32767)), code
+
+
+def decode(value, code):
+    return value * (outer(code) * F32(1 / TOP))
+
+
+def to_short(x):
+    return x.astype(jnp.int32).astype(jnp.int16)
+
+
+def from_short(x):
+    return x.astype(jnp.int32).astype(F32)
+
+
+def coded_rows(number, half_rows):
+    return number * half_rows + -(-number // 16) * 16
+
+
+def write_coded(out, coded):
+    half_rows = coded[0][0].shape[0]
+    number = len(coded)
+    shape = (out.shape[0] - number * half_rows, out.shape[1])
+    line = lax.broadcasted_iota(jnp.int32, shape, 0)
+    codes = jnp.zeros(shape, F32)
+    for i, (value, code) in enumerate(coded):
+        out[i * half_rows : (i + 1) * half_rows, :] = to_short(value)
+        codes = jnp.where(line == i, code, codes)
+    out[number * half_rows :, :] = to_short(codes)
+
+
+def read_coded(ref, number, half_rows):
+    codes = from_short(ref[number * half_rows :, :])
+    values = [from_short(ref[i * half_rows : (i + 1) * half_rows, :]) for i in range(number)]
+    return values, [codes[i : i + 1] for i in range(number)]
+
+
 def unpack(packed):
     rows, half = packed.shape[0], packed.shape[1] // 2
     low = lane_low(packed.shape, half)
@@ -222,6 +286,7 @@
     low = lane_low((blocks, 2 * blocks), blocks)
     for slot in range(slots):
         owner = slot_owner(direct, slot)
+        coded = []
         for i in range(per_slot):
             f = owner * per_slot + i
             if stage is None:
@@ -240,10 +305,14 @@
             s = s * F32(1.0 / blocks)
             top, bottom = s[:blocks], swap(s[blocks:])
             compact = jnp.where(low, top + bottom, top - bottom)
-            if direct:
-                grams[slot][i] = pack(compact)
+            if direct and slot:
+                coded.append(encode(pack(compact)))
+            elif direct:
+                grams[0][i] = pack(compact)
             else:
                 grams[0][f] = pack(compact)
+        if coded:
+            write_coded(grams[slot], coded)
 
 
 def gram(pieces, slots, direct, after):
@@ -251,15 +320,17 @@
     count, here, width = pieces[0].shape
     blocks = here * peers
     if direct:
-        shapes = [(count // slots, blocks // 2, 2 * blocks)] * slots
+        rows = coded_rows(count // slots, blocks // 2)
+        shapes = [((count // slots, blocks // 2, 2 * blocks), F32)]
+        shapes += [((rows, 2 * blocks), jnp.int16)] * (slots - 1)
     else:
-        shapes = [(count, blocks // 2, 2 * blocks)]
+        shapes = [((count, blocks // 2, 2 * blocks), F32)]
     out = pl.pallas_call(
         functools.partial(gram_kernel, peers, slots, direct, len(after)),
         in_specs=[whole_spec()] * peers + [any_spec()] * len(after),
         out_specs=[whole_spec()] * (2 + len(shapes)),
         out_shape=[jax.ShapeDtypeStruct((count, blocks, width), BF16), TOKEN]
-        + [jax.ShapeDtypeStruct(s, F32) for s in shapes],
+        + [jax.ShapeDtypeStruct(*s) for s in shapes],
         scratch_shapes=[pltpu.VMEM((blocks, width), F32)] if here % 16 else [],
         compiler_params=params(),
         cost_estimate=light(),
@@ -268,22 +339,25 @@
     return out[0], out[2:], out[1]
 
 
-def add_kernel(one, two, *refs):
+def add_kernel(own, other, *refs):
     out, token = refs[-2:]
     token[...] = jnp.zeros_like(token)
-    out[...] = one[...] + two[...]
-
-
-def add(one, two, after):
+    number, half_rows, _ = own.shape
+    values, codes = read_coded(other, number, half_rows)
+    sums = [own[i] + decode(values[i], codes[i]) for i in range(number)]
+    write_coded(out, each(encode, sums))
+
+
+def add(own, other, after):
     return pl.pallas_call(
         add_kernel,
         in_specs=[whole_spec()] * 2 + [any_spec()] * len(after),
         out_specs=[whole_spec()] * 2,
-        out_shape=[jax.ShapeDtypeStruct(one.shape, F32), TOKEN],
+        out_shape=[jax.ShapeDtypeStruct(other.shape, jnp.int16), TOKEN],
         compiler_params=params(),
         cost_estimate=light(),
         name="add",
-    )(one, two, *after)
+    )(own, other, *after)
 
 
 def split(x):
@@ -295,23 +369,23 @@
     return [fn(*items) for items in zip(*lists)]
 
 
-def solve_kernel(parts, *refs):
+def solve_kernel(parts, number, half_rows, *refs):
     ins, out, token = refs[:parts], refs[-2], refs[-1]
     token[...] = jnp.zeros_like(token)
-    number, half_rows, width = ins[0].shape
+    width = out.shape[1]
     half = width // 2
     shape = (half, width)
     row = lax.broadcasted_iota(jnp.int32, shape, 0)
     lane = lax.broadcasted_iota(jnp.int32, shape, 1)
     eye = jnp.where(row == lane, F32(1), F32(0))
 
-    def load(i):
-        total = ins[0][i]
-        for r in ins[1:]:
-            total = total + r[i]
-        return unpack(total)
-
-    grams = [load(i) for i in range(number)]
+    if parts == 1:
+        sums = [ins[0][i] for i in range(number)]
+    else:
+        one = each(decode, *read_coded(ins[0], number, half_rows))
+        two = each(decode, *read_coded(ins[1], number, half_rows))
+        sums = [p + q for p, q in zip(one, two)]
+    grams = each(unpack, sums)
     shift = each(lambda g: jnp.sum(g * eye, keepdims=True) * F32(1.0 / half), grams)
     system = each(lambda g, m: g / m + eye, grams, shift)
     both = each(lambda a: split(full(a)), system)
@@ -341,10 +415,8 @@
         step = each(lambda r, v: dot(r.astype(BF16), v), residual, xf)
         factor = 1.0 if kind == "last" else 2 * t * t / (2 * t * t - 1)
         x = each(lambda v, m: F32(factor) * (v + m), xw, step)
-    packed = each(lambda v: pack(eye - v), x)
-    for i in range(number):
-        out[i * half_rows : (i + 1) * half_rows, :] = packed[i]
-    filters = each(unpack, packed)
+    coded = each(lambda v: encode(pack(eye - v)), x)
+    filters = each(lambda c: unpack(decode(*c)), coded)
     rounded = each(lambda c: c.astype(BF16), filters)
     turned = each(lambda c: full(c.astype(F32)).astype(BF16), rounded)
     split_g = each(split, grams)
@@ -352,26 +424,26 @@
     energy = each(
         lambda c, h: jnp.sum(c.astype(F32) * h, keepdims=True) * F32(half), rounded, moved
     )
-    tail = out.shape[0] - number * half_rows
-    line = lax.broadcasted_iota(jnp.int32, (tail, width), 0)
-    totals = jnp.ones((tail, width), F32)
-    for i in range(number):
-        totals = jnp.where(line == i, energy[i], totals)
-    out[number * half_rows :, :] = totals
-
-
-def tail_rows(number):
-    return -(-number // 8) * 8
-
-
-def solve(parts, after):
-    number, half_rows, width = parts[0].shape
-    rows = number * half_rows + tail_rows(number)
+    spot = lax.broadcasted_iota(jnp.int32, (1, width), 1)
+
+    def with_total(c, e):
+        whole = jnp.floor(jnp.log(e) * F32(LOG_STEPS / math.log(2.0)))
+        rest = jnp.round((e * jnp.exp2(whole * F32(-1 / LOG_STEPS)) - 1.0) * F32(FINE))
+        return c[0], jnp.where(spot == half, whole, jnp.where(spot == half + 1, rest, c[1]))
+
+    write_coded(out, each(with_total, coded, energy))
+
+
+def solve(parts, number, half_rows, after):
+    width = parts[0].shape[-1]
     return pl.pallas_call(
-        functools.partial(solve_kernel, len(parts)),
+        functools.partial(solve_kernel, len(parts), number, half_rows),
         in_specs=[whole_spec()] * len(parts) + [any_spec()] * len(after),
         out_specs=[whole_spec()] * 2,
-        out_shape=[jax.ShapeDtypeStruct((rows, width), F32), TOKEN],
+        out_shape=[
+            jax.ShapeDtypeStruct((coded_rows(number, half_rows), width), jnp.int16),
+            TOKEN,
+        ],
         compiler_params=params(),
         cost_estimate=light(),
         name="filters",
@@ -391,12 +463,19 @@
     for slot in range(slots):
         owner = slot_owner(direct, slot)
         piece = pieces[slot] if direct else pieces[0].at[slot]
+        values, codes = read_coded(piece, per_slot, half_rows)
         for begin in range(0, per_slot, 4):
             some = range(begin, min(begin + 4, per_slot))
             at = [owner * per_slot + i for i in some]
-            packed = [piece[i * half_rows : (i + 1) * half_rows, :] for i in some]
-            tail = per_slot * half_rows
-            total = [piece[tail + i : tail + i + 1, 0:1] for i in some]
+            code = [codes[i] for i in some]
+            total = each(
+                lambda c: jnp.exp2(c[:, blocks : blocks + 1] * F32(1 / LOG_STEPS))
+                * (1.0 + c[:, blocks + 1 : blocks + 2] * F32(1 / FINE)),
+                code,
+            )
+            low = lane_low((1, 2 * blocks), blocks)
+            code = each(lambda c: jnp.where(low, c, swap(c)), code)
+            packed = each(decode, [values[i] for i in some], code)
             z = [merged[f] for f in at]
             compact = each(unpack, packed)
             both = each(lambda c: full(c.astype(BF16).astype(F32)).astype(BF16), compact)
@@ -523,7 +602,8 @@
 
     def do_solve(c):
         nonlocal token
-        own, done = solve(parts[c], token)
+        count = sizes[c] // halves
+        own, done = solve(parts[c], count, merged[c].shape[1] // 2, token)
         token = [done]
         if paired:
             pieces[c] = [own, permute(own, "space", 1)]

time: 83.6 us -> 82.3 us (0.984)
  Pallas kernels: 30.1 us -> 38.5 us
  waiting for transfers between devices: 29 us -> 21.2 us
  starting transfers between devices: 23.4 us -> 21.5 us
    ppermute x18, waiting for transfers between devices: 29 us -> 21.2 us  [permute(): return lax.ppermute(x, axis, pairs)]
    pallas_call x3, Pallas kernels: 7.78 us -> 11.5 us  [filtered(): pl.pallas_call(functools.partial(energy_kernel, slots, direct, len(pieces...]
    ppermute x18, starting transfers between devices: 23.4 us -> 21.5 us  [permute(): return lax.ppermute(x, axis, pairs)]
    pallas_call x3, Pallas kernels: 10.4 us -> 12.3 us  [solve(): pl.pallas_call(functools.partial(solve_kernel, len(parts), number, half_r...]
    pallas_call x3, Pallas kernels: 0.07 us -> 1.95 us  [add(): pl.pallas_call(add_kernel, in_specs=[whole_spec()] * 2 + [any_spec()] * l...]
  transfers between devices with their start and end apart: 18 -> 18, of which waited for: 10 -> 8; matrix products, arithmetic and copies ran while one was open for 0% -> 0% of each run, Pallas kernels for 28% -> 37%
where the time goes in v6:
time: 82.3 us; the launch traced here: 82.1 us
  Pallas kernels  38.5 us (47%)
  starting transfers between devices  21.5 us (26%)
  waiting for transfers between devices  21.2 us (26%)
  between operations  0.92 us (1%)
    ppermute x18, starting transfers between devices, permute(): return lax.ppermute(x, axis, pairs)  21.5 us
    ppermute x18, waiting for transfers between devices, permute(): return lax.ppermute(x, axis, pairs)  21.2 us
    pallas_call x3, Pallas kernels, solve(): pl.pallas_call(functools.partial(solve_kernel, len(parts), number, half_r...  12.3 us
    pallas_call x3, Pallas kernels, filtered(): pl.pallas_call(functools.partial(energy_kernel, slots, direct, len(pieces...  11.5 us
    pallas_call x2, Pallas kernels, transform(): pl.pallas_call(functools.partial(transform_kernel, peers, parts, group),...  9.73 us
    pallas_call x3, Pallas kernels, gram(): pl.pallas_call(functools.partial(gram_kernel, peers, slots, direct, len(a...  2.93 us
    pallas_call x3, Pallas kernels, add(): pl.pallas_call(add_kernel, in_specs=[whole_spec()] * 2 + [any_spec()] * l...  1.95 us
  transfers between devices with their start and end apart: 18, of which 8 were waited for; matrix products, arithmetic and copies ran while one was open for 0% of the time, Pallas kernels for 37%

profile of v6, /device:TPU:0, one launch (start us, length us, event | category | flops | bytes accessed | tf_op | source)
XLA Modules:
  0.0 82.1 jit_solution(6982700369168127911)
XLA Ops:
  0.6 4.3 %transform.2 = (bf16[24,16,512]{2,1,0:T(8,128)(2,1)S(1)}, bf16[24,16,512]{2,1,0:T(8,128)(2,1)S(1)}, bf16[24,16,512]{2,1,0:T(8,128)(2,1)S(1)}, bf16[24,16,512]{2,1,0:T(8,128)(2,1)S(1)}, f32[8,128]{1,0:T(8,128)S(1)}) custom-call(s32[256]{0:T(256)} %refs_0_.3, f32[1,256]{1,0:T(1,128)} %bitcast.1, bf16[16,512,256]{2,1,0:T(8,128)(2,1)} %refs_2_.3), custom_call_target="tpu_custom_call" | custom-call | flops 1024 | bytes 1024 | tf_op jit(solution)/shard_map/transform/pallas_call | solution.py:149
  4.9 0.5 collective-permute-start.6
  5.4 2.6 %collective-permute-start.7 = (bf16[24,16,512]{2,1,0:T(8,128)(2,1)S(1)}, bf16[24,16,512]{2,1,0:T(8,128)(2,1)S(1)}, u32[]{:S(2)}, u32[]{:S(2)}) collective-permute-start(bf16[24,16,512]{2,1,0:T(8,128)(2,1)S(1)} %get-tuple-element.59), channel_id=1, source_target_pairs={{0,2},{1,3},{2,0},{3,1},{4,6},{5,7},{6,4},{7,5},{8,10},{9,11},{10,... | collective-permute-start | bytes 1179656 | tf_op jit(solution)/shard_map/ppermute | solution.py:560
  8.0 0.1 collective-permute-start.8
  8.1 5.4 %transform.3 = (bf16[24,16,512]{2,1,0:T(8,128)(2,1)S(1)}, bf16[24,16,512]{2,1,0:T(8,128)(2,1)S(1)}, bf16[24,16,512]{2,1,0:T(8,128)(2,1)S(1)}, bf16[24,16,512]{2,...) custom-call(s32[256]{0:T(256)} %refs_0_.3, ...), custom_call_target="tpu_custom_call" | custom-call | flops 1024 | bytes 1024 | tf_op jit(solution)/shard_map/transform/pallas_call | solution.py:149
  13.5 0.2 collective-permute-start.3
  13.7 1.9 %collective-permute-start.4 = (bf16[24,16,512]{2,1,0:T(8,128)(2,1)S(1)}, bf16[24,16,512]{2,1,0:T(8,128)(2,1)S(1)}, u32[]{:S(2)}, u32[]{:S(2)}) collective-permute-start(bf16[24,16,512]{2,1,0:T(8,128)(2,1)S(1)} %get-tuple-element.55), channel_id=1, source_target_pairs={{0,2},{1,3},{2,0},{3,1},{4,6},{5,7},{6,4},{7,5},{8,10},{9,11},{10,... | collective-permute-start | bytes 1179656 | tf_op jit(solution)/shard_map/ppermute | solution.py:560
  15.7 0.0 collective-permute-done.6.refs_1_
  15.7 0.0 collective-permute-start.5
  15.7 2.3 %collective-permute-done.7.refs_2_ = bf16[24,16,512]{2,1,0:T(8,128)(2,1)S(1)} collective-permute-done((bf16[24,16,512]{2,1,0:T(8,128)(2,1)S(1)}, bf16[24,16,512]{2,1,0:T(8,128)(2,1)S(1)}, u32[]{:S(2)}, u32[]{:S(2)}) %collective-permute-start.7) | collective-permute-done | bytes 393248 | tf_op jit(solution)/shard_map/ppermute | solution.py:560
  18.0 7.9 %collective-permute-done.8.refs_3_ = bf16[24,16,512]{2,1,0:T(8,128)(2,1)S(1)} collective-permute-done((bf16[24,16,512]{2,1,0:T(8,128)(2,1)S(1)}, bf16[24,16,512]{2,1,0:T(8,128)(2,1)S(1)}, u32[]{:S(2)}, u32[]{:S(2)}) %collective-permute-start.8) | collective-permute-done | bytes 393248 | tf_op jit(solution)/shard_map/ppermute | solution.py:560
  25.9 1.0 %gram.3 = (bf16[24,64,512]{2,1,0:T(8,128)(2,1)S(1)}, f32[8,128]{1,0:T(8,128)S(1)}, f32[12,32,128]{2,1,0:T(8,128)S(1)}, s16[400,128]{1,0:T(8,128)(2,1)S(1)}) custom-call(bf16[24,16,512]{2,1,0:T(8,128)(2,1)S(1)} %get-tuple-element.57.refs_0_, bf16[24,16,512]{2,1,0:T(8,128)(2,1)S(1)} %collective-permute-done.6.refs_1_, ...), custom_call_target="tpu_custom_call" | custom-call | flops 1024 | bytes 1024 | tf_op jit(solution)/shard_map/gram/pallas_call | solution.py:328
  26.9 1.7 %collective-permute-start.9 = (s16[400,128]{1,0:T(8,128)(2,1)S(1)}, s16[400,128]{1,0:T(8,128)(2,1)S(1)}, u32[]{:S(2)}, u32[]{:S(2)}) collective-permute-start(s16[400,128]{1,0:T(8,128)(2,1)S(1)} %get-tuple-element.63), channel_id=1, source_target_pairs={{0,4},{4,0},{8,12},{12,8},{1,5},{5,1},{9,13},{13,9},{2,6},{6,2},{1... | collective-permute-start | bytes 307208 | tf_op jit(solution)/shard_map/ppermute | solution.py:560
  28.6 0.4 collective-permute-start
  29.1 0.0 collective-permute-done.3.refs_1_
  29.1 1.5 %collective-permute-start.1 = (bf16[16,16,512]{2,1,0:T(8,128)(2,1)S(1)}, bf16[16,16,512]{2,1,0:T(8,128)(2,1)S(1)}, u32[]{:S(2)}, u32[]{:S(2)}) collective-permute-start(bf16[16,16,512]{2,1,0:T(8,128)(2,1)S(1)} %get-tuple-element.51), channel_id=1, source_target_pairs={{0,2},{1,3},{2,0},{3,1},{4,6},{5,7},{6,4},{7,5},{8,10},{9,11},{10,... | collective-permute-start | bytes 786440 | tf_op jit(solution)/shard_map/ppermute | solution.py:560
  30.6 1.8 %collective-permute-done.9.other = s16[400,128]{1,0:T(8,128)(2,1)S(1)} collective-permute-done((s16[400,128]{1,0:T(8,128)(2,1)S(1)}, s16[400,128]{1,0:T(8,128)(2,1)S(1)}, u32[]{:S(2)}, u32[]{:S(2)}) %collective-permute-start.9) | collective-permute-done | bytes 102432 | tf_op jit(solution)/shard_map/ppermute | solution.py:560
  32.4 1.2 %collective-permute-start.2 = (bf16[16,16,512]{2,1,0:T(8,128)(2,1)S(1)}, bf16[16,16,512]{2,1,0:T(8,128)(2,1)S(1)}, u32[]{:S(2)}, u32[]{:S(2)}) collective-permute-start(bf16[16,16,512]{2,1,0:T(8,128)(2,1)S(1)} %get-tuple-element.52), channel_id=1, source_target_pairs={{0,3},{1,2},{2,1},{3,0},{4,7},{5,6},{6,5},{7,4},{8,11},{9,10},{10,... | collective-permute-start | bytes 786440 | tf_op jit(solution)/shard_map/ppermute | solution.py:560
  33.6 0.8 add.3
  34.4 0.5 collective-permute-done.4.refs_2_
  34.8 3.0 %collective-permute-start.11 = (s16[400,128]{1,0:T(8,128)(2,1)S(1)}, s16[400,128]{1,0:T(8,128)(2,1)S(1)}, u32[]{:S(2)}, u32[]{:S(2)}) collective-permute-start(s16[400,128]{1,0:T(8,128)(2,1)S(1)} %get-tuple-element.68.refs_0_), channel_id=1, source_target_pairs={{0,8},{4,12},{8,0},{12,4},{1,9},{5,13},{9,1},{13,5},{2,10},{6,14},... | collective-permute-start | bytes 307208 | tf_op jit(solution)/shard_map/ppermute | solution.py:560
  37.9 4.9 %collective-permute-done.5.refs_3_ = bf16[24,16,512]{2,1,0:T(8,128)(2,1)S(1)} collective-permute-done((bf16[24,16,512]{2,1,0:T(8,128)(2,1)S(1)}, bf16[24,16,512]{2,1,0:T(8,128)(2,1)S(1)}, u32[]{:S(2)}, u32[]{:S(2)}) %collective-permute-start.5) | collective-permute-done | bytes 393248 | tf_op jit(solution)/shard_map/ppermute | solution.py:560
  42.7 1.1 %gram.4 = (bf16[24,64,512]{2,1,0:T(8,128)(2,1)S(1)}, f32[8,128]{1,0:T(8,128)S(1)}, f32[12,32,128]{2,1,0:T(8,128)S(1)}, s16[400,128]{1,0:T(8,128)(2,1)S(1)}) custom-call(bf16[24,16,512]{2,1,0:T(8,128)(2,1)S(1)} %get-tuple-element.53.refs_0_, bf16[24,16,512]{2,1,0:T(8,128)(2,1)S(1)} %collective-permute-done.3.refs_1_, ...), custom_call_target="tpu_custom_call" | custom-call | flops 1024 | bytes 1024 | tf_op jit(solution)/shard_map/gram/pallas_call | solution.py:328
  43.8 1.7 %collective-permute-start.10 = (s16[400,128]{1,0:T(8,128)(2,1)S(1)}, s16[400,128]{1,0:T(8,128)(2,1)S(1)}, u32[]{:S(2)}, u32[]{:S(2)}) collective-permute-start(s16[400,128]{1,0:T(8,128)(2,1)S(1)} %get-tuple-element.67), channel_id=1, source_target_pairs={{0,4},{4,0},{8,12},{12,8},{1,5},{5,1},{9,13},{13,9},{2,6},{6,2},{1... | collective-permute-start | bytes 307208 | tf_op jit(solution)/shard_map/ppermute | solution.py:560
  45.5 0.0 collective-permute-done.11.refs_1_
  45.5 4.5 %filters.3 = (s16[400,128]{1,0:T(8,128)(2,1)S(1)}, f32[8,128]{1,0:T(8,128)S(1)}) custom-call(s16[400,128]{1,0:T(8,128)(2,1)S(1)} %get-tuple-element.68.refs_0_, s16[400,128]{1,0:T(8,128)(2,1)S(1)} %collective-permute-done.11.refs_1_, f32[8,128]{1,0:T(8,128)S(1)} %get-tuple-element.69.refs_2_), custom_call_target="tpu_custom_call" | custom-call | flops 1024 | bytes 1024 | tf_op jit(solution)/shard_map/filters/pallas_call | solution.py:439
  50.0 0.5 collective-permute-start.13
  50.5 0.0 collective-permute-done.10.other
  50.5 0.8 add.4
  51.3 0.0 collective-permute-done.refs_1_
  51.3 0.0 collective-permute-done.1.refs_2_
  51.3 2.7 %collective-permute-done.2.refs_3_ = bf16[16,16,512]{2,1,0:T(8,128)(2,1)S(1)} collective-permute-done((bf16[16,16,512]{2,1,0:T(8,128)(2,1)S(1)}, bf16[16,16,512]{2,1,0:T(8,128)(2,1)S(1)}, u32[]{:S(2)}, u32[]{:S(2)}) %collective-permute-start.2) | collective-permute-done | bytes 262176 | tf_op jit(solution)/shard_map/ppermute | solution.py:560
  54.0 0.8 %gram.5 = (bf16[16,64,512]{2,1,0:T(8,128)(2,1)S(1)}, f32[8,128]{1,0:T(8,128)S(1)}, f32[8,32,128]{2,1,0:T(8,128)S(1)}, s16[272,128]{1,0:T(8,128)(2,1)S(1)}) custom-call(bf16[16,16,512]{2,1,0:T(8,128)(2,1)S(1)} %get-tuple-element.49.refs_0_, bf16[16,16,512]{2,1,0:T(8,128)(2,1)S(1)} %collective-permute-done.refs_1_, ...), custom_call_target="tpu_custom_call" | custom-call | flops 1024 | bytes 1024 | tf_op jit(solution)/shard_map/gram/pallas_call | solution.py:328
  54.8 1.7 %collective-permute-start.12 = (s16[272,128]{1,0:T(8,128)(2,1)S(1)}, s16[272,128]{1,0:T(8,128)(2,1)S(1)}, u32[]{:S(2)}, u32[]{:S(2)}) collective-permute-start(s16[272,128]{1,0:T(8,128)(2,1)S(1)} %get-tuple-element.74), channel_id=1, source_target_pairs={{0,4},{4,0},{8,12},{12,8},{1,5},{5,1},{9,13},{13,9},{2,6},{6,2},{1... | collective-permute-start | bytes 208904 | tf_op jit(solution)/shard_map/ppermute | solution.py:560
  56.5 2.6 %collective-permute-start.15 = (s16[400,128]{1,0:T(8,128)(2,1)S(1)}, s16[400,128]{1,0:T(8,128)(2,1)S(1)}, u32[]{:S(2)}, u32[]{:S(2)}) collective-permute-start(s16[400,128]{1,0:T(8,128)(2,1)S(1)} %get-tuple-element.80.refs_0_), channel_id=1, source_target_pairs={{0,8},{4,12},{8,0},{12,4},{1,9},{5,13},{9,1},{13,5},{2,10},{6,14},... | collective-permute-start | bytes 307208 | tf_op jit(solution)/shard_map/ppermute | solution.py:560
  59.1 0.0 collective-permute-done.13.refs_1_
  59.1 4.0 %energy.3 = (f32[64,256]{1,0:T(8,128)}, f32[64,2,64,64]{3,2,1,0:T(8,128)}, f32[8,128]{1,0:T(8,128)S(1)}) custom-call(bf16[24,64,512]{2,1,0:T(8,128)(2,1)S(1)} %get-tuple-element.75.merged, s16[400,128]{1,0:T(8,128)(2,1)S(1)} %get-tuple-element.76.refs_0_, s16[400,128]{1,0:T(8,128)(2,1)S(1)} %collective-permute-done.13.refs_1_, ...), custom_call_target="tpu_custom_call" | custom-call | flops 1024 | bytes 1024 | tf_op jit(solution)/shard_map/energy/pallas_call | solution.py:512
  63.2 0.0 collective-permute-done.12.other
  63.2 0.4 add.5
  63.5 0.4 collective-permute-start.14
  63.9 0.5 collective-permute-done.15.refs_1_
  64.4 4.3 %filters.4 = (s16[400,128]{1,0:T(8,128)(2,1)S(1)}, f32[8,128]{1,0:T(8,128)S(1)}) custom-call(s16[400,128]{1,0:T(8,128)(2,1)S(1)} %get-tuple-element.80.refs_0_, s16[400,128]{1,0:T(8,128)(2,1)S(1)} %collective-permute-done.15.refs_1_, f32[8,128]{1,0:T(8,128)S(1)} %get-tuple-element.81.refs_2_), custom_call_target="tpu_custom_call" | custom-call | flops 1024 | bytes 1024 | tf_op jit(solution)/shard_map/filters/pallas_call | solution.py:439
  68.7 0.4 collective-permute-start.17
  69.1 0.7 collective-permute-done.14.refs_1_
  69.8 3.5 %filters.5 = (s16[272,128]{1,0:T(8,128)(2,1)S(1)}, f32[8,128]{1,0:T(8,128)S(1)}) custom-call(s16[272,128]{1,0:T(8,128)(2,1)S(1)} %get-tuple-element.79.refs_0_, s16[272,128]{1,0:T(8,128)(2,1)S(1)} %collective-permute-done.14.refs_1_, f32[8,128]{1,0:T(8,128)S(1)} %get-tuple-element.82.refs_2_), custom_call_target="tpu_custom_call" | custom-call | flops 1024 | bytes 1024 | tf_op jit(solution)/shard_map/filters/pallas_call | solution.py:439
  73.3 1.1 %collective-permute-start.16 = (s16[272,128]{1,0:T(8,128)(2,1)S(1)}, s16[272,128]{1,0:T(8,128)(2,1)S(1)}, u32[]{:S(2)}, u32[]{:S(2)}) collective-permute-start(s16[272,128]{1,0:T(8,128)(2,1)S(1)} %get-tuple-element.83.refs_0_), channel_id=1, source_target_pairs={{0,4},{4,0},{8,12},{12,8},{1,5},{5,1},{9,13},{13,9},{2,6},{6,2},{1... | collective-permute-start | bytes 208904 | tf_op jit(solution)/shard_map/ppermute | solution.py:560
  74.4 0.0 collective-permute-done.17.refs_1_
  74.4 4.0 %energy.4 = (f32[64,256]{1,0:T(8,128)}, f32[64,2,64,64]{3,2,1,0:T(8,128)}, f32[8,128]{1,0:T(8,128)S(1)}) custom-call(bf16[24,64,512]{2,1,0:T(8,128)(2,1)S(1)} %get-tuple-element.84.merged, s16[400,128]{1,0:T(8,128)(2,1)S(1)} %get-tuple-element.85.refs_0_, ...), custom_call_target="tpu_custom_call", output_to_operand_aliasing={{0}: (3, {}), {1}: (4, {})} | custom-call | flops 1024 | bytes 1024 | tf_op jit(solution)/shard_map/energy/pallas_call | solution.py:512
  78.4 0.0 collective-permute-done.16.refs_1_
  78.5 3.5 %energy.5 = (f32[64,256]{1,0:T(8,128)}, f32[64,2,64,64]{3,2,1,0:T(8,128)}, f32[8,128]{1,0:T(8,128)}) custom-call(bf16[16,64,512]{2,1,0:T(8,128)(2,1)S(1)} %get-tuple-element.72.merged, s16[272,128]{1,0:T(8,128)(2,1)S(1)} %get-tuple-element.83.refs_0_, ...), custom_call_target="tpu_custom_call", output_to_operand_aliasing={{0}: (3, {}), {1}: (4, {})} | custom-call | flops 1024 | bytes 1024 | tf_op jit(solution)/shard_map/energy/pallas_call | solution.py:512
Async XLA Ops:
  4.9 10.7 %collective-permute-start.6 = (bf16[24,16,512]{2,1,0:T(8,128)(2,1)S(1)}, bf16[24,16,512]{2,1,0:T(8,128)(2,1)S(1)}, u32[]{:S(2)}, u32[]{:S(2)}) collective-permute-start(bf16[24,16,512]{2,1,0:T(8,128)(2,1)S(1)} %get-tuple-element.58), channel_id=1, source_target_pairs={{0,1},{1,0},{2,3},{3,2},{4,5},{5,4},{6,7},{7,6},{8,9},{9,8},{10,11... | collective-permute-start | bytes 1179656 | tf_op jit(solution)/shard_map/ppermute | solution.py:560
  5.4 12.5 %collective-permute-start.7 = (bf16[24,16,512]{2,1,0:T(8,128)(2,1)S(1)}, bf16[24,16,512]{2,1,0:T(8,128)(2,1)S(1)}, u32[]{:S(2)}, u32[]{:S(2)}) collective-permute-start(bf16[24,16,512]{2,1,0:T(8,128)(2,1)S(1)} %get-tuple-element.59), channel_id=1, source_target_pairs={{0,2},{1,3},{2,0},{3,1},{4,6},{5,7},{6,4},{7,5},{8,10},{9,11},{10,... | collective-permute-start | bytes 1179656 | tf_op jit(solution)/shard_map/ppermute | solution.py:560
  8.0 17.9 %collective-permute-start.8 = (bf16[24,16,512]{2,1,0:T(8,128)(2,1)S(1)}, bf16[24,16,512]{2,1,0:T(8,128)(2,1)S(1)}, u32[]{:S(2)}, u32[]{:S(2)}) collective-permute-start(bf16[24,16,512]{2,1,0:T(8,128)(2,1)S(1)} %get-tuple-element.60), channel_id=1, source_target_pairs={{0,3},{1,2},{2,1},{3,0},{4,7},{5,6},{6,5},{7,4},{8,11},{9,10},{10,... | collective-permute-start | bytes 1179656 | tf_op jit(solution)/shard_map/ppermute | solution.py:560
  13.5 15.6 %collective-permute-start.3 = (bf16[24,16,512]{2,1,0:T(8,128)(2,1)S(1)}, bf16[24,16,512]{2,1,0:T(8,128)(2,1)S(1)}, u32[]{:S(2)}, u32[]{:S(2)}) collective-permute-start(bf16[24,16,512]{2,1,0:T(8,128)(2,1)S(1)} %get-tuple-element.54), channel_id=1, source_target_pairs={{0,1},{1,0},{2,3},{3,2},{4,5},{5,4},{6,7},{7,6},{8,9},{9,8},{10,11... | collective-permute-start | bytes 1179656 | tf_op jit(solution)/shard_map/ppermute | solution.py:560
  13.7 21.1 %collective-permute-start.4 = (bf16[24,16,512]{2,1,0:T(8,128)(2,1)S(1)}, bf16[24,16,512]{2,1,0:T(8,128)(2,1)S(1)}, u32[]{:S(2)}, u32[]{:S(2)}) collective-permute-start(bf16[24,16,512]{2,1,0:T(8,128)(2,1)S(1)} %get-tuple-element.55), channel_id=1, source_target_pairs={{0,2},{1,3},{2,0},{3,1},{4,6},{5,7},{6,4},{7,5},{8,10},{9,11},{10,... | collective-permute-start | bytes 1179656 | tf_op jit(solution)/shard_map/ppermute | solution.py:560
  15.7 27.1 %collective-permute-start.5 = (bf16[24,16,512]{2,1,0:T(8,128)(2,1)S(1)}, bf16[24,16,512]{2,1,0:T(8,128)(2,1)S(1)}, u32[]{:S(2)}, u32[]{:S(2)}) collective-permute-start(bf16[24,16,512]{2,1,0:T(8,128)(2,1)S(1)} %get-tuple-element.56), channel_id=1, source_target_pairs={{0,3},{1,2},{2,1},{3,0},{4,7},{5,6},{6,5},{7,4},{8,11},{9,10},{10,... | collective-permute-start | bytes 1179656 | tf_op jit(solution)/shard_map/ppermute | solution.py:560
  26.9 5.5 %collective-permute-start.9 = (s16[400,128]{1,0:T(8,128)(2,1)S(1)}, s16[400,128]{1,0:T(8,128)(2,1)S(1)}, u32[]{:S(2)}, u32[]{:S(2)}) collective-permute-start(s16[400,128]{1,0:T(8,128)(2,1)S(1)} %get-tuple-element.63), channel_id=1, source_target_pairs={{0,4},{4,0},{8,12},{12,8},{1,5},{5,1},{9,13},{13,9},{2,6},{6,2},{1... | collective-permute-start | bytes 307208 | tf_op jit(solution)/shard_map/ppermute | solution.py:560
  28.6 22.6 %collective-permute-start = (bf16[16,16,512]{2,1,0:T(8,128)(2,1)S(1)}, bf16[16,16,512]{2,1,0:T(8,128)(2,1)S(1)}, u32[]{:S(2)}, u32[]{:S(2)}) collective-permute-start(bf16[16,16,512]{2,1,0:T(8,128)(2,1)S(1)} %get-tuple-element.50), channel_id=1, source_target_pairs={{0,1},{1,0},{2,3},{3,2},{4,5},{5,4},{6,7},{7,6},{8,9},{9,8},{10,11... | collective-permute-start | bytes 786440 | tf_op jit(solution)/shard_map/ppermute | solution.py:560
  29.1 22.2 %collective-permute-start.1 = (bf16[16,16,512]{2,1,0:T(8,128)(2,1)S(1)}, bf16[16,16,512]{2,1,0:T(8,128)(2,1)S(1)}, u32[]{:S(2)}, u32[]{:S(2)}) collective-permute-start(bf16[16,16,512]{2,1,0:T(8,128)(2,1)S(1)} %get-tuple-element.51), channel_id=1, source_target_pairs={{0,2},{1,3},{2,0},{3,1},{4,6},{5,7},{6,4},{7,5},{8,10},{9,11},{10,... | collective-permute-start | bytes 786440 | tf_op jit(solution)/shard_map/ppermute | solution.py:560
  32.4 21.6 %collective-permute-start.2 = (bf16[16,16,512]{2,1,0:T(8,128)(2,1)S(1)}, bf16[16,16,512]{2,1,0:T(8,128)(2,1)S(1)}, u32[]{:S(2)}, u32[]{:S(2)}) collective-permute-start(bf16[16,16,512]{2,1,0:T(8,128)(2,1)S(1)} %get-tuple-element.52), channel_id=1, source_target_pairs={{0,3},{1,2},{2,1},{3,0},{4,7},{5,6},{6,5},{7,4},{8,11},{9,10},{10,... | collective-permute-start | bytes 786440 | tf_op jit(solution)/shard_map/ppermute | solution.py:560
  34.8 10.7 %collective-permute-start.11 = (s16[400,128]{1,0:T(8,128)(2,1)S(1)}, s16[400,128]{1,0:T(8,128)(2,1)S(1)}, u32[]{:S(2)}, u32[]{:S(2)}) collective-permute-start(s16[400,128]{1,0:T(8,128)(2,1)S(1)} %get-tuple-element.68.refs_0_), channel_id=1, source_target_pairs={{0,8},{4,12},{8,0},{12,4},{1,9},{5,13},{9,1},{13,5},{2,10},{6,14},... | collective-permute-start | bytes 307208 | tf_op jit(solution)/shard_map/ppermute | solution.py:560
  43.8 6.7 %collective-permute-start.10 = (s16[400,128]{1,0:T(8,128)(2,1)S(1)}, s16[400,128]{1,0:T(8,128)(2,1)S(1)}, u32[]{:S(2)}, u32[]{:S(2)}) collective-permute-start(s16[400,128]{1,0:T(8,128)(2,1)S(1)} %get-tuple-element.67), channel_id=1, source_target_pairs={{0,4},{4,0},{8,12},{12,8},{1,5},{5,1},{9,13},{13,9},{2,6},{6,2},{1... | collective-permute-start | bytes 307208 | tf_op jit(solution)/shard_map/ppermute | solution.py:560
  50.0 9.1 %collective-permute-start.13 = (s16[400,128]{1,0:T(8,128)(2,1)S(1)}, s16[400,128]{1,0:T(8,128)(2,1)S(1)}, u32[]{:S(2)}, u32[]{:S(2)}) collective-permute-start(s16[400,128]{1,0:T(8,128)(2,1)S(1)} %get-tuple-element.76.refs_0_), channel_id=1, source_target_pairs={{0,4},{4,0},{8,12},{12,8},{1,5},{5,1},{9,13},{13,9},{2,6},{6,2},{1... | collective-permute-start | bytes 307208 | tf_op jit(solution)/shard_map/ppermute | solution.py:560
  54.8 8.3 %collective-permute-start.12 = (s16[272,128]{1,0:T(8,128)(2,1)S(1)}, s16[272,128]{1,0:T(8,128)(2,1)S(1)}, u32[]{:S(2)}, u32[]{:S(2)}) collective-permute-start(s16[272,128]{1,0:T(8,128)(2,1)S(1)} %get-tuple-element.74), channel_id=1, source_target_pairs={{0,4},{4,0},{8,12},{12,8},{1,5},{5,1},{9,13},{13,9},{2,6},{6,2},{1... | collective-permute-start | bytes 208904 | tf_op jit(solution)/shard_map/ppermute | solution.py:560
  56.5 7.9 %collective-permute-start.15 = (s16[400,128]{1,0:T(8,128)(2,1)S(1)}, s16[400,128]{1,0:T(8,128)(2,1)S(1)}, u32[]{:S(2)}, u32[]{:S(2)}) collective-permute-start(s16[400,128]{1,0:T(8,128)(2,1)S(1)} %get-tuple-element.80.refs_0_), channel_id=1, source_target_pairs={{0,8},{4,12},{8,0},{12,4},{1,9},{5,13},{9,1},{13,5},{2,10},{6,14},... | collective-permute-start | bytes 307208 | tf_op jit(solution)/shard_map/ppermute | solution.py:560
  63.5 6.3 %collective-permute-start.14 = (s16[272,128]{1,0:T(8,128)(2,1)S(1)}, s16[272,128]{1,0:T(8,128)(2,1)S(1)}, u32[]{:S(2)}, u32[]{:S(2)}) collective-permute-start(s16[272,128]{1,0:T(8,128)(2,1)S(1)} %get-tuple-element.79.refs_0_), channel_id=1, source_target_pairs={{0,8},{4,12},{8,0},{12,4},{1,9},{5,13},{9,1},{13,5},{2,10},{6,14},... | collective-permute-start | bytes 208904 | tf_op jit(solution)/shard_map/ppermute | solution.py:560
  68.7 5.7 %collective-permute-start.17 = (s16[400,128]{1,0:T(8,128)(2,1)S(1)}, s16[400,128]{1,0:T(8,128)(2,1)S(1)}, u32[]{:S(2)}, u32[]{:S(2)}) collective-permute-start(s16[400,128]{1,0:T(8,128)(2,1)S(1)} %get-tuple-element.85.refs_0_), channel_id=1, source_target_pairs={{0,4},{4,0},{8,12},{12,8},{1,5},{5,1},{9,13},{13,9},{2,6},{6,2},{1... | collective-permute-start | bytes 307208 | tf_op jit(solution)/shard_map/ppermute | solution.py:560
  73.3 5.1 %collective-permute-start.16 = (s16[272,128]{1,0:T(8,128)(2,1)S(1)}, s16[272,128]{1,0:T(8,128)(2,1)S(1)}, u32[]{:S(2)}, u32[]{:S(2)}) collective-permute-start(s16[272,128]{1,0:T(8,128)(2,1)S(1)} %get-tuple-element.83.refs_0_), channel_id=1, source_target_pairs={{0,4},{4,0},{8,12},{12,8},{1,5},{5,1},{9,13},{13,9},{2,6},{6,2},{1... | collective-permute-start | bytes 208904 | tf_op jit(solution)/shard_map/ppermute | solution.py:560

commit v7 on v4

--- a/solution.py
+++ b/solution.py
@@ -175,14 +175,21 @@
     return pltpu.roll(x, x.shape[1] // 2, 1)
 
 
-def pack(compact):
-    half = compact.shape[0]
-    both = compact + swap(compact)
+def each(fn, *lists):
+    return [fn(*items) for items in zip(*lists)]
+
+
+def double(compact):
+    return compact + swap(compact)
+
+
+def pack(both):
+    half = both.shape[0]
     low = lane_low((half // 2, 2 * half), half)
     return jnp.where(low, both[: half // 2], both[half // 2 :])
 
 
-def unpack(packed):
+def unpack(packed, scale=None):
     rows, half = packed.shape[0], packed.shape[1] // 2
     low = lane_low(packed.shape, half)
     other = swap(packed)
@@ -193,7 +200,12 @@
     turned = jnp.where(lane_low((half, half), rows), turned[:half], turned[half:])
     turned = jnp.concatenate([turned, turned], 1)
     low = lane_low(both.shape, half)
-    return 0.5 * jnp.where(low, both + turned, both - turned)
+    total = both + turned
+    apart = both - turned
+    top = jnp.where(low, total, apart)
+    bottom = jnp.where(low, -apart, total)
+    scale = F32(0.5) if scale is None else scale
+    return scale * top, scale * bottom
 
 
 def full(compact):
@@ -201,6 +213,85 @@
     turned = swap(compact)
     low = lane_low(compact.shape, half)
     return jnp.concatenate([compact, jnp.where(low, -turned, turned)], 0)
+
+
+TOP = 23169.0
+LOG_STEPS = 64.0
+FINE = float(2**21)
+
+
+def place(lines, rows):
+    shape = (rows, lines[0].shape[1])
+    row = lax.broadcasted_iota(jnp.int32, shape, 0)
+    out = jnp.zeros(shape, F32)
+    for i, line in enumerate(lines):
+        out = jnp.where(row == i, line, out)
+    return out
+
+
+def pad_rows(number):
+    return -(-number // 16) * 16
+
+
+def scale_of(code):
+    exponent = jnp.floor(code * F32(1 / 256))
+    part = code - exponent * 256
+    return (jnp.exp2(exponent) * (1 + part * F32(1 / 128))).astype(BF16)
+
+
+def outer(scales, number):
+    half = scales.shape[1] // 2
+    wide = scales.astype(F32)
+    row = lax.broadcasted_iota(jnp.int32, scales.shape, 0)
+    turned = jnp.transpose(wide)[:half].astype(BF16)
+    return [
+        dot(turned, jnp.where(row == i, wide, F32(0)).astype(BF16)) for i in range(number)
+    ]
+
+
+def encode(both):
+    half, width = both[0].shape
+    row = lax.broadcasted_iota(jnp.int32, (half, width), 0)
+    lane = lax.broadcasted_iota(jnp.int32, (half, width), 1)
+    on = (lane == row) | (lane == row + half)
+    diagonal = each(lambda b: jnp.sum(jnp.where(on, b, F32(0)), axis=0, keepdims=True), both)
+    root = jnp.sqrt(jnp.maximum(place(diagonal, pad_rows(len(both))), F32(1e-30)))
+    exponent = jnp.floor(jnp.log(root) * F32(1 / math.log(2.0)))
+    part = jnp.maximum(jnp.ceil((root * jnp.exp2(-exponent) - 1) * 128), F32(0))
+    codes = exponent * 256 + part
+    products = outer(scale_of(codes), len(both))
+    value = each(lambda b, p: jnp.round(b * (F32(TOP) / p)), both, products)
+    return each(lambda v: pack(jnp.clip(v, F32(-32767), F32(32767))), value), codes
+
+
+def decode(values, codes):
+    products = outer(scale_of(codes), len(values))
+    return each(lambda v, p: unpack(v, p * F32(0.5 / TOP)), values, products)
+
+
+def to_short(x):
+    return x.astype(jnp.int32).astype(jnp.int16)
+
+
+def from_short(x):
+    return x.astype(jnp.int32).astype(F32)
+
+
+def coded_rows(number, half_rows):
+    return number * half_rows + pad_rows(number)
+
+
+def write_coded(out, values, codes):
+    half_rows = values[0].shape[0]
+    for i, value in enumerate(values):
+        out[i * half_rows : (i + 1) * half_rows, :] = to_short(value)
+    out[len(values) * half_rows :, :] = to_short(codes)
+
+
+def read_coded(ref, number, half_rows):
+    codes = from_short(ref[number * half_rows :, :])
+    values = [from_short(ref[i * half_rows : (i + 1) * half_rows, :]) for i in range(number)]
+    return values, codes
 
 
 def slot_owner(direct, slot):
@@ -222,6 +313,7 @@
     low = lane_low((blocks, 2 * blocks), blocks)
     for slot in range(slots):
         owner = slot_owner(direct, slot)
+        coded = []
         for i in range(per_slot):
             f = owner * per_slot + i
             if stage is None:
@@ -240,10 +332,14 @@
             s = s * F32(1.0 / blocks)
             top, bottom = s[:blocks], swap(s[blocks:])
             compact = jnp.where(low, top + bottom, top - bottom)
-            if direct:
-                grams[slot][i] = pack(compact)
+            if direct and slot:
+                coded.append(double(compact))
+            elif direct:
+                grams[0][i] = compact
             else:
-                grams[0][f] = pack(compact)
+                grams[0][f] = pack(double(compact))
+        if coded:
+            write_coded(grams[slot], *encode(coded))
 
 
 def gram(pieces, slots, direct, after):
@@ -251,15 +347,17 @@
     count, here, width = pieces[0].shape
     blocks = here * peers
     if direct:
-        shapes = [(count // slots, blocks // 2, 2 * blocks)] * slots
+        rows = coded_rows(count // slots, blocks // 2)
+        shapes = [((count // slots, blocks, 2 * blocks), F32)]
+        shapes += [((rows, 2 * blocks), jnp.int16)] * (slots - 1)
     else:
-        shapes = [(count, blocks // 2, 2 * blocks)]
+        shapes = [((count, blocks // 2, 2 * blocks), F32)]
     out = pl.pallas_call(
         functools.partial(gram_kernel, peers, slots, direct, len(after)),
         in_specs=[whole_spec()] * peers + [any_spec()] * len(after),
         out_specs=[whole_spec()] * (2 + len(shapes)),
         out_shape=[jax.ShapeDtypeStruct((count, blocks, width), BF16), TOKEN]
-        + [jax.ShapeDtypeStruct(s, F32) for s in shapes],
+        + [jax.ShapeDtypeStruct(*s) for s in shapes],
         scratch_shapes=[pltpu.VMEM((blocks, width), F32)] if here % 16 else [],
         compiler_params=params(),
         cost_estimate=light(),
@@ -268,22 +366,25 @@
     return out[0], out[2:], out[1]
 
 
-def add_kernel(one, two, *refs):
+def add_kernel(own, other, *refs):
     out, token = refs[-2:]
     token[...] = jnp.zeros_like(token)
-    out[...] = one[...] + two[...]
-
-
-def add(one, two, after):
+    number, blocks, _ = own.shape
+    received = decode(*read_coded(other, number, blocks // 2))
+    sums = [double(own[i] + received[i][0]) for i in range(number)]
+    write_coded(out, *encode(sums))
+
+
+def add(own, other, after):
     return pl.pallas_call(
         add_kernel,
         in_specs=[whole_spec()] * 2 + [any_spec()] * len(after),
         out_specs=[whole_spec()] * 2,
-        out_shape=[jax.ShapeDtypeStruct(one.shape, F32), TOKEN],
+        out_shape=[jax.ShapeDtypeStruct(other.shape, jnp.int16), TOKEN],
         compiler_params=params(),
         cost_estimate=light(),
         name="add",
-    )(one, two, *after)
+    )(own, other, *after)
 
 
 def split(x):
@@ -291,30 +392,28 @@
     return high, (x - high.astype(F32)).astype(BF16)
 
 
-def each(fn, *lists):
-    return [fn(*items) for items in zip(*lists)]
-
-
-def solve_kernel(parts, *refs):
+def solve_kernel(parts, number, half_rows, *refs):
     ins, out, token = refs[:parts], refs[-2], refs[-1]
     token[...] = jnp.zeros_like(token)
-    number, half_rows, width = ins[0].shape
+    width = out.shape[1]
     half = width // 2
     shape = (half, width)
     row = lax.broadcasted_iota(jnp.int32, shape, 0)
     lane = lax.broadcasted_iota(jnp.int32, shape, 1)
     eye = jnp.where(row == lane, F32(1), F32(0))
 
-    def load(i):
-        total = ins[0][i]
-        for r in ins[1:]:
-            total = total + r[i]
-        return unpack(total)
-
-    grams = [load(i) for i in range(number)]
+    if parts == 1:
+        both_halves = [unpack(ins[0][i]) for i in range(number)]
+    else:
+        one = decode(*read_coded(ins[0], number, half_rows))
+        two = decode(*read_coded(ins[1], number, half_rows))
+        both_halves = [(p[0] + q[0], p[1] + q[1]) for p, q in zip(one, two)]
+    grams = [h[0] for h in both_halves]
     shift = each(lambda g: jnp.sum(g * eye, keepdims=True) * F32(1.0 / half), grams)
+    eye_low = jnp.where(row + half == lane, F32(1), F32(0))
     system = each(lambda g, m: g / m + eye, grams, shift)
-    both = each(lambda a: split(full(a)), system)
+    under = each(lambda h, m: h[1] / m + eye_low, both_halves, shift)
+    both = each(lambda a, u: split(jnp.concatenate([a, u], 0)), system, under)
 
     low_end, high_end = 1.0, float(half + 1)
     mid, radius = (high_end + low_end) / 2, (high_end - low_end) / 2
@@ -341,37 +440,36 @@
         step = each(lambda r, v: dot(r.astype(BF16), v), residual, xf)
         factor = 1.0 if kind == "last" else 2 * t * t / (2 * t * t - 1)
         x = each(lambda v, m: F32(factor) * (v + m), xw, step)
-    packed = each(lambda v: pack(eye - v), x)
-    for i in range(number):
-        out[i * half_rows : (i + 1) * half_rows, :] = packed[i]
-    filters = each(unpack, packed)
-    rounded = each(lambda c: c.astype(BF16), filters)
-    turned = each(lambda c: full(c.astype(F32)).astype(BF16), rounded)
+    values, codes = encode(each(lambda v: double(eye - v), x))
+    filters = decode(values, codes)
+    rounded = each(lambda c: c[0].astype(BF16), filters)
+    turned = each(
+        lambda c: jnp.concatenate([c[0].astype(BF16), c[1].astype(BF16)], 0), filters
+    )
     split_g = each(split, grams)
     moved = each(lambda g, c: dot(g[0], c) + dot(g[1], c), split_g, turned)
     energy = each(
         lambda c, h: jnp.sum(c.astype(F32) * h, keepdims=True) * F32(half), rounded, moved
     )
-    tail = out.shape[0] - number * half_rows
-    line = lax.broadcasted_iota(jnp.int32, (tail, width), 0)
-    totals = jnp.ones((tail, width), F32)
-    for i in range(number):
-        totals = jnp.where(line == i, energy[i], totals)
-    out[number * half_rows :, :] = totals
-
-
-def tail_rows(number):
-    return -(-number // 8) * 8
-
-
-def solve(parts, after):
-    number, half_rows, width = parts[0].shape
-    rows = number * half_rows + tail_rows(number)
+    energy = place([jnp.broadcast_to(e, (1, width)) for e in energy], codes.shape[0])
+    energy = jnp.maximum(energy, F32(1e-30))
+    whole = jnp.floor(jnp.log(energy) * F32(LOG_STEPS / math.log(2.0)))
+    rest = jnp.round((energy * jnp.exp2(whole * F32(-1 / LOG_STEPS)) - 1.0) * F32(FINE))
+    spot = lax.broadcasted_iota(jnp.int32, codes.shape, 1)
+    codes = jnp.where(spot == half, whole, jnp.where(spot == half + 1, rest, codes))
+    write_coded(out, values, codes)
+
+
+def solve(parts, number, half_rows, after):
+    width = parts[0].shape[-1]
     return pl.pallas_call(
-        functools.partial(solve_kernel, len(parts)),
+        functools.partial(solve_kernel, len(parts), number, half_rows),
         in_specs=[whole_spec()] * len(parts) + [any_spec()] * len(after),
         out_specs=[whole_spec()] * 2,
-        out_shape=[jax.ShapeDtypeStruct((rows, width), F32), TOKEN],
+        out_shape=[
+            jax.ShapeDtypeStruct((coded_rows(number, half_rows), width), jnp.int16),
+            TOKEN,
+        ],
         compiler_params=params(),
         cost_estimate=light(),
         name="filters",
@@ -391,19 +489,28 @@
     for slot in range(slots):
         owner = slot_owner(direct, slot)
         piece = pieces[slot] if direct else pieces[0].at[slot]
+        values, codes = read_coded(piece, per_slot, half_rows)
+        whole = codes[:, blocks : blocks + 1]
+        rest = codes[:, blocks + 1 : blocks + 2]
+        total = jnp.exp2(whole * F32(1 / LOG_STEPS)) * (1.0 + rest * F32(1 / FINE))
+        gains = F32(states) / total
+        codes = jnp.where(lane_low(codes.shape, blocks), codes, swap(codes))
+        products = outer(scale_of(codes), per_slot)
         for begin in range(0, per_slot, 4):
             some = range(begin, min(begin + 4, per_slot))
             at = [owner * per_slot + i for i in some]
-            packed = [piece[i * half_rows : (i + 1) * half_rows, :] for i in some]
-            tail = per_slot * half_rows
-            total = [piece[tail + i : tail + i + 1, 0:1] for i in some]
             z = [merged[f] for f in at]
-            compact = each(unpack, packed)
-            both = each(lambda c: full(c.astype(BF16).astype(F32)).astype(BF16), compact)
+            scale = [products[i] * F32(0.5 / TOP) for i in some]
+            halves = each(unpack, [values[i] for i in some], scale)
+            compact = [h[0] for h in halves]
+            both = each(
+                lambda h: jnp.concatenate([h[0].astype(BF16), h[1].astype(BF16)], 0), halves
+            )
+            gain = [gains[i : i + 1] for i in some]
             w = each(lambda v: jnp.concatenate([v[:, :entries], v[:, entries:]], 0), z)
             r = each(dot, both, w)
             energy = each(
-                lambda v, t: jnp.sum(v * v, axis=0, keepdims=True) * (F32(states) / t), r, total
+                lambda v, t: jnp.sum(v * v, axis=0, keepdims=True) * t, r, gain
             )
             for f, c, e in zip(at, compact, energy):
                 filters[f, 0] = c[:, :blocks]
@@ -471,8 +578,8 @@
 
 SIZES = [24, 24, 16]
 ORDER = (
-    ("T", 0), ("T", 1), ("G", 0), ("A", 0), ("G", 1), ("F", 0), ("A", 1), ("G", 2),
-    ("E", 0), ("A", 2), ("F", 1), ("F", 2), ("E", 1), ("E", 2),
+    ("T", 0), ("T", 1), ("G", 0), ("A", 0), ("F", 0), ("G", 1), ("A", 1), ("E", 0),
+    ("G", 2), ("A", 2), ("F", 1), ("F", 2), ("E", 1), ("E", 2),
 )
 
 
@@ -505,9 +612,13 @@
             sent[k] = [pieces_out[0]] + [
                 permute(pieces_out[offset], "tm", offset) for offset in range(1, peers)
             ]
+        if c == 0 and len(sizes) > 1:
+            token.append(sent[0][1])
 
     def do_gram(c):
         nonlocal token
+        if c == 0:
+            token += [sent[k][1] for k in range(1, len(sizes))]
         merged[c], grams[c], done = gram(sent[c], halves, paired, token)
         token = [done]
         if paired:
@@ -523,7 +634,8 @@
 
     def do_solve(c):
         nonlocal token
-        own, done = solve(parts[c], token)
+        count = sizes[c] // halves
+        own, done = solve(parts[c], count, merged[c].shape[1] // 2, token)
         token = [done]
         if paired:
             pieces[c] = [own, permute(own, "space", 1)]

time: 83.6 us -> 82.9 us (level)
  waiting for transfers between devices: 29 us -> 21.4 us
  Pallas kernels: 30.1 us -> 35.8 us
  starting transfers between devices: 23.4 us -> 24.6 us
    ppermute x18, waiting for transfers between devices: 29 us -> 21.4 us  [permute(): return lax.ppermute(x, axis, pairs)]
    pallas_call x3, Pallas kernels: 0.07 us -> 2.66 us  [add(): pl.pallas_call(add_kernel, in_specs=[whole_spec()] * 2 + [any_spec()] * l...]
    pallas_call x3, Pallas kernels: 10.4 us -> 11.8 us  [solve(): pl.pallas_call(functools.partial(solve_kernel, len(parts), number, half_r...]
    pallas_call x3, Pallas kernels: 2.14 us -> 3.46 us  [gram(): pl.pallas_call(functools.partial(gram_kernel, peers, slots, direct, len(a...]
    ppermute x18, starting transfers between devices: 23.4 us -> 24.6 us  [permute(): return lax.ppermute(x, axis, pairs)]
  transfers between devices with their start and end apart: 18 -> 18, of which waited for: 10 -> 7; matrix products, arithmetic and copies ran while one was open for 0% -> 0% of each run, Pallas kernels for 28% -> 34%
where the time goes in v7:
time: 82.9 us; the launch traced here: 82.7 us
  Pallas kernels  35.8 us (43%)
  starting transfers between devices  24.6 us (30%)
  waiting for transfers between devices  21.4 us (26%)
  between operations  0.93 us (1%)
    ppermute x18, starting transfers between devices, permute(): return lax.ppermute(x, axis, pairs)  24.6 us
    ppermute x18, waiting for transfers between devices, permute(): return lax.ppermute(x, axis, pairs)  21.4 us
    pallas_call x3, Pallas kernels, solve(): pl.pallas_call(functools.partial(solve_kernel, len(parts), number, half_r...  11.8 us
    pallas_call x2, Pallas kernels, transform(): pl.pallas_call(functools.partial(transform_kernel, peers, parts, group),...  9.72 us
    pallas_call x3, Pallas kernels, filtered(): pl.pallas_call(functools.partial(energy_kernel, slots, direct, len(pieces...  8.17 us
    pallas_call x3, Pallas kernels, gram(): pl.pallas_call(functools.partial(gram_kernel, peers, slots, direct, len(a...  3.46 us
    pallas_call x3, Pallas kernels, add(): pl.pallas_call(add_kernel, in_specs=[whole_spec()] * 2 + [any_spec()] * l...  2.66 us
  transfers between devices with their start and end apart: 18, of which 7 were waited for; matrix products, arithmetic and copies ran while one was open for 0% of the time, Pallas kernels for 34%

profile of v7, /device:TPU:0, one launch (start us, length us, event | category | flops | bytes accessed | tf_op | source)
XLA Modules:
  0.0 82.7 jit_solution(12386253992059154042)
XLA Ops:
  0.6 4.3 %transform.2 = (bf16[24,16,512]{2,1,0:T(8,128)(2,1)S(1)}, bf16[24,16,512]{2,1,0:T(8,128)(2,1)S(1)}, bf16[24,16,512]{2,1,0:T(8,128)(2,1)S(1)}, bf16[24,16,512]{2,1,0:T(8,128)(2,1)S(1)}, f32[8,128]{1,0:T(8,128)S(1)}) custom-call(s32[256]{0:T(256)} %refs_0_.3, f32[1,256]{1,0:T(1,128)} %bitcast.1, bf16[16,512,256]{2,1,0:T(8,128)(2,1)} %refs_2_.3), custom_call_target="tpu_custom_call" | custom-call | flops 1024 | bytes 1024 | tf_op jit(solution)/shard_map/transform/pallas_call | solution.py:149
  4.9 0.5 collective-permute-start
  5.4 2.6 %collective-permute-start.4 = (bf16[24,16,512]{2,1,0:T(8,128)(2,1)S(1)}, bf16[24,16,512]{2,1,0:T(8,128)(2,1)S(1)}, u32[]{:S(2)}, u32[]{:S(2)}) collective-permute-start(bf16[24,16,512]{2,1,0:T(8,128)(2,1)S(1)} %get-tuple-element.55), channel_id=1, source_target_pairs={{0,2},{1,3},{2,0},{3,1},{4,6},{5,7},{6,4},{7,5},{8,10},{9,11},{10,... | collective-permute-start | bytes 1179656 | tf_op jit(solution)/shard_map/ppermute | solution.py:588
  8.0 0.1 collective-permute-start.5
  8.1 0.0 collective-permute-done.refs_4_.refs_1_
  8.1 5.4 %transform.3 = (bf16[24,16,512]{2,1,0:T(8,128)(2,1)S(1)}, bf16[24,16,512]{2,1,0:T(8,128)(2,1)S(1)}, bf16[24,16,512]{2,1,0:T(8,128)(2,1)S(1)}, bf16[24,16,512]{2,...) custom-call(s32[256]{0:T(256)} %refs_0_.3, ...), custom_call_target="tpu_custom_call" | custom-call | flops 1024 | bytes 1024 | tf_op jit(solution)/shard_map/transform/pallas_call | solution.py:149
  13.5 0.2 collective-permute-start.6
  13.7 0.4 collective-permute-start.1
  14.1 1.7 %collective-permute-start.10 = (bf16[24,16,512]{2,1,0:T(8,128)(2,1)S(1)}, bf16[24,16,512]{2,1,0:T(8,128)(2,1)S(1)}, u32[]{:S(2)}, u32[]{:S(2)}) collective-permute-start(bf16[24,16,512]{2,1,0:T(8,128)(2,1)S(1)} %get-tuple-element.67), channel_id=1, source_target_pairs={{0,2},{1,3},{2,0},{3,1},{4,6},{5,7},{6,4},{7,5},{8,10},{9,11},{10,... | collective-permute-start | bytes 1179656 | tf_op jit(solution)/shard_map/ppermute | solution.py:588
  15.8 2.1 %collective-permute-done.4.refs_2_ = bf16[24,16,512]{2,1,0:T(8,128)(2,1)S(1)} collective-permute-done((bf16[24,16,512]{2,1,0:T(8,128)(2,1)S(1)}, bf16[24,16,512]{2,1,0:T(8,128)(2,1)S(1)}, u32[]{:S(2)}, u32[]{:S(2)}) %collective-permute-start.4) | collective-permute-done | bytes 393248 | tf_op jit(solution)/shard_map/ppermute | solution.py:588
  18.0 0.8 collective-permute-start.11
  18.7 7.1 %collective-permute-done.5.refs_3_ = bf16[24,16,512]{2,1,0:T(8,128)(2,1)S(1)} collective-permute-done((bf16[24,16,512]{2,1,0:T(8,128)(2,1)S(1)}, bf16[24,16,512]{2,1,0:T(8,128)(2,1)S(1)}, u32[]{:S(2)}, u32[]{:S(2)}) %collective-permute-start.5) | collective-permute-done | bytes 393248 | tf_op jit(solution)/shard_map/ppermute | solution.py:588
  25.9 0.0 collective-permute-done.1.refs_6_.refs_1_
  25.9 0.0 collective-permute-done.6.refs_5_.refs_1_
  25.9 1.2 %gram.3 = (bf16[24,64,512]{2,1,0:T(8,128)(2,1)S(1)}, f32[8,128]{1,0:T(8,128)S(1)}, f32[12,64,128]{2,1,0:T(8,128)S(1)}, s16[400,128]{1,0:T(8,128)(2,1)S(1)}) custom-call(bf16[24,16,512]{2,1,0:T(8,128)(2,1)S(1)} %get-tuple-element.54.refs_0_, bf16[24,16,512]{2,1,0:T(8,128)(2,1)S(1)} %collective-permute-done.refs_4_.refs_1_, ...), custom_call_target="tpu_custom_call" | custom-call | flops 1024 | bytes 1024 | tf_op jit(solution)/shard_map/gram/pallas_call | solution.py:355
  27.0 1.7 %collective-permute-start.7 = (s16[400,128]{1,0:T(8,128)(2,1)S(1)}, s16[400,128]{1,0:T(8,128)(2,1)S(1)}, u32[]{:S(2)}, u32[]{:S(2)}) collective-permute-start(s16[400,128]{1,0:T(8,128)(2,1)S(1)} %get-tuple-element.61), channel_id=1, source_target_pairs={{0,4},{4,0},{8,12},{12,8},{1,5},{5,1},{9,13},{13,9},{2,6},{6,2},{1... | collective-permute-start | bytes 307208 | tf_op jit(solution)/shard_map/ppermute | solution.py:588
  28.8 1.5 %collective-permute-start.2 = (bf16[16,16,512]{2,1,0:T(8,128)(2,1)S(1)}, bf16[16,16,512]{2,1,0:T(8,128)(2,1)S(1)}, u32[]{:S(2)}, u32[]{:S(2)}) collective-permute-start(bf16[16,16,512]{2,1,0:T(8,128)(2,1)S(1)} %get-tuple-element.52), channel_id=1, source_target_pairs={{0,2},{1,3},{2,0},{3,1},{4,6},{5,7},{6,4},{7,5},{8,10},{9,11},{10,... | collective-permute-start | bytes 786440 | tf_op jit(solution)/shard_map/ppermute | solution.py:588
  30.3 0.3 collective-permute-start.3
  30.6 2.0 %collective-permute-done.7.other = s16[400,128]{1,0:T(8,128)(2,1)S(1)} collective-permute-done((s16[400,128]{1,0:T(8,128)(2,1)S(1)}, s16[400,128]{1,0:T(8,128)(2,1)S(1)}, u32[]{:S(2)}, u32[]{:S(2)}) %collective-permute-start.7) | collective-permute-done | bytes 102432 | tf_op jit(solution)/shard_map/ppermute | solution.py:588
  32.5 1.0 %add.3 = (s16[400,128]{1,0:T(8,128)(2,1)S(1)}, f32[8,128]{1,0:T(8,128)S(1)}) custom-call(f32[12,64,128]{2,1,0:T(8,128)S(1)} %get-tuple-element.60.own, s16[400,128]{1,0:T(8,128)(2,1)S(1)} %collective-permute-done.7.other, f32[8,128]{1,0:T(8,128)S(1)} %get-tuple-element.62.refs_0_), custom_call_target="tpu_custom_call" | custom-call | flops 1024 | bytes 1024 | tf_op jit(solution)/shard_map/add/pallas_call | solution.py:379
  33.5 2.8 %collective-permute-start.8 = (s16[400,128]{1,0:T(8,128)(2,1)S(1)}, s16[400,128]{1,0:T(8,128)(2,1)S(1)}, u32[]{:S(2)}, u32[]{:S(2)}) collective-permute-start(s16[400,128]{1,0:T(8,128)(2,1)S(1)} %get-tuple-element.63.refs_0_), channel_id=1, source_target_pairs={{0,8},{4,12},{8,0},{12,4},{1,9},{5,13},{9,1},{13,5},{2,10},{6,14},... | collective-permute-start | bytes 307208 | tf_op jit(solution)/shard_map/ppermute | solution.py:588
  36.3 5.1 %collective-permute-done.8.refs_1_ = s16[400,128]{1,0:T(8,128)(2,1)S(1)} collective-permute-done((s16[400,128]{1,0:T(8,128)(2,1)S(1)}, s16[400,128]{1,0:T(8,128)(2,1)S(1)}, u32[]{:S(2)}, u32[]{:S(2)}) %collective-permute-start.8) | collective-permute-done | bytes 102432 | tf_op jit(solution)/shard_map/ppermute | solution.py:588
  41.4 4.2 %filters.3 = (s16[400,128]{1,0:T(8,128)(2,1)S(1)}, f32[8,128]{1,0:T(8,128)S(1)}) custom-call(s16[400,128]{1,0:T(8,128)(2,1)S(1)} %get-tuple-element.63.refs_0_, s16[400,128]{1,0:T(8,128)(2,1)S(1)} %collective-permute-done.8.refs_1_, f32[8,128]{1,0:T(8,128)S(1)} %get-tuple-element.64.refs_2_), custom_call_target="tpu_custom_call" | custom-call | flops 1024 | bytes 1024 | tf_op jit(solution)/shard_map/filters/pallas_call | solution.py:465
  45.6 0.0 collective-permute-done.10.refs_2_
  45.6 0.0 collective-permute-done.11.refs_3_
  45.6 1.4 %gram.4 = (bf16[24,64,512]{2,1,0:T(8,128)(2,1)S(1)}, f32[8,128]{1,0:T(8,128)S(1)}, f32[12,64,128]{2,1,0:T(8,128)S(1)}, s16[400,128]{1,0:T(8,128)(2,1)S(1)}) custom-call(bf16[24,16,512]{2,1,0:T(8,128)(2,1)S(1)} %get-tuple-element.66.refs_0_, bf16[24,16,512]{2,1,0:T(8,128)(2,1)S(1)} %collective-permute-done.6.refs_5_.refs_1_, ...), custom_call_target="tpu_custom_call" | custom-call | flops 1024 | bytes 1024 | tf_op jit(solution)/shard_map/gram/pallas_call | solution.py:355
  47.0 0.8 collective-permute-start.12
  47.8 1.3 %collective-permute-start.9 = (s16[400,128]{1,0:T(8,128)(2,1)S(1)}, s16[400,128]{1,0:T(8,128)(2,1)S(1)}, u32[]{:S(2)}, u32[]{:S(2)}) collective-permute-start(s16[400,128]{1,0:T(8,128)(2,1)S(1)} %get-tuple-element.65.refs_0_), channel_id=1, source_target_pairs={{0,4},{4,0},{8,12},{12,8},{1,5},{5,1},{9,13},{13,9},{2,6},{6,2},{1... | collective-permute-start | bytes 307208 | tf_op jit(solution)/shard_map/ppermute | solution.py:588
  49.1 3.2 %collective-permute-done.12.other = s16[400,128]{1,0:T(8,128)(2,1)S(1)} collective-permute-done((s16[400,128]{1,0:T(8,128)(2,1)S(1)}, s16[400,128]{1,0:T(8,128)(2,1)S(1)}, u32[]{:S(2)}, u32[]{:S(2)}) %collective-permute-start.12) | collective-permute-done | bytes 102432 | tf_op jit(solution)/shard_map/ppermute | solution.py:588
  52.3 0.9 %add.4 = (s16[400,128]{1,0:T(8,128)(2,1)S(1)}, f32[8,128]{1,0:T(8,128)S(1)}) custom-call(f32[12,64,128]{2,1,0:T(8,128)S(1)} %get-tuple-element.70.own, s16[400,128]{1,0:T(8,128)(2,1)S(1)} %collective-permute-done.12.other, f32[8,128]{1,0:T(8,128)S(1)} %get-tuple-element.72.refs_0_), custom_call_target="tpu_custom_call" | custom-call | flops 1024 | bytes 1024 | tf_op jit(solution)/shard_map/add/pallas_call | solution.py:379
  53.3 0.1 collective-permute-done.9.refs_1_
  53.4 2.7 %energy.3 = (f32[64,256]{1,0:T(8,128)}, f32[64,2,64,64]{3,2,1,0:T(8,128)}, f32[8,128]{1,0:T(8,128)S(1)}) custom-call(bf16[24,64,512]{2,1,0:T(8,128)(2,1)S(1)} %get-tuple-element.59.merged, s16[400,128]{1,0:T(8,128)(2,1)S(1)} %get-tuple-element.65.refs_0_, s16[400,128]{1,0:T(8,128)(2,1)S(1)} %collective-permute-done.9.refs_1_, ...), custom_call_target="tpu_custom_call" | custom-call | flops 1024 | bytes 1024 | tf_op jit(solution)/shard_map/energy/pallas_call | solution.py:540
  56.1 0.0 collective-permute-done.2.refs_2_
  56.2 0.0 collective-permute-done.3.refs_3_
  56.2 1.0 %gram.5 = (bf16[16,64,512]{2,1,0:T(8,128)(2,1)S(1)}, f32[8,128]{1,0:T(8,128)S(1)}, f32[8,64,128]{2,1,0:T(8,128)S(1)}, s16[272,128]{1,0:T(8,128)(2,1)S(1)}) custom-call(bf16[16,16,512]{2,1,0:T(8,128)(2,1)S(1)} %get-tuple-element.50.refs_0_, bf16[16,16,512]{2,1,0:T(8,128)(2,1)S(1)} %collective-permute-done.1.refs_6_.refs_1_, ...), custom_call_target="tpu_custom_call" | custom-call | flops 1024 | bytes 1024 | tf_op jit(solution)/shard_map/gram/pallas_call | solution.py:355
  57.1 1.4 %collective-permute-start.13 = (s16[272,128]{1,0:T(8,128)(2,1)S(1)}, s16[272,128]{1,0:T(8,128)(2,1)S(1)}, u32[]{:S(2)}, u32[]{:S(2)}) collective-permute-start(s16[272,128]{1,0:T(8,128)(2,1)S(1)} %get-tuple-element.77), channel_id=1, source_target_pairs={{0,4},{4,0},{8,12},{12,8},{1,5},{5,1},{9,13},{13,9},{2,6},{6,2},{1... | collective-permute-start | bytes 208904 | tf_op jit(solution)/shard_map/ppermute | solution.py:588
  58.6 3.4 %collective-permute-start.15 = (s16[400,128]{1,0:T(8,128)(2,1)S(1)}, s16[400,128]{1,0:T(8,128)(2,1)S(1)}, u32[]{:S(2)}, u32[]{:S(2)}) collective-permute-start(s16[400,128]{1,0:T(8,128)(2,1)S(1)} %get-tuple-element.80.refs_0_), channel_id=1, source_target_pairs={{0,8},{4,12},{8,0},{12,4},{1,9},{5,13},{9,1},{13,5},{2,10},{6,14},... | collective-permute-start | bytes 307208 | tf_op jit(solution)/shard_map/ppermute | solution.py:588
  62.0 0.0 collective-permute-done.13.other
  62.0 0.8 add.5
  62.7 3.0 %collective-permute-start.14 = (s16[272,128]{1,0:T(8,128)(2,1)S(1)}, s16[272,128]{1,0:T(8,128)(2,1)S(1)}, u32[]{:S(2)}, u32[]{:S(2)}) collective-permute-start(s16[272,128]{1,0:T(8,128)(2,1)S(1)} %get-tuple-element.79.refs_0_), channel_id=1, source_target_pairs={{0,8},{4,12},{8,0},{12,4},{1,9},{5,13},{9,1},{13,5},{2,10},{6,14},... | collective-permute-start | bytes 208904 | tf_op jit(solution)/shard_map/ppermute | solution.py:588
  65.7 1.6 %collective-permute-done.15.refs_1_ = s16[400,128]{1,0:T(8,128)(2,1)S(1)} collective-permute-done((s16[400,128]{1,0:T(8,128)(2,1)S(1)}, s16[400,128]{1,0:T(8,128)(2,1)S(1)}, u32[]{:S(2)}, u32[]{:S(2)}) %collective-permute-start.15) | collective-permute-done | bytes 102432 | tf_op jit(solution)/shard_map/ppermute | solution.py:588
  67.3 4.2 %filters.4 = (s16[400,128]{1,0:T(8,128)(2,1)S(1)}, f32[8,128]{1,0:T(8,128)S(1)}) custom-call(s16[400,128]{1,0:T(8,128)(2,1)S(1)} %get-tuple-element.80.refs_0_, s16[400,128]{1,0:T(8,128)(2,1)S(1)} %collective-permute-done.15.refs_1_, f32[8,128]{1,0:T(8,128)S(1)} %get-tuple-element.81.refs_2_), custom_call_target="tpu_custom_call" | custom-call | flops 1024 | bytes 1024 | tf_op jit(solution)/shard_map/filters/pallas_call | solution.py:465
  71.5 0.2 collective-permute-start.17
  71.7 0.0 collective-permute-done.14.refs_1_
  71.7 3.4 %filters.5 = (s16[272,128]{1,0:T(8,128)(2,1)S(1)}, f32[8,128]{1,0:T(8,128)S(1)}) custom-call(s16[272,128]{1,0:T(8,128)(2,1)S(1)} %get-tuple-element.79.refs_0_, s16[272,128]{1,0:T(8,128)(2,1)S(1)} %collective-permute-done.14.refs_1_, f32[8,128]{1,0:T(8,128)S(1)} %get-tuple-element.82.refs_2_), custom_call_target="tpu_custom_call" | custom-call | flops 1024 | bytes 1024 | tf_op jit(solution)/shard_map/filters/pallas_call | solution.py:465
  75.1 2.0 %collective-permute-start.16 = (s16[272,128]{1,0:T(8,128)(2,1)S(1)}, s16[272,128]{1,0:T(8,128)(2,1)S(1)}, u32[]{:S(2)}, u32[]{:S(2)}) collective-permute-start(s16[272,128]{1,0:T(8,128)(2,1)S(1)} %get-tuple-element.83.refs_0_), channel_id=1, source_target_pairs={{0,4},{4,0},{8,12},{12,8},{1,5},{5,1},{9,13},{13,9},{2,6},{6,2},{1... | collective-permute-start | bytes 208904 | tf_op jit(solution)/shard_map/ppermute | solution.py:588
  77.1 0.0 collective-permute-done.17.refs_1_
  77.1 2.7 %energy.4 = (f32[64,256]{1,0:T(8,128)}, f32[64,2,64,64]{3,2,1,0:T(8,128)}, f32[8,128]{1,0:T(8,128)S(1)}) custom-call(bf16[24,64,512]{2,1,0:T(8,128)(2,1)S(1)} %get-tuple-element.84.merged, s16[400,128]{1,0:T(8,128)(2,1)S(1)} %get-tuple-element.85.refs_0_, ...), custom_call_target="tpu_custom_call", output_to_operand_aliasing={{0}: (3, {}), {1}: (4, {})} | custom-call | flops 1024 | bytes 1024 | tf_op jit(solution)/shard_map/energy/pallas_call | solution.py:540
  79.8 0.0 collective-permute-done.16.refs_1_
  79.8 2.7 %energy.5 = (f32[64,256]{1,0:T(8,128)}, f32[64,2,64,64]{3,2,1,0:T(8,128)}, f32[8,128]{1,0:T(8,128)}) custom-call(bf16[16,64,512]{2,1,0:T(8,128)(2,1)S(1)} %get-tuple-element.75.merged, s16[272,128]{1,0:T(8,128)(2,1)S(1)} %get-tuple-element.83.refs_0_, ...), custom_call_target="tpu_custom_call", output_to_operand_aliasing={{0}: (3, {}), {1}: (4, {})} | custom-call | flops 1024 | bytes 1024 | tf_op jit(solution)/shard_map/energy/pallas_call | solution.py:540
Async XLA Ops:
  4.9 3.2 %collective-permute-start = (bf16[24,16,512]{2,1,0:T(8,128)(2,1)S(1)}, bf16[24,16,512]{2,1,0:T(8,128)(2,1)S(1)}, u32[]{:S(2)}, u32[]{:S(2)}) collective-permute-start(bf16[24,16,512]{2,1,0:T(8,128)(2,1)S(1)} %get-tuple-element.49), channel_id=1, source_target_pairs={{0,1},{1,0},{2,3},{3,2},{4,5},{5,4},{6,7},{7,6},{8,9},{9,8},{10,11... | collective-permute-start | bytes 1179656 | tf_op jit(solution)/shard_map/ppermute | solution.py:588
  5.4 12.5 %collective-permute-start.4 = (bf16[24,16,512]{2,1,0:T(8,128)(2,1)S(1)}, bf16[24,16,512]{2,1,0:T(8,128)(2,1)S(1)}, u32[]{:S(2)}, u32[]{:S(2)}) collective-permute-start(bf16[24,16,512]{2,1,0:T(8,128)(2,1)S(1)} %get-tuple-element.55), channel_id=1, source_target_pairs={{0,2},{1,3},{2,0},{3,1},{4,6},{5,7},{6,4},{7,5},{8,10},{9,11},{10,... | collective-permute-start | bytes 1179656 | tf_op jit(solution)/shard_map/ppermute | solution.py:588
  8.0 17.9 %collective-permute-start.5 = (bf16[24,16,512]{2,1,0:T(8,128)(2,1)S(1)}, bf16[24,16,512]{2,1,0:T(8,128)(2,1)S(1)}, u32[]{:S(2)}, u32[]{:S(2)}) collective-permute-start(bf16[24,16,512]{2,1,0:T(8,128)(2,1)S(1)} %get-tuple-element.56), channel_id=1, source_target_pairs={{0,3},{1,2},{2,1},{3,0},{4,7},{5,6},{6,5},{7,4},{8,11},{9,10},{10,... | collective-permute-start | bytes 1179656 | tf_op jit(solution)/shard_map/ppermute | solution.py:588
  13.5 12.4 %collective-permute-start.6 = (bf16[24,16,512]{2,1,0:T(8,128)(2,1)S(1)}, bf16[24,16,512]{2,1,0:T(8,128)(2,1)S(1)}, u32[]{:S(2)}, u32[]{:S(2)}) collective-permute-start(bf16[24,16,512]{2,1,0:T(8,128)(2,1)S(1)} %get-tuple-element.58), channel_id=1, source_target_pairs={{0,1},{1,0},{2,3},{3,2},{4,5},{5,4},{6,7},{7,6},{8,9},{9,8},{10,11... | collective-permute-start | bytes 1179656 | tf_op jit(solution)/shard_map/ppermute | solution.py:588
  13.7 12.1 %collective-permute-start.1 = (bf16[16,16,512]{2,1,0:T(8,128)(2,1)S(1)}, bf16[16,16,512]{2,1,0:T(8,128)(2,1)S(1)}, u32[]{:S(2)}, u32[]{:S(2)}) collective-permute-start(bf16[16,16,512]{2,1,0:T(8,128)(2,1)S(1)} %get-tuple-element.51), channel_id=1, source_target_pairs={{0,1},{1,0},{2,3},{3,2},{4,5},{5,4},{6,7},{7,6},{8,9},{9,8},{10,11... | collective-permute-start | bytes 786440 | tf_op jit(solution)/shard_map/ppermute | solution.py:588
  14.1 31.5 %collective-permute-start.10 = (bf16[24,16,512]{2,1,0:T(8,128)(2,1)S(1)}, bf16[24,16,512]{2,1,0:T(8,128)(2,1)S(1)}, u32[]{:S(2)}, u32[]{:S(2)}) collective-permute-start(bf16[24,16,512]{2,1,0:T(8,128)(2,1)S(1)} %get-tuple-element.67), channel_id=1, source_target_pairs={{0,2},{1,3},{2,0},{3,1},{4,6},{5,7},{6,4},{7,5},{8,10},{9,11},{10,... | collective-permute-start | bytes 1179656 | tf_op jit(solution)/shard_map/ppermute | solution.py:588
  18.0 27.7 %collective-permute-start.11 = (bf16[24,16,512]{2,1,0:T(8,128)(2,1)S(1)}, bf16[24,16,512]{2,1,0:T(8,128)(2,1)S(1)}, u32[]{:S(2)}, u32[]{:S(2)}) collective-permute-start(bf16[24,16,512]{2,1,0:T(8,128)(2,1)S(1)} %get-tuple-element.68), channel_id=1, source_target_pairs={{0,3},{1,2},{2,1},{3,0},{4,7},{5,6},{6,5},{7,4},{8,11},{9,10},{10,... | collective-permute-start | bytes 1179656 | tf_op jit(solution)/shard_map/ppermute | solution.py:588
  27.0 5.5 %collective-permute-start.7 = (s16[400,128]{1,0:T(8,128)(2,1)S(1)}, s16[400,128]{1,0:T(8,128)(2,1)S(1)}, u32[]{:S(2)}, u32[]{:S(2)}) collective-permute-start(s16[400,128]{1,0:T(8,128)(2,1)S(1)} %get-tuple-element.61), channel_id=1, source_target_pairs={{0,4},{4,0},{8,12},{12,8},{1,5},{5,1},{9,13},{13,9},{2,6},{6,2},{1... | collective-permute-start | bytes 307208 | tf_op jit(solution)/shard_map/ppermute | solution.py:588
  28.8 27.4 %collective-permute-start.2 = (bf16[16,16,512]{2,1,0:T(8,128)(2,1)S(1)}, bf16[16,16,512]{2,1,0:T(8,128)(2,1)S(1)}, u32[]{:S(2)}, u32[]{:S(2)}) collective-permute-start(bf16[16,16,512]{2,1,0:T(8,128)(2,1)S(1)} %get-tuple-element.52), channel_id=1, source_target_pairs={{0,2},{1,3},{2,0},{3,1},{4,6},{5,7},{6,4},{7,5},{8,10},{9,11},{10,... | collective-permute-start | bytes 786440 | tf_op jit(solution)/shard_map/ppermute | solution.py:588
  30.3 25.9 %collective-permute-start.3 = (bf16[16,16,512]{2,1,0:T(8,128)(2,1)S(1)}, bf16[16,16,512]{2,1,0:T(8,128)(2,1)S(1)}, u32[]{:S(2)}, u32[]{:S(2)}) collective-permute-start(bf16[16,16,512]{2,1,0:T(8,128)(2,1)S(1)} %get-tuple-element.53), channel_id=1, source_target_pairs={{0,3},{1,2},{2,1},{3,0},{4,7},{5,6},{6,5},{7,4},{8,11},{9,10},{10,... | collective-permute-start | bytes 786440 | tf_op jit(solution)/shard_map/ppermute | solution.py:588
  33.5 7.9 %collective-permute-start.8 = (s16[400,128]{1,0:T(8,128)(2,1)S(1)}, s16[400,128]{1,0:T(8,128)(2,1)S(1)}, u32[]{:S(2)}, u32[]{:S(2)}) collective-permute-start(s16[400,128]{1,0:T(8,128)(2,1)S(1)} %get-tuple-element.63.refs_0_), channel_id=1, source_target_pairs={{0,8},{4,12},{8,0},{12,4},{1,9},{5,13},{9,1},{13,5},{2,10},{6,14},... | collective-permute-start | bytes 307208 | tf_op jit(solution)/shard_map/ppermute | solution.py:588
  47.0 5.3 %collective-permute-start.12 = (s16[400,128]{1,0:T(8,128)(2,1)S(1)}, s16[400,128]{1,0:T(8,128)(2,1)S(1)}, u32[]{:S(2)}, u32[]{:S(2)}) collective-permute-start(s16[400,128]{1,0:T(8,128)(2,1)S(1)} %get-tuple-element.71), channel_id=1, source_target_pairs={{0,4},{4,0},{8,12},{12,8},{1,5},{5,1},{9,13},{13,9},{2,6},{6,2},{1... | collective-permute-start | bytes 307208 | tf_op jit(solution)/shard_map/ppermute | solution.py:588
  47.8 5.6 %collective-permute-start.9 = (s16[400,128]{1,0:T(8,128)(2,1)S(1)}, s16[400,128]{1,0:T(8,128)(2,1)S(1)}, u32[]{:S(2)}, u32[]{:S(2)}) collective-permute-start(s16[400,128]{1,0:T(8,128)(2,1)S(1)} %get-tuple-element.65.refs_0_), channel_id=1, source_target_pairs={{0,4},{4,0},{8,12},{12,8},{1,5},{5,1},{9,13},{13,9},{2,6},{6,2},{1... | collective-permute-start | bytes 307208 | tf_op jit(solution)/shard_map/ppermute | solution.py:588
  57.1 4.8 %collective-permute-start.13 = (s16[272,128]{1,0:T(8,128)(2,1)S(1)}, s16[272,128]{1,0:T(8,128)(2,1)S(1)}, u32[]{:S(2)}, u32[]{:S(2)}) collective-permute-start(s16[272,128]{1,0:T(8,128)(2,1)S(1)} %get-tuple-element.77), channel_id=1, source_target_pairs={{0,4},{4,0},{8,12},{12,8},{1,5},{5,1},{9,13},{13,9},{2,6},{6,2},{1... | collective-permute-start | bytes 208904 | tf_op jit(solution)/shard_map/ppermute | solution.py:588
  58.6 8.8 %collective-permute-start.15 = (s16[400,128]{1,0:T(8,128)(2,1)S(1)}, s16[400,128]{1,0:T(8,128)(2,1)S(1)}, u32[]{:S(2)}, u32[]{:S(2)}) collective-permute-start(s16[400,128]{1,0:T(8,128)(2,1)S(1)} %get-tuple-element.80.refs_0_), channel_id=1, source_target_pairs={{0,8},{4,12},{8,0},{12,4},{1,9},{5,13},{9,1},{13,5},{2,10},{6,14},... | collective-permute-start | bytes 307208 | tf_op jit(solution)/shard_map/ppermute | solution.py:588
  62.7 9.0 %collective-permute-start.14 = (s16[272,128]{1,0:T(8,128)(2,1)S(1)}, s16[272,128]{1,0:T(8,128)(2,1)S(1)}, u32[]{:S(2)}, u32[]{:S(2)}) collective-permute-start(s16[272,128]{1,0:T(8,128)(2,1)S(1)} %get-tuple-element.79.refs_0_), channel_id=1, source_target_pairs={{0,8},{4,12},{8,0},{12,4},{1,9},{5,13},{9,1},{13,5},{2,10},{6,14},... | collective-permute-start | bytes 208904 | tf_op jit(solution)/shard_map/ppermute | solution.py:588
  71.5 5.5 %collective-permute-start.17 = (s16[400,128]{1,0:T(8,128)(2,1)S(1)}, s16[400,128]{1,0:T(8,128)(2,1)S(1)}, u32[]{:S(2)}, u32[]{:S(2)}) collective-permute-start(s16[400,128]{1,0:T(8,128)(2,1)S(1)} %get-tuple-element.85.refs_0_), channel_id=1, source_target_pairs={{0,4},{4,0},{8,12},{12,8},{1,5},{5,1},{9,13},{13,9},{2,6},{6,2},{1... | collective-permute-start | bytes 307208 | tf_op jit(solution)/shard_map/ppermute | solution.py:588
  75.1 4.7 %collective-permute-start.16 = (s16[272,128]{1,0:T(8,128)(2,1)S(1)}, s16[272,128]{1,0:T(8,128)(2,1)S(1)}, u32[]{:S(2)}, u32[]{:S(2)}) collective-permute-start(s16[272,128]{1,0:T(8,128)(2,1)S(1)} %get-tuple-element.83.refs_0_), channel_id=1, source_target_pairs={{0,4},{4,0},{8,12},{12,8},{1,5},{5,1},{9,13},{13,9},{2,6},{6,2},{1... | collective-permute-start | bytes 208904 | tf_op jit(solution)/shard_map/ppermute | solution.py:588

commit v8 on v7

--- a/solution.py
+++ b/solution.py
@@ -267,6 +267,11 @@
 def decode(values, codes):
     products = outer(scale_of(codes), len(values))
     return each(lambda v, p: unpack(v, p * F32(0.5 / TOP)), values, products)
+
+
+def spread(values, codes):
+    products = outer(scale_of(codes), len(values))
+    return each(lambda v, p: v * pack(p * F32(1 / TOP)), values, products)
 
 
 def to_short(x):
@@ -332,10 +337,8 @@
             s = s * F32(1.0 / blocks)
             top, bottom = s[:blocks], swap(s[blocks:])
             compact = jnp.where(low, top + bottom, top - bottom)
-            if direct and slot:
+            if direct:
                 coded.append(double(compact))
-            elif direct:
-                grams[0][i] = compact
             else:
                 grams[0][f] = pack(double(compact))
         if coded:
@@ -348,8 +351,7 @@
     blocks = here * peers
     if direct:
         rows = coded_rows(count // slots, blocks // 2)
-        shapes = [((count // slots, blocks, 2 * blocks), F32)]
-        shapes += [((rows, 2 * blocks), jnp.int16)] * (slots - 1)
+        shapes = [((rows, 2 * blocks), jnp.int16)] * slots
     else:
         shapes = [((count, blocks // 2, 2 * blocks), F32)]
     out = pl.pallas_call(
@@ -366,27 +368,6 @@
     return out[0], out[2:], out[1]
 
 
-def add_kernel(own, other, *refs):
-    out, token = refs[-2:]
-    token[...] = jnp.zeros_like(token)
-    number, blocks, _ = own.shape
-    received = decode(*read_coded(other, number, blocks // 2))
-    sums = [double(own[i] + received[i][0]) for i in range(number)]
-    write_coded(out, *encode(sums))
-
-
-def add(own, other, after):
-    return pl.pallas_call(
-        add_kernel,
-        in_specs=[whole_spec()] * 2 + [any_spec()] * len(after),
-        out_specs=[whole_spec()] * 2,
-        out_shape=[jax.ShapeDtypeStruct(other.shape, jnp.int16), TOKEN],
-        compiler_params=params(),
-        cost_estimate=light(),
-        name="add",
-    )(own, other, *after)
-
-
 def split(x):
     high = x.astype(BF16)
     return high, (x - high.astype(F32)).astype(BF16)
@@ -403,11 +384,11 @@
     eye = jnp.where(row == lane, F32(1), F32(0))
 
     if parts == 1:
-        both_halves = [unpack(ins[0][i]) for i in range(number)]
+        sums = [ins[0][i] for i in range(number)]
     else:
-        one = decode(*read_coded(ins[0], number, half_rows))
-        two = decode(*read_coded(ins[1], number, half_rows))
-        both_halves = [(p[0] + q[0], p[1] + q[1]) for p, q in zip(one, two)]
+        found = [spread(*read_coded(r, number, half_rows)) for r in ins]
+        sums = [(o + a) + (b + c) for o, a, b, c in zip(*found)]
+    both_halves = each(unpack, sums)
     grams = [h[0] for h in both_halves]
     shift = each(lambda g: jnp.sum(g * eye, keepdims=True) * F32(1.0 / half), grams)
     eye_low = jnp.where(row + half == lane, F32(1), F32(0))
@@ -576,10 +557,10 @@
     return SIZES, ORDER
 
 
-SIZES = [24, 24, 16]
+SIZES = [16, 24, 24]
 ORDER = (
-    ("T", 0), ("T", 1), ("G", 0), ("A", 0), ("F", 0), ("G", 1), ("A", 1), ("E", 0),
-    ("G", 2), ("A", 2), ("F", 1), ("F", 2), ("E", 1), ("E", 2),
+    ("T", 0), ("T", 1), ("G", 0), ("T", 2), ("F", 0), ("G", 1), ("E", 0), ("F", 1),
+    ("G", 2), ("E", 1), ("F", 2), ("E", 2),
 )
 
 
@@ -603,34 +584,26 @@
 
     def do_transform(c):
         nonlocal token
-        chunks = [0] if c == 0 else range(1, len(sizes))
-        out, done = transform(
-            snapshots, weight, freq_index, peers, [(starts[k], sizes[k]) for k in chunks], token
+        (out,), done = transform(
+            snapshots, weight, freq_index, peers, [(starts[c], sizes[c])], token
         )
-        token = [done]
-        for k, pieces_out in zip(chunks, out):
-            sent[k] = [pieces_out[0]] + [
-                permute(pieces_out[offset], "tm", offset) for offset in range(1, peers)
-            ]
-        if c == 0 and len(sizes) > 1:
-            token.append(sent[0][1])
+        sent[c] = [out[0]] + [permute(out[offset], "tm", offset) for offset in range(1, peers)]
+        token = [done, sent[c][1]] if c == 0 and len(sizes) > 1 else [done]
 
     def do_gram(c):
         nonlocal token
-        if c == 0:
-            token += [sent[k][1] for k in range(1, len(sizes))]
         merged[c], grams[c], done = gram(sent[c], halves, paired, token)
         token = [done]
         if paired:
-            grams[c] = [grams[c][0], permute(grams[c][1], "space", 1)]
+            own, other = grams[c]
+            parts[c] = [
+                own,
+                permute(own, "space", 2),
+                permute(other, "space", 1),
+                permute(other, "space", 3),
+            ]
         else:
             parts[c] = [lax.psum_scatter(grams[c][0], "space", scatter_dimension=0, tiled=True)]
-
-    def do_add(c):
-        nonlocal token
-        half, done = add(*grams[c], token)
-        token = [done]
-        parts[c] = [half, permute(half, "space", 2)]
 
     def do_solve(c):
         nonlocal token
@@ -649,7 +622,7 @@
         )
         token = [done]
 
-    stages = {"T": do_transform, "G": do_gram, "A": do_add, "F": do_solve, "E": do_energy}
+    stages = {"T": do_transform, "G": do_gram, "F": do_solve, "E": do_energy}
     for stage, c in order:
         stages[stage](c)
     return (carry[0], carry[1])

time: 82.9 us -> 88.6 us (1.069)
  waiting for transfers between devices: 21.4 us -> 27.8 us
  starting transfers between devices: 24.6 us -> 22.5 us
  Pallas kernels: 35.8 us -> 37.1 us
    ppermute x18 -> x21, waiting for transfers between devices: 21.4 us -> 27.8 us  [permute(): return lax.ppermute(x, axis, pairs)]
    pallas_call x3 -> x0, Pallas kernels: 2.66 us -> none  [add(): pl.pallas_call(add_kernel, in_specs=[whole_spec()] * 2 + [any_spec()] * l...]
    pallas_call x2 -> x3, Pallas kernels: 9.72 us -> 12.3 us  [transform(): pl.pallas_call(functools.partial(transform_kernel, peers, parts, group),...]
    ppermute x18 -> x21, starting transfers between devices: 24.6 us -> 22.5 us  [permute(): return lax.ppermute(x, axis, pairs)]
    pallas_call x3, Pallas kernels: 3.46 us -> 4.79 us  [gram(): pl.pallas_call(functools.partial(gram_kernel, peers, slots, direct, len(a...]
  transfers between devices with their start and end apart: 18 -> 21, of which waited for: 7 -> 8; matrix products, arithmetic and copies ran while one was open for 0% -> 0% of each run, Pallas kernels for 34% -> 29%
where the time goes in v8:
time: 88.6 us; the launch traced here: 88.4 us
  Pallas kernels  37.1 us (42%)
  waiting for transfers between devices  27.8 us (31%)
  starting transfers between devices  22.5 us (25%)
  between operations  0.94 us (1%)
    ppermute x21, waiting for transfers between devices, permute(): return lax.ppermute(x, axis, pairs)  27.8 us
    ppermute x21, starting transfers between devices, permute(): return lax.ppermute(x, axis, pairs)  22.5 us
    pallas_call x3, Pallas kernels, transform(): pl.pallas_call(functools.partial(transform_kernel, peers, parts, group),...  12.3 us
    pallas_call x3, Pallas kernels, solve(): pl.pallas_call(functools.partial(solve_kernel, len(parts), number, half_r...  12 us
    pallas_call x3, Pallas kernels, filtered(): pl.pallas_call(functools.partial(energy_kernel, slots, direct, len(pieces...  8.09 us
    pallas_call x3, Pallas kernels, gram(): pl.pallas_call(functools.partial(gram_kernel, peers, slots, direct, len(a...  4.79 us
  transfers between devices with their start and end apart: 21, of which 8 were waited for; matrix products, arithmetic and copies ran while one was open for 0% of the time, Pallas kernels for 29%

profile of v8, /device:TPU:0, one launch (start us, length us, event | category | flops | bytes accessed | tf_op | source)
XLA Modules:
  0.0 88.4 jit_solution(8070141875157760062)
XLA Ops:
  0.6 3.7 %transform.3 = (bf16[16,16,512]{2,1,0:T(8,128)(2,1)S(1)}, bf16[16,16,512]{2,1,0:T(8,128)(2,1)S(1)}, bf16[16,16,512]{2,1,0:T(8,128)(2,1)S(1)}, bf16[16,16,512]{2,1,0:T(8,128)(2,1)S(1)}, f32[8,128]{1,0:T(8,128)S(1)}) custom-call(s32[256]{0:T(256)} %refs_0_.5, f32[1,256]{1,0:T(1,128)} %bitcast.1, bf16[16,512,256]{2,1,0:T(8,128)(2,1)} %refs_2_.5), custom_call_target="tpu_custom_call" | custom-call | flops 1024 | bytes 1024 | tf_op jit(solution)/shard_map/transform/pallas_call | solution.py:149
  4.4 0.5 collective-permute-start
  4.9 2.6 %collective-permute-start.1 = (bf16[16,16,512]{2,1,0:T(8,128)(2,1)S(1)}, bf16[16,16,512]{2,1,0:T(8,128)(2,1)S(1)}, u32[]{:S(2)}, u32[]{:S(2)}) collective-permute-start(bf16[16,16,512]{2,1,0:T(8,128)(2,1)S(1)} %get-tuple-element.45), channel_id=1, source_target_pairs={{0,2},{1,3},{2,0},{3,1},{4,6},{5,7},{6,4},{7,5},{8,10},{9,11},{10,... | collective-permute-start | bytes 786440 | tf_op jit(solution)/shard_map/ppermute | solution.py:569
  7.4 0.1 collective-permute-start.2
  7.5 0.0 collective-permute-done.refs_4_.refs_1_
  7.5 4.3 %transform.4 = (bf16[24,16,512]{2,1,0:T(8,128)(2,1)S(1)}, bf16[24,16,512]{2,1,0:T(8,128)(2,1)S(1)}, bf16[24,16,512]{2,1,0:T(8,128)(2,1)S(1)}, bf16[24,16,512]{2,1,0:T(8,128)(2,1)S(1)}, f32[8,128]{1,0:T(8,128)S(1)}) custom-call(s32[256]{0:T(256)} %refs_0_.5, f32[1,256]{1,0:T(1,128)} %bitcast.2, bf16[16,512,256]{2,1,0:T(8,128)(2,1)} %refs_2_.5, ...), custom_call_target="tpu_custom_call" | custom-call | flops 1024 | bytes 1024 | tf_op jit(solution)/shard_map/transform/pallas_call | solution.py:149
  11.8 0.2 collective-permute-start.6
  12.0 1.9 %collective-permute-start.7 = (bf16[24,16,512]{2,1,0:T(8,128)(2,1)S(1)}, bf16[24,16,512]{2,1,0:T(8,128)(2,1)S(1)}, u32[]{:S(2)}, u32[]{:S(2)}) collective-permute-start(bf16[24,16,512]{2,1,0:T(8,128)(2,1)S(1)} %get-tuple-element.56), channel_id=1, source_target_pairs={{0,2},{1,3},{2,0},{3,1},{4,6},{5,7},{6,4},{7,5},{8,10},{9,11},{10,... | collective-permute-start | bytes 1179656 | tf_op jit(solution)/shard_map/ppermute | solution.py:569
  13.9 0.0 collective-permute-start.8
  13.9 0.7 collective-permute-done.1.refs_2_
  14.6 5.1 %collective-permute-done.2.refs_3_ = bf16[16,16,512]{2,1,0:T(8,128)(2,1)S(1)} collective-permute-done((bf16[16,16,512]{2,1,0:T(8,128)(2,1)S(1)}, bf16[16,16,512]{2,1,0:T(8,128)(2,1)S(1)}, u32[]{:S(2)}, u32[]{:S(2)}) %collective-permute-start.2) | collective-permute-done | bytes 262176 | tf_op jit(solution)/shard_map/ppermute | solution.py:569
  19.7 1.4 %gram.3 = (bf16[16,64,512]{2,1,0:T(8,128)(2,1)S(1)}, f32[8,128]{1,0:T(8,128)S(1)}, s16[272,128]{1,0:T(8,128)(2,1)S(1)}, s16[272,128]{1,0:T(8,128)(2,1)S(1)}) custom-call(bf16[16,16,512]{2,1,0:T(8,128)(2,1)S(1)} %get-tuple-element.43.refs_0_, bf16[16,16,512]{2,1,0:T(8,128)(2,1)S(1)} %collective-permute-done.refs_4_.refs_1_, ...), custom_call_target="tpu_custom_call" | custom-call | flops 1024 | bytes 1024 | tf_op jit(solution)/shard_map/gram/pallas_call | solution.py:357
  21.1 2.7 %collective-permute-start.9 = (s16[272,128]{1,0:T(8,128)(2,1)S(1)}, s16[272,128]{1,0:T(8,128)(2,1)S(1)}, u32[]{:S(2)}, u32[]{:S(2)}) collective-permute-start(s16[272,128]{1,0:T(8,128)(2,1)S(1)} %get-tuple-element.58.refs_0_), channel_id=1, source_target_pairs={{0,8},{4,12},{8,0},{12,4},{1,9},{5,13},{9,1},{13,5},{2,10},{6,14},... | collective-permute-start | bytes 208904 | tf_op jit(solution)/shard_map/ppermute | solution.py:569
  23.9 1.3 %collective-permute-start.11 = (s16[272,128]{1,0:T(8,128)(2,1)S(1)}, s16[272,128]{1,0:T(8,128)(2,1)S(1)}, u32[]{:S(2)}, u32[]{:S(2)}) collective-permute-start(s16[272,128]{1,0:T(8,128)(2,1)S(1)} %get-tuple-element.59), channel_id=1, source_target_pairs={{0,12},{4,8},{8,4},{12,0},{1,13},{5,9},{9,5},{13,1},{2,14},{6,10},... | collective-permute-start | bytes 208904 | tf_op jit(solution)/shard_map/ppermute | solution.py:569
  25.2 3.4 %collective-permute-done.9.refs_1_ = s16[272,128]{1,0:T(8,128)(2,1)S(1)} collective-permute-done((s16[272,128]{1,0:T(8,128)(2,1)S(1)}, s16[272,128]{1,0:T(8,128)(2,1)S(1)}, u32[]{:S(2)}, u32[]{:S(2)}) %collective-permute-start.9) | collective-permute-done | bytes 69664 | tf_op jit(solution)/shard_map/ppermute | solution.py:569
  28.6 2.0 %collective-permute-start.10 = (s16[272,128]{1,0:T(8,128)(2,1)S(1)}, s16[272,128]{1,0:T(8,128)(2,1)S(1)}, u32[]{:S(2)}, u32[]{:S(2)}) collective-permute-start(s16[272,128]{1,0:T(8,128)(2,1)S(1)} %get-tuple-element.59), channel_id=1, source_target_pairs={{0,4},{4,0},{8,12},{12,8},{1,5},{5,1},{9,13},{13,9},{2,6},{6,2},{1... | collective-permute-start | bytes 208904 | tf_op jit(solution)/shard_map/ppermute | solution.py:569
  30.7 4.3 %transform.5 = (bf16[24,16,512]{2,1,0:T(8,128)(2,1)S(1)}, bf16[24,16,512]{2,1,0:T(8,128)(2,1)S(1)}, bf16[24,16,512]{2,1,0:T(8,128)(2,1)S(1)}, bf16[24,16,512]{2,1,0:T(8,128)(2,1)S(1)}, f32[8,128]{1,0:T(8,128)S(1)}) custom-call(s32[256]{0:T(256)} %refs_0_.5, f32[1,256]{1,0:T(1,128)} %bitcast.3, bf16[16,512,256]{2,1,0:T(8,128)(2,1)} %refs_2_.5, ...), custom_call_target="tpu_custom_call" | custom-call | flops 1024 | bytes 1024 | tf_op jit(solution)/shard_map/transform/pallas_call | solution.py:149
  35.0 0.0 collective-permute-done.11.refs_3_
  35.0 0.1 collective-permute-start.3
  35.0 0.0 collective-permute-done.10.refs_2_
  35.1 1.6 %collective-permute-start.4 = (bf16[24,16,512]{2,1,0:T(8,128)(2,1)S(1)}, bf16[24,16,512]{2,1,0:T(8,128)(2,1)S(1)}, u32[]{:S(2)}, u32[]{:S(2)}) collective-permute-start(bf16[24,16,512]{2,1,0:T(8,128)(2,1)S(1)} %get-tuple-element.52), channel_id=1, source_target_pairs={{0,2},{1,3},{2,0},{3,1},{4,6},{5,7},{6,4},{7,5},{8,10},{9,11},{10,... | collective-permute-start | bytes 1179656 | tf_op jit(solution)/shard_map/ppermute | solution.py:569
  36.6 0.0 collective-permute-done.6.refs_1_
  36.6 0.3 collective-permute-start.5
  36.9 3.5 %filters.3 = (s16[272,128]{1,0:T(8,128)(2,1)S(1)}, f32[8,128]{1,0:T(8,128)S(1)}) custom-call(s16[272,128]{1,0:T(8,128)(2,1)S(1)} %get-tuple-element.58.refs_0_, s16[272,128]{1,0:T(8,128)(2,1)S(1)} %collective-permute-done.9.refs_1_, s16[272,128]{1,0:T(8,128)(2,1)S(1)} %collective-permute-done.10.refs_2_, ...), custom_call_target="tpu_custom_call" | custom-call | flops 1024 | bytes 1024 | tf_op jit(solution)/shard_map/filters/pallas_call | solution.py:446
  40.4 0.0 collective-permute-done.7.refs_2_
  40.4 0.0 collective-permute-done.8.refs_3_
  40.4 1.7 %gram.4 = (bf16[24,64,512]{2,1,0:T(8,128)(2,1)S(1)}, f32[8,128]{1,0:T(8,128)S(1)}, s16[400,128]{1,0:T(8,128)(2,1)S(1)}, s16[400,128]{1,0:T(8,128)(2,1)S(1)}) custom-call(bf16[24,16,512]{2,1,0:T(8,128)(2,1)S(1)} %get-tuple-element.54.refs_0_, bf16[24,16,512]{2,1,0:T(8,128)(2,1)S(1)} %collective-permute-done.6.refs_1_, ...), custom_call_target="tpu_custom_call" | custom-call | flops 1024 | bytes 1024 | tf_op jit(solution)/shard_map/gram/pallas_call | solution.py:357
  42.1 3.4 %collective-permute-start.12 = (s16[400,128]{1,0:T(8,128)(2,1)S(1)}, s16[400,128]{1,0:T(8,128)(2,1)S(1)}, u32[]{:S(2)}, u32[]{:S(2)}) collective-permute-start(s16[400,128]{1,0:T(8,128)(2,1)S(1)} %get-tuple-element.62.refs_0_), channel_id=1, source_target_pairs={{0,8},{4,12},{8,0},{12,4},{1,9},{5,13},{9,1},{13,5},{2,10},{6,14},... | collective-permute-start | bytes 307208 | tf_op jit(solution)/shard_map/ppermute | solution.py:569
  45.6 0.0 collective-permute-start.15
  45.6 6.2 %collective-permute-done.15.refs_1_ = s16[272,128]{1,0:T(8,128)(2,1)S(1)} collective-permute-done((s16[272,128]{1,0:T(8,128)(2,1)S(1)}, s16[272,128]{1,0:T(8,128)(2,1)S(1)}, u32[]{:S(2)}, u32[]{:S(2)}) %collective-permute-start.15) | collective-permute-done | bytes 69664 | tf_op jit(solution)/shard_map/ppermute | solution.py:569
  51.8 0.0 collective-permute-start.14
  51.8 0.0 collective-permute-done.12.refs_1_
  51.8 0.4 collective-permute-start.13
  52.3 2.1 %energy.3 = (f32[64,256]{1,0:T(8,128)}, f32[64,2,64,64]{3,2,1,0:T(8,128)}, f32[8,128]{1,0:T(8,128)S(1)}) custom-call(bf16[16,64,512]{2,1,0:T(8,128)(2,1)S(1)} %get-tuple-element.64.merged, s16[272,128]{1,0:T(8,128)(2,1)S(1)} %get-tuple-element.65.refs_0_, s16[272,128]{1,0:T(8,128)(2,1)S(1)} %collective-permute-done.15.refs_1_, ...), custom_call_target="tpu_custom_call" | custom-call | flops 1024 | bytes 1024 | tf_op jit(solution)/shard_map/energy/pallas_call | solution.py:521
  54.4 4.9 %collective-permute-done.14.refs_3_ = s16[400,128]{1,0:T(8,128)(2,1)S(1)} collective-permute-done((s16[400,128]{1,0:T(8,128)(2,1)S(1)}, s16[400,128]{1,0:T(8,128)(2,1)S(1)}, u32[]{:S(2)}, u32[]{:S(2)}) %collective-permute-start.14) | collective-permute-done | bytes 102432 | tf_op jit(solution)/shard_map/ppermute | solution.py:569
  59.3 0.0 collective-permute-done.13.refs_2_
  59.3 4.2 %filters.4 = (s16[400,128]{1,0:T(8,128)(2,1)S(1)}, f32[8,128]{1,0:T(8,128)S(1)}) custom-call(s16[400,128]{1,0:T(8,128)(2,1)S(1)} %get-tuple-element.62.refs_0_, s16[400,128]{1,0:T(8,128)(2,1)S(1)} %collective-permute-done.12.refs_1_, s16[400,128]{1,0:T(8,128)(2,1)S(1)} %collective-permute-done.13.refs_2_, ...), custom_call_target="tpu_custom_call" | custom-call | flops 1024 | bytes 1024 | tf_op jit(solution)/shard_map/filters/pallas_call | solution.py:446
  63.6 0.1 collective-permute-start.19
  63.6 0.0 collective-permute-done.3.refs_1_
  63.6 0.0 collective-permute-done.4.refs_2_
  63.7 0.0 collective-permute-done.5.refs_3_
  63.7 1.7 %gram.5 = (bf16[24,64,512]{2,1,0:T(8,128)(2,1)S(1)}, f32[8,128]{1,0:T(8,128)S(1)}, s16[400,128]{1,0:T(8,128)(2,1)S(1)}, s16[400,128]{1,0:T(8,128)(2,1)S(1)}) custom-call(bf16[24,16,512]{2,1,0:T(8,128)(2,1)S(1)} %get-tuple-element.50.refs_0_, bf16[24,16,512]{2,1,0:T(8,128)(2,1)S(1)} %collective-permute-done.3.refs_1_, ...), custom_call_target="tpu_custom_call" | custom-call | flops 1024 | bytes 1024 | tf_op jit(solution)/shard_map/gram/pallas_call | solution.py:357
  65.4 2.0 %collective-permute-start.16 = (s16[400,128]{1,0:T(8,128)(2,1)S(1)}, s16[400,128]{1,0:T(8,128)(2,1)S(1)}, u32[]{:S(2)}, u32[]{:S(2)}) collective-permute-start(s16[400,128]{1,0:T(8,128)(2,1)S(1)} %get-tuple-element.70.refs_0_), channel_id=1, source_target_pairs={{0,8},{4,12},{8,0},{12,4},{1,9},{5,13},{9,1},{13,5},{2,10},{6,14},... | collective-permute-start | bytes 307208 | tf_op jit(solution)/shard_map/ppermute | solution.py:569
  67.4 2.4 %collective-permute-start.18 = (s16[400,128]{1,0:T(8,128)(2,1)S(1)}, s16[400,128]{1,0:T(8,128)(2,1)S(1)}, u32[]{:S(2)}, u32[]{:S(2)}) collective-permute-start(s16[400,128]{1,0:T(8,128)(2,1)S(1)} %get-tuple-element.71), channel_id=1, source_target_pairs={{0,12},{4,8},{8,4},{12,0},{1,13},{5,9},{9,5},{13,1},{2,14},{6,10},... | collective-permute-start | bytes 307208 | tf_op jit(solution)/shard_map/ppermute | solution.py:569
  69.8 0.0 collective-permute-start.17
  69.8 0.0 collective-permute-done.19.refs_1_
  69.8 2.7 %energy.4 = (f32[64,256]{1,0:T(8,128)}, f32[64,2,64,64]{3,2,1,0:T(8,128)}, f32[8,128]{1,0:T(8,128)S(1)}) custom-call(bf16[24,64,512]{2,1,0:T(8,128)(2,1)S(1)} %get-tuple-element.72.merged, s16[400,128]{1,0:T(8,128)(2,1)S(1)} %get-tuple-element.73.refs_0_, ...), custom_call_target="tpu_custom_call", output_to_operand_aliasing={{0}: (3, {}), {1}: (4, {})} | custom-call | flops 1024 | bytes 1024 | tf_op jit(solution)/shard_map/energy/pallas_call | solution.py:521
  72.5 2.6 %collective-permute-done.16.refs_1_ = s16[400,128]{1,0:T(8,128)(2,1)S(1)} collective-permute-done((s16[400,128]{1,0:T(8,128)(2,1)S(1)}, s16[400,128]{1,0:T(8,128)(2,1)S(1)}, u32[]{:S(2)}, u32[]{:S(2)}) %collective-permute-start.16) | collective-permute-done | bytes 102432 | tf_op jit(solution)/shard_map/ppermute | solution.py:569
  75.1 0.0 collective-permute-done.18.refs_3_
  75.1 0.9 collective-permute-done.17.refs_2_
  76.0 4.2 %filters.5 = (s16[400,128]{1,0:T(8,128)(2,1)S(1)}, f32[8,128]{1,0:T(8,128)S(1)}) custom-call(s16[400,128]{1,0:T(8,128)(2,1)S(1)} %get-tuple-element.70.refs_0_, s16[400,128]{1,0:T(8,128)(2,1)S(1)} %collective-permute-done.16.refs_1_, s16[400,128]{1,0:T(8,128)(2,1)S(1)} %collective-permute-done.17.refs_2_, ...), custom_call_target="tpu_custom_call" | custom-call | flops 1024 | bytes 1024 | tf_op jit(solution)/shard_map/filters/pallas_call | solution.py:446
  80.2 0.8 collective-permute-start.20
  81.0 3.9 %collective-permute-done.20.refs_1_ = s16[400,128]{1,0:T(8,128)(2,1)S(1)} collective-permute-done((s16[400,128]{1,0:T(8,128)(2,1)S(1)}, s16[400,128]{1,0:T(8,128)(2,1)S(1)}, u32[]{:S(2)}, u32[]{:S(2)}) %collective-permute-start.20) | collective-permute-done | bytes 102432 | tf_op jit(solution)/shard_map/ppermute | solution.py:569
  85.0 3.3 %energy.5 = (f32[64,256]{1,0:T(8,128)}, f32[64,2,64,64]{3,2,1,0:T(8,128)}, f32[8,128]{1,0:T(8,128)}) custom-call(bf16[24,64,512]{2,1,0:T(8,128)(2,1)S(1)} %get-tuple-element.69.merged, s16[400,128]{1,0:T(8,128)(2,1)S(1)} %get-tuple-element.78.refs_0_, ...), custom_call_target="tpu_custom_call", output_to_operand_aliasing={{0}: (3, {}), {1}: (4, {})} | custom-call | flops 1024 | bytes 1024 | tf_op jit(solution)/shard_map/energy/pallas_call | solution.py:521
Async XLA Ops:
  4.4 3.2 %collective-permute-start = (bf16[16,16,512]{2,1,0:T(8,128)(2,1)S(1)}, bf16[16,16,512]{2,1,0:T(8,128)(2,1)S(1)}, u32[]{:S(2)}, u32[]{:S(2)}) collective-permute-start(bf16[16,16,512]{2,1,0:T(8,128)(2,1)S(1)} %get-tuple-element.44), channel_id=1, source_target_pairs={{0,1},{1,0},{2,3},{3,2},{4,5},{5,4},{6,7},{7,6},{8,9},{9,8},{10,11... | collective-permute-start | bytes 786440 | tf_op jit(solution)/shard_map/ppermute | solution.py:569
  4.9 9.7 %collective-permute-start.1 = (bf16[16,16,512]{2,1,0:T(8,128)(2,1)S(1)}, bf16[16,16,512]{2,1,0:T(8,128)(2,1)S(1)}, u32[]{:S(2)}, u32[]{:S(2)}) collective-permute-start(bf16[16,16,512]{2,1,0:T(8,128)(2,1)S(1)} %get-tuple-element.45), channel_id=1, source_target_pairs={{0,2},{1,3},{2,0},{3,1},{4,6},{5,7},{6,4},{7,5},{8,10},{9,11},{10,... | collective-permute-start | bytes 786440 | tf_op jit(solution)/shard_map/ppermute | solution.py:569
  7.4 12.3 %collective-permute-start.2 = (bf16[16,16,512]{2,1,0:T(8,128)(2,1)S(1)}, bf16[16,16,512]{2,1,0:T(8,128)(2,1)S(1)}, u32[]{:S(2)}, u32[]{:S(2)}) collective-permute-start(bf16[16,16,512]{2,1,0:T(8,128)(2,1)S(1)} %get-tuple-element.46), channel_id=1, source_target_pairs={{0,3},{1,2},{2,1},{3,0},{4,7},{5,6},{6,5},{7,4},{8,11},{9,10},{10,... | collective-permute-start | bytes 786440 | tf_op jit(solution)/shard_map/ppermute | solution.py:569
  11.8 24.8 %collective-permute-start.6 = (bf16[24,16,512]{2,1,0:T(8,128)(2,1)S(1)}, bf16[24,16,512]{2,1,0:T(8,128)(2,1)S(1)}, u32[]{:S(2)}, u32[]{:S(2)}) collective-permute-start(bf16[24,16,512]{2,1,0:T(8,128)(2,1)S(1)} %get-tuple-element.55), channel_id=1, source_target_pairs={{0,1},{1,0},{2,3},{3,2},{4,5},{5,4},{6,7},{7,6},{8,9},{9,8},{10,11... | collective-permute-start | bytes 1179656 | tf_op jit(solution)/shard_map/ppermute | solution.py:569
  12.0 28.4 %collective-permute-start.7 = (bf16[24,16,512]{2,1,0:T(8,128)(2,1)S(1)}, bf16[24,16,512]{2,1,0:T(8,128)(2,1)S(1)}, u32[]{:S(2)}, u32[]{:S(2)}) collective-permute-start(bf16[24,16,512]{2,1,0:T(8,128)(2,1)S(1)} %get-tuple-element.56), channel_id=1, source_target_pairs={{0,2},{1,3},{2,0},{3,1},{4,6},{5,7},{6,4},{7,5},{8,10},{9,11},{10,... | collective-permute-start | bytes 1179656 | tf_op jit(solution)/shard_map/ppermute | solution.py:569
  13.9 26.5 %collective-permute-start.8 = (bf16[24,16,512]{2,1,0:T(8,128)(2,1)S(1)}, bf16[24,16,512]{2,1,0:T(8,128)(2,1)S(1)}, u32[]{:S(2)}, u32[]{:S(2)}) collective-permute-start(bf16[24,16,512]{2,1,0:T(8,128)(2,1)S(1)} %get-tuple-element.57), channel_id=1, source_target_pairs={{0,3},{1,2},{2,1},{3,0},{4,7},{5,6},{6,5},{7,4},{8,11},{9,10},{10,... | collective-permute-start | bytes 1179656 | tf_op jit(solution)/shard_map/ppermute | solution.py:569
  21.1 7.5 %collective-permute-start.9 = (s16[272,128]{1,0:T(8,128)(2,1)S(1)}, s16[272,128]{1,0:T(8,128)(2,1)S(1)}, u32[]{:S(2)}, u32[]{:S(2)}) collective-permute-start(s16[272,128]{1,0:T(8,128)(2,1)S(1)} %get-tuple-element.58.refs_0_), channel_id=1, source_target_pairs={{0,8},{4,12},{8,0},{12,4},{1,9},{5,13},{9,1},{13,5},{2,10},{6,14},... | collective-permute-start | bytes 208904 | tf_op jit(solution)/shard_map/ppermute | solution.py:569
  23.9 11.1 %collective-permute-start.11 = (s16[272,128]{1,0:T(8,128)(2,1)S(1)}, s16[272,128]{1,0:T(8,128)(2,1)S(1)}, u32[]{:S(2)}, u32[]{:S(2)}) collective-permute-start(s16[272,128]{1,0:T(8,128)(2,1)S(1)} %get-tuple-element.59), channel_id=1, source_target_pairs={{0,12},{4,8},{8,4},{12,0},{1,13},{5,9},{9,5},{13,1},{2,14},{6,10},... | collective-permute-start | bytes 208904 | tf_op jit(solution)/shard_map/ppermute | solution.py:569
  28.6 6.4 %collective-permute-start.10 = (s16[272,128]{1,0:T(8,128)(2,1)S(1)}, s16[272,128]{1,0:T(8,128)(2,1)S(1)}, u32[]{:S(2)}, u32[]{:S(2)}) collective-permute-start(s16[272,128]{1,0:T(8,128)(2,1)S(1)} %get-tuple-element.59), channel_id=1, source_target_pairs={{0,4},{4,0},{8,12},{12,8},{1,5},{5,1},{9,13},{13,9},{2,6},{6,2},{1... | collective-permute-start | bytes 208904 | tf_op jit(solution)/shard_map/ppermute | solution.py:569
  35.0 28.7 %collective-permute-start.3 = (bf16[24,16,512]{2,1,0:T(8,128)(2,1)S(1)}, bf16[24,16,512]{2,1,0:T(8,128)(2,1)S(1)}, u32[]{:S(2)}, u32[]{:S(2)}) collective-permute-start(bf16[24,16,512]{2,1,0:T(8,128)(2,1)S(1)} %get-tuple-element.51), channel_id=1, source_target_pairs={{0,1},{1,0},{2,3},{3,2},{4,5},{5,4},{6,7},{7,6},{8,9},{9,8},{10,11... | collective-permute-start | bytes 1179656 | tf_op jit(solution)/shard_map/ppermute | solution.py:569
  35.1 28.6 %collective-permute-start.4 = (bf16[24,16,512]{2,1,0:T(8,128)(2,1)S(1)}, bf16[24,16,512]{2,1,0:T(8,128)(2,1)S(1)}, u32[]{:S(2)}, u32[]{:S(2)}) collective-permute-start(bf16[24,16,512]{2,1,0:T(8,128)(2,1)S(1)} %get-tuple-element.52), channel_id=1, source_target_pairs={{0,2},{1,3},{2,0},{3,1},{4,6},{5,7},{6,4},{7,5},{8,10},{9,11},{10,... | collective-permute-start | bytes 1179656 | tf_op jit(solution)/shard_map/ppermute | solution.py:569
  36.6 27.0 %collective-permute-start.5 = (bf16[24,16,512]{2,1,0:T(8,128)(2,1)S(1)}, bf16[24,16,512]{2,1,0:T(8,128)(2,1)S(1)}, u32[]{:S(2)}, u32[]{:S(2)}) collective-permute-start(bf16[24,16,512]{2,1,0:T(8,128)(2,1)S(1)} %get-tuple-element.53), channel_id=1, source_target_pairs={{0,3},{1,2},{2,1},{3,0},{4,7},{5,6},{6,5},{7,4},{8,11},{9,10},{10,... | collective-permute-start | bytes 1179656 | tf_op jit(solution)/shard_map/ppermute | solution.py:569
  42.1 9.7 %collective-permute-start.12 = (s16[400,128]{1,0:T(8,128)(2,1)S(1)}, s16[400,128]{1,0:T(8,128)(2,1)S(1)}, u32[]{:S(2)}, u32[]{:S(2)}) collective-permute-start(s16[400,128]{1,0:T(8,128)(2,1)S(1)} %get-tuple-element.62.refs_0_), channel_id=1, source_target_pairs={{0,8},{4,12},{8,0},{12,4},{1,9},{5,13},{9,1},{13,5},{2,10},{6,14},... | collective-permute-start | bytes 307208 | tf_op jit(solution)/shard_map/ppermute | solution.py:569
  45.6 6.3 %collective-permute-start.15 = (s16[272,128]{1,0:T(8,128)(2,1)S(1)}, s16[272,128]{1,0:T(8,128)(2,1)S(1)}, u32[]{:S(2)}, u32[]{:S(2)}) collective-permute-start(s16[272,128]{1,0:T(8,128)(2,1)S(1)} %get-tuple-element.65.refs_0_), channel_id=1, source_target_pairs={{0,4},{4,0},{8,12},{12,8},{1,5},{5,1},{9,13},{13,9},{2,6},{6,2},{1... | collective-permute-start | bytes 208904 | tf_op jit(solution)/shard_map/ppermute | solution.py:569
  51.8 7.5 %collective-permute-start.14 = (s16[400,128]{1,0:T(8,128)(2,1)S(1)}, s16[400,128]{1,0:T(8,128)(2,1)S(1)}, u32[]{:S(2)}, u32[]{:S(2)}) collective-permute-start(s16[400,128]{1,0:T(8,128)(2,1)S(1)} %get-tuple-element.63), channel_id=1, source_target_pairs={{0,12},{4,8},{8,4},{12,0},{1,13},{5,9},{9,5},{13,1},{2,14},{6,10},... | collective-permute-start | bytes 307208 | tf_op jit(solution)/shard_map/ppermute | solution.py:569
  51.8 7.5 %collective-permute-start.13 = (s16[400,128]{1,0:T(8,128)(2,1)S(1)}, s16[400,128]{1,0:T(8,128)(2,1)S(1)}, u32[]{:S(2)}, u32[]{:S(2)}) collective-permute-start(s16[400,128]{1,0:T(8,128)(2,1)S(1)} %get-tuple-element.63), channel_id=1, source_target_pairs={{0,4},{4,0},{8,12},{12,8},{1,5},{5,1},{9,13},{13,9},{2,6},{6,2},{1... | collective-permute-start | bytes 307208 | tf_op jit(solution)/shard_map/ppermute | solution.py:569
  63.6 6.2 %collective-permute-start.19 = (s16[400,128]{1,0:T(8,128)(2,1)S(1)}, s16[400,128]{1,0:T(8,128)(2,1)S(1)}, u32[]{:S(2)}, u32[]{:S(2)}) collective-permute-start(s16[400,128]{1,0:T(8,128)(2,1)S(1)} %get-tuple-element.73.refs_0_), channel_id=1, source_target_pairs={{0,4},{4,0},{8,12},{12,8},{1,5},{5,1},{9,13},{13,9},{2,6},{6,2},{1... | collective-permute-start | bytes 307208 | tf_op jit(solution)/shard_map/ppermute | solution.py:569
  65.4 9.8 %collective-permute-start.16 = (s16[400,128]{1,0:T(8,128)(2,1)S(1)}, s16[400,128]{1,0:T(8,128)(2,1)S(1)}, u32[]{:S(2)}, u32[]{:S(2)}) collective-permute-start(s16[400,128]{1,0:T(8,128)(2,1)S(1)} %get-tuple-element.70.refs_0_), channel_id=1, source_target_pairs={{0,8},{4,12},{8,0},{12,4},{1,9},{5,13},{9,1},{13,5},{2,10},{6,14},... | collective-permute-start | bytes 307208 | tf_op jit(solution)/shard_map/ppermute | solution.py:569
  67.4 7.7 %collective-permute-start.18 = (s16[400,128]{1,0:T(8,128)(2,1)S(1)}, s16[400,128]{1,0:T(8,128)(2,1)S(1)}, u32[]{:S(2)}, u32[]{:S(2)}) collective-permute-start(s16[400,128]{1,0:T(8,128)(2,1)S(1)} %get-tuple-element.71), channel_id=1, source_target_pairs={{0,12},{4,8},{8,4},{12,0},{1,13},{5,9},{9,5},{13,1},{2,14},{6,10},... | collective-permute-start | bytes 307208 | tf_op jit(solution)/shard_map/ppermute | solution.py:569
  69.8 6.2 %collective-permute-start.17 = (s16[400,128]{1,0:T(8,128)(2,1)S(1)}, s16[400,128]{1,0:T(8,128)(2,1)S(1)}, u32[]{:S(2)}, u32[]{:S(2)}) collective-permute-start(s16[400,128]{1,0:T(8,128)(2,1)S(1)} %get-tuple-element.71), channel_id=1, source_target_pairs={{0,4},{4,0},{8,12},{12,8},{1,5},{5,1},{9,13},{13,9},{2,6},{6,2},{1... | collective-permute-start | bytes 307208 | tf_op jit(solution)/shard_map/ppermute | solution.py:569
  80.2 4.7 %collective-permute-start.20 = (s16[400,128]{1,0:T(8,128)(2,1)S(1)}, s16[400,128]{1,0:T(8,128)(2,1)S(1)}, u32[]{:S(2)}, u32[]{:S(2)}) collective-permute-start(s16[400,128]{1,0:T(8,128)(2,1)S(1)} %get-tuple-element.78.refs_0_), channel_id=1, source_target_pairs={{0,4},{4,0},{8,12},{12,8},{1,5},{5,1},{9,13},{13,9},{2,6},{6,2},{1... | collective-permute-start | bytes 307208 | tf_op jit(solution)/shard_map/ppermute | solution.py:569

commit v9 on v8

--- a/solution.py
+++ b/solution.py
@@ -394,7 +394,14 @@
     eye_low = jnp.where(row + half == lane, F32(1), F32(0))
     system = each(lambda g, m: g / m + eye, grams, shift)
     under = each(lambda h, m: h[1] / m + eye_low, both_halves, shift)
-    both = each(lambda a, u: split(jnp.concatenate([a, u], 0)), system, under)
+    both = each(
+        lambda a, u: jnp.concatenate(split(jnp.concatenate([a, u], 0)), 1), system, under
+    )
+
+    def times(v, a):
+        wide = dot(v, a)
+        return wide[:, :width] + wide[:, width:]
+
 
     low_end, high_end = 1.0, float(half + 1)
     mid, radius = (high_end + low_end) / 2, (high_end - low_end) / 2
@@ -402,7 +409,7 @@
     t = 2 * ratio * ratio - 1
     scale = 2.0 / (radius * radius * t)
     x = each(lambda a: (F32(scale) * (F32(2 * mid) * eye - a)).astype(BF16), system)
-    p = each(lambda v, a: eye - (dot(v, a[0]) + dot(v, a[1])), x, both)
+    p = each(lambda v, a: eye - times(v, a), x, both)
     x = each(lambda v: v.astype(F32), x)
     for _ in range(3):
         t_next = 2 * t * t - 1
@@ -417,7 +424,7 @@
         xb = each(lambda v: v.astype(BF16), x)
         xw = each(lambda v: v.astype(F32), xb)
         xf = each(lambda v: full(v).astype(BF16), xw)
-        residual = each(lambda v, a: eye - (dot(v, a[0]) + dot(v, a[1])), xb, both)
+        residual = each(lambda v, a: eye - times(v, a), xb, both)
         step = each(lambda r, v: dot(r.astype(BF16), v), residual, xf)
         factor = 1.0 if kind == "last" else 2 * t * t / (2 * t * t - 1)
         x = each(lambda v, m: F32(factor) * (v + m), xw, step)
@@ -427,8 +434,9 @@
     turned = each(
         lambda c: jnp.concatenate([c[0].astype(BF16), c[1].astype(BF16)], 0), filters
     )
-    split_g = each(split, grams)
-    moved = each(lambda g, c: dot(g[0], c) + dot(g[1], c), split_g, turned)
+    split_g = each(lambda g: jnp.concatenate(split(g), 0), grams)
+    moved = each(dot, split_g, turned)
+    moved = each(lambda m: m[:half] + m[half:], moved)
     energy = each(
         lambda c, h: jnp.sum(c.astype(F32) * h, keepdims=True) * F32(half), rounded, moved
     )
@@ -559,7 +567,7 @@
 
 SIZES = [16, 24, 24]
 ORDER = (
-    ("T", 0), ("T", 1), ("G", 0), ("T", 2), ("F", 0), ("G", 1), ("E", 0), ("F", 1),
+    ("T", 0), ("T", 1), ("T", 2), ("G", 0), ("F", 0), ("G", 1), ("E", 0), ("F", 1),
     ("G", 2), ("E", 1), ("F", 2), ("E", 2),
 )
 

time: 88.6 us -> 86.3 us (0.974)
  waiting for transfers between devices: 27.8 us -> 20.7 us
  starting transfers between devices: 22.5 us -> 27.7 us
    ppermute x21, waiting for transfers between devices: 27.8 us -> 20.7 us  [permute(): return lax.ppermute(x, axis, pairs)]
    ppermute x21, starting transfers between devices: 22.5 us -> 27.7 us  [permute(): return lax.ppermute(x, axis, pairs)]
  transfers between devices with their start and end apart: 21 -> 21, of which waited for: 8 -> 9; matrix products, arithmetic and copies ran while one was open for 0% -> 0% of each run, Pallas kernels for 29% -> 30%
where the time goes in v9:
time: 86.3 us; the launch traced here: 86.1 us
  Pallas kernels  36.9 us (43%)
  starting transfers between devices  27.7 us (32%)
  waiting for transfers between devices  20.7 us (24%)
  between operations  0.9 us (1%)
    ppermute x21, starting transfers between devices, permute(): return lax.ppermute(x, axis, pairs)  27.7 us
    ppermute x21, waiting for transfers between devices, permute(): return lax.ppermute(x, axis, pairs)  20.7 us
    pallas_call x3, Pallas kernels, transform(): pl.pallas_call(functools.partial(transform_kernel, peers, parts, group),...  12.3 us
    pallas_call x3, Pallas kernels, solve(): pl.pallas_call(functools.partial(solve_kernel, len(parts), number, half_r...  11.7 us
    pallas_call x3, Pallas kernels, filtered(): pl.pallas_call(functools.partial(energy_kernel, slots, direct, len(pieces...  8.09 us
    pallas_call x3, Pallas kernels, gram(): pl.pallas_call(functools.partial(gram_kernel, peers, slots, direct, len(a...  4.81 us
  transfers between devices with their start and end apart: 21, of which 9 were waited for; matrix products, arithmetic and copies ran while one was open for 0% of the time, Pallas kernels for 30%

profile of v9, /device:TPU:0, one launch (start us, length us, event | category | flops | bytes accessed | tf_op | source)
XLA Modules:
  0.0 86.1 jit_solution(11599643521605101345)
XLA Ops:
  0.6 3.7 %transform.3 = (bf16[16,16,512]{2,1,0:T(8,128)(2,1)S(1)}, bf16[16,16,512]{2,1,0:T(8,128)(2,1)S(1)}, bf16[16,16,512]{2,1,0:T(8,128)(2,1)S(1)}, bf16[16,16,512]{2,1,0:T(8,128)(2,1)S(1)}, f32[8,128]{1,0:T(8,128)S(1)}) custom-call(s32[256]{0:T(256)} %refs_0_.5, f32[1,256]{1,0:T(1,128)} %bitcast.1, bf16[16,512,256]{2,1,0:T(8,128)(2,1)} %refs_2_.5), custom_call_target="tpu_custom_call" | custom-call | flops 1024 | bytes 1024 | tf_op jit(solution)/shard_map/transform/pallas_call | solution.py:149
  4.4 0.5 collective-permute-start
  4.9 2.6 %collective-permute-start.7 = (bf16[16,16,512]{2,1,0:T(8,128)(2,1)S(1)}, bf16[16,16,512]{2,1,0:T(8,128)(2,1)S(1)}, u32[]{:S(2)}, u32[]{:S(2)}) collective-permute-start(bf16[16,16,512]{2,1,0:T(8,128)(2,1)S(1)} %get-tuple-element.55), channel_id=1, source_target_pairs={{0,2},{1,3},{2,0},{3,1},{4,6},{5,7},{6,4},{7,5},{8,10},{9,11},{10,... | collective-permute-start | bytes 786440 | tf_op jit(solution)/shard_map/ppermute | solution.py:577
  7.5 0.1 collective-permute-start.8
  7.5 0.0 collective-permute-done.refs_4_.refs_1_
  7.5 4.3 %transform.4 = (bf16[24,16,512]{2,1,0:T(8,128)(2,1)S(1)}, bf16[24,16,512]{2,1,0:T(8,128)(2,1)S(1)}, bf16[24,16,512]{2,1,0:T(8,128)(2,1)S(1)}, bf16[24,16,512]{2,1,0:T(8,128)(2,1)S(1)}, f32[8,128]{1,0:T(8,128)S(1)}) custom-call(s32[256]{0:T(256)} %refs_0_.5, f32[1,256]{1,0:T(1,128)} %bitcast.2, bf16[16,512,256]{2,1,0:T(8,128)(2,1)} %refs_2_.5, ...), custom_call_target="tpu_custom_call" | custom-call | flops 1024 | bytes 1024 | tf_op jit(solution)/shard_map/transform/pallas_call | solution.py:149
  11.8 0.2 collective-permute-start.4
  12.1 1.9 %collective-permute-start.5 = (bf16[24,16,512]{2,1,0:T(8,128)(2,1)S(1)}, bf16[24,16,512]{2,1,0:T(8,128)(2,1)S(1)}, u32[]{:S(2)}, u32[]{:S(2)}) collective-permute-start(bf16[24,16,512]{2,1,0:T(8,128)(2,1)S(1)} %get-tuple-element.52), channel_id=1, source_target_pairs={{0,2},{1,3},{2,0},{3,1},{4,6},{5,7},{6,4},{7,5},{8,10},{9,11},{10,... | collective-permute-start | bytes 1179656 | tf_op jit(solution)/shard_map/ppermute | solution.py:577
  14.0 0.0 collective-permute-start.6
  14.0 4.3 %transform.5 = (bf16[24,16,512]{2,1,0:T(8,128)(2,1)S(1)}, bf16[24,16,512]{2,1,0:T(8,128)(2,1)S(1)}, bf16[24,16,512]{2,1,0:T(8,128)(2,1)S(1)}, bf16[24,16,512]{2,1,0:T(8,128)(2,1)S(1)}, f32[8,128]{1,0:T(8,128)S(1)}) custom-call(s32[256]{0:T(256)} %refs_0_.5, f32[1,256]{1,0:T(1,128)} %bitcast.3, bf16[16,512,256]{2,1,0:T(8,128)(2,1)} %refs_2_.5, ...), custom_call_target="tpu_custom_call" | custom-call | flops 1024 | bytes 1024 | tf_op jit(solution)/shard_map/transform/pallas_call | solution.py:149
  18.3 0.0 collective-permute-done.7.refs_2_
  18.3 1.4 %collective-permute-done.8.refs_3_ = bf16[16,16,512]{2,1,0:T(8,128)(2,1)S(1)} collective-permute-done((bf16[16,16,512]{2,1,0:T(8,128)(2,1)S(1)}, bf16[16,16,512]{2,1,0:T(8,128)(2,1)S(1)}, u32[]{:S(2)}, u32[]{:S(2)}) %collective-permute-start.8) | collective-permute-done | bytes 262176 | tf_op jit(solution)/shard_map/ppermute | solution.py:577
  19.7 1.4 %gram.3 = (bf16[16,64,512]{2,1,0:T(8,128)(2,1)S(1)}, f32[8,128]{1,0:T(8,128)S(1)}, s16[272,128]{1,0:T(8,128)(2,1)S(1)}, s16[272,128]{1,0:T(8,128)(2,1)S(1)}) custom-call(bf16[16,16,512]{2,1,0:T(8,128)(2,1)S(1)} %get-tuple-element.54.refs_0_, bf16[16,16,512]{2,1,0:T(8,128)(2,1)S(1)} %collective-permute-done.refs_4_.refs_1_, ...), custom_call_target="tpu_custom_call" | custom-call | flops 1024 | bytes 1024 | tf_op jit(solution)/shard_map/gram/pallas_call | solution.py:357
  21.2 2.7 %collective-permute-start.9 = (s16[272,128]{1,0:T(8,128)(2,1)S(1)}, s16[272,128]{1,0:T(8,128)(2,1)S(1)}, u32[]{:S(2)}, u32[]{:S(2)}) collective-permute-start(s16[272,128]{1,0:T(8,128)(2,1)S(1)} %get-tuple-element.58.refs_0_), channel_id=1, source_target_pairs={{0,8},{4,12},{8,0},{12,4},{1,9},{5,13},{9,1},{13,5},{2,10},{6,14},... | collective-permute-start | bytes 208904 | tf_op jit(solution)/shard_map/ppermute | solution.py:577
  23.9 1.3 %collective-permute-start.11 = (s16[272,128]{1,0:T(8,128)(2,1)S(1)}, s16[272,128]{1,0:T(8,128)(2,1)S(1)}, u32[]{:S(2)}, u32[]{:S(2)}) collective-permute-start(s16[272,128]{1,0:T(8,128)(2,1)S(1)} %get-tuple-element.59), channel_id=1, source_target_pairs={{0,12},{4,8},{8,4},{12,0},{1,13},{5,9},{9,5},{13,1},{2,14},{6,10},... | collective-permute-start | bytes 208904 | tf_op jit(solution)/shard_map/ppermute | solution.py:577
  25.2 3.5 %collective-permute-done.9.refs_1_ = s16[272,128]{1,0:T(8,128)(2,1)S(1)} collective-permute-done((s16[272,128]{1,0:T(8,128)(2,1)S(1)}, s16[272,128]{1,0:T(8,128)(2,1)S(1)}, u32[]{:S(2)}, u32[]{:S(2)}) %collective-permute-start.9) | collective-permute-done | bytes 69664 | tf_op jit(solution)/shard_map/ppermute | solution.py:577
  28.7 2.0 %collective-permute-start.10 = (s16[272,128]{1,0:T(8,128)(2,1)S(1)}, s16[272,128]{1,0:T(8,128)(2,1)S(1)}, u32[]{:S(2)}, u32[]{:S(2)}) collective-permute-start(s16[272,128]{1,0:T(8,128)(2,1)S(1)} %get-tuple-element.59), channel_id=1, source_target_pairs={{0,4},{4,0},{8,12},{12,8},{1,5},{5,1},{9,13},{13,9},{2,6},{6,2},{1... | collective-permute-start | bytes 208904 | tf_op jit(solution)/shard_map/ppermute | solution.py:577
  30.7 0.0 collective-permute-done.11.refs_3_
  30.7 0.0 collective-permute-start.1
  30.7 2.4 %collective-permute-done.10.refs_2_ = s16[272,128]{1,0:T(8,128)(2,1)S(1)} collective-permute-done((s16[272,128]{1,0:T(8,128)(2,1)S(1)}, s16[272,128]{1,0:T(8,128)(2,1)S(1)}, u32[]{:S(2)}, u32[]{:S(2)}) %collective-permute-start.10) | collective-permute-done | bytes 69664 | tf_op jit(solution)/shard_map/ppermute | solution.py:577
  33.1 1.5 %collective-permute-start.2 = (bf16[24,16,512]{2,1,0:T(8,128)(2,1)S(1)}, bf16[24,16,512]{2,1,0:T(8,128)(2,1)S(1)}, u32[]{:S(2)}, u32[]{:S(2)}) collective-permute-start(bf16[24,16,512]{2,1,0:T(8,128)(2,1)S(1)} %get-tuple-element.48), channel_id=1, source_target_pairs={{0,2},{1,3},{2,0},{3,1},{4,6},{5,7},{6,4},{7,5},{8,10},{9,11},{10,... | collective-permute-start | bytes 1179656 | tf_op jit(solution)/shard_map/ppermute | solution.py:577
  34.6 0.0 collective-permute-done.4.refs_1_
  34.6 0.0 collective-permute-start.3
  34.6 3.5 %filters.3 = (s16[272,128]{1,0:T(8,128)(2,1)S(1)}, f32[8,128]{1,0:T(8,128)S(1)}) custom-call(s16[272,128]{1,0:T(8,128)(2,1)S(1)} %get-tuple-element.58.refs_0_, s16[272,128]{1,0:T(8,128)(2,1)S(1)} %collective-permute-done.9.refs_1_, s16[272,128]{1,0:T(8,128)(2,1)S(1)} %collective-permute-done.10.refs_2_, ...), custom_call_target="tpu_custom_call" | custom-call | flops 1024 | bytes 1024 | tf_op jit(solution)/shard_map/filters/pallas_call | solution.py:454
  38.1 0.0 collective-permute-done.5.refs_2_
  38.1 0.0 collective-permute-done.6.refs_3_
  38.1 1.7 %gram.4 = (bf16[24,64,512]{2,1,0:T(8,128)(2,1)S(1)}, f32[8,128]{1,0:T(8,128)S(1)}, s16[400,128]{1,0:T(8,128)(2,1)S(1)}, s16[400,128]{1,0:T(8,128)(2,1)S(1)}) custom-call(bf16[24,16,512]{2,1,0:T(8,128)(2,1)S(1)} %get-tuple-element.50.refs_0_, bf16[24,16,512]{2,1,0:T(8,128)(2,1)S(1)} %collective-permute-done.4.refs_1_, ...), custom_call_target="tpu_custom_call" | custom-call | flops 1024 | bytes 1024 | tf_op jit(solution)/shard_map/gram/pallas_call | solution.py:357
  39.8 3.6 %collective-permute-start.12 = (s16[400,128]{1,0:T(8,128)(2,1)S(1)}, s16[400,128]{1,0:T(8,128)(2,1)S(1)}, u32[]{:S(2)}, u32[]{:S(2)}) collective-permute-start(s16[400,128]{1,0:T(8,128)(2,1)S(1)} %get-tuple-element.62.refs_0_), channel_id=1, source_target_pairs={{0,8},{4,12},{8,0},{12,4},{1,9},{5,13},{9,1},{13,5},{2,10},{6,14},... | collective-permute-start | bytes 307208 | tf_op jit(solution)/shard_map/ppermute | solution.py:577
  43.4 1.9 %collective-permute-start.15 = (s16[272,128]{1,0:T(8,128)(2,1)S(1)}, s16[272,128]{1,0:T(8,128)(2,1)S(1)}, u32[]{:S(2)}, u32[]{:S(2)}) collective-permute-start(s16[272,128]{1,0:T(8,128)(2,1)S(1)} %get-tuple-element.65.refs_0_), channel_id=1, source_target_pairs={{0,4},{4,0},{8,12},{12,8},{1,5},{5,1},{9,13},{13,9},{2,6},{6,2},{1... | collective-permute-start | bytes 208904 | tf_op jit(solution)/shard_map/ppermute | solution.py:577
  45.3 2.7 %collective-permute-done.15.refs_1_ = s16[272,128]{1,0:T(8,128)(2,1)S(1)} collective-permute-done((s16[272,128]{1,0:T(8,128)(2,1)S(1)}, s16[272,128]{1,0:T(8,128)(2,1)S(1)}, u32[]{:S(2)}, u32[]{:S(2)}) %collective-permute-start.15) | collective-permute-done | bytes 69664 | tf_op jit(solution)/shard_map/ppermute | solution.py:577
  48.0 1.6 %collective-permute-start.14 = (s16[400,128]{1,0:T(8,128)(2,1)S(1)}, s16[400,128]{1,0:T(8,128)(2,1)S(1)}, u32[]{:S(2)}, u32[]{:S(2)}) collective-permute-start(s16[400,128]{1,0:T(8,128)(2,1)S(1)} %get-tuple-element.63), channel_id=1, source_target_pairs={{0,12},{4,8},{8,4},{12,0},{1,13},{5,9},{9,5},{13,1},{2,14},{6,10},... | collective-permute-start | bytes 307208 | tf_op jit(solution)/shard_map/ppermute | solution.py:577
  49.6 0.0 collective-permute-done.12.refs_1_
  49.6 1.5 %collective-permute-start.13 = (s16[400,128]{1,0:T(8,128)(2,1)S(1)}, s16[400,128]{1,0:T(8,128)(2,1)S(1)}, u32[]{:S(2)}, u32[]{:S(2)}) collective-permute-start(s16[400,128]{1,0:T(8,128)(2,1)S(1)} %get-tuple-element.63), channel_id=1, source_target_pairs={{0,4},{4,0},{8,12},{12,8},{1,5},{5,1},{9,13},{13,9},{2,6},{6,2},{1... | collective-permute-start | bytes 307208 | tf_op jit(solution)/shard_map/ppermute | solution.py:577
  51.1 2.1 %energy.3 = (f32[64,256]{1,0:T(8,128)}, f32[64,2,64,64]{3,2,1,0:T(8,128)}, f32[8,128]{1,0:T(8,128)S(1)}) custom-call(bf16[16,64,512]{2,1,0:T(8,128)(2,1)S(1)} %get-tuple-element.64.merged, s16[272,128]{1,0:T(8,128)(2,1)S(1)} %get-tuple-element.65.refs_0_, s16[272,128]{1,0:T(8,128)(2,1)S(1)} %collective-permute-done.15.refs_1_, ...), custom_call_target="tpu_custom_call" | custom-call | flops 1024 | bytes 1024 | tf_op jit(solution)/shard_map/energy/pallas_call | solution.py:529
  53.2 2.0 %collective-permute-done.14.refs_3_ = s16[400,128]{1,0:T(8,128)(2,1)S(1)} collective-permute-done((s16[400,128]{1,0:T(8,128)(2,1)S(1)}, s16[400,128]{1,0:T(8,128)(2,1)S(1)}, u32[]{:S(2)}, u32[]{:S(2)}) %collective-permute-start.14) | collective-permute-done | bytes 102432 | tf_op jit(solution)/shard_map/ppermute | solution.py:577
  55.2 1.1 %collective-permute-done.13.refs_2_ = s16[400,128]{1,0:T(8,128)(2,1)S(1)} collective-permute-done((s16[400,128]{1,0:T(8,128)(2,1)S(1)}, s16[400,128]{1,0:T(8,128)(2,1)S(1)}, u32[]{:S(2)}, u32[]{:S(2)}) %collective-permute-start.13) | collective-permute-done | bytes 102432 | tf_op jit(solution)/shard_map/ppermute | solution.py:577
  56.3 4.1 %filters.4 = (s16[400,128]{1,0:T(8,128)(2,1)S(1)}, f32[8,128]{1,0:T(8,128)S(1)}) custom-call(s16[400,128]{1,0:T(8,128)(2,1)S(1)} %get-tuple-element.62.refs_0_, s16[400,128]{1,0:T(8,128)(2,1)S(1)} %collective-permute-done.12.refs_1_, s16[400,128]{1,0:T(8,128)(2,1)S(1)} %collective-permute-done.13.refs_2_, ...), custom_call_target="tpu_custom_call" | custom-call | flops 1024 | bytes 1024 | tf_op jit(solution)/shard_map/filters/pallas_call | solution.py:454
  60.4 0.8 collective-permute-start.19
  61.2 0.0 collective-permute-done.1.refs_1_
  61.2 0.0 collective-permute-done.2.refs_2_
  61.2 0.0 collective-permute-done.3.refs_3_
  61.2 1.7 %gram.5 = (bf16[24,64,512]{2,1,0:T(8,128)(2,1)S(1)}, f32[8,128]{1,0:T(8,128)S(1)}, s16[400,128]{1,0:T(8,128)(2,1)S(1)}, s16[400,128]{1,0:T(8,128)(2,1)S(1)}) custom-call(bf16[24,16,512]{2,1,0:T(8,128)(2,1)S(1)} %get-tuple-element.46.refs_0_, bf16[24,16,512]{2,1,0:T(8,128)(2,1)S(1)} %collective-permute-done.1.refs_1_, ...), custom_call_target="tpu_custom_call" | custom-call | flops 1024 | bytes 1024 | tf_op jit(solution)/shard_map/gram/pallas_call | solution.py:357
  62.9 2.0 %collective-permute-start.16 = (s16[400,128]{1,0:T(8,128)(2,1)S(1)}, s16[400,128]{1,0:T(8,128)(2,1)S(1)}, u32[]{:S(2)}, u32[]{:S(2)}) collective-permute-start(s16[400,128]{1,0:T(8,128)(2,1)S(1)} %get-tuple-element.70.refs_0_), channel_id=1, source_target_pairs={{0,8},{4,12},{8,0},{12,4},{1,9},{5,13},{9,1},{13,5},{2,10},{6,14},... | collective-permute-start | bytes 307208 | tf_op jit(solution)/shard_map/ppermute | solution.py:577
  64.9 1.7 %collective-permute-start.18 = (s16[400,128]{1,0:T(8,128)(2,1)S(1)}, s16[400,128]{1,0:T(8,128)(2,1)S(1)}, u32[]{:S(2)}, u32[]{:S(2)}) collective-permute-start(s16[400,128]{1,0:T(8,128)(2,1)S(1)} %get-tuple-element.71), channel_id=1, source_target_pairs={{0,12},{4,8},{8,4},{12,0},{1,13},{5,9},{9,5},{13,1},{2,14},{6,10},... | collective-permute-start | bytes 307208 | tf_op jit(solution)/shard_map/ppermute | solution.py:577
  66.6 0.0 collective-permute-start.17
  66.6 0.0 collective-permute-done.19.refs_1_
  66.6 2.7 %energy.4 = (f32[64,256]{1,0:T(8,128)}, f32[64,2,64,64]{3,2,1,0:T(8,128)}, f32[8,128]{1,0:T(8,128)S(1)}) custom-call(bf16[24,64,512]{2,1,0:T(8,128)(2,1)S(1)} %get-tuple-element.72.merged, s16[400,128]{1,0:T(8,128)(2,1)S(1)} %get-tuple-element.73.refs_0_, ...), custom_call_target="tpu_custom_call", output_to_operand_aliasing={{0}: (3, {}), {1}: (4, {})} | custom-call | flops 1024 | bytes 1024 | tf_op jit(solution)/shard_map/energy/pallas_call | solution.py:529
  69.3 4.1 %collective-permute-done.16.refs_1_ = s16[400,128]{1,0:T(8,128)(2,1)S(1)} collective-permute-done((s16[400,128]{1,0:T(8,128)(2,1)S(1)}, s16[400,128]{1,0:T(8,128)(2,1)S(1)}, u32[]{:S(2)}, u32[]{:S(2)}) %collective-permute-start.16) | collective-permute-done | bytes 102432 | tf_op jit(solution)/shard_map/ppermute | solution.py:577
  73.4 0.0 collective-permute-done.18.refs_3_
  73.4 0.4 collective-permute-done.17.refs_2_
  73.9 4.1 %filters.5 = (s16[400,128]{1,0:T(8,128)(2,1)S(1)}, f32[8,128]{1,0:T(8,128)S(1)}) custom-call(s16[400,128]{1,0:T(8,128)(2,1)S(1)} %get-tuple-element.70.refs_0_, s16[400,128]{1,0:T(8,128)(2,1)S(1)} %collective-permute-done.16.refs_1_, s16[400,128]{1,0:T(8,128)(2,1)S(1)} %collective-permute-done.17.refs_2_, ...), custom_call_target="tpu_custom_call" | custom-call | flops 1024 | bytes 1024 | tf_op jit(solution)/shard_map/filters/pallas_call | solution.py:454
  78.0 1.7 %collective-permute-start.20 = (s16[400,128]{1,0:T(8,128)(2,1)S(1)}, s16[400,128]{1,0:T(8,128)(2,1)S(1)}, u32[]{:S(2)}, u32[]{:S(2)}) collective-permute-start(s16[400,128]{1,0:T(8,128)(2,1)S(1)} %get-tuple-element.78.refs_0_), channel_id=1, source_target_pairs={{0,4},{4,0},{8,12},{12,8},{1,5},{5,1},{9,13},{13,9},{2,6},{6,2},{1... | collective-permute-start | bytes 307208 | tf_op jit(solution)/shard_map/ppermute | solution.py:577
  79.7 3.0 %collective-permute-done.20.refs_1_ = s16[400,128]{1,0:T(8,128)(2,1)S(1)} collective-permute-done((s16[400,128]{1,0:T(8,128)(2,1)S(1)}, s16[400,128]{1,0:T(8,128)(2,1)S(1)}, u32[]{:S(2)}, u32[]{:S(2)}) %collective-permute-start.20) | collective-permute-done | bytes 102432 | tf_op jit(solution)/shard_map/ppermute | solution.py:577
  82.7 3.3 %energy.5 = (f32[64,256]{1,0:T(8,128)}, f32[64,2,64,64]{3,2,1,0:T(8,128)}, f32[8,128]{1,0:T(8,128)}) custom-call(bf16[24,64,512]{2,1,0:T(8,128)(2,1)S(1)} %get-tuple-element.69.merged, s16[400,128]{1,0:T(8,128)(2,1)S(1)} %get-tuple-element.78.refs_0_, ...), custom_call_target="tpu_custom_call", output_to_operand_aliasing={{0}: (3, {}), {1}: (4, {})} | custom-call | flops 1024 | bytes 1024 | tf_op jit(solution)/shard_map/energy/pallas_call | solution.py:529
Async XLA Ops:
  4.4 3.2 %collective-permute-start = (bf16[16,16,512]{2,1,0:T(8,128)(2,1)S(1)}, bf16[16,16,512]{2,1,0:T(8,128)(2,1)S(1)}, u32[]{:S(2)}, u32[]{:S(2)}) collective-permute-start(bf16[16,16,512]{2,1,0:T(8,128)(2,1)S(1)} %get-tuple-element.44), channel_id=1, source_target_pairs={{0,1},{1,0},{2,3},{3,2},{4,5},{5,4},{6,7},{7,6},{8,9},{9,8},{10,11... | collective-permute-start | bytes 786440 | tf_op jit(solution)/shard_map/ppermute | solution.py:577
  4.9 13.4 %collective-permute-start.7 = (bf16[16,16,512]{2,1,0:T(8,128)(2,1)S(1)}, bf16[16,16,512]{2,1,0:T(8,128)(2,1)S(1)}, u32[]{:S(2)}, u32[]{:S(2)}) collective-permute-start(bf16[16,16,512]{2,1,0:T(8,128)(2,1)S(1)} %get-tuple-element.55), channel_id=1, source_target_pairs={{0,2},{1,3},{2,0},{3,1},{4,6},{5,7},{6,4},{7,5},{8,10},{9,11},{10,... | collective-permute-start | bytes 786440 | tf_op jit(solution)/shard_map/ppermute | solution.py:577
  7.5 12.3 %collective-permute-start.8 = (bf16[16,16,512]{2,1,0:T(8,128)(2,1)S(1)}, bf16[16,16,512]{2,1,0:T(8,128)(2,1)S(1)}, u32[]{:S(2)}, u32[]{:S(2)}) collective-permute-start(bf16[16,16,512]{2,1,0:T(8,128)(2,1)S(1)} %get-tuple-element.56), channel_id=1, source_target_pairs={{0,3},{1,2},{2,1},{3,0},{4,7},{5,6},{6,5},{7,4},{8,11},{9,10},{10,... | collective-permute-start | bytes 786440 | tf_op jit(solution)/shard_map/ppermute | solution.py:577
  11.8 22.8 %collective-permute-start.4 = (bf16[24,16,512]{2,1,0:T(8,128)(2,1)S(1)}, bf16[24,16,512]{2,1,0:T(8,128)(2,1)S(1)}, u32[]{:S(2)}, u32[]{:S(2)}) collective-permute-start(bf16[24,16,512]{2,1,0:T(8,128)(2,1)S(1)} %get-tuple-element.51), channel_id=1, source_target_pairs={{0,1},{1,0},{2,3},{3,2},{4,5},{5,4},{6,7},{7,6},{8,9},{9,8},{10,11... | collective-permute-start | bytes 1179656 | tf_op jit(solution)/shard_map/ppermute | solution.py:577
  12.1 26.0 %collective-permute-start.5 = (bf16[24,16,512]{2,1,0:T(8,128)(2,1)S(1)}, bf16[24,16,512]{2,1,0:T(8,128)(2,1)S(1)}, u32[]{:S(2)}, u32[]{:S(2)}) collective-permute-start(bf16[24,16,512]{2,1,0:T(8,128)(2,1)S(1)} %get-tuple-element.52), channel_id=1, source_target_pairs={{0,2},{1,3},{2,0},{3,1},{4,6},{5,7},{6,4},{7,5},{8,10},{9,11},{10,... | collective-permute-start | bytes 1179656 | tf_op jit(solution)/shard_map/ppermute | solution.py:577
  14.0 24.1 %collective-permute-start.6 = (bf16[24,16,512]{2,1,0:T(8,128)(2,1)S(1)}, bf16[24,16,512]{2,1,0:T(8,128)(2,1)S(1)}, u32[]{:S(2)}, u32[]{:S(2)}) collective-permute-start(bf16[24,16,512]{2,1,0:T(8,128)(2,1)S(1)} %get-tuple-element.53), channel_id=1, source_target_pairs={{0,3},{1,2},{2,1},{3,0},{4,7},{5,6},{6,5},{7,4},{8,11},{9,10},{10,... | collective-permute-start | bytes 1179656 | tf_op jit(solution)/shard_map/ppermute | solution.py:577
  21.2 7.5 %collective-permute-start.9 = (s16[272,128]{1,0:T(8,128)(2,1)S(1)}, s16[272,128]{1,0:T(8,128)(2,1)S(1)}, u32[]{:S(2)}, u32[]{:S(2)}) collective-permute-start(s16[272,128]{1,0:T(8,128)(2,1)S(1)} %get-tuple-element.58.refs_0_), channel_id=1, source_target_pairs={{0,8},{4,12},{8,0},{12,4},{1,9},{5,13},{9,1},{13,5},{2,10},{6,14},... | collective-permute-start | bytes 208904 | tf_op jit(solution)/shard_map/ppermute | solution.py:577
  23.9 6.8 %collective-permute-start.11 = (s16[272,128]{1,0:T(8,128)(2,1)S(1)}, s16[272,128]{1,0:T(8,128)(2,1)S(1)}, u32[]{:S(2)}, u32[]{:S(2)}) collective-permute-start(s16[272,128]{1,0:T(8,128)(2,1)S(1)} %get-tuple-element.59), channel_id=1, source_target_pairs={{0,12},{4,8},{8,4},{12,0},{1,13},{5,9},{9,5},{13,1},{2,14},{6,10},... | collective-permute-start | bytes 208904 | tf_op jit(solution)/shard_map/ppermute | solution.py:577
  28.7 4.4 %collective-permute-start.10 = (s16[272,128]{1,0:T(8,128)(2,1)S(1)}, s16[272,128]{1,0:T(8,128)(2,1)S(1)}, u32[]{:S(2)}, u32[]{:S(2)}) collective-permute-start(s16[272,128]{1,0:T(8,128)(2,1)S(1)} %get-tuple-element.59), channel_id=1, source_target_pairs={{0,4},{4,0},{8,12},{12,8},{1,5},{5,1},{9,13},{13,9},{2,6},{6,2},{1... | collective-permute-start | bytes 208904 | tf_op jit(solution)/shard_map/ppermute | solution.py:577
  30.7 30.5 %collective-permute-start.1 = (bf16[24,16,512]{2,1,0:T(8,128)(2,1)S(1)}, bf16[24,16,512]{2,1,0:T(8,128)(2,1)S(1)}, u32[]{:S(2)}, u32[]{:S(2)}) collective-permute-start(bf16[24,16,512]{2,1,0:T(8,128)(2,1)S(1)} %get-tuple-element.47), channel_id=1, source_target_pairs={{0,1},{1,0},{2,3},{3,2},{4,5},{5,4},{6,7},{7,6},{8,9},{9,8},{10,11... | collective-permute-start | bytes 1179656 | tf_op jit(solution)/shard_map/ppermute | solution.py:577
  33.1 28.1 %collective-permute-start.2 = (bf16[24,16,512]{2,1,0:T(8,128)(2,1)S(1)}, bf16[24,16,512]{2,1,0:T(8,128)(2,1)S(1)}, u32[]{:S(2)}, u32[]{:S(2)}) collective-permute-start(bf16[24,16,512]{2,1,0:T(8,128)(2,1)S(1)} %get-tuple-element.48), channel_id=1, source_target_pairs={{0,2},{1,3},{2,0},{3,1},{4,6},{5,7},{6,4},{7,5},{8,10},{9,11},{10,... | collective-permute-start | bytes 1179656 | tf_op jit(solution)/shard_map/ppermute | solution.py:577
  34.6 26.6 %collective-permute-start.3 = (bf16[24,16,512]{2,1,0:T(8,128)(2,1)S(1)}, bf16[24,16,512]{2,1,0:T(8,128)(2,1)S(1)}, u32[]{:S(2)}, u32[]{:S(2)}) collective-permute-start(bf16[24,16,512]{2,1,0:T(8,128)(2,1)S(1)} %get-tuple-element.49), channel_id=1, source_target_pairs={{0,3},{1,2},{2,1},{3,0},{4,7},{5,6},{6,5},{7,4},{8,11},{9,10},{10,... | collective-permute-start | bytes 1179656 | tf_op jit(solution)/shard_map/ppermute | solution.py:577
  39.8 9.8 %collective-permute-start.12 = (s16[400,128]{1,0:T(8,128)(2,1)S(1)}, s16[400,128]{1,0:T(8,128)(2,1)S(1)}, u32[]{:S(2)}, u32[]{:S(2)}) collective-permute-start(s16[400,128]{1,0:T(8,128)(2,1)S(1)} %get-tuple-element.62.refs_0_), channel_id=1, source_target_pairs={{0,8},{4,12},{8,0},{12,4},{1,9},{5,13},{9,1},{13,5},{2,10},{6,14},... | collective-permute-start | bytes 307208 | tf_op jit(solution)/shard_map/ppermute | solution.py:577
  43.4 4.6 %collective-permute-start.15 = (s16[272,128]{1,0:T(8,128)(2,1)S(1)}, s16[272,128]{1,0:T(8,128)(2,1)S(1)}, u32[]{:S(2)}, u32[]{:S(2)}) collective-permute-start(s16[272,128]{1,0:T(8,128)(2,1)S(1)} %get-tuple-element.65.refs_0_), channel_id=1, source_target_pairs={{0,4},{4,0},{8,12},{12,8},{1,5},{5,1},{9,13},{13,9},{2,6},{6,2},{1... | collective-permute-start | bytes 208904 | tf_op jit(solution)/shard_map/ppermute | solution.py:577
  48.0 7.2 %collective-permute-start.14 = (s16[400,128]{1,0:T(8,128)(2,1)S(1)}, s16[400,128]{1,0:T(8,128)(2,1)S(1)}, u32[]{:S(2)}, u32[]{:S(2)}) collective-permute-start(s16[400,128]{1,0:T(8,128)(2,1)S(1)} %get-tuple-element.63), channel_id=1, source_target_pairs={{0,12},{4,8},{8,4},{12,0},{1,13},{5,9},{9,5},{13,1},{2,14},{6,10},... | collective-permute-start | bytes 307208 | tf_op jit(solution)/shard_map/ppermute | solution.py:577
  49.6 6.7 %collective-permute-start.13 = (s16[400,128]{1,0:T(8,128)(2,1)S(1)}, s16[400,128]{1,0:T(8,128)(2,1)S(1)}, u32[]{:S(2)}, u32[]{:S(2)}) collective-permute-start(s16[400,128]{1,0:T(8,128)(2,1)S(1)} %get-tuple-element.63), channel_id=1, source_target_pairs={{0,4},{4,0},{8,12},{12,8},{1,5},{5,1},{9,13},{13,9},{2,6},{6,2},{1... | collective-permute-start | bytes 307208 | tf_op jit(solution)/shard_map/ppermute | solution.py:577
  60.4 6.2 %collective-permute-start.19 = (s16[400,128]{1,0:T(8,128)(2,1)S(1)}, s16[400,128]{1,0:T(8,128)(2,1)S(1)}, u32[]{:S(2)}, u32[]{:S(2)}) collective-permute-start(s16[400,128]{1,0:T(8,128)(2,1)S(1)} %get-tuple-element.73.refs_0_), channel_id=1, source_target_pairs={{0,4},{4,0},{8,12},{12,8},{1,5},{5,1},{9,13},{13,9},{2,6},{6,2},{1... | collective-permute-start | bytes 307208 | tf_op jit(solution)/shard_map/ppermute | solution.py:577
  62.9 10.5 %collective-permute-start.16 = (s16[400,128]{1,0:T(8,128)(2,1)S(1)}, s16[400,128]{1,0:T(8,128)(2,1)S(1)}, u32[]{:S(2)}, u32[]{:S(2)}) collective-permute-start(s16[400,128]{1,0:T(8,128)(2,1)S(1)} %get-tuple-element.70.refs_0_), channel_id=1, source_target_pairs={{0,8},{4,12},{8,0},{12,4},{1,9},{5,13},{9,1},{13,5},{2,10},{6,14},... | collective-permute-start | bytes 307208 | tf_op jit(solution)/shard_map/ppermute | solution.py:577
  64.9 8.5 %collective-permute-start.18 = (s16[400,128]{1,0:T(8,128)(2,1)S(1)}, s16[400,128]{1,0:T(8,128)(2,1)S(1)}, u32[]{:S(2)}, u32[]{:S(2)}) collective-permute-start(s16[400,128]{1,0:T(8,128)(2,1)S(1)} %get-tuple-element.71), channel_id=1, source_target_pairs={{0,12},{4,8},{8,4},{12,0},{1,13},{5,9},{9,5},{13,1},{2,14},{6,10},... | collective-permute-start | bytes 307208 | tf_op jit(solution)/shard_map/ppermute | solution.py:577
  66.6 7.2 %collective-permute-start.17 = (s16[400,128]{1,0:T(8,128)(2,1)S(1)}, s16[400,128]{1,0:T(8,128)(2,1)S(1)}, u32[]{:S(2)}, u32[]{:S(2)}) collective-permute-start(s16[400,128]{1,0:T(8,128)(2,1)S(1)} %get-tuple-element.71), channel_id=1, source_target_pairs={{0,4},{4,0},{8,12},{12,8},{1,5},{5,1},{9,13},{13,9},{2,6},{6,2},{1... | collective-permute-start | bytes 307208 | tf_op jit(solution)/shard_map/ppermute | solution.py:577
  78.0 4.7 %collective-permute-start.20 = (s16[400,128]{1,0:T(8,128)(2,1)S(1)}, s16[400,128]{1,0:T(8,128)(2,1)S(1)}, u32[]{:S(2)}, u32[]{:S(2)}) collective-permute-start(s16[400,128]{1,0:T(8,128)(2,1)S(1)} %get-tuple-element.78.refs_0_), channel_id=1, source_target_pairs={{0,4},{4,0},{8,12},{12,8},{1,5},{5,1},{9,13},{13,9},{2,6},{6,2},{1... | collective-permute-start | bytes 307208 | tf_op jit(solution)/shard_map/ppermute | solution.py:577

commit v10 on v9

--- a/solution.py
+++ b/solution.py
@@ -249,6 +249,20 @@
     ]
 
 
+def inverse_outer(scales, number):
+    half = scales.shape[1] // 2
+    rows = scales.shape[0]
+    inverse = 1.0 / scales.astype(F32)
+    high = inverse.astype(BF16).astype(F32)
+    low = inverse - high
+    left = jnp.transpose(jnp.concatenate([high, high, low], 0))[:half].astype(BF16)
+    right = jnp.concatenate([high, low, high], 0)
+    row = lax.broadcasted_iota(jnp.int32, right.shape, 0) & (rows - 1)
+    return [
+        dot(left, jnp.where(row == i, right, F32(0)).astype(BF16)) for i in range(number)
+    ]
+
+
 def encode(both):
     half, width = both[0].shape
     row = lax.broadcasted_iota(jnp.int32, (half, width), 0)
@@ -259,14 +273,10 @@
     exponent = jnp.floor(jnp.log(root) * F32(1 / math.log(2.0)))
     part = jnp.maximum(jnp.ceil((root * jnp.exp2(-exponent) - 1) * 128), F32(0))
     codes = exponent * 256 + part
-    products = outer(scale_of(codes), len(both))
-    value = each(lambda b, p: jnp.round(b * (F32(TOP) / p)), both, products)
-    return each(lambda v: pack(jnp.clip(v, F32(-32767), F32(32767))), value), codes
-
-
-def decode(values, codes):
-    products = outer(scale_of(codes), len(values))
-    return each(lambda v, p: unpack(v, p * F32(0.5 / TOP)), values, products)
+    scales = scale_of(codes)
+    inverse = inverse_outer(scales, len(both))
+    value = each(lambda b, p: jnp.round((b * F32(TOP)) * p), both, inverse)
+    return each(lambda v: pack(jnp.clip(v, F32(-32767), F32(32767))), value), codes, scales
 
 
 def spread(values, codes):
@@ -337,21 +347,25 @@
             s = s * F32(1.0 / blocks)
             top, bottom = s[:blocks], swap(s[blocks:])
             compact = jnp.where(low, top + bottom, top - bottom)
-            if direct:
+            if direct and slot == 0 and grams[0].dtype == F32:
+                grams[0][i] = compact
+            elif direct:
                 coded.append(double(compact))
             else:
                 grams[0][f] = pack(double(compact))
         if coded:
-            write_coded(grams[slot], *encode(coded))
-
-
-def gram(pieces, slots, direct, after):
+            write_coded(grams[slot], *encode(coded)[:2])
+
+
+def gram(pieces, slots, direct, in_steps, after):
     peers = len(pieces)
     count, here, width = pieces[0].shape
     blocks = here * peers
     if direct:
         rows = coded_rows(count // slots, blocks // 2)
         shapes = [((rows, 2 * blocks), jnp.int16)] * slots
+        if in_steps:
+            shapes[0] = ((count // slots, blocks, 2 * blocks), F32)
     else:
         shapes = [((count, blocks // 2, 2 * blocks), F32)]
     out = pl.pallas_call(
@@ -368,6 +382,27 @@
     return out[0], out[2:], out[1]
 
 
+def add_kernel(own, other, *refs):
+    out, token = refs[-2:]
+    token[...] = jnp.zeros_like(token)
+    number, blocks, _ = own.shape
+    received = spread(*read_coded(other, number, blocks // 2))
+    sums = [double(own[i] + unpack(received[i])[0]) for i in range(number)]
+    write_coded(out, *encode(sums)[:2])
+
+
+def add(own, other, after):
+    return pl.pallas_call(
+        add_kernel,
+        in_specs=[whole_spec()] * 2 + [any_spec()] * len(after),
+        out_specs=[whole_spec()] * 2,
+        out_shape=[jax.ShapeDtypeStruct(other.shape, jnp.int16), TOKEN],
+        compiler_params=params(),
+        cost_estimate=light(),
+        name="add",
+    )(own, other, *after)
+
+
 def split(x):
     high = x.astype(BF16)
     return high, (x - high.astype(F32)).astype(BF16)
@@ -387,13 +422,16 @@
         sums = [ins[0][i] for i in range(number)]
     else:
         found = [spread(*read_coded(r, number, half_rows)) for r in ins]
-        sums = [(o + a) + (b + c) for o, a, b, c in zip(*found)]
+        sums = [p + q for p, q in zip(found[0], found[1])]
+        if parts == 4:
+            sums = [p + (q + r) for p, q, r in zip(sums, found[2], found[3])]
     both_halves = each(unpack, sums)
     grams = [h[0] for h in both_halves]
     shift = each(lambda g: jnp.sum(g * eye, keepdims=True) * F32(1.0 / half), grams)
     eye_low = jnp.where(row + half == lane, F32(1), F32(0))
-    system = each(lambda g, m: g / m + eye, grams, shift)
-    under = each(lambda h, m: h[1] / m + eye_low, both_halves, shift)
+    inverse = each(lambda m: 1.0 / m, shift)
+    system = each(lambda g, m: g * m + eye, grams, inverse)
+    under = each(lambda h, m: h[1] * m + eye_low, both_halves, inverse)
     both = each(
         lambda a, u: jnp.concatenate(split(jnp.concatenate([a, u], 0)), 1), system, under
     )
@@ -428,8 +466,9 @@
         step = each(lambda r, v: dot(r.astype(BF16), v), residual, xf)
         factor = 1.0 if kind == "last" else 2 * t * t / (2 * t * t - 1)
         x = each(lambda v, m: F32(factor) * (v + m), xw, step)
-    values, codes = encode(each(lambda v: double(eye - v), x))
-    filters = decode(values, codes)
+    values, codes, scales = encode(each(lambda v: double(eye - v), x))
+    products = outer(scales, number)
+    filters = each(lambda v, p: unpack(v, p * F32(0.5 / TOP)), values, products)
     rounded = each(lambda c: c[0].astype(BF16), filters)
     turned = each(
         lambda c: jnp.concatenate([c[0].astype(BF16), c[1].astype(BF16)], 0), filters
@@ -565,11 +604,14 @@
     return SIZES, ORDER
 
 
-SIZES = [16, 24, 24]
+SIZES = [24, 24, 16]
 ORDER = (
-    ("T", 0), ("T", 1), ("T", 2), ("G", 0), ("F", 0), ("G", 1), ("E", 0), ("F", 1),
-    ("G", 2), ("E", 1), ("F", 2), ("E", 2),
+    ("T", 0), ("T", 1), ("G", 0), ("A", 0), ("F", 0), ("G", 1), ("E", 0), ("A", 1),
+    ("G", 2), ("F", 1), ("F", 2), ("E", 1), ("E", 2),
 )
+
+
+TIES = {("T", 1): (0,)}
 
 
 def permute(x, axis, offset):
@@ -592,17 +634,22 @@
 
     def do_transform(c):
         nonlocal token
-        (out,), done = transform(
-            snapshots, weight, freq_index, peers, [(starts[c], sizes[c])], token
+        joint = [k for k in range(c, len(sizes)) if k == c or ("T", k) not in order]
+        out, done = transform(
+            snapshots, weight, freq_index, peers, [(starts[k], sizes[k]) for k in joint], token
         )
-        sent[c] = [out[0]] + [permute(out[offset], "tm", offset) for offset in range(1, peers)]
-        token = [done, sent[c][1]] if c == 0 and len(sizes) > 1 else [done]
+        token = [done]
+        for k, own in zip(joint, out):
+            sent[k] = [own[0]] + [permute(own[i], "tm", i) for i in range(1, peers)]
 
     def do_gram(c):
         nonlocal token
-        merged[c], grams[c], done = gram(sent[c], halves, paired, token)
+        in_steps = paired and ("A", c) in order
+        merged[c], grams[c], done = gram(sent[c], halves, paired, in_steps, token)
         token = [done]
-        if paired:
+        if in_steps:
+            grams[c] = [grams[c][0], permute(grams[c][1], "space", 1)]
+        elif paired:
             own, other = grams[c]
             parts[c] = [
                 own,
@@ -613,6 +660,12 @@
         else:
             parts[c] = [lax.psum_scatter(grams[c][0], "space", scatter_dimension=0, tiled=True)]
 
+    def do_add(c):
+        nonlocal token
+        half, done = add(*grams[c], token)
+        token = [done]
+        parts[c] = [half, permute(half, "space", 2)]
+
     def do_solve(c):
         nonlocal token
         count = sizes[c] // halves
@@ -630,8 +683,9 @@
         )
         token = [done]
 
-    stages = {"T": do_transform, "G": do_gram, "F": do_solve, "E": do_energy}
+    stages = {"T": do_transform, "G": do_gram, "A": do_add, "F": do_solve, "E": do_energy}
     for stage, c in order:
+        token = token + [sent[k][1] for k in TIES.get((stage, c), ()) if k in sent]
         stages[stage](c)
     return (carry[0], carry[1])
 

time: 86.3 us -> 84.3 us (0.977)
  starting transfers between devices: 27.7 us -> 22.6 us
  waiting for transfers between devices: 20.7 us -> 23.1 us
    ppermute x21 -> x19, starting transfers between devices: 27.7 us -> 22.6 us  [permute(): return lax.ppermute(x, axis, pairs)]
    pallas_call x0 -> x2, Pallas kernels: none -> 2.6 us  [add(): pl.pallas_call(add_kernel, in_specs=[whole_spec()] * 2 + [any_spec()] * l...]
    ppermute x21 -> x19, waiting for transfers between devices: 20.7 us -> 23.1 us  [permute(): return lax.ppermute(x, axis, pairs)]
    pallas_call x3, Pallas kernels: 4.81 us -> 3.72 us  [gram(): pl.pallas_call(functools.partial(gram_kernel, peers, slots, direct, len(a...]
    pallas_call x3 -> x2, Pallas kernels: 12.3 us -> 11.8 us  [transform(): pl.pallas_call(functools.partial(transform_kernel, peers, parts, group),...]
  transfers between devices with their start and end apart: 21 -> 19, of which waited for: 9 -> 6; matrix products, arithmetic and copies ran while one was open for 0% -> 0% of each run, Pallas kernels for 30% -> 34%
where the time goes in v10:
time: 84.3 us; the launch traced here: 84.1 us
  Pallas kernels  37.4 us (44%)
  waiting for transfers between devices  23.1 us (27%)
  starting transfers between devices  22.6 us (27%)
  between operations  0.9 us (1%)
    ppermute x19, waiting for transfers between devices, permute(): return lax.ppermute(x, axis, pairs)  23.1 us
    ppermute x19, starting transfers between devices, permute(): return lax.ppermute(x, axis, pairs)  22.6 us
    pallas_call x2, Pallas kernels, transform(): pl.pallas_call(functools.partial(transform_kernel, peers, parts, group),...  11.8 us
    pallas_call x3, Pallas kernels, solve(): pl.pallas_call(functools.partial(solve_kernel, len(parts), number, half_r...  11.2 us
    pallas_call x3, Pallas kernels, filtered(): pl.pallas_call(functools.partial(energy_kernel, slots, direct, len(pieces...  8.14 us
    pallas_call x3, Pallas kernels, gram(): pl.pallas_call(functools.partial(gram_kernel, peers, slots, direct, len(a...  3.72 us
    pallas_call x2, Pallas kernels, add(): pl.pallas_call(add_kernel, in_specs=[whole_spec()] * 2 + [any_spec()] * l...  2.6 us
  transfers between devices with their start and end apart: 19, of which 6 were waited for; matrix products, arithmetic and copies ran while one was open for 0% of the time, Pallas kernels for 34%

profile of v10, /device:TPU:0, one launch (start us, length us, event | category | flops | bytes accessed | tf_op | source)
XLA Modules:
  0.0 84.1 jit_solution(10034215399347365396)
XLA Ops:
  0.6 6.4 %transform.2 = (bf16[24,16,512]{2,1,0:T(8,128)(2,1)S(1)}, bf16[24,16,512]{2,1,0:T(8,128)(2,1)S(1)}, bf16[24,16,512]{2,1,0:T(8,128)(2,1)S(1)}, bf16[24,16,512]{2,...) custom-call(s32[256]{0:T(256)} %refs_0_.3, ...), custom_call_target="tpu_custom_call" | custom-call | flops 1024 | bytes 1024 | tf_op jit(solution)/shard_map/transform/pallas_call | solution.py:149
  7.0 0.5 collective-permute-start
  7.5 2.6 %collective-permute-start.7 = (bf16[24,16,512]{2,1,0:T(8,128)(2,1)S(1)}, bf16[24,16,512]{2,1,0:T(8,128)(2,1)S(1)}, u32[]{:S(2)}, u32[]{:S(2)}) collective-permute-start(bf16[24,16,512]{2,1,0:T(8,128)(2,1)S(1)} %get-tuple-element.57), channel_id=1, source_target_pairs={{0,2},{1,3},{2,0},{3,1},{4,6},{5,7},{6,4},{7,5},{8,10},{9,11},{10,... | collective-permute-start | bytes 1179656 | tf_op jit(solution)/shard_map/ppermute | solution.py:619
  10.1 0.1 collective-permute-start.8
  10.2 0.0 collective-permute-done.refs_4_.refs_1_
  10.2 5.4 %transform.3 = (bf16[24,16,512]{2,1,0:T(8,128)(2,1)S(1)}, bf16[24,16,512]{2,1,0:T(8,128)(2,1)S(1)}, bf16[24,16,512]{2,1,0:T(8,128)(2,1)S(1)}, bf16[24,16,512]{2,...) custom-call(s32[256]{0:T(256)} %refs_0_.3, ...), custom_call_target="tpu_custom_call" | custom-call | flops 1024 | bytes 1024 | tf_op jit(solution)/shard_map/transform/pallas_call | solution.py:149
  15.6 0.2 collective-permute-start.4
  15.8 1.9 %collective-permute-start.5 = (bf16[24,16,512]{2,1,0:T(8,128)(2,1)S(1)}, bf16[24,16,512]{2,1,0:T(8,128)(2,1)S(1)}, u32[]{:S(2)}, u32[]{:S(2)}) collective-permute-start(bf16[24,16,512]{2,1,0:T(8,128)(2,1)S(1)} %get-tuple-element.54), channel_id=1, source_target_pairs={{0,2},{1,3},{2,0},{3,1},{4,6},{5,7},{6,4},{7,5},{8,10},{9,11},{10,... | collective-permute-start | bytes 1179656 | tf_op jit(solution)/shard_map/ppermute | solution.py:619
  17.8 0.0 collective-permute-start.6
  17.8 2.3 %collective-permute-done.7.refs_2_ = bf16[24,16,512]{2,1,0:T(8,128)(2,1)S(1)} collective-permute-done((bf16[24,16,512]{2,1,0:T(8,128)(2,1)S(1)}, bf16[24,16,512]{2,1,0:T(8,128)(2,1)S(1)}, u32[]{:S(2)}, u32[]{:S(2)}) %collective-permute-start.7) | collective-permute-done | bytes 393248 | tf_op jit(solution)/shard_map/ppermute | solution.py:619
  20.1 7.9 %collective-permute-done.8.refs_3_ = bf16[24,16,512]{2,1,0:T(8,128)(2,1)S(1)} collective-permute-done((bf16[24,16,512]{2,1,0:T(8,128)(2,1)S(1)}, bf16[24,16,512]{2,1,0:T(8,128)(2,1)S(1)}, u32[]{:S(2)}, u32[]{:S(2)}) %collective-permute-start.8) | collective-permute-done | bytes 393248 | tf_op jit(solution)/shard_map/ppermute | solution.py:619
  28.0 1.1 %gram.3 = (bf16[24,64,512]{2,1,0:T(8,128)(2,1)S(1)}, f32[8,128]{1,0:T(8,128)S(1)}, f32[12,64,128]{2,1,0:T(8,128)S(1)}, s16[400,128]{1,0:T(8,128)(2,1)S(1)}) custom-call(bf16[24,16,512]{2,1,0:T(8,128)(2,1)S(1)} %get-tuple-element.56.refs_0_, bf16[24,16,512]{2,1,0:T(8,128)(2,1)S(1)} %collective-permute-done.refs_4_.refs_1_, ...), custom_call_target="tpu_custom_call" | custom-call | flops 1024 | bytes 1024 | tf_op jit(solution)/shard_map/gram/pallas_call | solution.py:371
  29.1 1.7 %collective-permute-start.9 = (s16[400,128]{1,0:T(8,128)(2,1)S(1)}, s16[400,128]{1,0:T(8,128)(2,1)S(1)}, u32[]{:S(2)}, u32[]{:S(2)}) collective-permute-start(s16[400,128]{1,0:T(8,128)(2,1)S(1)} %get-tuple-element.61), channel_id=1, source_target_pairs={{0,4},{4,0},{8,12},{12,8},{1,5},{5,1},{9,13},{13,9},{2,6},{6,2},{1... | collective-permute-start | bytes 307208 | tf_op jit(solution)/shard_map/ppermute | solution.py:619
  30.8 3.8 %collective-permute-done.9.other = s16[400,128]{1,0:T(8,128)(2,1)S(1)} collective-permute-done((s16[400,128]{1,0:T(8,128)(2,1)S(1)}, s16[400,128]{1,0:T(8,128)(2,1)S(1)}, u32[]{:S(2)}, u32[]{:S(2)}) %collective-permute-start.9) | collective-permute-done | bytes 102432 | tf_op jit(solution)/shard_map/ppermute | solution.py:619
  34.6 1.3 %add.2 = (s16[400,128]{1,0:T(8,128)(2,1)S(1)}, f32[8,128]{1,0:T(8,128)S(1)}) custom-call(f32[12,64,128]{2,1,0:T(8,128)S(1)} %get-tuple-element.60.own, s16[400,128]{1,0:T(8,128)(2,1)S(1)} %collective-permute-done.9.other, f32[8,128]{1,0:T(8,128)S(1)} %get-tuple-element.62.refs_0_), custom_call_target="tpu_custom_call" | custom-call | flops 1024 | bytes 1024 | tf_op jit(solution)/shard_map/add/pallas_call | solution.py:395
  35.9 2.8 %collective-permute-start.10 = (s16[400,128]{1,0:T(8,128)(2,1)S(1)}, s16[400,128]{1,0:T(8,128)(2,1)S(1)}, u32[]{:S(2)}, u32[]{:S(2)}) collective-permute-start(s16[400,128]{1,0:T(8,128)(2,1)S(1)} %get-tuple-element.63.refs_0_), channel_id=1, source_target_pairs={{0,8},{4,12},{8,0},{12,4},{1,9},{5,13},{9,1},{13,5},{2,10},{6,14},... | collective-permute-start | bytes 307208 | tf_op jit(solution)/shard_map/ppermute | solution.py:619
  38.7 0.0 collective-permute-start.1
  38.7 5.1 %collective-permute-done.10.refs_1_ = s16[400,128]{1,0:T(8,128)(2,1)S(1)} collective-permute-done((s16[400,128]{1,0:T(8,128)(2,1)S(1)}, s16[400,128]{1,0:T(8,128)(2,1)S(1)}, u32[]{:S(2)}, u32[]{:S(2)}) %collective-permute-start.10) | collective-permute-done | bytes 102432 | tf_op jit(solution)/shard_map/ppermute | solution.py:619
  43.8 1.6 %collective-permute-start.2 = (bf16[16,16,512]{2,1,0:T(8,128)(2,1)S(1)}, bf16[16,16,512]{2,1,0:T(8,128)(2,1)S(1)}, u32[]{:S(2)}, u32[]{:S(2)}) collective-permute-start(bf16[16,16,512]{2,1,0:T(8,128)(2,1)S(1)} %get-tuple-element.50), channel_id=1, source_target_pairs={{0,2},{1,3},{2,0},{3,1},{4,6},{5,7},{6,4},{7,5},{8,10},{9,11},{10,... | collective-permute-start | bytes 786440 | tf_op jit(solution)/shard_map/ppermute | solution.py:619
  45.4 0.0 collective-permute-done.4.refs_1_
  45.4 0.0 collective-permute-start.3
  45.4 3.9 %filters.3 = (s16[400,128]{1,0:T(8,128)(2,1)S(1)}, f32[8,128]{1,0:T(8,128)S(1)}) custom-call(s16[400,128]{1,0:T(8,128)(2,1)S(1)} %get-tuple-element.63.refs_0_, s16[400,128]{1,0:T(8,128)(2,1)S(1)} %collective-permute-done.10.refs_1_, f32[8,128]{1,0:T(8,128)S(1)} %get-tuple-element.64.refs_2_), custom_call_target="tpu_custom_call" | custom-call | flops 1024 | bytes 1024 | tf_op jit(solution)/shard_map/filters/pallas_call | solution.py:493
  49.4 0.0 collective-permute-done.5.refs_2_
  49.4 0.7 collective-permute-start.12
  50.1 0.0 collective-permute-done.6.refs_3_
  50.1 1.1 %gram.4 = (bf16[24,64,512]{2,1,0:T(8,128)(2,1)S(1)}, f32[8,128]{1,0:T(8,128)S(1)}, f32[12,64,128]{2,1,0:T(8,128)S(1)}, s16[400,128]{1,0:T(8,128)(2,1)S(1)}) custom-call(bf16[24,16,512]{2,1,0:T(8,128)(2,1)S(1)} %get-tuple-element.52.refs_0_, bf16[24,16,512]{2,1,0:T(8,128)(2,1)S(1)} %collective-permute-done.4.refs_1_, ...), custom_call_target="tpu_custom_call" | custom-call | flops 1024 | bytes 1024 | tf_op jit(solution)/shard_map/gram/pallas_call | solution.py:371
  51.2 1.4 %collective-permute-start.11 = (s16[400,128]{1,0:T(8,128)(2,1)S(1)}, s16[400,128]{1,0:T(8,128)(2,1)S(1)}, u32[]{:S(2)}, u32[]{:S(2)}) collective-permute-start(s16[400,128]{1,0:T(8,128)(2,1)S(1)} %get-tuple-element.67), channel_id=1, source_target_pairs={{0,4},{4,0},{8,12},{12,8},{1,5},{5,1},{9,13},{13,9},{2,6},{6,2},{1... | collective-permute-start | bytes 307208 | tf_op jit(solution)/shard_map/ppermute | solution.py:619
  52.7 2.4 %collective-permute-done.12.refs_1_ = s16[400,128]{1,0:T(8,128)(2,1)S(1)} collective-permute-done((s16[400,128]{1,0:T(8,128)(2,1)S(1)}, s16[400,128]{1,0:T(8,128)(2,1)S(1)}, u32[]{:S(2)}, u32[]{:S(2)}) %collective-permute-start.12) | collective-permute-done | bytes 102432 | tf_op jit(solution)/shard_map/ppermute | solution.py:619
  55.1 2.7 %energy.3 = (f32[64,256]{1,0:T(8,128)}, f32[64,2,64,64]{3,2,1,0:T(8,128)}, f32[8,128]{1,0:T(8,128)S(1)}) custom-call(bf16[24,64,512]{2,1,0:T(8,128)(2,1)S(1)} %get-tuple-element.68.merged, s16[400,128]{1,0:T(8,128)(2,1)S(1)} %get-tuple-element.69.refs_0_, s16[400,128]{1,0:T(8,128)(2,1)S(1)} %collective-permute-done.12.refs_1_, ...), custom_call_target="tpu_custom_call" | custom-call | flops 1024 | bytes 1024 | tf_op jit(solution)/shard_map/energy/pallas_call | solution.py:568
  57.8 0.0 collective-permute-done.11.other
  57.8 1.3 %add.3 = (s16[400,128]{1,0:T(8,128)(2,1)S(1)}, f32[8,128]{1,0:T(8,128)S(1)}) custom-call(f32[12,64,128]{2,1,0:T(8,128)S(1)} %get-tuple-element.66.own, s16[400,128]{1,0:T(8,128)(2,1)S(1)} %collective-permute-done.11.other, f32[8,128]{1,0:T(8,128)S(1)} %get-tuple-element.71.refs_0_), custom_call_target="tpu_custom_call" | custom-call | flops 1024 | bytes 1024 | tf_op jit(solution)/shard_map/add/pallas_call | solution.py:395
  59.2 2.1 %collective-permute-start.16 = (s16[400,128]{1,0:T(8,128)(2,1)S(1)}, s16[400,128]{1,0:T(8,128)(2,1)S(1)}, u32[]{:S(2)}, u32[]{:S(2)}) collective-permute-start(s16[400,128]{1,0:T(8,128)(2,1)S(1)} %get-tuple-element.76.refs_0_), channel_id=1, source_target_pairs={{0,8},{4,12},{8,0},{12,4},{1,9},{5,13},{9,1},{13,5},{2,10},{6,14},... | collective-permute-start | bytes 307208 | tf_op jit(solution)/shard_map/ppermute | solution.py:619
  61.3 0.0 collective-permute-done.1.refs_1_
  61.3 0.0 collective-permute-done.2.refs_2_
  61.3 0.0 collective-permute-done.3.refs_3_
  61.3 1.5 %gram.5 = (bf16[16,64,512]{2,1,0:T(8,128)(2,1)S(1)}, f32[8,128]{1,0:T(8,128)S(1)}, s16[272,128]{1,0:T(8,128)(2,1)S(1)}, s16[272,128]{1,0:T(8,128)(2,1)S(1)}) custom-call(bf16[16,16,512]{2,1,0:T(8,128)(2,1)S(1)} %get-tuple-element.48.refs_0_, bf16[16,16,512]{2,1,0:T(8,128)(2,1)S(1)} %collective-permute-done.1.refs_1_, ...), custom_call_target="tpu_custom_call" | custom-call | flops 1024 | bytes 1024 | tf_op jit(solution)/shard_map/gram/pallas_call | solution.py:371
  62.8 0.9 %collective-permute-start.13 = (s16[272,128]{1,0:T(8,128)(2,1)S(1)}, s16[272,128]{1,0:T(8,128)(2,1)S(1)}, u32[]{:S(2)}, u32[]{:S(2)}) collective-permute-start(s16[272,128]{1,0:T(8,128)(2,1)S(1)} %get-tuple-element.74.refs_0_), channel_id=1, source_target_pairs={{0,8},{4,12},{8,0},{12,4},{1,9},{5,13},{9,1},{13,5},{2,10},{6,14},... | collective-permute-start | bytes 208904 | tf_op jit(solution)/shard_map/ppermute | solution.py:619
  63.7 1.3 %collective-permute-start.14 = (s16[272,128]{1,0:T(8,128)(2,1)S(1)}, s16[272,128]{1,0:T(8,128)(2,1)S(1)}, u32[]{:S(2)}, u32[]{:S(2)}) collective-permute-start(s16[272,128]{1,0:T(8,128)(2,1)S(1)} %get-tuple-element.75), channel_id=1, source_target_pairs={{0,4},{4,0},{8,12},{12,8},{1,5},{5,1},{9,13},{13,9},{2,6},{6,2},{1... | collective-permute-start | bytes 208904 | tf_op jit(solution)/shard_map/ppermute | solution.py:619
  65.0 2.3 %collective-permute-start.15 = (s16[272,128]{1,0:T(8,128)(2,1)S(1)}, s16[272,128]{1,0:T(8,128)(2,1)S(1)}, u32[]{:S(2)}, u32[]{:S(2)}) collective-permute-start(s16[272,128]{1,0:T(8,128)(2,1)S(1)} %get-tuple-element.75), channel_id=1, source_target_pairs={{0,12},{4,8},{8,4},{12,0},{1,13},{5,9},{9,5},{13,1},{2,14},{6,10},... | collective-permute-start | bytes 208904 | tf_op jit(solution)/shard_map/ppermute | solution.py:619
  67.3 0.0 collective-permute-done.16.refs_1_
  67.3 3.8 %filters.4 = (s16[400,128]{1,0:T(8,128)(2,1)S(1)}, f32[8,128]{1,0:T(8,128)S(1)}) custom-call(s16[400,128]{1,0:T(8,128)(2,1)S(1)} %get-tuple-element.76.refs_0_, s16[400,128]{1,0:T(8,128)(2,1)S(1)} %collective-permute-done.16.refs_1_, f32[8,128]{1,0:T(8,128)S(1)} %get-tuple-element.77.refs_2_), custom_call_target="tpu_custom_call" | custom-call | flops 1024 | bytes 1024 | tf_op jit(solution)/shard_map/filters/pallas_call | solution.py:493
  71.0 2.3 %collective-permute-start.18 = (s16[400,128]{1,0:T(8,128)(2,1)S(1)}, s16[400,128]{1,0:T(8,128)(2,1)S(1)}, u32[]{:S(2)}, u32[]{:S(2)}) collective-permute-start(s16[400,128]{1,0:T(8,128)(2,1)S(1)} %get-tuple-element.81.refs_0_), channel_id=1, source_target_pairs={{0,4},{4,0},{8,12},{12,8},{1,5},{5,1},{9,13},{13,9},{2,6},{6,2},{1... | collective-permute-start | bytes 307208 | tf_op jit(solution)/shard_map/ppermute | solution.py:619
  73.4 0.0 collective-permute-done.13.refs_1_
  73.4 0.0 collective-permute-done.14.refs_2_
  73.4 0.0 collective-permute-done.15.refs_3_
  73.4 3.5 %filters.5 = (s16[272,128]{1,0:T(8,128)(2,1)S(1)}, f32[8,128]{1,0:T(8,128)S(1)}) custom-call(s16[272,128]{1,0:T(8,128)(2,1)S(1)} %get-tuple-element.74.refs_0_, s16[272,128]{1,0:T(8,128)(2,1)S(1)} %collective-permute-done.13.refs_1_, s16[272,128]{1,0:T(8,128)(2,1)S(1)} %collective-permute-done.14.refs_2_, ...), custom_call_target="tpu_custom_call" | custom-call | flops 1024 | bytes 1024 | tf_op jit(solution)/shard_map/filters/pallas_call | solution.py:493
  76.9 0.1 collective-permute-start.17
  77.0 0.0 collective-permute-done.18.refs_1_
  77.0 2.7 %energy.4 = (f32[64,256]{1,0:T(8,128)}, f32[64,2,64,64]{3,2,1,0:T(8,128)}, f32[8,128]{1,0:T(8,128)S(1)}) custom-call(bf16[24,64,512]{2,1,0:T(8,128)(2,1)S(1)} %get-tuple-element.80.merged, s16[400,128]{1,0:T(8,128)(2,1)S(1)} %get-tuple-element.81.refs_0_, ...), custom_call_target="tpu_custom_call", output_to_operand_aliasing={{0}: (3, {}), {1}: (4, {})} | custom-call | flops 1024 | bytes 1024 | tf_op jit(solution)/shard_map/energy/pallas_call | solution.py:568
  79.7 1.5 %collective-permute-done.17.refs_1_ = s16[272,128]{1,0:T(8,128)(2,1)S(1)} collective-permute-done((s16[272,128]{1,0:T(8,128)(2,1)S(1)}, s16[272,128]{1,0:T(8,128)(2,1)S(1)}, u32[]{:S(2)}, u32[]{:S(2)}) %collective-permute-start.17) | collective-permute-done | bytes 69664 | tf_op jit(solution)/shard_map/ppermute | solution.py:619
  81.2 2.7 %energy.5 = (f32[64,256]{1,0:T(8,128)}, f32[64,2,64,64]{3,2,1,0:T(8,128)}, f32[8,128]{1,0:T(8,128)}) custom-call(bf16[16,64,512]{2,1,0:T(8,128)(2,1)S(1)} %get-tuple-element.73.merged, s16[272,128]{1,0:T(8,128)(2,1)S(1)} %get-tuple-element.79.refs_0_, ...), custom_call_target="tpu_custom_call", output_to_operand_aliasing={{0}: (3, {}), {1}: (4, {})} | custom-call | flops 1024 | bytes 1024 | tf_op jit(solution)/shard_map/energy/pallas_call | solution.py:568
Async XLA Ops:
  7.0 3.2 %collective-permute-start = (bf16[24,16,512]{2,1,0:T(8,128)(2,1)S(1)}, bf16[24,16,512]{2,1,0:T(8,128)(2,1)S(1)}, u32[]{:S(2)}, u32[]{:S(2)}) collective-permute-start(bf16[24,16,512]{2,1,0:T(8,128)(2,1)S(1)} %get-tuple-element.47), channel_id=1, source_target_pairs={{0,1},{1,0},{2,3},{3,2},{4,5},{5,4},{6,7},{7,6},{8,9},{9,8},{10,11... | collective-permute-start | bytes 1179656 | tf_op jit(solution)/shard_map/ppermute | solution.py:619
  7.5 12.5 %collective-permute-start.7 = (bf16[24,16,512]{2,1,0:T(8,128)(2,1)S(1)}, bf16[24,16,512]{2,1,0:T(8,128)(2,1)S(1)}, u32[]{:S(2)}, u32[]{:S(2)}) collective-permute-start(bf16[24,16,512]{2,1,0:T(8,128)(2,1)S(1)} %get-tuple-element.57), channel_id=1, source_target_pairs={{0,2},{1,3},{2,0},{3,1},{4,6},{5,7},{6,4},{7,5},{8,10},{9,11},{10,... | collective-permute-start | bytes 1179656 | tf_op jit(solution)/shard_map/ppermute | solution.py:619
  10.1 17.9 %collective-permute-start.8 = (bf16[24,16,512]{2,1,0:T(8,128)(2,1)S(1)}, bf16[24,16,512]{2,1,0:T(8,128)(2,1)S(1)}, u32[]{:S(2)}, u32[]{:S(2)}) collective-permute-start(bf16[24,16,512]{2,1,0:T(8,128)(2,1)S(1)} %get-tuple-element.58), channel_id=1, source_target_pairs={{0,3},{1,2},{2,1},{3,0},{4,7},{5,6},{6,5},{7,4},{8,11},{9,10},{10,... | collective-permute-start | bytes 1179656 | tf_op jit(solution)/shard_map/ppermute | solution.py:619
  15.6 29.8 %collective-permute-start.4 = (bf16[24,16,512]{2,1,0:T(8,128)(2,1)S(1)}, bf16[24,16,512]{2,1,0:T(8,128)(2,1)S(1)}, u32[]{:S(2)}, u32[]{:S(2)}) collective-permute-start(bf16[24,16,512]{2,1,0:T(8,128)(2,1)S(1)} %get-tuple-element.53), channel_id=1, source_target_pairs={{0,1},{1,0},{2,3},{3,2},{4,5},{5,4},{6,7},{7,6},{8,9},{9,8},{10,11... | collective-permute-start | bytes 1179656 | tf_op jit(solution)/shard_map/ppermute | solution.py:619
  15.8 33.5 %collective-permute-start.5 = (bf16[24,16,512]{2,1,0:T(8,128)(2,1)S(1)}, bf16[24,16,512]{2,1,0:T(8,128)(2,1)S(1)}, u32[]{:S(2)}, u32[]{:S(2)}) collective-permute-start(bf16[24,16,512]{2,1,0:T(8,128)(2,1)S(1)} %get-tuple-element.54), channel_id=1, source_target_pairs={{0,2},{1,3},{2,0},{3,1},{4,6},{5,7},{6,4},{7,5},{8,10},{9,11},{10,... | collective-permute-start | bytes 1179656 | tf_op jit(solution)/shard_map/ppermute | solution.py:619
  17.8 32.4 %collective-permute-start.6 = (bf16[24,16,512]{2,1,0:T(8,128)(2,1)S(1)}, bf16[24,16,512]{2,1,0:T(8,128)(2,1)S(1)}, u32[]{:S(2)}, u32[]{:S(2)}) collective-permute-start(bf16[24,16,512]{2,1,0:T(8,128)(2,1)S(1)} %get-tuple-element.55), channel_id=1, source_target_pairs={{0,3},{1,2},{2,1},{3,0},{4,7},{5,6},{6,5},{7,4},{8,11},{9,10},{10,... | collective-permute-start | bytes 1179656 | tf_op jit(solution)/shard_map/ppermute | solution.py:619
  29.1 5.5 %collective-permute-start.9 = (s16[400,128]{1,0:T(8,128)(2,1)S(1)}, s16[400,128]{1,0:T(8,128)(2,1)S(1)}, u32[]{:S(2)}, u32[]{:S(2)}) collective-permute-start(s16[400,128]{1,0:T(8,128)(2,1)S(1)} %get-tuple-element.61), channel_id=1, source_target_pairs={{0,4},{4,0},{8,12},{12,8},{1,5},{5,1},{9,13},{13,9},{2,6},{6,2},{1... | collective-permute-start | bytes 307208 | tf_op jit(solution)/shard_map/ppermute | solution.py:619
  35.9 7.9 %collective-permute-start.10 = (s16[400,128]{1,0:T(8,128)(2,1)S(1)}, s16[400,128]{1,0:T(8,128)(2,1)S(1)}, u32[]{:S(2)}, u32[]{:S(2)}) collective-permute-start(s16[400,128]{1,0:T(8,128)(2,1)S(1)} %get-tuple-element.63.refs_0_), channel_id=1, source_target_pairs={{0,8},{4,12},{8,0},{12,4},{1,9},{5,13},{9,1},{13,5},{2,10},{6,14},... | collective-permute-start | bytes 307208 | tf_op jit(solution)/shard_map/ppermute | solution.py:619
  38.7 22.6 %collective-permute-start.1 = (bf16[16,16,512]{2,1,0:T(8,128)(2,1)S(1)}, bf16[16,16,512]{2,1,0:T(8,128)(2,1)S(1)}, u32[]{:S(2)}, u32[]{:S(2)}) collective-permute-start(bf16[16,16,512]{2,1,0:T(8,128)(2,1)S(1)} %get-tuple-element.49), channel_id=1, source_target_pairs={{0,1},{1,0},{2,3},{3,2},{4,5},{5,4},{6,7},{7,6},{8,9},{9,8},{10,11... | collective-permute-start | bytes 786440 | tf_op jit(solution)/shard_map/ppermute | solution.py:619
  43.8 17.4 %collective-permute-start.2 = (bf16[16,16,512]{2,1,0:T(8,128)(2,1)S(1)}, bf16[16,16,512]{2,1,0:T(8,128)(2,1)S(1)}, u32[]{:S(2)}, u32[]{:S(2)}) collective-permute-start(bf16[16,16,512]{2,1,0:T(8,128)(2,1)S(1)} %get-tuple-element.50), channel_id=1, source_target_pairs={{0,2},{1,3},{2,0},{3,1},{4,6},{5,7},{6,4},{7,5},{8,10},{9,11},{10,... | collective-permute-start | bytes 786440 | tf_op jit(solution)/shard_map/ppermute | solution.py:619
  45.4 15.9 %collective-permute-start.3 = (bf16[16,16,512]{2,1,0:T(8,128)(2,1)S(1)}, bf16[16,16,512]{2,1,0:T(8,128)(2,1)S(1)}, u32[]{:S(2)}, u32[]{:S(2)}) collective-permute-start(bf16[16,16,512]{2,1,0:T(8,128)(2,1)S(1)} %get-tuple-element.51), channel_id=1, source_target_pairs={{0,3},{1,2},{2,1},{3,0},{4,7},{5,6},{6,5},{7,4},{8,11},{9,10},{10,... | collective-permute-start | bytes 786440 | tf_op jit(solution)/shard_map/ppermute | solution.py:619
  49.4 5.7 %collective-permute-start.12 = (s16[400,128]{1,0:T(8,128)(2,1)S(1)}, s16[400,128]{1,0:T(8,128)(2,1)S(1)}, u32[]{:S(2)}, u32[]{:S(2)}) collective-permute-start(s16[400,128]{1,0:T(8,128)(2,1)S(1)} %get-tuple-element.69.refs_0_), channel_id=1, source_target_pairs={{0,4},{4,0},{8,12},{12,8},{1,5},{5,1},{9,13},{13,9},{2,6},{6,2},{1... | collective-permute-start | bytes 307208 | tf_op jit(solution)/shard_map/ppermute | solution.py:619
  51.2 6.6 %collective-permute-start.11 = (s16[400,128]{1,0:T(8,128)(2,1)S(1)}, s16[400,128]{1,0:T(8,128)(2,1)S(1)}, u32[]{:S(2)}, u32[]{:S(2)}) collective-permute-start(s16[400,128]{1,0:T(8,128)(2,1)S(1)} %get-tuple-element.67), channel_id=1, source_target_pairs={{0,4},{4,0},{8,12},{12,8},{1,5},{5,1},{9,13},{13,9},{2,6},{6,2},{1... | collective-permute-start | bytes 307208 | tf_op jit(solution)/shard_map/ppermute | solution.py:619
  59.2 8.1 %collective-permute-start.16 = (s16[400,128]{1,0:T(8,128)(2,1)S(1)}, s16[400,128]{1,0:T(8,128)(2,1)S(1)}, u32[]{:S(2)}, u32[]{:S(2)}) collective-permute-start(s16[400,128]{1,0:T(8,128)(2,1)S(1)} %get-tuple-element.76.refs_0_), channel_id=1, source_target_pairs={{0,8},{4,12},{8,0},{12,4},{1,9},{5,13},{9,1},{13,5},{2,10},{6,14},... | collective-permute-start | bytes 307208 | tf_op jit(solution)/shard_map/ppermute | solution.py:619
  62.8 10.6 %collective-permute-start.13 = (s16[272,128]{1,0:T(8,128)(2,1)S(1)}, s16[272,128]{1,0:T(8,128)(2,1)S(1)}, u32[]{:S(2)}, u32[]{:S(2)}) collective-permute-start(s16[272,128]{1,0:T(8,128)(2,1)S(1)} %get-tuple-element.74.refs_0_), channel_id=1, source_target_pairs={{0,8},{4,12},{8,0},{12,4},{1,9},{5,13},{9,1},{13,5},{2,10},{6,14},... | collective-permute-start | bytes 208904 | tf_op jit(solution)/shard_map/ppermute | solution.py:619
  63.7 9.7 %collective-permute-start.14 = (s16[272,128]{1,0:T(8,128)(2,1)S(1)}, s16[272,128]{1,0:T(8,128)(2,1)S(1)}, u32[]{:S(2)}, u32[]{:S(2)}) collective-permute-start(s16[272,128]{1,0:T(8,128)(2,1)S(1)} %get-tuple-element.75), channel_id=1, source_target_pairs={{0,4},{4,0},{8,12},{12,8},{1,5},{5,1},{9,13},{13,9},{2,6},{6,2},{1... | collective-permute-start | bytes 208904 | tf_op jit(solution)/shard_map/ppermute | solution.py:619
  65.0 8.4 %collective-permute-start.15 = (s16[272,128]{1,0:T(8,128)(2,1)S(1)}, s16[272,128]{1,0:T(8,128)(2,1)S(1)}, u32[]{:S(2)}, u32[]{:S(2)}) collective-permute-start(s16[272,128]{1,0:T(8,128)(2,1)S(1)} %get-tuple-element.75), channel_id=1, source_target_pairs={{0,12},{4,8},{8,4},{12,0},{1,13},{5,9},{9,5},{13,1},{2,14},{6,10},... | collective-permute-start | bytes 208904 | tf_op jit(solution)/shard_map/ppermute | solution.py:619
  71.0 5.9 %collective-permute-start.18 = (s16[400,128]{1,0:T(8,128)(2,1)S(1)}, s16[400,128]{1,0:T(8,128)(2,1)S(1)}, u32[]{:S(2)}, u32[]{:S(2)}) collective-permute-start(s16[400,128]{1,0:T(8,128)(2,1)S(1)} %get-tuple-element.81.refs_0_), channel_id=1, source_target_pairs={{0,4},{4,0},{8,12},{12,8},{1,5},{5,1},{9,13},{13,9},{2,6},{6,2},{1... | collective-permute-start | bytes 307208 | tf_op jit(solution)/shard_map/ppermute | solution.py:619
  76.9 4.4 %collective-permute-start.17 = (s16[272,128]{1,0:T(8,128)(2,1)S(1)}, s16[272,128]{1,0:T(8,128)(2,1)S(1)}, u32[]{:S(2)}, u32[]{:S(2)}) collective-permute-start(s16[272,128]{1,0:T(8,128)(2,1)S(1)} %get-tuple-element.79.refs_0_), channel_id=1, source_target_pairs={{0,4},{4,0},{8,12},{12,8},{1,5},{5,1},{9,13},{13,9},{2,6},{6,2},{1... | collective-permute-start | bytes 208904 | tf_op jit(solution)/shard_map/ppermute | solution.py:619

commit v11 on v10

--- a/solution.py
+++ b/solution.py
@@ -604,10 +604,10 @@
     return SIZES, ORDER
 
 
-SIZES = [24, 24, 16]
+SIZES = [40, 24]
 ORDER = (
-    ("T", 0), ("T", 1), ("G", 0), ("A", 0), ("F", 0), ("G", 1), ("E", 0), ("A", 1),
-    ("G", 2), ("F", 1), ("F", 2), ("E", 1), ("E", 2),
+    ("T", 0), ("T", 1), ("G", 0), ("A", 0), ("G", 1), ("F", 0), ("F", 1), ("E", 0),
+    ("E", 1),
 )
 
 
@@ -634,7 +634,7 @@
 
     def do_transform(c):
         nonlocal token
-        joint = [k for k in range(c, len(sizes)) if k == c or ("T", k) not in order]
+        joint = [k for k in range(c, len(sizes)) if k == c or c and ("T", k) not in order]
         out, done = transform(
             snapshots, weight, freq_index, peers, [(starts[k], sizes[k]) for k in joint], token
         )

time: 84.3 us -> 81.7 us (0.969)
  waiting for transfers between devices: 23.1 us -> 32.2 us
  Pallas kernels: 37.4 us -> 31 us
  starting transfers between devices: 22.6 us -> 17.4 us
    ppermute x19 -> x13, waiting for transfers between devices: 23.1 us -> 32.2 us  [permute(): return lax.ppermute(x, axis, pairs)]
    ppermute x19 -> x13, starting transfers between devices: 22.6 us -> 17.4 us  [permute(): return lax.ppermute(x, axis, pairs)]
    pallas_call x2, Pallas kernels: 11.8 us -> 9.74 us  [transform(): pl.pallas_call(functools.partial(transform_kernel, peers, parts, group),...]
    pallas_call x3 -> x2, Pallas kernels: 11.2 us -> 9.25 us  [solve(): pl.pallas_call(functools.partial(solve_kernel, len(parts), number, half_r...]
    pallas_call x3 -> x2, Pallas kernels: 8.14 us -> 6.8 us  [filtered(): pl.pallas_call(functools.partial(energy_kernel, slots, direct, len(pieces...]
    pallas_call x2 -> x1, Pallas kernels: 2.6 us -> 2.01 us  [add(): pl.pallas_call(add_kernel, in_specs=[whole_spec()] * 2 + [any_spec()] * l...]
    pallas_call x3 -> x2, Pallas kernels: 3.72 us -> 3.17 us  [gram(): pl.pallas_call(functools.partial(gram_kernel, peers, slots, direct, len(a...]
  transfers between devices with their start and end apart: 19 -> 13, of which waited for: 6 -> 5; matrix products, arithmetic and copies ran while one was open for 0% -> 0% of each run, Pallas kernels for 34% -> 27%
where the time goes in v11:
time: 81.7 us; the launch traced here: 81.5 us
  waiting for transfers between devices  32.2 us (39%)
  Pallas kernels  31 us (38%)
  starting transfers between devices  17.4 us (21%)
  between operations  0.86 us (1%)
    ppermute x13, waiting for transfers between devices, permute(): return lax.ppermute(x, axis, pairs)  32.2 us
    ppermute x13, starting transfers between devices, permute(): return lax.ppermute(x, axis, pairs)  17.4 us
    pallas_call x2, Pallas kernels, transform(): pl.pallas_call(functools.partial(transform_kernel, peers, parts, group),...  9.74 us
    pallas_call x2, Pallas kernels, solve(): pl.pallas_call(functools.partial(solve_kernel, len(parts), number, half_r...  9.25 us
    pallas_call x2, Pallas kernels, filtered(): pl.pallas_call(functools.partial(energy_kernel, slots, direct, len(pieces...  6.8 us
    pallas_call x2, Pallas kernels, gram(): pl.pallas_call(functools.partial(gram_kernel, peers, slots, direct, len(a...  3.17 us
    pallas_call x1, Pallas kernels, add(): pl.pallas_call(add_kernel, in_specs=[whole_spec()] * 2 + [any_spec()] * l...  2.01 us
  transfers between devices with their start and end apart: 13, of which 5 were waited for; matrix products, arithmetic and copies ran while one was open for 0% of the time, Pallas kernels for 27%

profile of v11, /device:TPU:0, one launch (start us, length us, event | category | flops | bytes accessed | tf_op | source)
XLA Modules:
  0.0 81.5 jit_solution(14650126977776813589)
XLA Ops:
  0.6 5.4 %transform.2 = (bf16[40,16,512]{2,1,0:T(8,128)(2,1)S(1)}, bf16[40,16,512]{2,1,0:T(8,128)(2,1)S(1)}, bf16[40,16,512]{2,1,0:T(8,128)(2,1)S(1)}, bf16[40,16,512]{2,1,0:T(8,128)(2,1)S(1)}, f32[8,128]{1,0:T(8,128)S(1)}) custom-call(s32[256]{0:T(256)} %refs_0_.3, f32[1,256]{1,0:T(1,128)} %bitcast.1, bf16[16,512,256]{2,1,0:T(8,128)(2,1)} %refs_2_.3), custom_call_target="tpu_custom_call" | custom-call | flops 1024 | bytes 1024 | tf_op jit(solution)/shard_map/transform/pallas_call | solution.py:149
  6.1 0.5 collective-permute-start
  6.6 2.6 %collective-permute-start.4 = (bf16[40,16,512]{2,1,0:T(8,128)(2,1)S(1)}, bf16[40,16,512]{2,1,0:T(8,128)(2,1)S(1)}, u32[]{:S(2)}, u32[]{:S(2)}) collective-permute-start(bf16[40,16,512]{2,1,0:T(8,128)(2,1)S(1)} %get-tuple-element.38), channel_id=1, source_target_pairs={{0,2},{1,3},{2,0},{3,1},{4,6},{5,7},{6,4},{7,5},{8,10},{9,11},{10,... | collective-permute-start | bytes 1966088 | tf_op jit(solution)/shard_map/ppermute | solution.py:619
  9.2 0.1 collective-permute-start.5
  9.2 0.0 collective-permute-done.refs_4_.refs_1_
  9.2 4.3 %transform.3 = (bf16[24,16,512]{2,1,0:T(8,128)(2,1)S(1)}, bf16[24,16,512]{2,1,0:T(8,128)(2,1)S(1)}, bf16[24,16,512]{2,1,0:T(8,128)(2,1)S(1)}, bf16[24,16,512]{2,1,0:T(8,128)(2,1)S(1)}, f32[8,128]{1,0:T(8,128)S(1)}) custom-call(s32[256]{0:T(256)} %refs_0_.3, f32[1,256]{1,0:T(1,128)} %bitcast.2, bf16[16,512,256]{2,1,0:T(8,128)(2,1)} %refs_2_.3, ...), custom_call_target="tpu_custom_call" | custom-call | flops 1024 | bytes 1024 | tf_op jit(solution)/shard_map/transform/pallas_call | solution.py:149
  13.5 0.2 collective-permute-start.1
  13.7 2.0 %collective-permute-start.2 = (bf16[24,16,512]{2,1,0:T(8,128)(2,1)S(1)}, bf16[24,16,512]{2,1,0:T(8,128)(2,1)S(1)}, u32[]{:S(2)}, u32[]{:S(2)}) collective-permute-start(bf16[24,16,512]{2,1,0:T(8,128)(2,1)S(1)} %get-tuple-element.35), channel_id=1, source_target_pairs={{0,2},{1,3},{2,0},{3,1},{4,6},{5,7},{6,4},{7,5},{8,10},{9,11},{10,... | collective-permute-start | bytes 1179656 | tf_op jit(solution)/shard_map/ppermute | solution.py:619
  15.7 0.0 collective-permute-start.3
  15.7 9.0 %collective-permute-done.4.refs_2_ = bf16[40,16,512]{2,1,0:T(8,128)(2,1)S(1)} collective-permute-done((bf16[40,16,512]{2,1,0:T(8,128)(2,1)S(1)}, bf16[40,16,512]{2,1,0:T(8,128)(2,1)S(1)}, u32[]{:S(2)}, u32[]{:S(2)}) %collective-permute-start.4) | collective-permute-done | bytes 655392 | tf_op jit(solution)/shard_map/ppermute | solution.py:619
  24.7 13.5 %collective-permute-done.5.refs_3_ = bf16[40,16,512]{2,1,0:T(8,128)(2,1)S(1)} collective-permute-done((bf16[40,16,512]{2,1,0:T(8,128)(2,1)S(1)}, bf16[40,16,512]{2,1,0:T(8,128)(2,1)S(1)}, u32[]{:S(2)}, u32[]{:S(2)}) %collective-permute-start.5) | collective-permute-done | bytes 655392 | tf_op jit(solution)/shard_map/ppermute | solution.py:619
  38.3 1.5 %gram.2 = (bf16[40,64,512]{2,1,0:T(8,128)(2,1)S(1)}, f32[8,128]{1,0:T(8,128)S(1)}, f32[20,64,128]{2,1,0:T(8,128)S(1)}, s16[672,128]{1,0:T(8,128)(2,1)S(1)}) custom-call(bf16[40,16,512]{2,1,0:T(8,128)(2,1)S(1)} %get-tuple-element.37.refs_0_, bf16[40,16,512]{2,1,0:T(8,128)(2,1)S(1)} %collective-permute-done.refs_4_.refs_1_, ...), custom_call_target="tpu_custom_call" | custom-call | flops 1024 | bytes 1024 | tf_op jit(solution)/shard_map/gram/pallas_call | solution.py:371
  39.7 1.7 %collective-permute-start.6 = (s16[672,128]{1,0:T(8,128)(2,1)S(1)}, s16[672,128]{1,0:T(8,128)(2,1)S(1)}, u32[]{:S(2)}, u32[]{:S(2)}) collective-permute-start(s16[672,128]{1,0:T(8,128)(2,1)S(1)} %get-tuple-element.42), channel_id=1, source_target_pairs={{0,4},{4,0},{8,12},{12,8},{1,5},{5,1},{9,13},{13,9},{2,6},{6,2},{1... | collective-permute-start | bytes 516104 | tf_op jit(solution)/shard_map/ppermute | solution.py:619
  41.4 5.3 %collective-permute-done.6.other = s16[672,128]{1,0:T(8,128)(2,1)S(1)} collective-permute-done((s16[672,128]{1,0:T(8,128)(2,1)S(1)}, s16[672,128]{1,0:T(8,128)(2,1)S(1)}, u32[]{:S(2)}, u32[]{:S(2)}) %collective-permute-start.6) | collective-permute-done | bytes 172064 | tf_op jit(solution)/shard_map/ppermute | solution.py:619
  46.7 2.0 %add.1 = (s16[672,128]{1,0:T(8,128)(2,1)S(1)}, f32[8,128]{1,0:T(8,128)S(1)}) custom-call(f32[20,64,128]{2,1,0:T(8,128)S(1)} %get-tuple-element.41.own, s16[672,128]{1,0:T(8,128)(2,1)S(1)} %collective-permute-done.6.other, f32[8,128]{1,0:T(8,128)S(1)} %get-tuple-element.43.refs_0_), custom_call_target="tpu_custom_call" | custom-call | flops 1024 | bytes 1024 | tf_op jit(solution)/shard_map/add/pallas_call | solution.py:395
  48.7 2.8 %collective-permute-start.10 = (s16[672,128]{1,0:T(8,128)(2,1)S(1)}, s16[672,128]{1,0:T(8,128)(2,1)S(1)}, u32[]{:S(2)}, u32[]{:S(2)}) collective-permute-start(s16[672,128]{1,0:T(8,128)(2,1)S(1)} %get-tuple-element.48.refs_0_), channel_id=1, source_target_pairs={{0,8},{4,12},{8,0},{12,4},{1,9},{5,13},{9,1},{13,5},{2,10},{6,14},... | collective-permute-start | bytes 516104 | tf_op jit(solution)/shard_map/ppermute | solution.py:619
  51.6 0.0 collective-permute-done.1.refs_1_
  51.6 0.0 collective-permute-done.2.refs_2_
  51.6 3.6 %collective-permute-done.3.refs_3_ = bf16[24,16,512]{2,1,0:T(8,128)(2,1)S(1)} collective-permute-done((bf16[24,16,512]{2,1,0:T(8,128)(2,1)S(1)}, bf16[24,16,512]{2,1,0:T(8,128)(2,1)S(1)}, u32[]{:S(2)}, u32[]{:S(2)}) %collective-permute-start.3) | collective-permute-done | bytes 393248 | tf_op jit(solution)/shard_map/ppermute | solution.py:619
  55.1 1.7 %gram.3 = (bf16[24,64,512]{2,1,0:T(8,128)(2,1)S(1)}, f32[8,128]{1,0:T(8,128)S(1)}, s16[400,128]{1,0:T(8,128)(2,1)S(1)}, s16[400,128]{1,0:T(8,128)(2,1)S(1)}) custom-call(bf16[24,16,512]{2,1,0:T(8,128)(2,1)S(1)} %get-tuple-element.33.refs_0_, bf16[24,16,512]{2,1,0:T(8,128)(2,1)S(1)} %collective-permute-done.1.refs_1_, ...), custom_call_target="tpu_custom_call" | custom-call | flops 1024 | bytes 1024 | tf_op jit(solution)/shard_map/gram/pallas_call | solution.py:371
  56.8 2.7 %collective-permute-start.7 = (s16[400,128]{1,0:T(8,128)(2,1)S(1)}, s16[400,128]{1,0:T(8,128)(2,1)S(1)}, u32[]{:S(2)}, u32[]{:S(2)}) collective-permute-start(s16[400,128]{1,0:T(8,128)(2,1)S(1)} %get-tuple-element.46.refs_0_), channel_id=1, source_target_pairs={{0,8},{4,12},{8,0},{12,4},{1,9},{5,13},{9,1},{13,5},{2,10},{6,14},... | collective-permute-start | bytes 307208 | tf_op jit(solution)/shard_map/ppermute | solution.py:619
  59.5 1.3 %collective-permute-start.9 = (s16[400,128]{1,0:T(8,128)(2,1)S(1)}, s16[400,128]{1,0:T(8,128)(2,1)S(1)}, u32[]{:S(2)}, u32[]{:S(2)}) collective-permute-start(s16[400,128]{1,0:T(8,128)(2,1)S(1)} %get-tuple-element.47), channel_id=1, source_target_pairs={{0,12},{4,8},{8,4},{12,0},{1,13},{5,9},{9,5},{13,1},{2,14},{6,10},... | collective-permute-start | bytes 307208 | tf_op jit(solution)/shard_map/ppermute | solution.py:619
  60.9 0.2 collective-permute-start.8
  61.1 0.0 collective-permute-done.10.refs_1_
  61.1 5.2 %filters.2 = (s16[672,128]{1,0:T(8,128)(2,1)S(1)}, f32[8,128]{1,0:T(8,128)S(1)}) custom-call(s16[672,128]{1,0:T(8,128)(2,1)S(1)} %get-tuple-element.48.refs_0_, s16[672,128]{1,0:T(8,128)(2,1)S(1)} %collective-permute-done.10.refs_1_, f32[8,128]{1,0:T(8,128)S(1)} %get-tuple-element.49.refs_2_), custom_call_target="tpu_custom_call" | custom-call | flops 1024 | bytes 1024 | tf_op jit(solution)/shard_map/filters/pallas_call | solution.py:493
  66.3 1.9 %collective-permute-start.12 = (s16[672,128]{1,0:T(8,128)(2,1)S(1)}, s16[672,128]{1,0:T(8,128)(2,1)S(1)}, u32[]{:S(2)}, u32[]{:S(2)}) collective-permute-start(s16[672,128]{1,0:T(8,128)(2,1)S(1)} %get-tuple-element.53.refs_0_), channel_id=1, source_target_pairs={{0,4},{4,0},{8,12},{12,8},{1,5},{5,1},{9,13},{13,9},{2,6},{6,2},{1... | collective-permute-start | bytes 516104 | tf_op jit(solution)/shard_map/ppermute | solution.py:619
  68.2 0.0 collective-permute-done.7.refs_1_
  68.2 0.0 collective-permute-done.9.refs_3_
  68.2 0.8 %collective-permute-done.8.refs_2_ = s16[400,128]{1,0:T(8,128)(2,1)S(1)} collective-permute-done((s16[400,128]{1,0:T(8,128)(2,1)S(1)}, s16[400,128]{1,0:T(8,128)(2,1)S(1)}, u32[]{:S(2)}, u32[]{:S(2)}) %collective-permute-start.8) | collective-permute-done | bytes 102432 | tf_op jit(solution)/shard_map/ppermute | solution.py:619
  69.0 4.1 %filters.3 = (s16[400,128]{1,0:T(8,128)(2,1)S(1)}, f32[8,128]{1,0:T(8,128)S(1)}) custom-call(s16[400,128]{1,0:T(8,128)(2,1)S(1)} %get-tuple-element.46.refs_0_, s16[400,128]{1,0:T(8,128)(2,1)S(1)} %collective-permute-done.7.refs_1_, s16[400,128]{1,0:T(8,128)(2,1)S(1)} %collective-permute-done.8.refs_2_, s16[400,128]{1,0:T(8,128)(2,1)S(1)} %collective-permute-done.9.refs_3_, ...), custom_call_target="tpu_custom_call" | custom-call | flops 1024 | bytes 1024 | tf_op jit(solution)/shard_map/filters/pallas_call | solution.py:493
  73.1 1.4 %collective-permute-start.11 = (s16[400,128]{1,0:T(8,128)(2,1)S(1)}, s16[400,128]{1,0:T(8,128)(2,1)S(1)}, u32[]{:S(2)}, u32[]{:S(2)}) collective-permute-start(s16[400,128]{1,0:T(8,128)(2,1)S(1)} %get-tuple-element.51.refs_0_), channel_id=1, source_target_pairs={{0,4},{4,0},{8,12},{12,8},{1,5},{5,1},{9,13},{13,9},{2,6},{6,2},{1... | collective-permute-start | bytes 307208 | tf_op jit(solution)/shard_map/ppermute | solution.py:619
  74.5 0.0 collective-permute-done.12.refs_1_
  74.5 3.5 %energy.2 = (f32[64,256]{1,0:T(8,128)}, f32[64,2,64,64]{3,2,1,0:T(8,128)}, f32[8,128]{1,0:T(8,128)S(1)}) custom-call(bf16[40,64,512]{2,1,0:T(8,128)(2,1)S(1)} %get-tuple-element.52.merged, s16[672,128]{1,0:T(8,128)(2,1)S(1)} %get-tuple-element.53.refs_0_, s16[672,128]{1,0:T(8,128)(2,1)S(1)} %collective-permute-done.12.refs_1_, ...), custom_call_target="tpu_custom_call" | custom-call | flops 1024 | bytes 1024 | tf_op jit(solution)/shard_map/energy/pallas_call | solution.py:568
  78.0 0.0 collective-permute-done.11.refs_1_
  78.0 3.3 %energy.3 = (f32[64,256]{1,0:T(8,128)}, f32[64,2,64,64]{3,2,1,0:T(8,128)}, f32[8,128]{1,0:T(8,128)}) custom-call(bf16[24,64,512]{2,1,0:T(8,128)(2,1)S(1)} %get-tuple-element.45.merged, s16[400,128]{1,0:T(8,128)(2,1)S(1)} %get-tuple-element.51.refs_0_, ...), custom_call_target="tpu_custom_call", output_to_operand_aliasing={{0}: (3, {}), {1}: (4, {})} | custom-call | flops 1024 | bytes 1024 | tf_op jit(solution)/shard_map/energy/pallas_call | solution.py:568
Async XLA Ops:
  6.1 3.2 %collective-permute-start = (bf16[40,16,512]{2,1,0:T(8,128)(2,1)S(1)}, bf16[40,16,512]{2,1,0:T(8,128)(2,1)S(1)}, u32[]{:S(2)}, u32[]{:S(2)}) collective-permute-start(bf16[40,16,512]{2,1,0:T(8,128)(2,1)S(1)} %get-tuple-element.32), channel_id=1, source_target_pairs={{0,1},{1,0},{2,3},{3,2},{4,5},{5,4},{6,7},{7,6},{8,9},{9,8},{10,11... | collective-permute-start | bytes 1966088 | tf_op jit(solution)/shard_map/ppermute | solution.py:619
  6.6 18.1 %collective-permute-start.4 = (bf16[40,16,512]{2,1,0:T(8,128)(2,1)S(1)}, bf16[40,16,512]{2,1,0:T(8,128)(2,1)S(1)}, u32[]{:S(2)}, u32[]{:S(2)}) collective-permute-start(bf16[40,16,512]{2,1,0:T(8,128)(2,1)S(1)} %get-tuple-element.38), channel_id=1, source_target_pairs={{0,2},{1,3},{2,0},{3,1},{4,6},{5,7},{6,4},{7,5},{8,10},{9,11},{10,... | collective-permute-start | bytes 1966088 | tf_op jit(solution)/shard_map/ppermute | solution.py:619
  9.2 29.1 %collective-permute-start.5 = (bf16[40,16,512]{2,1,0:T(8,128)(2,1)S(1)}, bf16[40,16,512]{2,1,0:T(8,128)(2,1)S(1)}, u32[]{:S(2)}, u32[]{:S(2)}) collective-permute-start(bf16[40,16,512]{2,1,0:T(8,128)(2,1)S(1)} %get-tuple-element.39), channel_id=1, source_target_pairs={{0,3},{1,2},{2,1},{3,0},{4,7},{5,6},{6,5},{7,4},{8,11},{9,10},{10,... | collective-permute-start | bytes 1966088 | tf_op jit(solution)/shard_map/ppermute | solution.py:619
  13.5 38.0 %collective-permute-start.1 = (bf16[24,16,512]{2,1,0:T(8,128)(2,1)S(1)}, bf16[24,16,512]{2,1,0:T(8,128)(2,1)S(1)}, u32[]{:S(2)}, u32[]{:S(2)}) collective-permute-start(bf16[24,16,512]{2,1,0:T(8,128)(2,1)S(1)} %get-tuple-element.34), channel_id=1, source_target_pairs={{0,1},{1,0},{2,3},{3,2},{4,5},{5,4},{6,7},{7,6},{8,9},{9,8},{10,11... | collective-permute-start | bytes 1179656 | tf_op jit(solution)/shard_map/ppermute | solution.py:619
  13.7 37.8 %collective-permute-start.2 = (bf16[24,16,512]{2,1,0:T(8,128)(2,1)S(1)}, bf16[24,16,512]{2,1,0:T(8,128)(2,1)S(1)}, u32[]{:S(2)}, u32[]{:S(2)}) collective-permute-start(bf16[24,16,512]{2,1,0:T(8,128)(2,1)S(1)} %get-tuple-element.35), channel_id=1, source_target_pairs={{0,2},{1,3},{2,0},{3,1},{4,6},{5,7},{6,4},{7,5},{8,10},{9,11},{10,... | collective-permute-start | bytes 1179656 | tf_op jit(solution)/shard_map/ppermute | solution.py:619
  15.7 39.4 %collective-permute-start.3 = (bf16[24,16,512]{2,1,0:T(8,128)(2,1)S(1)}, bf16[24,16,512]{2,1,0:T(8,128)(2,1)S(1)}, u32[]{:S(2)}, u32[]{:S(2)}) collective-permute-start(bf16[24,16,512]{2,1,0:T(8,128)(2,1)S(1)} %get-tuple-element.36), channel_id=1, source_target_pairs={{0,3},{1,2},{2,1},{3,0},{4,7},{5,6},{6,5},{7,4},{8,11},{9,10},{10,... | collective-permute-start | bytes 1179656 | tf_op jit(solution)/shard_map/ppermute | solution.py:619
  39.7 7.0 %collective-permute-start.6 = (s16[672,128]{1,0:T(8,128)(2,1)S(1)}, s16[672,128]{1,0:T(8,128)(2,1)S(1)}, u32[]{:S(2)}, u32[]{:S(2)}) collective-permute-start(s16[672,128]{1,0:T(8,128)(2,1)S(1)} %get-tuple-element.42), channel_id=1, source_target_pairs={{0,4},{4,0},{8,12},{12,8},{1,5},{5,1},{9,13},{13,9},{2,6},{6,2},{1... | collective-permute-start | bytes 516104 | tf_op jit(solution)/shard_map/ppermute | solution.py:619
  48.7 12.4 %collective-permute-start.10 = (s16[672,128]{1,0:T(8,128)(2,1)S(1)}, s16[672,128]{1,0:T(8,128)(2,1)S(1)}, u32[]{:S(2)}, u32[]{:S(2)}) collective-permute-start(s16[672,128]{1,0:T(8,128)(2,1)S(1)} %get-tuple-element.48.refs_0_), channel_id=1, source_target_pairs={{0,8},{4,12},{8,0},{12,4},{1,9},{5,13},{9,1},{13,5},{2,10},{6,14},... | collective-permute-start | bytes 516104 | tf_op jit(solution)/shard_map/ppermute | solution.py:619
  56.8 11.3 %collective-permute-start.7 = (s16[400,128]{1,0:T(8,128)(2,1)S(1)}, s16[400,128]{1,0:T(8,128)(2,1)S(1)}, u32[]{:S(2)}, u32[]{:S(2)}) collective-permute-start(s16[400,128]{1,0:T(8,128)(2,1)S(1)} %get-tuple-element.46.refs_0_), channel_id=1, source_target_pairs={{0,8},{4,12},{8,0},{12,4},{1,9},{5,13},{9,1},{13,5},{2,10},{6,14},... | collective-permute-start | bytes 307208 | tf_op jit(solution)/shard_map/ppermute | solution.py:619
  59.5 8.6 %collective-permute-start.9 = (s16[400,128]{1,0:T(8,128)(2,1)S(1)}, s16[400,128]{1,0:T(8,128)(2,1)S(1)}, u32[]{:S(2)}, u32[]{:S(2)}) collective-permute-start(s16[400,128]{1,0:T(8,128)(2,1)S(1)} %get-tuple-element.47), channel_id=1, source_target_pairs={{0,12},{4,8},{8,4},{12,0},{1,13},{5,9},{9,5},{13,1},{2,14},{6,10},... | collective-permute-start | bytes 307208 | tf_op jit(solution)/shard_map/ppermute | solution.py:619
  60.9 8.1 %collective-permute-start.8 = (s16[400,128]{1,0:T(8,128)(2,1)S(1)}, s16[400,128]{1,0:T(8,128)(2,1)S(1)}, u32[]{:S(2)}, u32[]{:S(2)}) collective-permute-start(s16[400,128]{1,0:T(8,128)(2,1)S(1)} %get-tuple-element.47), channel_id=1, source_target_pairs={{0,4},{4,0},{8,12},{12,8},{1,5},{5,1},{9,13},{13,9},{2,6},{6,2},{1... | collective-permute-start | bytes 307208 | tf_op jit(solution)/shard_map/ppermute | solution.py:619
  66.3 8.2 %collective-permute-start.12 = (s16[672,128]{1,0:T(8,128)(2,1)S(1)}, s16[672,128]{1,0:T(8,128)(2,1)S(1)}, u32[]{:S(2)}, u32[]{:S(2)}) collective-permute-start(s16[672,128]{1,0:T(8,128)(2,1)S(1)} %get-tuple-element.53.refs_0_), channel_id=1, source_target_pairs={{0,4},{4,0},{8,12},{12,8},{1,5},{5,1},{9,13},{13,9},{2,6},{6,2},{1... | collective-permute-start | bytes 516104 | tf_op jit(solution)/shard_map/ppermute | solution.py:619
  73.1 4.9 %collective-permute-start.11 = (s16[400,128]{1,0:T(8,128)(2,1)S(1)}, s16[400,128]{1,0:T(8,128)(2,1)S(1)}, u32[]{:S(2)}, u32[]{:S(2)}) collective-permute-start(s16[400,128]{1,0:T(8,128)(2,1)S(1)} %get-tuple-element.51.refs_0_), channel_id=1, source_target_pairs={{0,4},{4,0},{8,12},{12,8},{1,5},{5,1},{9,13},{13,9},{2,6},{6,2},{1... | collective-permute-start | bytes 307208 | tf_op jit(solution)/shard_map/ppermute | solution.py:619

commit v12 on v11

--- a/solution.py
+++ b/solution.py
@@ -408,8 +408,8 @@
     return high, (x - high.astype(F32)).astype(BF16)
 
 
-def solve_kernel(parts, number, half_rows, *refs):
-    ins, out, token = refs[:parts], refs[-2], refs[-1]
+def solve_kernel(chunks, half_rows, *refs):
+    out, token = refs[-2:]
     token[...] = jnp.zeros_like(token)
     width = out.shape[1]
     half = width // 2
@@ -418,16 +418,26 @@
     lane = lax.broadcasted_iota(jnp.int32, shape, 1)
     eye = jnp.where(row == lane, F32(1), F32(0))
 
-    if parts == 1:
-        sums = [ins[0][i] for i in range(number)]
-    else:
-        found = [spread(*read_coded(r, number, half_rows)) for r in ins]
-        sums = [p + q for p, q in zip(found[0], found[1])]
+    sums, at = [], 0
+    for parts, count in chunks:
+        ins, at = refs[at : at + parts], at + parts
+        if parts == 1:
+            sums += [ins[0][i] for i in range(count)]
+            continue
+        found = [spread(*read_coded(r, count, half_rows)) for r in ins]
+        added = each(lambda p, q: p + q, found[0], found[1])
         if parts == 4:
-            sums = [p + (q + r) for p, q, r in zip(sums, found[2], found[3])]
+            added = each(lambda p, q, r: p + (q + r), added, found[2], found[3])
+        sums += added
+    number = len(sums)
     both_halves = each(unpack, sums)
     grams = [h[0] for h in both_halves]
-    shift = each(lambda g: jnp.sum(g * eye, keepdims=True) * F32(1.0 / half), grams)
+    spots = lax.broadcasted_iota(jnp.int32, sums[0].shape, 1)
+    lines = lax.broadcasted_iota(jnp.int32, sums[0].shape, 0)
+    on = (spots == lines) | (spots == lines + 3 * half_rows)
+    shift = each(
+        lambda p: jnp.sum(jnp.where(on, p, F32(0)), keepdims=True) * F32(1.0 / half), sums
+    )
     eye_low = jnp.where(row + half == lane, F32(1), F32(0))
     inverse = each(lambda m: 1.0 / m, shift)
     system = each(lambda g, m: g * m + eye, grams, inverse)
@@ -488,11 +498,14 @@
     write_coded(out, values, codes)
 
 
-def solve(parts, number, half_rows, after):
-    width = parts[0].shape[-1]
+def solve(chunks, half_rows, after):
+    args = [x for parts, _ in chunks for x in parts]
+    width = args[0].shape[-1]
+    number = sum(count for _, count in chunks)
+    shape = [(len(parts), count) for parts, count in chunks]
     return pl.pallas_call(
-        functools.partial(solve_kernel, len(parts), number, half_rows),
-        in_specs=[whole_spec()] * len(parts) + [any_spec()] * len(after),
+        functools.partial(solve_kernel, shape, half_rows),
+        in_specs=[whole_spec()] * len(args) + [any_spec()] * len(after),
         out_specs=[whole_spec()] * 2,
         out_shape=[
             jax.ShapeDtypeStruct((coded_rows(number, half_rows), width), jnp.int16),
@@ -501,16 +514,17 @@
         compiler_params=params(),
         cost_estimate=light(),
         name="filters",
-    )(*parts, *after)
-
-
-def energy_kernel(slots, direct, number, first, merged, *refs):
-    pieces = refs[:number]
+    )(*args, *after)
+
+
+def energy_kernel(slots, direct, number, chunks, first, *refs):
+    merged, pieces = refs[:chunks], refs[chunks : chunks + number]
     energies_out, filters_out, token, energies, filters, energies_sem, filters_sem = refs[-7:]
     token[...] = jnp.zeros_like(token)
-    count, blocks, width = merged.shape
+    blocks, width = merged[0].shape[1:]
     entries = width // 2
-    per_slot = count // slots
+    counts = [m.shape[0] for m in merged]
+    per_slot = sum(counts) // slots
     half_rows = blocks // 2
     states = entries * lax.axis_size("space")
     puts = []
@@ -524,35 +538,39 @@
         gains = F32(states) / total
         codes = jnp.where(lane_low(codes.shape, blocks), codes, swap(codes))
         products = outer(scale_of(codes), per_slot)
-        for begin in range(0, per_slot, 4):
-            some = range(begin, min(begin + 4, per_slot))
-            at = [owner * per_slot + i for i in some]
-            z = [merged[f] for f in at]
-            scale = [products[i] * F32(0.5 / TOP) for i in some]
-            halves = each(unpack, [values[i] for i in some], scale)
-            compact = [h[0] for h in halves]
-            both = each(
-                lambda h: jnp.concatenate([h[0].astype(BF16), h[1].astype(BF16)], 0), halves
-            )
-            gain = [gains[i : i + 1] for i in some]
-            w = each(lambda v: jnp.concatenate([v[:, :entries], v[:, entries:]], 0), z)
-            r = each(dot, both, w)
-            energy = each(
-                lambda v, t: jnp.sum(v * v, axis=0, keepdims=True) * t, r, gain
-            )
-            for f, c, e in zip(at, compact, energy):
-                filters[f, 0] = c[:, :blocks]
-                filters[f, 1] = c[:, blocks:]
-                energies[pl.ds(f, 1), :] = e
-            put = pltpu.make_async_copy(
-                filters.at[pl.ds(at[0], len(at))],
-                filters_out.at[pl.ds(first + at[0], len(at))],
-                filters_sem.at[len(puts)],
-            )
-            put.start()
-            puts.append(put)
+        base = 0
+        for chunk, count in enumerate(counts):
+            own = count // slots
+            size = 4 if own % 4 == 0 else 1
+            for begin in range(0, own, size):
+                start = sum(counts[:chunk]) + owner * own + begin
+                some = range(base + begin, base + begin + size)
+                z = [merged[chunk][owner * own + begin + i] for i in range(size)]
+                scale = [products[i] * F32(0.5 / TOP) for i in some]
+                halves = each(unpack, [values[i] for i in some], scale)
+                both = each(
+                    lambda h: jnp.concatenate([h[0].astype(BF16), h[1].astype(BF16)], 0), halves
+                )
+                w = each(lambda v: jnp.concatenate([v[:, :entries], v[:, entries:]], 0), z)
+                r = each(dot, both, w)
+                gain = [gains[i : i + 1] for i in some]
+                energy = each(
+                    lambda v, t: jnp.sum(v * v, axis=0, keepdims=True) * t, r, gain
+                )
+                for i in range(size):
+                    filters[start + i, 0] = halves[i][0][:, :blocks]
+                    filters[start + i, 1] = halves[i][0][:, blocks:]
+                    energies[pl.ds(start + i, 1), :] = energy[i]
+                put = pltpu.make_async_copy(
+                    filters.at[pl.ds(start, size)],
+                    filters_out.at[pl.ds(first + start, size)],
+                    filters_sem.at[len(puts)],
+                )
+                put.start()
+                puts.append(put)
+            base += own
     put = pltpu.make_async_copy(
-        energies, energies_out.at[pl.ds(first, count)], energies_sem.at[0]
+        energies, energies_out.at[pl.ds(first, sum(counts))], energies_sem.at[0]
     )
     put.start()
     for p in [*puts, put]:
@@ -560,13 +578,15 @@
 
 
 def filtered(merged, pieces, slots, direct, carry, owned, first, after):
-    count, blocks, width = merged.shape
+    _, blocks, width = merged[0].shape
+    count = sum(m.shape[0] for m in merged)
+    copies = sum(slots * (m.shape[0] // slots) for m in merged)
     entries = width // 2
-    fixed = 1 + len(pieces)
-    args = [merged, *pieces] + ([] if carry is None else list(carry)) + list(after)
+    fixed = len(merged) + len(pieces)
+    args = [*merged, *pieces] + ([] if carry is None else list(carry)) + list(after)
     hbm = pl.BlockSpec(memory_space=pltpu.HBM)
     return pl.pallas_call(
-        functools.partial(energy_kernel, slots, direct, len(pieces), first),
+        functools.partial(energy_kernel, slots, direct, len(pieces), len(merged), first),
         in_specs=[whole_spec()] * fixed
         + ([] if carry is None else [hbm] * 2)
         + [any_spec()] * len(after),
@@ -581,7 +601,7 @@
             pltpu.VMEM((count, entries), F32),
             pltpu.VMEM((count, 2, blocks, blocks), F32),
             pltpu.SemaphoreType.DMA((1,)),
-            pltpu.SemaphoreType.DMA((slots * -(-(count // slots) // 4),)),
+            pltpu.SemaphoreType.DMA((copies,)),
         ],
         compiler_params=params(),
         cost_estimate=light(),
@@ -604,10 +624,10 @@
     return SIZES, ORDER
 
 
-SIZES = [40, 24]
+SIZES = [24, 24, 16]
 ORDER = (
-    ("T", 0), ("T", 1), ("G", 0), ("A", 0), ("G", 1), ("F", 0), ("F", 1), ("E", 0),
-    ("E", 1),
+    ("T", 0), ("T", 1), ("G", 0), ("A", 0), ("G", 1), ("F", 0), ("A", 1), ("G", 2),
+    ("E", 0), ("F", 1), ("E", 1),
 )
 
 
@@ -666,10 +686,16 @@
         token = [done]
         parts[c] = [half, permute(half, "space", 2)]
 
+    def joined(stage, c):
+        last = c + 1
+        while last < len(sizes) and (stage, last) not in order:
+            last += 1
+        return range(c, last)
+
     def do_solve(c):
         nonlocal token
-        count = sizes[c] // halves
-        own, done = solve(parts[c], count, merged[c].shape[1] // 2, token)
+        work = [(parts[k], sizes[k] // halves) for k in joined("F", c)]
+        own, done = solve(work, merged[c].shape[1] // 2, token)
         token = [done]
         if paired:
             pieces[c] = [own, permute(own, "space", 1)]
@@ -678,8 +704,9 @@
 
     def do_energy(c):
         nonlocal token, carry
+        work = [merged[k] for k in joined("E", c)]
         *carry, done = filtered(
-            merged[c], pieces[c], halves, paired, carry, owned, starts[c], token
+            work, pieces[c], halves, paired, carry, owned, starts[c], token
         )
         token = [done]
 

time: 81.7 us -> 80.9 us (level)
  waiting for transfers between devices: 32.2 us -> 26 us
  starting transfers between devices: 17.4 us -> 21.9 us
  Pallas kernels: 31 us -> 32.1 us
    ppermute x13 -> x18, waiting for transfers between devices: 32.2 us -> 26 us  [permute(): return lax.ppermute(x, axis, pairs)]
    ppermute x13 -> x18, starting transfers between devices: 17.4 us -> 21.9 us  [permute(): return lax.ppermute(x, axis, pairs)]
    pallas_call x1 -> x2, Pallas kernels: 2.01 us -> 2.59 us  [add(): pl.pallas_call(add_kernel, in_specs=[whole_spec()] * 2 + [any_spec()] * l...]
    pallas_call x2 -> x3, Pallas kernels: 3.17 us -> 3.71 us  [gram(): pl.pallas_call(functools.partial(gram_kernel, peers, slots, direct, len(a...]
  transfers between devices with their start and end apart: 13 -> 18, of which waited for: 5 -> 8; matrix products, arithmetic and copies ran while one was open for 0% -> 0% of each run, Pallas kernels for 27% -> 23%
where the time goes in v12:
time: 80.9 us; the launch traced here: 80.8 us
  Pallas kernels  32.1 us (40%)
  waiting for transfers between devices  26 us (32%)
  starting transfers between devices  21.9 us (27%)
  between operations  0.88 us (1%)
    ppermute x18, waiting for transfers between devices, permute(): return lax.ppermute(x, axis, pairs)  26 us
    ppermute x18, starting transfers between devices, permute(): return lax.ppermute(x, axis, pairs)  21.9 us
    pallas_call x2, Pallas kernels, transform(): pl.pallas_call(functools.partial(transform_kernel, peers, parts, group),...  9.73 us
    pallas_call x2, Pallas kernels, solve(): pl.pallas_call(functools.partial(solve_kernel, shape, half_rows), in_spec...  8.77 us
    pallas_call x2, Pallas kernels, filtered(): pl.pallas_call(functools.partial(energy_kernel, slots, direct, len(pieces...  7.26 us
    pallas_call x3, Pallas kernels, gram(): pl.pallas_call(functools.partial(gram_kernel, peers, slots, direct, len(a...  3.71 us
    pallas_call x2, Pallas kernels, add(): pl.pallas_call(add_kernel, in_specs=[whole_spec()] * 2 + [any_spec()] * l...  2.59 us
  transfers between devices with their start and end apart: 18, of which 8 were waited for; matrix products, arithmetic and copies ran while one was open for 0% of the time, Pallas kernels for 23%

profile of v12, /device:TPU:0, one launch (start us, length us, event | category | flops | bytes accessed | tf_op | source)
XLA Modules:
  0.0 80.8 jit_solution(2314046921829147567)
XLA Ops:
  0.6 4.3 %transform.2 = (bf16[24,16,512]{2,1,0:T(8,128)(2,1)S(1)}, bf16[24,16,512]{2,1,0:T(8,128)(2,1)S(1)}, bf16[24,16,512]{2,1,0:T(8,128)(2,1)S(1)}, bf16[24,16,512]{2,1,0:T(8,128)(2,1)S(1)}, f32[8,128]{1,0:T(8,128)S(1)}) custom-call(s32[256]{0:T(256)} %refs_0_.3, f32[1,256]{1,0:T(1,128)} %bitcast.1, bf16[16,512,256]{2,1,0:T(8,128)(2,1)} %refs_2_.3), custom_call_target="tpu_custom_call" | custom-call | flops 1024 | bytes 1024 | tf_op jit(solution)/shard_map/transform/pallas_call | solution.py:149
  4.9 0.5 collective-permute-start
  5.5 2.6 %collective-permute-start.4 = (bf16[24,16,512]{2,1,0:T(8,128)(2,1)S(1)}, bf16[24,16,512]{2,1,0:T(8,128)(2,1)S(1)}, u32[]{:S(2)}, u32[]{:S(2)}) collective-permute-start(bf16[24,16,512]{2,1,0:T(8,128)(2,1)S(1)} %get-tuple-element.48), channel_id=1, source_target_pairs={{0,2},{1,3},{2,0},{3,1},{4,6},{5,7},{6,4},{7,5},{8,10},{9,11},{10,... | collective-permute-start | bytes 1179656 | tf_op jit(solution)/shard_map/ppermute | solution.py:639
  8.0 0.1 collective-permute-start.5
  8.1 0.0 collective-permute-done.refs_4_.refs_1_
  8.1 5.4 %transform.3 = (bf16[24,16,512]{2,1,0:T(8,128)(2,1)S(1)}, bf16[24,16,512]{2,1,0:T(8,128)(2,1)S(1)}, bf16[24,16,512]{2,1,0:T(8,128)(2,1)S(1)}, bf16[24,16,512]{2,...) custom-call(s32[256]{0:T(256)} %refs_0_.3, ...), custom_call_target="tpu_custom_call" | custom-call | flops 1024 | bytes 1024 | tf_op jit(solution)/shard_map/transform/pallas_call | solution.py:149
  13.5 0.2 collective-permute-start.1
  13.7 1.9 %collective-permute-start.2 = (bf16[24,16,512]{2,1,0:T(8,128)(2,1)S(1)}, bf16[24,16,512]{2,1,0:T(8,128)(2,1)S(1)}, u32[]{:S(2)}, u32[]{:S(2)}) collective-permute-start(bf16[24,16,512]{2,1,0:T(8,128)(2,1)S(1)} %get-tuple-element.45), channel_id=1, source_target_pairs={{0,2},{1,3},{2,0},{3,1},{4,6},{5,7},{6,4},{7,5},{8,10},{9,11},{10,... | collective-permute-start | bytes 1179656 | tf_op jit(solution)/shard_map/ppermute | solution.py:639
  15.7 0.0 collective-permute-start.3
  15.7 2.3 %collective-permute-done.4.refs_2_ = bf16[24,16,512]{2,1,0:T(8,128)(2,1)S(1)} collective-permute-done((bf16[24,16,512]{2,1,0:T(8,128)(2,1)S(1)}, bf16[24,16,512]{2,1,0:T(8,128)(2,1)S(1)}, u32[]{:S(2)}, u32[]{:S(2)}) %collective-permute-start.4) | collective-permute-done | bytes 393248 | tf_op jit(solution)/shard_map/ppermute | solution.py:639
  18.0 7.9 %collective-permute-done.5.refs_3_ = bf16[24,16,512]{2,1,0:T(8,128)(2,1)S(1)} collective-permute-done((bf16[24,16,512]{2,1,0:T(8,128)(2,1)S(1)}, bf16[24,16,512]{2,1,0:T(8,128)(2,1)S(1)}, u32[]{:S(2)}, u32[]{:S(2)}) %collective-permute-start.5) | collective-permute-done | bytes 393248 | tf_op jit(solution)/shard_map/ppermute | solution.py:639
  25.9 1.1 %gram.3 = (bf16[24,64,512]{2,1,0:T(8,128)(2,1)S(1)}, f32[8,128]{1,0:T(8,128)S(1)}, f32[12,64,128]{2,1,0:T(8,128)S(1)}, s16[400,128]{1,0:T(8,128)(2,1)S(1)}) custom-call(bf16[24,16,512]{2,1,0:T(8,128)(2,1)S(1)} %get-tuple-element.47.refs_0_, bf16[24,16,512]{2,1,0:T(8,128)(2,1)S(1)} %collective-permute-done.refs_4_.refs_1_, ...), custom_call_target="tpu_custom_call" | custom-call | flops 1024 | bytes 1024 | tf_op jit(solution)/shard_map/gram/pallas_call | solution.py:371
  27.0 1.7 %collective-permute-start.6 = (s16[400,128]{1,0:T(8,128)(2,1)S(1)}, s16[400,128]{1,0:T(8,128)(2,1)S(1)}, u32[]{:S(2)}, u32[]{:S(2)}) collective-permute-start(s16[400,128]{1,0:T(8,128)(2,1)S(1)} %get-tuple-element.52), channel_id=1, source_target_pairs={{0,4},{4,0},{8,12},{12,8},{1,5},{5,1},{9,13},{13,9},{2,6},{6,2},{1... | collective-permute-start | bytes 307208 | tf_op jit(solution)/shard_map/ppermute | solution.py:639
  28.7 0.5 collective-permute-start.7
  29.2 3.3 %collective-permute-done.6.other = s16[400,128]{1,0:T(8,128)(2,1)S(1)} collective-permute-done((s16[400,128]{1,0:T(8,128)(2,1)S(1)}, s16[400,128]{1,0:T(8,128)(2,1)S(1)}, u32[]{:S(2)}, u32[]{:S(2)}) %collective-permute-start.6) | collective-permute-done | bytes 102432 | tf_op jit(solution)/shard_map/ppermute | solution.py:639
  32.5 1.7 %collective-permute-start.8 = (bf16[16,16,512]{2,1,0:T(8,128)(2,1)S(1)}, bf16[16,16,512]{2,1,0:T(8,128)(2,1)S(1)}, u32[]{:S(2)}, u32[]{:S(2)}) collective-permute-start(bf16[16,16,512]{2,1,0:T(8,128)(2,1)S(1)} %get-tuple-element.58), channel_id=1, source_target_pairs={{0,2},{1,3},{2,0},{3,1},{4,6},{5,7},{6,4},{7,5},{8,10},{9,11},{10,... | collective-permute-start | bytes 786440 | tf_op jit(solution)/shard_map/ppermute | solution.py:639
  34.2 0.0 collective-permute-done.1.refs_1_
  34.2 0.0 collective-permute-start.9
  34.2 1.3 %add.2 = (s16[400,128]{1,0:T(8,128)(2,1)S(1)}, f32[8,128]{1,0:T(8,128)S(1)}) custom-call(f32[12,64,128]{2,1,0:T(8,128)S(1)} %get-tuple-element.51.own, s16[400,128]{1,0:T(8,128)(2,1)S(1)} %collective-permute-done.6.other, f32[8,128]{1,0:T(8,128)S(1)} %get-tuple-element.53.refs_0_), custom_call_target="tpu_custom_call" | custom-call | flops 1024 | bytes 1024 | tf_op jit(solution)/shard_map/add/pallas_call | solution.py:395
  35.5 0.0 collective-permute-done.2.refs_2_
  35.5 2.7 %collective-permute-start.11 = (s16[400,128]{1,0:T(8,128)(2,1)S(1)}, s16[400,128]{1,0:T(8,128)(2,1)S(1)}, u32[]{:S(2)}, u32[]{:S(2)}) collective-permute-start(s16[400,128]{1,0:T(8,128)(2,1)S(1)} %get-tuple-element.62.refs_0_), channel_id=1, source_target_pairs={{0,8},{4,12},{8,0},{12,4},{1,9},{5,13},{9,1},{13,5},{2,10},{6,14},... | collective-permute-start | bytes 307208 | tf_op jit(solution)/shard_map/ppermute | solution.py:639
  38.2 4.6 %collective-permute-done.3.refs_3_ = bf16[24,16,512]{2,1,0:T(8,128)(2,1)S(1)} collective-permute-done((bf16[24,16,512]{2,1,0:T(8,128)(2,1)S(1)}, bf16[24,16,512]{2,1,0:T(8,128)(2,1)S(1)}, u32[]{:S(2)}, u32[]{:S(2)}) %collective-permute-start.3) | collective-permute-done | bytes 393248 | tf_op jit(solution)/shard_map/ppermute | solution.py:639
  42.7 1.1 %gram.4 = (bf16[24,64,512]{2,1,0:T(8,128)(2,1)S(1)}, f32[8,128]{1,0:T(8,128)S(1)}, f32[12,64,128]{2,1,0:T(8,128)S(1)}, s16[400,128]{1,0:T(8,128)(2,1)S(1)}) custom-call(bf16[24,16,512]{2,1,0:T(8,128)(2,1)S(1)} %get-tuple-element.43.refs_0_, bf16[24,16,512]{2,1,0:T(8,128)(2,1)S(1)} %collective-permute-done.1.refs_1_, ...), custom_call_target="tpu_custom_call" | custom-call | flops 1024 | bytes 1024 | tf_op jit(solution)/shard_map/gram/pallas_call | solution.py:371
  43.9 1.7 %collective-permute-start.10 = (s16[400,128]{1,0:T(8,128)(2,1)S(1)}, s16[400,128]{1,0:T(8,128)(2,1)S(1)}, u32[]{:S(2)}, u32[]{:S(2)}) collective-permute-start(s16[400,128]{1,0:T(8,128)(2,1)S(1)} %get-tuple-element.61), channel_id=1, source_target_pairs={{0,4},{4,0},{8,12},{12,8},{1,5},{5,1},{9,13},{13,9},{2,6},{6,2},{1... | collective-permute-start | bytes 307208 | tf_op jit(solution)/shard_map/ppermute | solution.py:639
  45.6 0.0 collective-permute-done.11.refs_1_
  45.6 3.9 %filters.2 = (s16[400,128]{1,0:T(8,128)(2,1)S(1)}, f32[8,128]{1,0:T(8,128)S(1)}) custom-call(s16[400,128]{1,0:T(8,128)(2,1)S(1)} %get-tuple-element.62.refs_0_, s16[400,128]{1,0:T(8,128)(2,1)S(1)} %collective-permute-done.11.refs_1_, f32[8,128]{1,0:T(8,128)S(1)} %get-tuple-element.63.refs_2_), custom_call_target="tpu_custom_call" | custom-call | flops 1024 | bytes 1024 | tf_op jit(solution)/shard_map/filters/pallas_call | solution.py:506
  49.5 0.5 collective-permute-start.16
  50.0 0.0 collective-permute-done.10.other
  50.0 1.3 %add.3 = (s16[400,128]{1,0:T(8,128)(2,1)S(1)}, f32[8,128]{1,0:T(8,128)S(1)}) custom-call(f32[12,64,128]{2,1,0:T(8,128)S(1)} %get-tuple-element.60.own, s16[400,128]{1,0:T(8,128)(2,1)S(1)} %collective-permute-done.10.other, f32[8,128]{1,0:T(8,128)S(1)} %get-tuple-element.64.refs_0_), custom_call_target="tpu_custom_call" | custom-call | flops 1024 | bytes 1024 | tf_op jit(solution)/shard_map/add/pallas_call | solution.py:395
  51.3 2.7 %collective-permute-start.12 = (s16[400,128]{1,0:T(8,128)(2,1)S(1)}, s16[400,128]{1,0:T(8,128)(2,1)S(1)}, u32[]{:S(2)}, u32[]{:S(2)}) collective-permute-start(s16[400,128]{1,0:T(8,128)(2,1)S(1)} %get-tuple-element.67.refs_0_), channel_id=1, source_target_pairs={{0,8},{4,12},{8,0},{12,4},{1,9},{5,13},{9,1},{13,5},{2,10},{6,14},... | collective-permute-start | bytes 307208 | tf_op jit(solution)/shard_map/ppermute | solution.py:639
  54.0 0.0 collective-permute-done.7.refs_1_
  54.0 0.0 collective-permute-done.8.refs_2_
  54.0 0.0 collective-permute-done.9.refs_3_
  54.0 1.5 %gram.5 = (bf16[16,64,512]{2,1,0:T(8,128)(2,1)S(1)}, f32[8,128]{1,0:T(8,128)S(1)}, s16[272,128]{1,0:T(8,128)(2,1)S(1)}, s16[272,128]{1,0:T(8,128)(2,1)S(1)}) custom-call(bf16[16,16,512]{2,1,0:T(8,128)(2,1)S(1)} %get-tuple-element.56.refs_0_, bf16[16,16,512]{2,1,0:T(8,128)(2,1)S(1)} %collective-permute-done.7.refs_1_, ...), custom_call_target="tpu_custom_call" | custom-call | flops 1024 | bytes 1024 | tf_op jit(solution)/shard_map/gram/pallas_call | solution.py:371
  55.5 2.7 %collective-permute-start.13 = (s16[272,128]{1,0:T(8,128)(2,1)S(1)}, s16[272,128]{1,0:T(8,128)(2,1)S(1)}, u32[]{:S(2)}, u32[]{:S(2)}) collective-permute-start(s16[272,128]{1,0:T(8,128)(2,1)S(1)} %get-tuple-element.68.refs_2_), channel_id=1, source_target_pairs={{0,8},{4,12},{8,0},{12,4},{1,9},{5,13},{9,1},{13,5},{2,10},{6,14},... | collective-permute-start | bytes 208904 | tf_op jit(solution)/shard_map/ppermute | solution.py:639
  58.2 1.3 %collective-permute-start.15 = (s16[272,128]{1,0:T(8,128)(2,1)S(1)}, s16[272,128]{1,0:T(8,128)(2,1)S(1)}, u32[]{:S(2)}, u32[]{:S(2)}) collective-permute-start(s16[272,128]{1,0:T(8,128)(2,1)S(1)} %get-tuple-element.69), channel_id=1, source_target_pairs={{0,12},{4,8},{8,4},{12,0},{1,13},{5,9},{9,5},{13,1},{2,14},{6,10},... | collective-permute-start | bytes 208904 | tf_op jit(solution)/shard_map/ppermute | solution.py:639
  59.5 0.2 collective-permute-start.14
  59.8 0.0 collective-permute-done.16.refs_2_
  59.8 2.9 %energy.2 = (f32[64,256]{1,0:T(8,128)}, f32[64,2,64,64]{3,2,1,0:T(8,128)}, f32[8,128]{1,0:T(8,128)S(1)}) custom-call(bf16[24,64,512]{2,1,0:T(8,128)(2,1)S(1)} %get-tuple-element.70.refs_0_, s16[400,128]{1,0:T(8,128)(2,1)S(1)} %get-tuple-element.71.refs_1_, s16[400,128]{1,0:T(8,128)(2,1)S(1)} %collective-permute-done.16.refs_2_, ...), custom_call_target="tpu_custom_call" | custom-call | flops 1024 | bytes 1024 | tf_op jit(solution)/shard_map/energy/pallas_call | solution.py:588
  62.6 0.3 collective-permute-done.13.refs_3_
  62.9 2.1 %collective-permute-done.15.refs_5_ = s16[272,128]{1,0:T(8,128)(2,1)S(1)} collective-permute-done((s16[272,128]{1,0:T(8,128)(2,1)S(1)}, s16[272,128]{1,0:T(8,128)(2,1)S(1)}, u32[]{:S(2)}, u32[]{:S(2)}) %collective-permute-start.15) | collective-permute-done | bytes 69664 | tf_op jit(solution)/shard_map/ppermute | solution.py:639
  65.0 0.5 collective-permute-done.14.refs_4_
  65.5 0.0 collective-permute-done.12.refs_1_
  65.5 4.9 %filters.3 = (s16[672,128]{1,0:T(8,128)(2,1)S(1)}, f32[8,128]{1,0:T(8,128)S(1)}) custom-call(s16[400,128]{1,0:T(8,128)(2,1)S(1)} %get-tuple-element.67.refs_0_, s16[400,128]{1,0:T(8,128)(2,1)S(1)} %collective-permute-done.12.refs_1_, s16[272,128]{1,0:T(8,128)(2,1)S(1)} %get-tuple-element.68.refs_2_, s16[272,128]{1,0:T(8,128)(2,1)S(1)} %collective-permute-done.13.refs_3_, ...), custom_call_target="tpu_custom_call" | custom-call | flops 1024 | bytes 1024 | tf_op jit(solution)/shard_map/filters/pallas_call | solution.py:506
  70.3 0.9 %collective-permute-start.17 = (s16[672,128]{1,0:T(8,128)(2,1)S(1)}, s16[672,128]{1,0:T(8,128)(2,1)S(1)}, u32[]{:S(2)}, u32[]{:S(2)}) collective-permute-start(s16[672,128]{1,0:T(8,128)(2,1)S(1)} %get-tuple-element.74.refs_2_), channel_id=1, source_target_pairs={{0,4},{4,0},{8,12},{12,8},{1,5},{5,1},{9,13},{13,9},{2,6},{6,2},{1... | collective-permute-start | bytes 516104 | tf_op jit(solution)/shard_map/ppermute | solution.py:639
  71.2 5.0 %collective-permute-done.17.refs_3_ = s16[672,128]{1,0:T(8,128)(2,1)S(1)} collective-permute-done((s16[672,128]{1,0:T(8,128)(2,1)S(1)}, s16[672,128]{1,0:T(8,128)(2,1)S(1)}, u32[]{:S(2)}, u32[]{:S(2)}) %collective-permute-start.17) | collective-permute-done | bytes 172064 | tf_op jit(solution)/shard_map/ppermute | solution.py:639
  76.2 4.4 %energy.3 = (f32[64,256]{1,0:T(8,128)}, f32[64,2,64,64]{3,2,1,0:T(8,128)}, f32[8,128]{1,0:T(8,128)}) custom-call(bf16[24,64,512]{2,1,0:T(8,128)(2,1)S(1)} %get-tuple-element.55.refs_0_, bf16[16,64,512]{2,1,0:T(8,128)(2,1)S(1)} %get-tuple-element.66.refs_1_, ...), custom_call_target="tpu_custom_call", output_to_operand_aliasing={{0}: (4, {}), {1}: (5, {})} | custom-call | flops 1024 | bytes 1024 | tf_op jit(solution)/shard_map/energy/pallas_call | solution.py:588
Async XLA Ops:
  4.9 3.2 %collective-permute-start = (bf16[24,16,512]{2,1,0:T(8,128)(2,1)S(1)}, bf16[24,16,512]{2,1,0:T(8,128)(2,1)S(1)}, u32[]{:S(2)}, u32[]{:S(2)}) collective-permute-start(bf16[24,16,512]{2,1,0:T(8,128)(2,1)S(1)} %get-tuple-element.42), channel_id=1, source_target_pairs={{0,1},{1,0},{2,3},{3,2},{4,5},{5,4},{6,7},{7,6},{8,9},{9,8},{10,11... | collective-permute-start | bytes 1179656 | tf_op jit(solution)/shard_map/ppermute | solution.py:639
  5.5 12.5 %collective-permute-start.4 = (bf16[24,16,512]{2,1,0:T(8,128)(2,1)S(1)}, bf16[24,16,512]{2,1,0:T(8,128)(2,1)S(1)}, u32[]{:S(2)}, u32[]{:S(2)}) collective-permute-start(bf16[24,16,512]{2,1,0:T(8,128)(2,1)S(1)} %get-tuple-element.48), channel_id=1, source_target_pairs={{0,2},{1,3},{2,0},{3,1},{4,6},{5,7},{6,4},{7,5},{8,10},{9,11},{10,... | collective-permute-start | bytes 1179656 | tf_op jit(solution)/shard_map/ppermute | solution.py:639
  8.0 17.9 %collective-permute-start.5 = (bf16[24,16,512]{2,1,0:T(8,128)(2,1)S(1)}, bf16[24,16,512]{2,1,0:T(8,128)(2,1)S(1)}, u32[]{:S(2)}, u32[]{:S(2)}) collective-permute-start(bf16[24,16,512]{2,1,0:T(8,128)(2,1)S(1)} %get-tuple-element.49), channel_id=1, source_target_pairs={{0,3},{1,2},{2,1},{3,0},{4,7},{5,6},{6,5},{7,4},{8,11},{9,10},{10,... | collective-permute-start | bytes 1179656 | tf_op jit(solution)/shard_map/ppermute | solution.py:639
  13.5 20.7 %collective-permute-start.1 = (bf16[24,16,512]{2,1,0:T(8,128)(2,1)S(1)}, bf16[24,16,512]{2,1,0:T(8,128)(2,1)S(1)}, u32[]{:S(2)}, u32[]{:S(2)}) collective-permute-start(bf16[24,16,512]{2,1,0:T(8,128)(2,1)S(1)} %get-tuple-element.44), channel_id=1, source_target_pairs={{0,1},{1,0},{2,3},{3,2},{4,5},{5,4},{6,7},{7,6},{8,9},{9,8},{10,11... | collective-permute-start | bytes 1179656 | tf_op jit(solution)/shard_map/ppermute | solution.py:639
  13.7 21.8 %collective-permute-start.2 = (bf16[24,16,512]{2,1,0:T(8,128)(2,1)S(1)}, bf16[24,16,512]{2,1,0:T(8,128)(2,1)S(1)}, u32[]{:S(2)}, u32[]{:S(2)}) collective-permute-start(bf16[24,16,512]{2,1,0:T(8,128)(2,1)S(1)} %get-tuple-element.45), channel_id=1, source_target_pairs={{0,2},{1,3},{2,0},{3,1},{4,6},{5,7},{6,4},{7,5},{8,10},{9,11},{10,... | collective-permute-start | bytes 1179656 | tf_op jit(solution)/shard_map/ppermute | solution.py:639
  15.7 27.1 %collective-permute-start.3 = (bf16[24,16,512]{2,1,0:T(8,128)(2,1)S(1)}, bf16[24,16,512]{2,1,0:T(8,128)(2,1)S(1)}, u32[]{:S(2)}, u32[]{:S(2)}) collective-permute-start(bf16[24,16,512]{2,1,0:T(8,128)(2,1)S(1)} %get-tuple-element.46), channel_id=1, source_target_pairs={{0,3},{1,2},{2,1},{3,0},{4,7},{5,6},{6,5},{7,4},{8,11},{9,10},{10,... | collective-permute-start | bytes 1179656 | tf_op jit(solution)/shard_map/ppermute | solution.py:639
  27.0 5.5 %collective-permute-start.6 = (s16[400,128]{1,0:T(8,128)(2,1)S(1)}, s16[400,128]{1,0:T(8,128)(2,1)S(1)}, u32[]{:S(2)}, u32[]{:S(2)}) collective-permute-start(s16[400,128]{1,0:T(8,128)(2,1)S(1)} %get-tuple-element.52), channel_id=1, source_target_pairs={{0,4},{4,0},{8,12},{12,8},{1,5},{5,1},{9,13},{13,9},{2,6},{6,2},{1... | collective-permute-start | bytes 307208 | tf_op jit(solution)/shard_map/ppermute | solution.py:639
  28.7 25.3 %collective-permute-start.7 = (bf16[16,16,512]{2,1,0:T(8,128)(2,1)S(1)}, bf16[16,16,512]{2,1,0:T(8,128)(2,1)S(1)}, u32[]{:S(2)}, u32[]{:S(2)}) collective-permute-start(bf16[16,16,512]{2,1,0:T(8,128)(2,1)S(1)} %get-tuple-element.57), channel_id=1, source_target_pairs={{0,1},{1,0},{2,3},{3,2},{4,5},{5,4},{6,7},{7,6},{8,9},{9,8},{10,11... | collective-permute-start | bytes 786440 | tf_op jit(solution)/shard_map/ppermute | solution.py:639
  32.5 21.5 %collective-permute-start.8 = (bf16[16,16,512]{2,1,0:T(8,128)(2,1)S(1)}, bf16[16,16,512]{2,1,0:T(8,128)(2,1)S(1)}, u32[]{:S(2)}, u32[]{:S(2)}) collective-permute-start(bf16[16,16,512]{2,1,0:T(8,128)(2,1)S(1)} %get-tuple-element.58), channel_id=1, source_target_pairs={{0,2},{1,3},{2,0},{3,1},{4,6},{5,7},{6,4},{7,5},{8,10},{9,11},{10,... | collective-permute-start | bytes 786440 | tf_op jit(solution)/shard_map/ppermute | solution.py:639
  34.2 19.8 %collective-permute-start.9 = (bf16[16,16,512]{2,1,0:T(8,128)(2,1)S(1)}, bf16[16,16,512]{2,1,0:T(8,128)(2,1)S(1)}, u32[]{:S(2)}, u32[]{:S(2)}) collective-permute-start(bf16[16,16,512]{2,1,0:T(8,128)(2,1)S(1)} %get-tuple-element.59), channel_id=1, source_target_pairs={{0,3},{1,2},{2,1},{3,0},{4,7},{5,6},{6,5},{7,4},{8,11},{9,10},{10,... | collective-permute-start | bytes 786440 | tf_op jit(solution)/shard_map/ppermute | solution.py:639
  35.5 10.1 %collective-permute-start.11 = (s16[400,128]{1,0:T(8,128)(2,1)S(1)}, s16[400,128]{1,0:T(8,128)(2,1)S(1)}, u32[]{:S(2)}, u32[]{:S(2)}) collective-permute-start(s16[400,128]{1,0:T(8,128)(2,1)S(1)} %get-tuple-element.62.refs_0_), channel_id=1, source_target_pairs={{0,8},{4,12},{8,0},{12,4},{1,9},{5,13},{9,1},{13,5},{2,10},{6,14},... | collective-permute-start | bytes 307208 | tf_op jit(solution)/shard_map/ppermute | solution.py:639
  43.9 6.1 %collective-permute-start.10 = (s16[400,128]{1,0:T(8,128)(2,1)S(1)}, s16[400,128]{1,0:T(8,128)(2,1)S(1)}, u32[]{:S(2)}, u32[]{:S(2)}) collective-permute-start(s16[400,128]{1,0:T(8,128)(2,1)S(1)} %get-tuple-element.61), channel_id=1, source_target_pairs={{0,4},{4,0},{8,12},{12,8},{1,5},{5,1},{9,13},{13,9},{2,6},{6,2},{1... | collective-permute-start | bytes 307208 | tf_op jit(solution)/shard_map/ppermute | solution.py:639
  49.5 10.3 %collective-permute-start.16 = (s16[400,128]{1,0:T(8,128)(2,1)S(1)}, s16[400,128]{1,0:T(8,128)(2,1)S(1)}, u32[]{:S(2)}, u32[]{:S(2)}) collective-permute-start(s16[400,128]{1,0:T(8,128)(2,1)S(1)} %get-tuple-element.71.refs_1_), channel_id=1, source_target_pairs={{0,4},{4,0},{8,12},{12,8},{1,5},{5,1},{9,13},{13,9},{2,6},{6,2},{1... | collective-permute-start | bytes 307208 | tf_op jit(solution)/shard_map/ppermute | solution.py:639
  51.3 14.2 %collective-permute-start.12 = (s16[400,128]{1,0:T(8,128)(2,1)S(1)}, s16[400,128]{1,0:T(8,128)(2,1)S(1)}, u32[]{:S(2)}, u32[]{:S(2)}) collective-permute-start(s16[400,128]{1,0:T(8,128)(2,1)S(1)} %get-tuple-element.67.refs_0_), channel_id=1, source_target_pairs={{0,8},{4,12},{8,0},{12,4},{1,9},{5,13},{9,1},{13,5},{2,10},{6,14},... | collective-permute-start | bytes 307208 | tf_op jit(solution)/shard_map/ppermute | solution.py:639
  55.5 7.4 %collective-permute-start.13 = (s16[272,128]{1,0:T(8,128)(2,1)S(1)}, s16[272,128]{1,0:T(8,128)(2,1)S(1)}, u32[]{:S(2)}, u32[]{:S(2)}) collective-permute-start(s16[272,128]{1,0:T(8,128)(2,1)S(1)} %get-tuple-element.68.refs_2_), channel_id=1, source_target_pairs={{0,8},{4,12},{8,0},{12,4},{1,9},{5,13},{9,1},{13,5},{2,10},{6,14},... | collective-permute-start | bytes 208904 | tf_op jit(solution)/shard_map/ppermute | solution.py:639
  58.2 6.8 %collective-permute-start.15 = (s16[272,128]{1,0:T(8,128)(2,1)S(1)}, s16[272,128]{1,0:T(8,128)(2,1)S(1)}, u32[]{:S(2)}, u32[]{:S(2)}) collective-permute-start(s16[272,128]{1,0:T(8,128)(2,1)S(1)} %get-tuple-element.69), channel_id=1, source_target_pairs={{0,12},{4,8},{8,4},{12,0},{1,13},{5,9},{9,5},{13,1},{2,14},{6,10},... | collective-permute-start | bytes 208904 | tf_op jit(solution)/shard_map/ppermute | solution.py:639
  59.5 5.9 %collective-permute-start.14 = (s16[272,128]{1,0:T(8,128)(2,1)S(1)}, s16[272,128]{1,0:T(8,128)(2,1)S(1)}, u32[]{:S(2)}, u32[]{:S(2)}) collective-permute-start(s16[272,128]{1,0:T(8,128)(2,1)S(1)} %get-tuple-element.69), channel_id=1, source_target_pairs={{0,4},{4,0},{8,12},{12,8},{1,5},{5,1},{9,13},{13,9},{2,6},{6,2},{1... | collective-permute-start | bytes 208904 | tf_op jit(solution)/shard_map/ppermute | solution.py:639
  70.3 5.9 %collective-permute-start.17 = (s16[672,128]{1,0:T(8,128)(2,1)S(1)}, s16[672,128]{1,0:T(8,128)(2,1)S(1)}, u32[]{:S(2)}, u32[]{:S(2)}) collective-permute-start(s16[672,128]{1,0:T(8,128)(2,1)S(1)} %get-tuple-element.74.refs_2_), channel_id=1, source_target_pairs={{0,4},{4,0},{8,12},{12,8},{1,5},{5,1},{9,13},{13,9},{2,6},{6,2},{1... | collective-permute-start | bytes 516104 | tf_op jit(solution)/shard_map/ppermute | solution.py:639

commit v13 on v12

--- a/solution.py
+++ b/solution.py
@@ -559,7 +559,7 @@
                 )
                 for i in range(size):
                     filters[start + i, 0] = halves[i][0][:, :blocks]
-                    filters[start + i, 1] = halves[i][0][:, blocks:]
+                    filters[start + i, 1] = -halves[i][1][:, :blocks]
                     energies[pl.ds(start + i, 1), :] = energy[i]
                 put = pltpu.make_async_copy(
                     filters.at[pl.ds(start, size)],
@@ -627,7 +627,7 @@
 SIZES = [24, 24, 16]
 ORDER = (
     ("T", 0), ("T", 1), ("G", 0), ("A", 0), ("G", 1), ("F", 0), ("A", 1), ("G", 2),
-    ("E", 0), ("F", 1), ("E", 1),
+    ("E", 0), ("F", 1), ("F", 2), ("E", 1), ("E", 2),
 )
 
 

time: 80.9 us -> 77.3 us (0.956)
  waiting for transfers between devices: 26 us -> 18.8 us
  Pallas kernels: 32.1 us -> 34.1 us
  starting transfers between devices: 21.9 us -> 23.3 us
    ppermute x18 -> x19, waiting for transfers between devices: 26 us -> 18.8 us  [permute(): return lax.ppermute(x, axis, pairs)]
    pallas_call x2 -> x3, Pallas kernels: 8.77 us -> 11 us  [solve(): pl.pallas_call(functools.partial(solve_kernel, shape, half_rows), in_spec...]
    ppermute x18 -> x19, starting transfers between devices: 21.9 us -> 23.3 us  [permute(): return lax.ppermute(x, axis, pairs)]
    pallas_call x2 -> x3, Pallas kernels: 7.26 us -> 7.03 us  [filtered(): pl.pallas_call(functools.partial(energy_kernel, slots, direct, len(pieces...]
  transfers between devices with their start and end apart: 18 -> 19, of which waited for: 8 -> 5; matrix products, arithmetic and copies ran while one was open for 0% -> 0% of each run, Pallas kernels for 23% -> 36%
where the time goes in v13:
time: 77.3 us; the launch traced here: 77.1 us
  Pallas kernels  34.1 us (44%)
  starting transfers between devices  23.3 us (30%)
  waiting for transfers between devices  18.8 us (24%)
  between operations  0.9 us (1%)
    ppermute x19, starting transfers between devices, permute(): return lax.ppermute(x, axis, pairs)  23.3 us
    ppermute x19, waiting for transfers between devices, permute(): return lax.ppermute(x, axis, pairs)  18.8 us
    pallas_call x3, Pallas kernels, solve(): pl.pallas_call(functools.partial(solve_kernel, shape, half_rows), in_spec...  11 us
    pallas_call x2, Pallas kernels, transform(): pl.pallas_call(functools.partial(transform_kernel, peers, parts, group),...  9.73 us
    pallas_call x3, Pallas kernels, filtered(): pl.pallas_call(functools.partial(energy_kernel, slots, direct, len(pieces...  7.03 us
    pallas_call x3, Pallas kernels, gram(): pl.pallas_call(functools.partial(gram_kernel, peers, slots, direct, len(a...  3.71 us
    pallas_call x2, Pallas kernels, add(): pl.pallas_call(add_kernel, in_specs=[whole_spec()] * 2 + [any_spec()] * l...  2.6 us
  transfers between devices with their start and end apart: 19, of which 5 were waited for; matrix products, arithmetic and copies ran while one was open for 0% of the time, Pallas kernels for 36%

profile of v13, /device:TPU:0, one launch (start us, length us, event | category | flops | bytes accessed | tf_op | source)
XLA Modules:
  0.0 77.1 jit_solution(16543177068409458486)
XLA Ops:
  0.6 4.3 %transform.2 = (bf16[24,16,512]{2,1,0:T(8,128)(2,1)S(1)}, bf16[24,16,512]{2,1,0:T(8,128)(2,1)S(1)}, bf16[24,16,512]{2,1,0:T(8,128)(2,1)S(1)}, bf16[24,16,512]{2,1,0:T(8,128)(2,1)S(1)}, f32[8,128]{1,0:T(8,128)S(1)}) custom-call(s32[256]{0:T(256)} %refs_0_.3, f32[1,256]{1,0:T(1,128)} %bitcast.1, bf16[16,512,256]{2,1,0:T(8,128)(2,1)} %refs_2_.3), custom_call_target="tpu_custom_call" | custom-call | flops 1024 | bytes 1024 | tf_op jit(solution)/shard_map/transform/pallas_call | solution.py:149
  4.9 0.5 collective-permute-start
  5.5 2.6 %collective-permute-start.7 = (bf16[24,16,512]{2,1,0:T(8,128)(2,1)S(1)}, bf16[24,16,512]{2,1,0:T(8,128)(2,1)S(1)}, u32[]{:S(2)}, u32[]{:S(2)}) collective-permute-start(bf16[24,16,512]{2,1,0:T(8,128)(2,1)S(1)} %get-tuple-element.57), channel_id=1, source_target_pairs={{0,2},{1,3},{2,0},{3,1},{4,6},{5,7},{6,4},{7,5},{8,10},{9,11},{10,... | collective-permute-start | bytes 1179656 | tf_op jit(solution)/shard_map/ppermute | solution.py:639
  8.0 0.1 collective-permute-start.8
  8.1 0.0 collective-permute-done.refs_4_.refs_1_
  8.1 5.4 %transform.3 = (bf16[24,16,512]{2,1,0:T(8,128)(2,1)S(1)}, bf16[24,16,512]{2,1,0:T(8,128)(2,1)S(1)}, bf16[24,16,512]{2,1,0:T(8,128)(2,1)S(1)}, bf16[24,16,512]{2,...) custom-call(s32[256]{0:T(256)} %refs_0_.3, ...), custom_call_target="tpu_custom_call" | custom-call | flops 1024 | bytes 1024 | tf_op jit(solution)/shard_map/transform/pallas_call | solution.py:149
  13.5 0.2 collective-permute-start.4
  13.7 1.9 %collective-permute-start.5 = (bf16[24,16,512]{2,1,0:T(8,128)(2,1)S(1)}, bf16[24,16,512]{2,1,0:T(8,128)(2,1)S(1)}, u32[]{:S(2)}, u32[]{:S(2)}) collective-permute-start(bf16[24,16,512]{2,1,0:T(8,128)(2,1)S(1)} %get-tuple-element.54), channel_id=1, source_target_pairs={{0,2},{1,3},{2,0},{3,1},{4,6},{5,7},{6,4},{7,5},{8,10},{9,11},{10,... | collective-permute-start | bytes 1179656 | tf_op jit(solution)/shard_map/ppermute | solution.py:639
  15.7 0.0 collective-permute-start.6
  15.7 2.3 %collective-permute-done.7.refs_2_ = bf16[24,16,512]{2,1,0:T(8,128)(2,1)S(1)} collective-permute-done((bf16[24,16,512]{2,1,0:T(8,128)(2,1)S(1)}, bf16[24,16,512]{2,1,0:T(8,128)(2,1)S(1)}, u32[]{:S(2)}, u32[]{:S(2)}) %collective-permute-start.7) | collective-permute-done | bytes 393248 | tf_op jit(solution)/shard_map/ppermute | solution.py:639
  18.0 7.9 %collective-permute-done.8.refs_3_ = bf16[24,16,512]{2,1,0:T(8,128)(2,1)S(1)} collective-permute-done((bf16[24,16,512]{2,1,0:T(8,128)(2,1)S(1)}, bf16[24,16,512]{2,1,0:T(8,128)(2,1)S(1)}, u32[]{:S(2)}, u32[]{:S(2)}) %collective-permute-start.8) | collective-permute-done | bytes 393248 | tf_op jit(solution)/shard_map/ppermute | solution.py:639
  25.9 1.1 %gram.3 = (bf16[24,64,512]{2,1,0:T(8,128)(2,1)S(1)}, f32[8,128]{1,0:T(8,128)S(1)}, f32[12,64,128]{2,1,0:T(8,128)S(1)}, s16[400,128]{1,0:T(8,128)(2,1)S(1)}) custom-call(bf16[24,16,512]{2,1,0:T(8,128)(2,1)S(1)} %get-tuple-element.56.refs_0_, bf16[24,16,512]{2,1,0:T(8,128)(2,1)S(1)} %collective-permute-done.refs_4_.refs_1_, ...), custom_call_target="tpu_custom_call" | custom-call | flops 1024 | bytes 1024 | tf_op jit(solution)/shard_map/gram/pallas_call | solution.py:371
  27.0 1.7 %collective-permute-start.9 = (s16[400,128]{1,0:T(8,128)(2,1)S(1)}, s16[400,128]{1,0:T(8,128)(2,1)S(1)}, u32[]{:S(2)}, u32[]{:S(2)}) collective-permute-start(s16[400,128]{1,0:T(8,128)(2,1)S(1)} %get-tuple-element.61), channel_id=1, source_target_pairs={{0,4},{4,0},{8,12},{12,8},{1,5},{5,1},{9,13},{13,9},{2,6},{6,2},{1... | collective-permute-start | bytes 307208 | tf_op jit(solution)/shard_map/ppermute | solution.py:639
  28.7 0.5 collective-permute-start.1
  29.2 3.3 %collective-permute-done.9.other = s16[400,128]{1,0:T(8,128)(2,1)S(1)} collective-permute-done((s16[400,128]{1,0:T(8,128)(2,1)S(1)}, s16[400,128]{1,0:T(8,128)(2,1)S(1)}, u32[]{:S(2)}, u32[]{:S(2)}) %collective-permute-start.9) | collective-permute-done | bytes 102432 | tf_op jit(solution)/shard_map/ppermute | solution.py:639
  32.5 1.7 %collective-permute-start.2 = (bf16[16,16,512]{2,1,0:T(8,128)(2,1)S(1)}, bf16[16,16,512]{2,1,0:T(8,128)(2,1)S(1)}, u32[]{:S(2)}, u32[]{:S(2)}) collective-permute-start(bf16[16,16,512]{2,1,0:T(8,128)(2,1)S(1)} %get-tuple-element.50), channel_id=1, source_target_pairs={{0,2},{1,3},{2,0},{3,1},{4,6},{5,7},{6,4},{7,5},{8,10},{9,11},{10,... | collective-permute-start | bytes 786440 | tf_op jit(solution)/shard_map/ppermute | solution.py:639
  34.2 0.0 collective-permute-done.4.refs_1_
  34.2 0.0 collective-permute-start.3
  34.2 1.3 %add.2 = (s16[400,128]{1,0:T(8,128)(2,1)S(1)}, f32[8,128]{1,0:T(8,128)S(1)}) custom-call(f32[12,64,128]{2,1,0:T(8,128)S(1)} %get-tuple-element.60.own, s16[400,128]{1,0:T(8,128)(2,1)S(1)} %collective-permute-done.9.other, f32[8,128]{1,0:T(8,128)S(1)} %get-tuple-element.62.refs_0_), custom_call_target="tpu_custom_call" | custom-call | flops 1024 | bytes 1024 | tf_op jit(solution)/shard_map/add/pallas_call | solution.py:395
  35.5 0.0 collective-permute-done.5.refs_2_
  35.5 2.7 %collective-permute-start.11 = (s16[400,128]{1,0:T(8,128)(2,1)S(1)}, s16[400,128]{1,0:T(8,128)(2,1)S(1)}, u32[]{:S(2)}, u32[]{:S(2)}) collective-permute-start(s16[400,128]{1,0:T(8,128)(2,1)S(1)} %get-tuple-element.66.refs_0_), channel_id=1, source_target_pairs={{0,8},{4,12},{8,0},{12,4},{1,9},{5,13},{9,1},{13,5},{2,10},{6,14},... | collective-permute-start | bytes 307208 | tf_op jit(solution)/shard_map/ppermute | solution.py:639
  38.2 4.6 %collective-permute-done.6.refs_3_ = bf16[24,16,512]{2,1,0:T(8,128)(2,1)S(1)} collective-permute-done((bf16[24,16,512]{2,1,0:T(8,128)(2,1)S(1)}, bf16[24,16,512]{2,1,0:T(8,128)(2,1)S(1)}, u32[]{:S(2)}, u32[]{:S(2)}) %collective-permute-start.6) | collective-permute-done | bytes 393248 | tf_op jit(solution)/shard_map/ppermute | solution.py:639
  42.7 1.1 %gram.4 = (bf16[24,64,512]{2,1,0:T(8,128)(2,1)S(1)}, f32[8,128]{1,0:T(8,128)S(1)}, f32[12,64,128]{2,1,0:T(8,128)S(1)}, s16[400,128]{1,0:T(8,128)(2,1)S(1)}) custom-call(bf16[24,16,512]{2,1,0:T(8,128)(2,1)S(1)} %get-tuple-element.52.refs_0_, bf16[24,16,512]{2,1,0:T(8,128)(2,1)S(1)} %collective-permute-done.4.refs_1_, ...), custom_call_target="tpu_custom_call" | custom-call | flops 1024 | bytes 1024 | tf_op jit(solution)/shard_map/gram/pallas_call | solution.py:371
  43.9 1.7 %collective-permute-start.10 = (s16[400,128]{1,0:T(8,128)(2,1)S(1)}, s16[400,128]{1,0:T(8,128)(2,1)S(1)}, u32[]{:S(2)}, u32[]{:S(2)}) collective-permute-start(s16[400,128]{1,0:T(8,128)(2,1)S(1)} %get-tuple-element.65), channel_id=1, source_target_pairs={{0,4},{4,0},{8,12},{12,8},{1,5},{5,1},{9,13},{13,9},{2,6},{6,2},{1... | collective-permute-start | bytes 307208 | tf_op jit(solution)/shard_map/ppermute | solution.py:639
  45.6 0.0 collective-permute-done.11.refs_1_
  45.6 3.9 %filters.3 = (s16[400,128]{1,0:T(8,128)(2,1)S(1)}, f32[8,128]{1,0:T(8,128)S(1)}) custom-call(s16[400,128]{1,0:T(8,128)(2,1)S(1)} %get-tuple-element.66.refs_0_, s16[400,128]{1,0:T(8,128)(2,1)S(1)} %collective-permute-done.11.refs_1_, f32[8,128]{1,0:T(8,128)S(1)} %get-tuple-element.67.refs_2_), custom_call_target="tpu_custom_call" | custom-call | flops 1024 | bytes 1024 | tf_op jit(solution)/shard_map/filters/pallas_call | solution.py:506
  49.5 0.5 collective-permute-start.16
  50.0 0.0 collective-permute-done.10.other
  50.0 1.3 %add.3 = (s16[400,128]{1,0:T(8,128)(2,1)S(1)}, f32[8,128]{1,0:T(8,128)S(1)}) custom-call(f32[12,64,128]{2,1,0:T(8,128)S(1)} %get-tuple-element.64.own, s16[400,128]{1,0:T(8,128)(2,1)S(1)} %collective-permute-done.10.other, f32[8,128]{1,0:T(8,128)S(1)} %get-tuple-element.68.refs_0_), custom_call_target="tpu_custom_call" | custom-call | flops 1024 | bytes 1024 | tf_op jit(solution)/shard_map/add/pallas_call | solution.py:395
  51.3 2.7 %collective-permute-start.15 = (s16[400,128]{1,0:T(8,128)(2,1)S(1)}, s16[400,128]{1,0:T(8,128)(2,1)S(1)}, u32[]{:S(2)}, u32[]{:S(2)}) collective-permute-start(s16[400,128]{1,0:T(8,128)(2,1)S(1)} %get-tuple-element.73.refs_0_), channel_id=1, source_target_pairs={{0,8},{4,12},{8,0},{12,4},{1,9},{5,13},{9,1},{13,5},{2,10},{6,14},... | collective-permute-start | bytes 307208 | tf_op jit(solution)/shard_map/ppermute | solution.py:639
  54.0 0.0 collective-permute-done.1.refs_1_
  54.0 0.0 collective-permute-done.2.refs_2_
  54.0 0.0 collective-permute-done.3.refs_3_
  54.0 1.5 %gram.5 = (bf16[16,64,512]{2,1,0:T(8,128)(2,1)S(1)}, f32[8,128]{1,0:T(8,128)S(1)}, s16[272,128]{1,0:T(8,128)(2,1)S(1)}, s16[272,128]{1,0:T(8,128)(2,1)S(1)}) custom-call(bf16[16,16,512]{2,1,0:T(8,128)(2,1)S(1)} %get-tuple-element.48.refs_0_, bf16[16,16,512]{2,1,0:T(8,128)(2,1)S(1)} %collective-permute-done.1.refs_1_, ...), custom_call_target="tpu_custom_call" | custom-call | flops 1024 | bytes 1024 | tf_op jit(solution)/shard_map/gram/pallas_call | solution.py:371
  55.5 2.7 %collective-permute-start.12 = (s16[272,128]{1,0:T(8,128)(2,1)S(1)}, s16[272,128]{1,0:T(8,128)(2,1)S(1)}, u32[]{:S(2)}, u32[]{:S(2)}) collective-permute-start(s16[272,128]{1,0:T(8,128)(2,1)S(1)} %get-tuple-element.71.refs_0_), channel_id=1, source_target_pairs={{0,8},{4,12},{8,0},{12,4},{1,9},{5,13},{9,1},{13,5},{2,10},{6,14},... | collective-permute-start | bytes 208904 | tf_op jit(solution)/shard_map/ppermute | solution.py:639
  58.2 1.6 %collective-permute-start.13 = (s16[272,128]{1,0:T(8,128)(2,1)S(1)}, s16[272,128]{1,0:T(8,128)(2,1)S(1)}, u32[]{:S(2)}, u32[]{:S(2)}) collective-permute-start(s16[272,128]{1,0:T(8,128)(2,1)S(1)} %get-tuple-element.72), channel_id=1, source_target_pairs={{0,4},{4,0},{8,12},{12,8},{1,5},{5,1},{9,13},{13,9},{2,6},{6,2},{1... | collective-permute-start | bytes 208904 | tf_op jit(solution)/shard_map/ppermute | solution.py:639
  59.7 0.2 collective-permute-start.14
  59.9 0.0 collective-permute-done.16.refs_2_
  59.9 2.3 %energy.3 = (f32[64,256]{1,0:T(8,128)}, f32[64,2,64,64]{3,2,1,0:T(8,128)}, f32[8,128]{1,0:T(8,128)S(1)}) custom-call(bf16[24,64,512]{2,1,0:T(8,128)(2,1)S(1)} %get-tuple-element.74.refs_0_, s16[400,128]{1,0:T(8,128)(2,1)S(1)} %get-tuple-element.75.refs_1_, s16[400,128]{1,0:T(8,128)(2,1)S(1)} %collective-permute-done.16.refs_2_, ...), custom_call_target="tpu_custom_call" | custom-call | flops 1024 | bytes 1024 | tf_op jit(solution)/shard_map/energy/pallas_call | solution.py:588
  62.3 0.0 collective-permute-done.15.refs_1_
  62.3 3.7 %filters.4 = (s16[400,128]{1,0:T(8,128)(2,1)S(1)}, f32[8,128]{1,0:T(8,128)S(1)}) custom-call(s16[400,128]{1,0:T(8,128)(2,1)S(1)} %get-tuple-element.73.refs_0_, s16[400,128]{1,0:T(8,128)(2,1)S(1)} %collective-permute-done.15.refs_1_, f32[8,128]{1,0:T(8,128)S(1)} %get-tuple-element.77.refs_2_), custom_call_target="tpu_custom_call" | custom-call | flops 1024 | bytes 1024 | tf_op jit(solution)/shard_map/filters/pallas_call | solution.py:506
  66.0 0.8 collective-permute-start.18
  66.8 0.0 collective-permute-done.12.refs_1_
  66.8 0.0 collective-permute-done.13.refs_2_
  66.8 0.0 collective-permute-done.14.refs_3_
  66.8 3.4 %filters.5 = (s16[272,128]{1,0:T(8,128)(2,1)S(1)}, f32[8,128]{1,0:T(8,128)S(1)}) custom-call(s16[272,128]{1,0:T(8,128)(2,1)S(1)} %get-tuple-element.71.refs_0_, s16[272,128]{1,0:T(8,128)(2,1)S(1)} %collective-permute-done.12.refs_1_, s16[272,128]{1,0:T(8,128)(2,1)S(1)} %collective-permute-done.13.refs_2_, ...), custom_call_target="tpu_custom_call" | custom-call | flops 1024 | bytes 1024 | tf_op jit(solution)/shard_map/filters/pallas_call | solution.py:506
  70.2 1.4 %collective-permute-start.17 = (s16[272,128]{1,0:T(8,128)(2,1)S(1)}, s16[272,128]{1,0:T(8,128)(2,1)S(1)}, u32[]{:S(2)}, u32[]{:S(2)}) collective-permute-start(s16[272,128]{1,0:T(8,128)(2,1)S(1)} %get-tuple-element.79.refs_1_), channel_id=1, source_target_pairs={{0,4},{4,0},{8,12},{12,8},{1,5},{5,1},{9,13},{13,9},{2,6},{6,2},{1... | collective-permute-start | bytes 208904 | tf_op jit(solution)/shard_map/ppermute | solution.py:639
  71.6 0.0 collective-permute-done.18.refs_2_
  71.6 2.3 %energy.4 = (f32[64,256]{1,0:T(8,128)}, f32[64,2,64,64]{3,2,1,0:T(8,128)}, f32[8,128]{1,0:T(8,128)S(1)}) custom-call(bf16[24,64,512]{2,1,0:T(8,128)(2,1)S(1)} %get-tuple-element.80.refs_0_, s16[400,128]{1,0:T(8,128)(2,1)S(1)} %get-tuple-element.81.refs_1_, ...), custom_call_target="tpu_custom_call", output_to_operand_aliasing={{0}: (3, {}), {1}: (4, {})} | custom-call | flops 1024 | bytes 1024 | tf_op jit(solution)/shard_map/energy/pallas_call | solution.py:588
  73.9 0.6 collective-permute-done.17.refs_2_
  74.6 2.4 %energy.5 = (f32[64,256]{1,0:T(8,128)}, f32[64,2,64,64]{3,2,1,0:T(8,128)}, f32[8,128]{1,0:T(8,128)}) custom-call(bf16[16,64,512]{2,1,0:T(8,128)(2,1)S(1)} %get-tuple-element.70.refs_0_, s16[272,128]{1,0:T(8,128)(2,1)S(1)} %get-tuple-element.79.refs_1_, ...), custom_call_target="tpu_custom_call", output_to_operand_aliasing={{0}: (3, {}), {1}: (4, {})} | custom-call | flops 1024 | bytes 1024 | tf_op jit(solution)/shard_map/energy/pallas_call | solution.py:588
Async XLA Ops:
  4.9 3.2 %collective-permute-start = (bf16[24,16,512]{2,1,0:T(8,128)(2,1)S(1)}, bf16[24,16,512]{2,1,0:T(8,128)(2,1)S(1)}, u32[]{:S(2)}, u32[]{:S(2)}) collective-permute-start(bf16[24,16,512]{2,1,0:T(8,128)(2,1)S(1)} %get-tuple-element.47), channel_id=1, source_target_pairs={{0,1},{1,0},{2,3},{3,2},{4,5},{5,4},{6,7},{7,6},{8,9},{9,8},{10,11... | collective-permute-start | bytes 1179656 | tf_op jit(solution)/shard_map/ppermute | solution.py:639
  5.5 12.5 %collective-permute-start.7 = (bf16[24,16,512]{2,1,0:T(8,128)(2,1)S(1)}, bf16[24,16,512]{2,1,0:T(8,128)(2,1)S(1)}, u32[]{:S(2)}, u32[]{:S(2)}) collective-permute-start(bf16[24,16,512]{2,1,0:T(8,128)(2,1)S(1)} %get-tuple-element.57), channel_id=1, source_target_pairs={{0,2},{1,3},{2,0},{3,1},{4,6},{5,7},{6,4},{7,5},{8,10},{9,11},{10,... | collective-permute-start | bytes 1179656 | tf_op jit(solution)/shard_map/ppermute | solution.py:639
  8.0 17.9 %collective-permute-start.8 = (bf16[24,16,512]{2,1,0:T(8,128)(2,1)S(1)}, bf16[24,16,512]{2,1,0:T(8,128)(2,1)S(1)}, u32[]{:S(2)}, u32[]{:S(2)}) collective-permute-start(bf16[24,16,512]{2,1,0:T(8,128)(2,1)S(1)} %get-tuple-element.58), channel_id=1, source_target_pairs={{0,3},{1,2},{2,1},{3,0},{4,7},{5,6},{6,5},{7,4},{8,11},{9,10},{10,... | collective-permute-start | bytes 1179656 | tf_op jit(solution)/shard_map/ppermute | solution.py:639
  13.5 20.7 %collective-permute-start.4 = (bf16[24,16,512]{2,1,0:T(8,128)(2,1)S(1)}, bf16[24,16,512]{2,1,0:T(8,128)(2,1)S(1)}, u32[]{:S(2)}, u32[]{:S(2)}) collective-permute-start(bf16[24,16,512]{2,1,0:T(8,128)(2,1)S(1)} %get-tuple-element.53), channel_id=1, source_target_pairs={{0,1},{1,0},{2,3},{3,2},{4,5},{5,4},{6,7},{7,6},{8,9},{9,8},{10,11... | collective-permute-start | bytes 1179656 | tf_op jit(solution)/shard_map/ppermute | solution.py:639
  13.7 21.8 %collective-permute-start.5 = (bf16[24,16,512]{2,1,0:T(8,128)(2,1)S(1)}, bf16[24,16,512]{2,1,0:T(8,128)(2,1)S(1)}, u32[]{:S(2)}, u32[]{:S(2)}) collective-permute-start(bf16[24,16,512]{2,1,0:T(8,128)(2,1)S(1)} %get-tuple-element.54), channel_id=1, source_target_pairs={{0,2},{1,3},{2,0},{3,1},{4,6},{5,7},{6,4},{7,5},{8,10},{9,11},{10,... | collective-permute-start | bytes 1179656 | tf_op jit(solution)/shard_map/ppermute | solution.py:639
  15.7 27.1 %collective-permute-start.6 = (bf16[24,16,512]{2,1,0:T(8,128)(2,1)S(1)}, bf16[24,16,512]{2,1,0:T(8,128)(2,1)S(1)}, u32[]{:S(2)}, u32[]{:S(2)}) collective-permute-start(bf16[24,16,512]{2,1,0:T(8,128)(2,1)S(1)} %get-tuple-element.55), channel_id=1, source_target_pairs={{0,3},{1,2},{2,1},{3,0},{4,7},{5,6},{6,5},{7,4},{8,11},{9,10},{10,... | collective-permute-start | bytes 1179656 | tf_op jit(solution)/shard_map/ppermute | solution.py:639
  27.0 5.5 %collective-permute-start.9 = (s16[400,128]{1,0:T(8,128)(2,1)S(1)}, s16[400,128]{1,0:T(8,128)(2,1)S(1)}, u32[]{:S(2)}, u32[]{:S(2)}) collective-permute-start(s16[400,128]{1,0:T(8,128)(2,1)S(1)} %get-tuple-element.61), channel_id=1, source_target_pairs={{0,4},{4,0},{8,12},{12,8},{1,5},{5,1},{9,13},{13,9},{2,6},{6,2},{1... | collective-permute-start | bytes 307208 | tf_op jit(solution)/shard_map/ppermute | solution.py:639
  28.7 25.3 %collective-permute-start.1 = (bf16[16,16,512]{2,1,0:T(8,128)(2,1)S(1)}, bf16[16,16,512]{2,1,0:T(8,128)(2,1)S(1)}, u32[]{:S(2)}, u32[]{:S(2)}) collective-permute-start(bf16[16,16,512]{2,1,0:T(8,128)(2,1)S(1)} %get-tuple-element.49), channel_id=1, source_target_pairs={{0,1},{1,0},{2,3},{3,2},{4,5},{5,4},{6,7},{7,6},{8,9},{9,8},{10,11... | collective-permute-start | bytes 786440 | tf_op jit(solution)/shard_map/ppermute | solution.py:639
  32.5 21.5 %collective-permute-start.2 = (bf16[16,16,512]{2,1,0:T(8,128)(2,1)S(1)}, bf16[16,16,512]{2,1,0:T(8,128)(2,1)S(1)}, u32[]{:S(2)}, u32[]{:S(2)}) collective-permute-start(bf16[16,16,512]{2,1,0:T(8,128)(2,1)S(1)} %get-tuple-element.50), channel_id=1, source_target_pairs={{0,2},{1,3},{2,0},{3,1},{4,6},{5,7},{6,4},{7,5},{8,10},{9,11},{10,... | collective-permute-start | bytes 786440 | tf_op jit(solution)/shard_map/ppermute | solution.py:639
  34.2 19.8 %collective-permute-start.3 = (bf16[16,16,512]{2,1,0:T(8,128)(2,1)S(1)}, bf16[16,16,512]{2,1,0:T(8,128)(2,1)S(1)}, u32[]{:S(2)}, u32[]{:S(2)}) collective-permute-start(bf16[16,16,512]{2,1,0:T(8,128)(2,1)S(1)} %get-tuple-element.51), channel_id=1, source_target_pairs={{0,3},{1,2},{2,1},{3,0},{4,7},{5,6},{6,5},{7,4},{8,11},{9,10},{10,... | collective-permute-start | bytes 786440 | tf_op jit(solution)/shard_map/ppermute | solution.py:639
  35.5 10.1 %collective-permute-start.11 = (s16[400,128]{1,0:T(8,128)(2,1)S(1)}, s16[400,128]{1,0:T(8,128)(2,1)S(1)}, u32[]{:S(2)}, u32[]{:S(2)}) collective-permute-start(s16[400,128]{1,0:T(8,128)(2,1)S(1)} %get-tuple-element.66.refs_0_), channel_id=1, source_target_pairs={{0,8},{4,12},{8,0},{12,4},{1,9},{5,13},{9,1},{13,5},{2,10},{6,14},... | collective-permute-start | bytes 307208 | tf_op jit(solution)/shard_map/ppermute | solution.py:639
  43.9 6.1 %collective-permute-start.10 = (s16[400,128]{1,0:T(8,128)(2,1)S(1)}, s16[400,128]{1,0:T(8,128)(2,1)S(1)}, u32[]{:S(2)}, u32[]{:S(2)}) collective-permute-start(s16[400,128]{1,0:T(8,128)(2,1)S(1)} %get-tuple-element.65), channel_id=1, source_target_pairs={{0,4},{4,0},{8,12},{12,8},{1,5},{5,1},{9,13},{13,9},{2,6},{6,2},{1... | collective-permute-start | bytes 307208 | tf_op jit(solution)/shard_map/ppermute | solution.py:639
  49.5 10.4 %collective-permute-start.16 = (s16[400,128]{1,0:T(8,128)(2,1)S(1)}, s16[400,128]{1,0:T(8,128)(2,1)S(1)}, u32[]{:S(2)}, u32[]{:S(2)}) collective-permute-start(s16[400,128]{1,0:T(8,128)(2,1)S(1)} %get-tuple-element.75.refs_1_), channel_id=1, source_target_pairs={{0,4},{4,0},{8,12},{12,8},{1,5},{5,1},{9,13},{13,9},{2,6},{6,2},{1... | collective-permute-start | bytes 307208 | tf_op jit(solution)/shard_map/ppermute | solution.py:639
  51.3 11.0 %collective-permute-start.15 = (s16[400,128]{1,0:T(8,128)(2,1)S(1)}, s16[400,128]{1,0:T(8,128)(2,1)S(1)}, u32[]{:S(2)}, u32[]{:S(2)}) collective-permute-start(s16[400,128]{1,0:T(8,128)(2,1)S(1)} %get-tuple-element.73.refs_0_), channel_id=1, source_target_pairs={{0,8},{4,12},{8,0},{12,4},{1,9},{5,13},{9,1},{13,5},{2,10},{6,14},... | collective-permute-start | bytes 307208 | tf_op jit(solution)/shard_map/ppermute | solution.py:639
  55.5 11.3 %collective-permute-start.12 = (s16[272,128]{1,0:T(8,128)(2,1)S(1)}, s16[272,128]{1,0:T(8,128)(2,1)S(1)}, u32[]{:S(2)}, u32[]{:S(2)}) collective-permute-start(s16[272,128]{1,0:T(8,128)(2,1)S(1)} %get-tuple-element.71.refs_0_), channel_id=1, source_target_pairs={{0,8},{4,12},{8,0},{12,4},{1,9},{5,13},{9,1},{13,5},{2,10},{6,14},... | collective-permute-start | bytes 208904 | tf_op jit(solution)/shard_map/ppermute | solution.py:639
  58.2 8.6 %collective-permute-start.13 = (s16[272,128]{1,0:T(8,128)(2,1)S(1)}, s16[272,128]{1,0:T(8,128)(2,1)S(1)}, u32[]{:S(2)}, u32[]{:S(2)}) collective-permute-start(s16[272,128]{1,0:T(8,128)(2,1)S(1)} %get-tuple-element.72), channel_id=1, source_target_pairs={{0,4},{4,0},{8,12},{12,8},{1,5},{5,1},{9,13},{13,9},{2,6},{6,2},{1... | collective-permute-start | bytes 208904 | tf_op jit(solution)/shard_map/ppermute | solution.py:639
  59.7 7.1 %collective-permute-start.14 = (s16[272,128]{1,0:T(8,128)(2,1)S(1)}, s16[272,128]{1,0:T(8,128)(2,1)S(1)}, u32[]{:S(2)}, u32[]{:S(2)}) collective-permute-start(s16[272,128]{1,0:T(8,128)(2,1)S(1)} %get-tuple-element.72), channel_id=1, source_target_pairs={{0,12},{4,8},{8,4},{12,0},{1,13},{5,9},{9,5},{13,1},{2,14},{6,10},... | collective-permute-start | bytes 208904 | tf_op jit(solution)/shard_map/ppermute | solution.py:639
  66.0 5.6 %collective-permute-start.18 = (s16[400,128]{1,0:T(8,128)(2,1)S(1)}, s16[400,128]{1,0:T(8,128)(2,1)S(1)}, u32[]{:S(2)}, u32[]{:S(2)}) collective-permute-start(s16[400,128]{1,0:T(8,128)(2,1)S(1)} %get-tuple-element.81.refs_1_), channel_id=1, source_target_pairs={{0,4},{4,0},{8,12},{12,8},{1,5},{5,1},{9,13},{13,9},{2,6},{6,2},{1... | collective-permute-start | bytes 307208 | tf_op jit(solution)/shard_map/ppermute | solution.py:639
  70.2 4.4 %collective-permute-start.17 = (s16[272,128]{1,0:T(8,128)(2,1)S(1)}, s16[272,128]{1,0:T(8,128)(2,1)S(1)}, u32[]{:S(2)}, u32[]{:S(2)}) collective-permute-start(s16[272,128]{1,0:T(8,128)(2,1)S(1)} %get-tuple-element.79.refs_1_), channel_id=1, source_target_pairs={{0,4},{4,0},{8,12},{12,8},{1,5},{5,1},{9,13},{13,9},{2,6},{6,2},{1... | collective-permute-start | bytes 208904 | tf_op jit(solution)/shard_map/ppermute | solution.py:639

commit v14 on v13

--- a/solution.py
+++ b/solution.py
@@ -517,9 +517,25 @@
     )(*args, *after)
 
 
-def energy_kernel(slots, direct, number, chunks, first, *refs):
+def energy_kernel(slots, direct, number, chunks, first, before, last, *refs):
     merged, pieces = refs[:chunks], refs[chunks : chunks + number]
-    energies_out, filters_out, token, energies, filters, energies_sem, filters_sem = refs[-7:]
+    earlier = refs[chunks + number : chunks + number + 2]
+    puts = []
+    if last:
+        energies_out, filters_out, token, energies, filters = refs[-8:-3]
+    else:
+        energies, filters, token = refs[-6:-3]
+        if before is not None:
+            energies_out, filters_out = refs[-8:-6]
+    energies_sem, filters_sem, before_sem = refs[-3:]
+    if before is not None:
+        for i, (source, target) in enumerate(zip(earlier, (energies_out, filters_out))):
+            put = pltpu.make_async_copy(
+                source, target.at[pl.ds(before, source.shape[0])], before_sem.at[i]
+            )
+            put.start()
+            puts.append(put)
+    own_puts = 0
     token[...] = jnp.zeros_like(token)
     blocks, width = merged[0].shape[1:]
     entries = width // 2
@@ -527,7 +543,6 @@
     per_slot = sum(counts) // slots
     half_rows = blocks // 2
     states = entries * lax.axis_size("space")
-    puts = []
     for slot in range(slots):
         owner = slot_owner(direct, slot)
         piece = pieces[slot] if direct else pieces[0].at[slot]
@@ -561,61 +576,70 @@
                     filters[start + i, 0] = halves[i][0][:, :blocks]
                     filters[start + i, 1] = -halves[i][1][:, :blocks]
                     energies[pl.ds(start + i, 1), :] = energy[i]
-                put = pltpu.make_async_copy(
-                    filters.at[pl.ds(start, size)],
-                    filters_out.at[pl.ds(first + start, size)],
-                    filters_sem.at[len(puts)],
-                )
-                put.start()
-                puts.append(put)
+                if last:
+                    put = pltpu.make_async_copy(
+                        filters.at[pl.ds(start, size)],
+                        filters_out.at[pl.ds(first + start, size)],
+                        filters_sem.at[own_puts],
+                    )
+                    put.start()
+                    puts.append(put)
+                    own_puts += 1
             base += own
-    put = pltpu.make_async_copy(
-        energies, energies_out.at[pl.ds(first, sum(counts))], energies_sem.at[0]
-    )
-    put.start()
-    for p in [*puts, put]:
-        p.wait()
-
-
-def filtered(merged, pieces, slots, direct, carry, owned, first, after):
+    if last:
+        put = pltpu.make_async_copy(
+            energies, energies_out.at[pl.ds(first, sum(counts))], energies_sem.at[0]
+        )
+        put.start()
+        puts.append(put)
+    for put in puts:
+        put.wait()
+
+
+def filtered(merged, pieces, slots, direct, earlier, carry, owned, first, last, after):
     _, blocks, width = merged[0].shape
     count = sum(m.shape[0] for m in merged)
     copies = sum(slots * (m.shape[0] // slots) for m in merged)
     entries = width // 2
-    fixed = len(merged) + len(pieces)
-    args = [*merged, *pieces] + ([] if carry is None else list(carry)) + list(after)
+    fixed = len(merged) + len(pieces) + (2 if earlier else 0)
+    args = [*merged, *pieces, *(earlier[:2] if earlier else ()), *(carry or ()), *after]
     hbm = pl.BlockSpec(memory_space=pltpu.HBM)
-    return pl.pallas_call(
-        functools.partial(energy_kernel, slots, direct, len(pieces), len(merged), first),
+    writes = bool(earlier) or last
+    own = [
+        jax.ShapeDtypeStruct((count, entries), F32),
+        jax.ShapeDtypeStruct((count, 2, blocks, blocks), F32),
+    ]
+    whole = [
+        jax.ShapeDtypeStruct((owned, entries), F32),
+        jax.ShapeDtypeStruct((owned, 2, blocks, blocks), F32),
+    ]
+    scratch = [pltpu.VMEM(o.shape, F32) for o in own] if last else []
+    out = pl.pallas_call(
+        functools.partial(
+            energy_kernel, slots, direct, len(pieces), len(merged), first,
+            earlier[2] if earlier else None, last,
+        ),
         in_specs=[whole_spec()] * fixed
-        + ([] if carry is None else [hbm] * 2)
+        + ([hbm] * 2 if carry else [])
         + [any_spec()] * len(after),
-        out_specs=[hbm] * 2 + [whole_spec()],
-        out_shape=[
-            jax.ShapeDtypeStruct((owned, entries), F32),
-            jax.ShapeDtypeStruct((owned, 2, blocks, blocks), F32),
-            TOKEN,
-        ],
-        input_output_aliases={} if carry is None else {fixed: 0, fixed + 1: 1},
-        scratch_shapes=[
-            pltpu.VMEM((count, entries), F32),
-            pltpu.VMEM((count, 2, blocks, blocks), F32),
+        out_specs=([hbm] * 2 if writes else [])
+        + ([] if last else [whole_spec()] * 2)
+        + [whole_spec()],
+        out_shape=(whole if writes else []) + ([] if last else own) + [TOKEN],
+        input_output_aliases={fixed: 0, fixed + 1: 1} if carry else {},
+        scratch_shapes=scratch
+        + [
             pltpu.SemaphoreType.DMA((1,)),
             pltpu.SemaphoreType.DMA((copies,)),
+            pltpu.SemaphoreType.DMA((2,)),
         ],
         compiler_params=params(),
         cost_estimate=light(),
         name="energy",
     )(*args)
-
-
-def exchange(arrays, axis):
-    size = lax.axis_size(axis)
-    got = [arrays[0]]
-    for offset in range(1, size):
-        pairs = [(i, i ^ offset) for i in range(size)]
-        got.append(lax.ppermute(arrays[offset], axis, pairs))
-    return got
+    carry = list(out[:2]) if writes else None
+    earlier = None if last else (*out[-3:-1], first)
+    return carry, earlier, out[-1]
 
 
 def plan(owned, slots):
@@ -650,6 +674,7 @@
     weight = entry_weight.reshape(1, -1)
     sent, merged, grams, parts, pieces = {}, {}, {}, {}, {}
     carry = None
+    earlier = None
     token = []
 
     def do_transform(c):
@@ -703,10 +728,11 @@
             pieces[c] = [lax.all_gather(own, "space", axis=0, tiled=False)]
 
     def do_energy(c):
-        nonlocal token, carry
-        work = [merged[k] for k in joined("E", c)]
-        *carry, done = filtered(
-            work, pieces[c], halves, paired, carry, owned, starts[c], token
+        nonlocal token, carry, earlier
+        chunks = joined("E", c)
+        carry, earlier, done = filtered(
+            [merged[k] for k in chunks], pieces[c], halves, paired, earlier, carry, owned,
+            starts[c], chunks[-1] == len(sizes) - 1, token,
         )
         token = [done]
 

time: 77.3 us -> 77.7 us (level)
  transfers between devices with their start and end apart: 19 -> 19, of which waited for: 5 -> 5; matrix products, arithmetic and copies ran while one was open for 0% -> 0% of each run, Pallas kernels for 36% -> 35%
where the time goes in v14:
time: 77.7 us; the launch traced here: 77.5 us
  Pallas kernels  34 us (44%)
  starting transfers between devices  23.1 us (30%)
  waiting for transfers between devices  19.5 us (25%)
  between operations  0.9 us (1%)
    ppermute x19, starting transfers between devices, permute(): return lax.ppermute(x, axis, pairs)  23.1 us
    ppermute x19, waiting for transfers between devices, permute(): return lax.ppermute(x, axis, pairs)  19.5 us
    pallas_call x3, Pallas kernels, solve(): pl.pallas_call(functools.partial(solve_kernel, shape, half_rows), in_spec...  11 us
    pallas_call x2, Pallas kernels, transform(): pl.pallas_call(functools.partial(transform_kernel, peers, parts, group),...  9.73 us
    pallas_call x3, Pallas kernels, filtered(): pl.pallas_call(functools.partial(energy_kernel, slots, direct, len(pieces...  6.89 us
    pallas_call x3, Pallas kernels, gram(): pl.pallas_call(functools.partial(gram_kernel, peers, slots, direct, len(a...  3.71 us
    pallas_call x2, Pallas kernels, add(): pl.pallas_call(add_kernel, in_specs=[whole_spec()] * 2 + [any_spec()] * l...  2.59 us
  transfers between devices with their start and end apart: 19, of which 5 were waited for; matrix products, arithmetic and copies ran while one was open for 0% of the time, Pallas kernels for 35%

profile of v14, /device:TPU:0, one launch (start us, length us, event | category | flops | bytes accessed | tf_op | source)
XLA Modules:
  0.0 77.5 jit_solution(12883762412073300283)
XLA Ops:
  0.6 4.3 %transform.2 = (bf16[24,16,512]{2,1,0:T(8,128)(2,1)S(1)}, bf16[24,16,512]{2,1,0:T(8,128)(2,1)S(1)}, bf16[24,16,512]{2,1,0:T(8,128)(2,1)S(1)}, bf16[24,16,512]{2,1,0:T(8,128)(2,1)S(1)}, f32[8,128]{1,0:T(8,128)S(1)}) custom-call(s32[256]{0:T(256)} %refs_0_.3, f32[1,256]{1,0:T(1,128)} %bitcast.1, bf16[16,512,256]{2,1,0:T(8,128)(2,1)} %refs_2_.3), custom_call_target="tpu_custom_call" | custom-call | flops 1024 | bytes 1024 | tf_op jit(solution)/shard_map/transform/pallas_call | solution.py:149
  4.9 0.5 collective-permute-start
  5.5 2.6 %collective-permute-start.7 = (bf16[24,16,512]{2,1,0:T(8,128)(2,1)S(1)}, bf16[24,16,512]{2,1,0:T(8,128)(2,1)S(1)}, u32[]{:S(2)}, u32[]{:S(2)}) collective-permute-start(bf16[24,16,512]{2,1,0:T(8,128)(2,1)S(1)} %get-tuple-element.59), channel_id=1, source_target_pairs={{0,2},{1,3},{2,0},{3,1},{4,6},{5,7},{6,4},{7,5},{8,10},{9,11},{10,... | collective-permute-start | bytes 1179656 | tf_op jit(solution)/shard_map/ppermute | solution.py:663
  8.0 0.1 collective-permute-start.8
  8.1 0.0 collective-permute-done.refs_4_.refs_1_
  8.1 5.4 %transform.3 = (bf16[24,16,512]{2,1,0:T(8,128)(2,1)S(1)}, bf16[24,16,512]{2,1,0:T(8,128)(2,1)S(1)}, bf16[24,16,512]{2,1,0:T(8,128)(2,1)S(1)}, bf16[24,16,512]{2,...) custom-call(s32[256]{0:T(256)} %refs_0_.3, ...), custom_call_target="tpu_custom_call" | custom-call | flops 1024 | bytes 1024 | tf_op jit(solution)/shard_map/transform/pallas_call | solution.py:149
  13.5 0.2 collective-permute-start.4
  13.7 1.9 %collective-permute-start.5 = (bf16[24,16,512]{2,1,0:T(8,128)(2,1)S(1)}, bf16[24,16,512]{2,1,0:T(8,128)(2,1)S(1)}, u32[]{:S(2)}, u32[]{:S(2)}) collective-permute-start(bf16[24,16,512]{2,1,0:T(8,128)(2,1)S(1)} %get-tuple-element.56), channel_id=1, source_target_pairs={{0,2},{1,3},{2,0},{3,1},{4,6},{5,7},{6,4},{7,5},{8,10},{9,11},{10,... | collective-permute-start | bytes 1179656 | tf_op jit(solution)/shard_map/ppermute | solution.py:663
  15.7 0.0 collective-permute-start.6
  15.7 2.3 %collective-permute-done.7.refs_2_ = bf16[24,16,512]{2,1,0:T(8,128)(2,1)S(1)} collective-permute-done((bf16[24,16,512]{2,1,0:T(8,128)(2,1)S(1)}, bf16[24,16,512]{2,1,0:T(8,128)(2,1)S(1)}, u32[]{:S(2)}, u32[]{:S(2)}) %collective-permute-start.7) | collective-permute-done | bytes 393248 | tf_op jit(solution)/shard_map/ppermute | solution.py:663
  18.0 7.9 %collective-permute-done.8.refs_3_ = bf16[24,16,512]{2,1,0:T(8,128)(2,1)S(1)} collective-permute-done((bf16[24,16,512]{2,1,0:T(8,128)(2,1)S(1)}, bf16[24,16,512]{2,1,0:T(8,128)(2,1)S(1)}, u32[]{:S(2)}, u32[]{:S(2)}) %collective-permute-start.8) | collective-permute-done | bytes 393248 | tf_op jit(solution)/shard_map/ppermute | solution.py:663
  25.9 1.1 %gram.3 = (bf16[24,64,512]{2,1,0:T(8,128)(2,1)S(1)}, f32[8,128]{1,0:T(8,128)S(1)}, f32[12,64,128]{2,1,0:T(8,128)S(1)}, s16[400,128]{1,0:T(8,128)(2,1)S(1)}) custom-call(bf16[24,16,512]{2,1,0:T(8,128)(2,1)S(1)} %get-tuple-element.58.refs_0_, bf16[24,16,512]{2,1,0:T(8,128)(2,1)S(1)} %collective-permute-done.refs_4_.refs_1_, ...), custom_call_target="tpu_custom_call" | custom-call | flops 1024 | bytes 1024 | tf_op jit(solution)/shard_map/gram/pallas_call | solution.py:371
  27.0 1.7 %collective-permute-start.9 = (s16[400,128]{1,0:T(8,128)(2,1)S(1)}, s16[400,128]{1,0:T(8,128)(2,1)S(1)}, u32[]{:S(2)}, u32[]{:S(2)}) collective-permute-start(s16[400,128]{1,0:T(8,128)(2,1)S(1)} %get-tuple-element.63), channel_id=1, source_target_pairs={{0,4},{4,0},{8,12},{12,8},{1,5},{5,1},{9,13},{13,9},{2,6},{6,2},{1... | collective-permute-start | bytes 307208 | tf_op jit(solution)/shard_map/ppermute | solution.py:663
  28.7 0.5 collective-permute-start.1
  29.2 3.3 %collective-permute-done.9.other = s16[400,128]{1,0:T(8,128)(2,1)S(1)} collective-permute-done((s16[400,128]{1,0:T(8,128)(2,1)S(1)}, s16[400,128]{1,0:T(8,128)(2,1)S(1)}, u32[]{:S(2)}, u32[]{:S(2)}) %collective-permute-start.9) | collective-permute-done | bytes 102432 | tf_op jit(solution)/shard_map/ppermute | solution.py:663
  32.5 1.7 %collective-permute-start.2 = (bf16[16,16,512]{2,1,0:T(8,128)(2,1)S(1)}, bf16[16,16,512]{2,1,0:T(8,128)(2,1)S(1)}, u32[]{:S(2)}, u32[]{:S(2)}) collective-permute-start(bf16[16,16,512]{2,1,0:T(8,128)(2,1)S(1)} %get-tuple-element.52), channel_id=1, source_target_pairs={{0,2},{1,3},{2,0},{3,1},{4,6},{5,7},{6,4},{7,5},{8,10},{9,11},{10,... | collective-permute-start | bytes 786440 | tf_op jit(solution)/shard_map/ppermute | solution.py:663
  34.2 0.0 collective-permute-done.4.refs_1_
  34.2 0.0 collective-permute-start.3
  34.2 1.3 %add.2 = (s16[400,128]{1,0:T(8,128)(2,1)S(1)}, f32[8,128]{1,0:T(8,128)S(1)}) custom-call(f32[12,64,128]{2,1,0:T(8,128)S(1)} %get-tuple-element.62.own, s16[400,128]{1,0:T(8,128)(2,1)S(1)} %collective-permute-done.9.other, f32[8,128]{1,0:T(8,128)S(1)} %get-tuple-element.64.refs_0_), custom_call_target="tpu_custom_call" | custom-call | flops 1024 | bytes 1024 | tf_op jit(solution)/shard_map/add/pallas_call | solution.py:395
  35.5 0.0 collective-permute-done.5.refs_2_
  35.5 2.7 %collective-permute-start.11 = (s16[400,128]{1,0:T(8,128)(2,1)S(1)}, s16[400,128]{1,0:T(8,128)(2,1)S(1)}, u32[]{:S(2)}, u32[]{:S(2)}) collective-permute-start(s16[400,128]{1,0:T(8,128)(2,1)S(1)} %get-tuple-element.68.refs_0_), channel_id=1, source_target_pairs={{0,8},{4,12},{8,0},{12,4},{1,9},{5,13},{9,1},{13,5},{2,10},{6,14},... | collective-permute-start | bytes 307208 | tf_op jit(solution)/shard_map/ppermute | solution.py:663
  38.2 4.6 %collective-permute-done.6.refs_3_ = bf16[24,16,512]{2,1,0:T(8,128)(2,1)S(1)} collective-permute-done((bf16[24,16,512]{2,1,0:T(8,128)(2,1)S(1)}, bf16[24,16,512]{2,1,0:T(8,128)(2,1)S(1)}, u32[]{:S(2)}, u32[]{:S(2)}) %collective-permute-start.6) | collective-permute-done | bytes 393248 | tf_op jit(solution)/shard_map/ppermute | solution.py:663
  42.7 1.1 %gram.4 = (bf16[24,64,512]{2,1,0:T(8,128)(2,1)S(1)}, f32[8,128]{1,0:T(8,128)S(1)}, f32[12,64,128]{2,1,0:T(8,128)S(1)}, s16[400,128]{1,0:T(8,128)(2,1)S(1)}) custom-call(bf16[24,16,512]{2,1,0:T(8,128)(2,1)S(1)} %get-tuple-element.54.refs_0_, bf16[24,16,512]{2,1,0:T(8,128)(2,1)S(1)} %collective-permute-done.4.refs_1_, ...), custom_call_target="tpu_custom_call" | custom-call | flops 1024 | bytes 1024 | tf_op jit(solution)/shard_map/gram/pallas_call | solution.py:371
  43.9 1.7 %collective-permute-start.10 = (s16[400,128]{1,0:T(8,128)(2,1)S(1)}, s16[400,128]{1,0:T(8,128)(2,1)S(1)}, u32[]{:S(2)}, u32[]{:S(2)}) collective-permute-start(s16[400,128]{1,0:T(8,128)(2,1)S(1)} %get-tuple-element.67), channel_id=1, source_target_pairs={{0,4},{4,0},{8,12},{12,8},{1,5},{5,1},{9,13},{13,9},{2,6},{6,2},{1... | collective-permute-start | bytes 307208 | tf_op jit(solution)/shard_map/ppermute | solution.py:663
  45.6 0.0 collective-permute-done.11.refs_1_
  45.6 3.9 %filters.3 = (s16[400,128]{1,0:T(8,128)(2,1)S(1)}, f32[8,128]{1,0:T(8,128)S(1)}) custom-call(s16[400,128]{1,0:T(8,128)(2,1)S(1)} %get-tuple-element.68.refs_0_, s16[400,128]{1,0:T(8,128)(2,1)S(1)} %collective-permute-done.11.refs_1_, f32[8,128]{1,0:T(8,128)S(1)} %get-tuple-element.69.refs_2_), custom_call_target="tpu_custom_call" | custom-call | flops 1024 | bytes 1024 | tf_op jit(solution)/shard_map/filters/pallas_call | solution.py:506
  49.5 0.5 collective-permute-start.16
  50.0 0.0 collective-permute-done.10.other
  50.0 1.3 %add.3 = (s16[400,128]{1,0:T(8,128)(2,1)S(1)}, f32[8,128]{1,0:T(8,128)S(1)}) custom-call(f32[12,64,128]{2,1,0:T(8,128)S(1)} %get-tuple-element.66.own, s16[400,128]{1,0:T(8,128)(2,1)S(1)} %collective-permute-done.10.other, f32[8,128]{1,0:T(8,128)S(1)} %get-tuple-element.70.refs_0_), custom_call_target="tpu_custom_call" | custom-call | flops 1024 | bytes 1024 | tf_op jit(solution)/shard_map/add/pallas_call | solution.py:395
  51.3 2.7 %collective-permute-start.15 = (s16[400,128]{1,0:T(8,128)(2,1)S(1)}, s16[400,128]{1,0:T(8,128)(2,1)S(1)}, u32[]{:S(2)}, u32[]{:S(2)}) collective-permute-start(s16[400,128]{1,0:T(8,128)(2,1)S(1)} %get-tuple-element.75.refs_0_), channel_id=1, source_target_pairs={{0,8},{4,12},{8,0},{12,4},{1,9},{5,13},{9,1},{13,5},{2,10},{6,14},... | collective-permute-start | bytes 307208 | tf_op jit(solution)/shard_map/ppermute | solution.py:663
  54.0 0.0 collective-permute-done.1.refs_1_
  54.0 0.0 collective-permute-done.2.refs_2_
  54.0 0.0 collective-permute-done.3.refs_3_
  54.0 1.5 %gram.5 = (bf16[16,64,512]{2,1,0:T(8,128)(2,1)S(1)}, f32[8,128]{1,0:T(8,128)S(1)}, s16[272,128]{1,0:T(8,128)(2,1)S(1)}, s16[272,128]{1,0:T(8,128)(2,1)S(1)}) custom-call(bf16[16,16,512]{2,1,0:T(8,128)(2,1)S(1)} %get-tuple-element.50.refs_0_, bf16[16,16,512]{2,1,0:T(8,128)(2,1)S(1)} %collective-permute-done.1.refs_1_, ...), custom_call_target="tpu_custom_call" | custom-call | flops 1024 | bytes 1024 | tf_op jit(solution)/shard_map/gram/pallas_call | solution.py:371
  55.5 2.7 %collective-permute-start.12 = (s16[272,128]{1,0:T(8,128)(2,1)S(1)}, s16[272,128]{1,0:T(8,128)(2,1)S(1)}, u32[]{:S(2)}, u32[]{:S(2)}) collective-permute-start(s16[272,128]{1,0:T(8,128)(2,1)S(1)} %get-tuple-element.73.refs_0_), channel_id=1, source_target_pairs={{0,8},{4,12},{8,0},{12,4},{1,9},{5,13},{9,1},{13,5},{2,10},{6,14},... | collective-permute-start | bytes 208904 | tf_op jit(solution)/shard_map/ppermute | solution.py:663
  58.2 1.3 %collective-permute-start.14 = (s16[272,128]{1,0:T(8,128)(2,1)S(1)}, s16[272,128]{1,0:T(8,128)(2,1)S(1)}, u32[]{:S(2)}, u32[]{:S(2)}) collective-permute-start(s16[272,128]{1,0:T(8,128)(2,1)S(1)} %get-tuple-element.74), channel_id=1, source_target_pairs={{0,12},{4,8},{8,4},{12,0},{1,13},{5,9},{9,5},{13,1},{2,14},{6,10},... | collective-permute-start | bytes 208904 | tf_op jit(solution)/shard_map/ppermute | solution.py:663
  59.5 0.2 collective-permute-start.13
  59.8 0.0 collective-permute-done.16.refs_2_
  59.8 1.8 %energy.3 = (f32[24,256]{1,0:T(8,128)S(1)}, f32[24,2,64,64]{3,2,1,0:T(8,128)S(1)}, f32[8,128]{1,0:T(8,128)S(1)}) custom-call(bf16[24,64,512]{2,1,0:T(8,128)(2,1)S(1)} %get-tuple-element.76.refs_0_, s16[400,128]{1,0:T(8,128)(2,1)S(1)} %get-tuple-element.77.refs_1_, s16[400,128]{1,0:T(8,128)(2,1)S(1)} %collective-permute-done.16.refs_2_, ...), custom_call_target="tpu_custom_call" | custom-call | flops 1024 | bytes 1024 | tf_op jit(solution)/shard_map/energy/pallas_call | solution.py:617
  61.6 0.0 collective-permute-done.15.refs_1_
  61.6 3.7 %filters.4 = (s16[400,128]{1,0:T(8,128)(2,1)S(1)}, f32[8,128]{1,0:T(8,128)S(1)}) custom-call(s16[400,128]{1,0:T(8,128)(2,1)S(1)} %get-tuple-element.75.refs_0_, s16[400,128]{1,0:T(8,128)(2,1)S(1)} %collective-permute-done.15.refs_1_, f32[8,128]{1,0:T(8,128)S(1)} %get-tuple-element.79.refs_2_), custom_call_target="tpu_custom_call" | custom-call | flops 1024 | bytes 1024 | tf_op jit(solution)/shard_map/filters/pallas_call | solution.py:506
  65.3 1.9 %collective-permute-start.18 = (s16[400,128]{1,0:T(8,128)(2,1)S(1)}, s16[400,128]{1,0:T(8,128)(2,1)S(1)}, u32[]{:S(2)}, u32[]{:S(2)}) collective-permute-start(s16[400,128]{1,0:T(8,128)(2,1)S(1)} %get-tuple-element.83.refs_1_), channel_id=1, source_target_pairs={{0,4},{4,0},{8,12},{12,8},{1,5},{5,1},{9,13},{13,9},{2,6},{6,2},{1... | collective-permute-start | bytes 307208 | tf_op jit(solution)/shard_map/ppermute | solution.py:663
  67.2 0.0 collective-permute-done.12.refs_1_
  67.2 0.0 collective-permute-done.14.refs_3_
  67.2 0.0 collective-permute-done.13.refs_2_
  67.2 3.4 %filters.5 = (s16[272,128]{1,0:T(8,128)(2,1)S(1)}, f32[8,128]{1,0:T(8,128)S(1)}) custom-call(s16[272,128]{1,0:T(8,128)(2,1)S(1)} %get-tuple-element.73.refs_0_, s16[272,128]{1,0:T(8,128)(2,1)S(1)} %collective-permute-done.12.refs_1_, s16[272,128]{1,0:T(8,128)(2,1)S(1)} %collective-permute-done.13.refs_2_, ...), custom_call_target="tpu_custom_call" | custom-call | flops 1024 | bytes 1024 | tf_op jit(solution)/shard_map/filters/pallas_call | solution.py:506
  70.6 0.3 collective-permute-start.17
  70.9 0.0 collective-permute-done.18.refs_2_
  70.9 2.7 %energy.4 = (f32[64,256]{1,0:T(8,128)}, f32[64,2,64,64]{3,2,1,0:T(8,128)}, f32[24,256]{1,0:T(8,128)S(1)}, f32[24,2,64,64]{3,2,1,0:T(8,128)S(1)}, f32[8,128]{1,0:T(8,128)S(1)}) custom-call(bf16[24,64,512]{2,1,0:T(8,128)(2,1)S(1)} %get-tuple-element.82.refs_0_, s16[400,128]{1,0:T(8,128)(2,1)S(1)} %get-tuple-element.83.refs_1_, ...), custom_call_target="tpu_custom_call" | custom-call | flops 1024 | bytes 1024 | tf_op jit(solution)/shard_map/energy/pallas_call | solution.py:617
  73.6 1.4 %collective-permute-done.17.refs_2_ = s16[272,128]{1,0:T(8,128)(2,1)S(1)} collective-permute-done((s16[272,128]{1,0:T(8,128)(2,1)S(1)}, s16[272,128]{1,0:T(8,128)(2,1)S(1)}, u32[]{:S(2)}, u32[]{:S(2)}) %collective-permute-start.17) | collective-permute-done | bytes 69664 | tf_op jit(solution)/shard_map/ppermute | solution.py:663
  75.0 2.4 %energy.5 = (f32[64,256]{1,0:T(8,128)}, f32[64,2,64,64]{3,2,1,0:T(8,128)}, f32[8,128]{1,0:T(8,128)}) custom-call(bf16[16,64,512]{2,1,0:T(8,128)(2,1)S(1)} %get-tuple-element.72.refs_0_, s16[272,128]{1,0:T(8,128)(2,1)S(1)} %get-tuple-element.81.refs_1_, ...), custom_call_target="tpu_custom_call", output_to_operand_aliasing={{0}: (5, {}), {1}: (6, {})} | custom-call | flops 1024 | bytes 1024 | tf_op jit(solution)/shard_map/energy/pallas_call | solution.py:617
Async XLA Ops:
  4.9 3.2 %collective-permute-start = (bf16[24,16,512]{2,1,0:T(8,128)(2,1)S(1)}, bf16[24,16,512]{2,1,0:T(8,128)(2,1)S(1)}, u32[]{:S(2)}, u32[]{:S(2)}) collective-permute-start(bf16[24,16,512]{2,1,0:T(8,128)(2,1)S(1)} %get-tuple-element.49), channel_id=1, source_target_pairs={{0,1},{1,0},{2,3},{3,2},{4,5},{5,4},{6,7},{7,6},{8,9},{9,8},{10,11... | collective-permute-start | bytes 1179656 | tf_op jit(solution)/shard_map/ppermute | solution.py:663
  5.5 12.5 %collective-permute-start.7 = (bf16[24,16,512]{2,1,0:T(8,128)(2,1)S(1)}, bf16[24,16,512]{2,1,0:T(8,128)(2,1)S(1)}, u32[]{:S(2)}, u32[]{:S(2)}) collective-permute-start(bf16[24,16,512]{2,1,0:T(8,128)(2,1)S(1)} %get-tuple-element.59), channel_id=1, source_target_pairs={{0,2},{1,3},{2,0},{3,1},{4,6},{5,7},{6,4},{7,5},{8,10},{9,11},{10,... | collective-permute-start | bytes 1179656 | tf_op jit(solution)/shard_map/ppermute | solution.py:663
  8.0 17.9 %collective-permute-start.8 = (bf16[24,16,512]{2,1,0:T(8,128)(2,1)S(1)}, bf16[24,16,512]{2,1,0:T(8,128)(2,1)S(1)}, u32[]{:S(2)}, u32[]{:S(2)}) collective-permute-start(bf16[24,16,512]{2,1,0:T(8,128)(2,1)S(1)} %get-tuple-element.60), channel_id=1, source_target_pairs={{0,3},{1,2},{2,1},{3,0},{4,7},{5,6},{6,5},{7,4},{8,11},{9,10},{10,... | collective-permute-start | bytes 1179656 | tf_op jit(solution)/shard_map/ppermute | solution.py:663
  13.5 20.7 %collective-permute-start.4 = (bf16[24,16,512]{2,1,0:T(8,128)(2,1)S(1)}, bf16[24,16,512]{2,1,0:T(8,128)(2,1)S(1)}, u32[]{:S(2)}, u32[]{:S(2)}) collective-permute-start(bf16[24,16,512]{2,1,0:T(8,128)(2,1)S(1)} %get-tuple-element.55), channel_id=1, source_target_pairs={{0,1},{1,0},{2,3},{3,2},{4,5},{5,4},{6,7},{7,6},{8,9},{9,8},{10,11... | collective-permute-start | bytes 1179656 | tf_op jit(solution)/shard_map/ppermute | solution.py:663
  13.7 21.8 %collective-permute-start.5 = (bf16[24,16,512]{2,1,0:T(8,128)(2,1)S(1)}, bf16[24,16,512]{2,1,0:T(8,128)(2,1)S(1)}, u32[]{:S(2)}, u32[]{:S(2)}) collective-permute-start(bf16[24,16,512]{2,1,0:T(8,128)(2,1)S(1)} %get-tuple-element.56), channel_id=1, source_target_pairs={{0,2},{1,3},{2,0},{3,1},{4,6},{5,7},{6,4},{7,5},{8,10},{9,11},{10,... | collective-permute-start | bytes 1179656 | tf_op jit(solution)/shard_map/ppermute | solution.py:663
  15.7 27.1 %collective-permute-start.6 = (bf16[24,16,512]{2,1,0:T(8,128)(2,1)S(1)}, bf16[24,16,512]{2,1,0:T(8,128)(2,1)S(1)}, u32[]{:S(2)}, u32[]{:S(2)}) collective-permute-start(bf16[24,16,512]{2,1,0:T(8,128)(2,1)S(1)} %get-tuple-element.57), channel_id=1, source_target_pairs={{0,3},{1,2},{2,1},{3,0},{4,7},{5,6},{6,5},{7,4},{8,11},{9,10},{10,... | collective-permute-start | bytes 1179656 | tf_op jit(solution)/shard_map/ppermute | solution.py:663
  27.0 5.5 %collective-permute-start.9 = (s16[400,128]{1,0:T(8,128)(2,1)S(1)}, s16[400,128]{1,0:T(8,128)(2,1)S(1)}, u32[]{:S(2)}, u32[]{:S(2)}) collective-permute-start(s16[400,128]{1,0:T(8,128)(2,1)S(1)} %get-tuple-element.63), channel_id=1, source_target_pairs={{0,4},{4,0},{8,12},{12,8},{1,5},{5,1},{9,13},{13,9},{2,6},{6,2},{1... | collective-permute-start | bytes 307208 | tf_op jit(solution)/shard_map/ppermute | solution.py:663
  28.7 25.3 %collective-permute-start.1 = (bf16[16,16,512]{2,1,0:T(8,128)(2,1)S(1)}, bf16[16,16,512]{2,1,0:T(8,128)(2,1)S(1)}, u32[]{:S(2)}, u32[]{:S(2)}) collective-permute-start(bf16[16,16,512]{2,1,0:T(8,128)(2,1)S(1)} %get-tuple-element.51), channel_id=1, source_target_pairs={{0,1},{1,0},{2,3},{3,2},{4,5},{5,4},{6,7},{7,6},{8,9},{9,8},{10,11... | collective-permute-start | bytes 786440 | tf_op jit(solution)/shard_map/ppermute | solution.py:663
  32.5 21.5 %collective-permute-start.2 = (bf16[16,16,512]{2,1,0:T(8,128)(2,1)S(1)}, bf16[16,16,512]{2,1,0:T(8,128)(2,1)S(1)}, u32[]{:S(2)}, u32[]{:S(2)}) collective-permute-start(bf16[16,16,512]{2,1,0:T(8,128)(2,1)S(1)} %get-tuple-element.52), channel_id=1, source_target_pairs={{0,2},{1,3},{2,0},{3,1},{4,6},{5,7},{6,4},{7,5},{8,10},{9,11},{10,... | collective-permute-start | bytes 786440 | tf_op jit(solution)/shard_map/ppermute | solution.py:663
  34.2 19.8 %collective-permute-start.3 = (bf16[16,16,512]{2,1,0:T(8,128)(2,1)S(1)}, bf16[16,16,512]{2,1,0:T(8,128)(2,1)S(1)}, u32[]{:S(2)}, u32[]{:S(2)}) collective-permute-start(bf16[16,16,512]{2,1,0:T(8,128)(2,1)S(1)} %get-tuple-element.53), channel_id=1, source_target_pairs={{0,3},{1,2},{2,1},{3,0},{4,7},{5,6},{6,5},{7,4},{8,11},{9,10},{10,... | collective-permute-start | bytes 786440 | tf_op jit(solution)/shard_map/ppermute | solution.py:663
  35.5 10.1 %collective-permute-start.11 = (s16[400,128]{1,0:T(8,128)(2,1)S(1)}, s16[400,128]{1,0:T(8,128)(2,1)S(1)}, u32[]{:S(2)}, u32[]{:S(2)}) collective-permute-start(s16[400,128]{1,0:T(8,128)(2,1)S(1)} %get-tuple-element.68.refs_0_), channel_id=1, source_target_pairs={{0,8},{4,12},{8,0},{12,4},{1,9},{5,13},{9,1},{13,5},{2,10},{6,14},... | collective-permute-start | bytes 307208 | tf_op jit(solution)/shard_map/ppermute | solution.py:663
  43.9 6.1 %collective-permute-start.10 = (s16[400,128]{1,0:T(8,128)(2,1)S(1)}, s16[400,128]{1,0:T(8,128)(2,1)S(1)}, u32[]{:S(2)}, u32[]{:S(2)}) collective-permute-start(s16[400,128]{1,0:T(8,128)(2,1)S(1)} %get-tuple-element.67), channel_id=1, source_target_pairs={{0,4},{4,0},{8,12},{12,8},{1,5},{5,1},{9,13},{13,9},{2,6},{6,2},{1... | collective-permute-start | bytes 307208 | tf_op jit(solution)/shard_map/ppermute | solution.py:663
  49.5 10.3 %collective-permute-start.16 = (s16[400,128]{1,0:T(8,128)(2,1)S(1)}, s16[400,128]{1,0:T(8,128)(2,1)S(1)}, u32[]{:S(2)}, u32[]{:S(2)}) collective-permute-start(s16[400,128]{1,0:T(8,128)(2,1)S(1)} %get-tuple-element.77.refs_1_), channel_id=1, source_target_pairs={{0,4},{4,0},{8,12},{12,8},{1,5},{5,1},{9,13},{13,9},{2,6},{6,2},{1... | collective-permute-start | bytes 307208 | tf_op jit(solution)/shard_map/ppermute | solution.py:663
  51.3 10.3 %collective-permute-start.15 = (s16[400,128]{1,0:T(8,128)(2,1)S(1)}, s16[400,128]{1,0:T(8,128)(2,1)S(1)}, u32[]{:S(2)}, u32[]{:S(2)}) collective-permute-start(s16[400,128]{1,0:T(8,128)(2,1)S(1)} %get-tuple-element.75.refs_0_), channel_id=1, source_target_pairs={{0,8},{4,12},{8,0},{12,4},{1,9},{5,13},{9,1},{13,5},{2,10},{6,14},... | collective-permute-start | bytes 307208 | tf_op jit(solution)/shard_map/ppermute | solution.py:663
  55.5 11.7 %collective-permute-start.12 = (s16[272,128]{1,0:T(8,128)(2,1)S(1)}, s16[272,128]{1,0:T(8,128)(2,1)S(1)}, u32[]{:S(2)}, u32[]{:S(2)}) collective-permute-start(s16[272,128]{1,0:T(8,128)(2,1)S(1)} %get-tuple-element.73.refs_0_), channel_id=1, source_target_pairs={{0,8},{4,12},{8,0},{12,4},{1,9},{5,13},{9,1},{13,5},{2,10},{6,14},... | collective-permute-start | bytes 208904 | tf_op jit(solution)/shard_map/ppermute | solution.py:663
  58.2 9.0 %collective-permute-start.14 = (s16[272,128]{1,0:T(8,128)(2,1)S(1)}, s16[272,128]{1,0:T(8,128)(2,1)S(1)}, u32[]{:S(2)}, u32[]{:S(2)}) collective-permute-start(s16[272,128]{1,0:T(8,128)(2,1)S(1)} %get-tuple-element.74), channel_id=1, source_target_pairs={{0,12},{4,8},{8,4},{12,0},{1,13},{5,9},{9,5},{13,1},{2,14},{6,10},... | collective-permute-start | bytes 208904 | tf_op jit(solution)/shard_map/ppermute | solution.py:663
  59.5 7.7 %collective-permute-start.13 = (s16[272,128]{1,0:T(8,128)(2,1)S(1)}, s16[272,128]{1,0:T(8,128)(2,1)S(1)}, u32[]{:S(2)}, u32[]{:S(2)}) collective-permute-start(s16[272,128]{1,0:T(8,128)(2,1)S(1)} %get-tuple-element.74), channel_id=1, source_target_pairs={{0,4},{4,0},{8,12},{12,8},{1,5},{5,1},{9,13},{13,9},{2,6},{6,2},{1... | collective-permute-start | bytes 208904 | tf_op jit(solution)/shard_map/ppermute | solution.py:663
  65.3 5.6 %collective-permute-start.18 = (s16[400,128]{1,0:T(8,128)(2,1)S(1)}, s16[400,128]{1,0:T(8,128)(2,1)S(1)}, u32[]{:S(2)}, u32[]{:S(2)}) collective-permute-start(s16[400,128]{1,0:T(8,128)(2,1)S(1)} %get-tuple-element.83.refs_1_), channel_id=1, source_target_pairs={{0,4},{4,0},{8,12},{12,8},{1,5},{5,1},{9,13},{13,9},{2,6},{6,2},{1... | collective-permute-start | bytes 307208 | tf_op jit(solution)/shard_map/ppermute | solution.py:663
  70.6 4.4 %collective-permute-start.17 = (s16[272,128]{1,0:T(8,128)(2,1)S(1)}, s16[272,128]{1,0:T(8,128)(2,1)S(1)}, u32[]{:S(2)}, u32[]{:S(2)}) collective-permute-start(s16[272,128]{1,0:T(8,128)(2,1)S(1)} %get-tuple-element.81.refs_1_), channel_id=1, source_target_pairs={{0,4},{4,0},{8,12},{12,8},{1,5},{5,1},{9,13},{13,9},{2,6},{6,2},{1... | collective-permute-start | bytes 208904 | tf_op jit(solution)/shard_map/ppermute | solution.py:663

commit v15 on v14

--- a/solution.py
+++ b/solution.py
@@ -529,9 +529,17 @@
             energies_out, filters_out = refs[-8:-6]
     energies_sem, filters_sem, before_sem = refs[-3:]
     if before is not None:
-        for i, (source, target) in enumerate(zip(earlier, (energies_out, filters_out))):
+        number_before = earlier[0].shape[0]
+        put = pltpu.make_async_copy(
+            earlier[0], energies_out.at[pl.ds(before, number_before)], before_sem.at[0]
+        )
+        put.start()
+        puts.append(put)
+        for i in range(number_before // 2):
             put = pltpu.make_async_copy(
-                source, target.at[pl.ds(before, source.shape[0])], before_sem.at[i]
+                earlier[1].at[pl.ds(2 * i, 2)],
+                filters_out.at[pl.ds(before + 2 * i, 2)],
+                before_sem.at[1 + i],
             )
             put.start()
             puts.append(put)
@@ -631,7 +639,7 @@
         + [
             pltpu.SemaphoreType.DMA((1,)),
             pltpu.SemaphoreType.DMA((copies,)),
-            pltpu.SemaphoreType.DMA((2,)),
+            pltpu.SemaphoreType.DMA((1 + owned // 2,)),
         ],
         compiler_params=params(),
         cost_estimate=light(),

time: 77.7 us -> 78.2 us (level)
  Pallas kernels: 34 us -> 34.9 us
    pallas_call x3, Pallas kernels: 6.89 us -> 7.81 us  [filtered(): pl.pallas_call(functools.partial(energy_kernel, slots, direct, len(pieces...]
  transfers between devices with their start and end apart: 19 -> 19, of which waited for: 5 -> 5; matrix products, arithmetic and copies ran while one was open for 0% -> 0% of each run, Pallas kernels for 35% -> 36%
where the time goes in v15:
time: 78.2 us; the launch traced here: 78.1 us
  Pallas kernels  34.9 us (45%)
  starting transfers between devices  23.1 us (30%)
  waiting for transfers between devices  19.2 us (25%)
  between operations  0.9 us (1%)
    ppermute x19, starting transfers between devices, permute(): return lax.ppermute(x, axis, pairs)  23.1 us
    ppermute x19, waiting for transfers between devices, permute(): return lax.ppermute(x, axis, pairs)  19.2 us
    pallas_call x3, Pallas kernels, solve(): pl.pallas_call(functools.partial(solve_kernel, shape, half_rows), in_spec...  11 us
    pallas_call x2, Pallas kernels, transform(): pl.pallas_call(functools.partial(transform_kernel, peers, parts, group),...  9.73 us
    pallas_call x3, Pallas kernels, filtered(): pl.pallas_call(functools.partial(energy_kernel, slots, direct, len(pieces...  7.81 us
    pallas_call x3, Pallas kernels, gram(): pl.pallas_call(functools.partial(gram_kernel, peers, slots, direct, len(a...  3.71 us
    pallas_call x2, Pallas kernels, add(): pl.pallas_call(add_kernel, in_specs=[whole_spec()] * 2 + [any_spec()] * l...  2.59 us
  transfers between devices with their start and end apart: 19, of which 5 were waited for; matrix products, arithmetic and copies ran while one was open for 0% of the time, Pallas kernels for 36%

profile of v15, /device:TPU:0, one launch (start us, length us, event | category | flops | bytes accessed | tf_op | source)
XLA Modules:
  0.0 78.1 jit_solution(18386394455204834259)
XLA Ops:
  0.6 4.3 %transform.2 = (bf16[24,16,512]{2,1,0:T(8,128)(2,1)S(1)}, bf16[24,16,512]{2,1,0:T(8,128)(2,1)S(1)}, bf16[24,16,512]{2,1,0:T(8,128)(2,1)S(1)}, bf16[24,16,512]{2,1,0:T(8,128)(2,1)S(1)}, f32[8,128]{1,0:T(8,128)S(1)}) custom-call(s32[256]{0:T(256)} %refs_0_.3, f32[1,256]{1,0:T(1,128)} %bitcast.1, bf16[16,512,256]{2,1,0:T(8,128)(2,1)} %refs_2_.3), custom_call_target="tpu_custom_call" | custom-call | flops 1024 | bytes 1024 | tf_op jit(solution)/shard_map/transform/pallas_call | solution.py:149
  4.9 0.5 collective-permute-start
  5.5 2.6 %collective-permute-start.7 = (bf16[24,16,512]{2,1,0:T(8,128)(2,1)S(1)}, bf16[24,16,512]{2,1,0:T(8,128)(2,1)S(1)}, u32[]{:S(2)}, u32[]{:S(2)}) collective-permute-start(bf16[24,16,512]{2,1,0:T(8,128)(2,1)S(1)} %get-tuple-element.59), channel_id=1, source_target_pairs={{0,2},{1,3},{2,0},{3,1},{4,6},{5,7},{6,4},{7,5},{8,10},{9,11},{10,... | collective-permute-start | bytes 1179656 | tf_op jit(solution)/shard_map/ppermute | solution.py:671
  8.0 0.1 collective-permute-start.8
  8.1 0.0 collective-permute-done.refs_4_.refs_1_
  8.1 5.4 %transform.3 = (bf16[24,16,512]{2,1,0:T(8,128)(2,1)S(1)}, bf16[24,16,512]{2,1,0:T(8,128)(2,1)S(1)}, bf16[24,16,512]{2,1,0:T(8,128)(2,1)S(1)}, bf16[24,16,512]{2,...) custom-call(s32[256]{0:T(256)} %refs_0_.3, ...), custom_call_target="tpu_custom_call" | custom-call | flops 1024 | bytes 1024 | tf_op jit(solution)/shard_map/transform/pallas_call | solution.py:149
  13.5 0.2 collective-permute-start.4
  13.7 1.9 %collective-permute-start.5 = (bf16[24,16,512]{2,1,0:T(8,128)(2,1)S(1)}, bf16[24,16,512]{2,1,0:T(8,128)(2,1)S(1)}, u32[]{:S(2)}, u32[]{:S(2)}) collective-permute-start(bf16[24,16,512]{2,1,0:T(8,128)(2,1)S(1)} %get-tuple-element.56), channel_id=1, source_target_pairs={{0,2},{1,3},{2,0},{3,1},{4,6},{5,7},{6,4},{7,5},{8,10},{9,11},{10,... | collective-permute-start | bytes 1179656 | tf_op jit(solution)/shard_map/ppermute | solution.py:671
  15.7 0.0 collective-permute-start.6
  15.7 2.3 %collective-permute-done.7.refs_2_ = bf16[24,16,512]{2,1,0:T(8,128)(2,1)S(1)} collective-permute-done((bf16[24,16,512]{2,1,0:T(8,128)(2,1)S(1)}, bf16[24,16,512]{2,1,0:T(8,128)(2,1)S(1)}, u32[]{:S(2)}, u32[]{:S(2)}) %collective-permute-start.7) | collective-permute-done | bytes 393248 | tf_op jit(solution)/shard_map/ppermute | solution.py:671
  18.0 7.9 %collective-permute-done.8.refs_3_ = bf16[24,16,512]{2,1,0:T(8,128)(2,1)S(1)} collective-permute-done((bf16[24,16,512]{2,1,0:T(8,128)(2,1)S(1)}, bf16[24,16,512]{2,1,0:T(8,128)(2,1)S(1)}, u32[]{:S(2)}, u32[]{:S(2)}) %collective-permute-start.8) | collective-permute-done | bytes 393248 | tf_op jit(solution)/shard_map/ppermute | solution.py:671
  25.9 1.1 %gram.3 = (bf16[24,64,512]{2,1,0:T(8,128)(2,1)S(1)}, f32[8,128]{1,0:T(8,128)S(1)}, f32[12,64,128]{2,1,0:T(8,128)S(1)}, s16[400,128]{1,0:T(8,128)(2,1)S(1)}) custom-call(bf16[24,16,512]{2,1,0:T(8,128)(2,1)S(1)} %get-tuple-element.58.refs_0_, bf16[24,16,512]{2,1,0:T(8,128)(2,1)S(1)} %collective-permute-done.refs_4_.refs_1_, ...), custom_call_target="tpu_custom_call" | custom-call | flops 1024 | bytes 1024 | tf_op jit(solution)/shard_map/gram/pallas_call | solution.py:371
  27.0 1.7 %collective-permute-start.9 = (s16[400,128]{1,0:T(8,128)(2,1)S(1)}, s16[400,128]{1,0:T(8,128)(2,1)S(1)}, u32[]{:S(2)}, u32[]{:S(2)}) collective-permute-start(s16[400,128]{1,0:T(8,128)(2,1)S(1)} %get-tuple-element.63), channel_id=1, source_target_pairs={{0,4},{4,0},{8,12},{12,8},{1,5},{5,1},{9,13},{13,9},{2,6},{6,2},{1... | collective-permute-start | bytes 307208 | tf_op jit(solution)/shard_map/ppermute | solution.py:671
  28.7 0.5 collective-permute-start.1
  29.2 3.3 %collective-permute-done.9.other = s16[400,128]{1,0:T(8,128)(2,1)S(1)} collective-permute-done((s16[400,128]{1,0:T(8,128)(2,1)S(1)}, s16[400,128]{1,0:T(8,128)(2,1)S(1)}, u32[]{:S(2)}, u32[]{:S(2)}) %collective-permute-start.9) | collective-permute-done | bytes 102432 | tf_op jit(solution)/shard_map/ppermute | solution.py:671
  32.5 1.7 %collective-permute-start.2 = (bf16[16,16,512]{2,1,0:T(8,128)(2,1)S(1)}, bf16[16,16,512]{2,1,0:T(8,128)(2,1)S(1)}, u32[]{:S(2)}, u32[]{:S(2)}) collective-permute-start(bf16[16,16,512]{2,1,0:T(8,128)(2,1)S(1)} %get-tuple-element.52), channel_id=1, source_target_pairs={{0,2},{1,3},{2,0},{3,1},{4,6},{5,7},{6,4},{7,5},{8,10},{9,11},{10,... | collective-permute-start | bytes 786440 | tf_op jit(solution)/shard_map/ppermute | solution.py:671
  34.2 0.0 collective-permute-done.4.refs_1_
  34.2 0.0 collective-permute-start.3
  34.2 1.3 %add.2 = (s16[400,128]{1,0:T(8,128)(2,1)S(1)}, f32[8,128]{1,0:T(8,128)S(1)}) custom-call(f32[12,64,128]{2,1,0:T(8,128)S(1)} %get-tuple-element.62.own, s16[400,128]{1,0:T(8,128)(2,1)S(1)} %collective-permute-done.9.other, f32[8,128]{1,0:T(8,128)S(1)} %get-tuple-element.64.refs_0_), custom_call_target="tpu_custom_call" | custom-call | flops 1024 | bytes 1024 | tf_op jit(solution)/shard_map/add/pallas_call | solution.py:395
  35.5 0.0 collective-permute-done.5.refs_2_
  35.5 2.7 %collective-permute-start.11 = (s16[400,128]{1,0:T(8,128)(2,1)S(1)}, s16[400,128]{1,0:T(8,128)(2,1)S(1)}, u32[]{:S(2)}, u32[]{:S(2)}) collective-permute-start(s16[400,128]{1,0:T(8,128)(2,1)S(1)} %get-tuple-element.68.refs_0_), channel_id=1, source_target_pairs={{0,8},{4,12},{8,0},{12,4},{1,9},{5,13},{9,1},{13,5},{2,10},{6,14},... | collective-permute-start | bytes 307208 | tf_op jit(solution)/shard_map/ppermute | solution.py:671
  38.2 4.6 %collective-permute-done.6.refs_3_ = bf16[24,16,512]{2,1,0:T(8,128)(2,1)S(1)} collective-permute-done((bf16[24,16,512]{2,1,0:T(8,128)(2,1)S(1)}, bf16[24,16,512]{2,1,0:T(8,128)(2,1)S(1)}, u32[]{:S(2)}, u32[]{:S(2)}) %collective-permute-start.6) | collective-permute-done | bytes 393248 | tf_op jit(solution)/shard_map/ppermute | solution.py:671
  42.7 1.1 %gram.4 = (bf16[24,64,512]{2,1,0:T(8,128)(2,1)S(1)}, f32[8,128]{1,0:T(8,128)S(1)}, f32[12,64,128]{2,1,0:T(8,128)S(1)}, s16[400,128]{1,0:T(8,128)(2,1)S(1)}) custom-call(bf16[24,16,512]{2,1,0:T(8,128)(2,1)S(1)} %get-tuple-element.54.refs_0_, bf16[24,16,512]{2,1,0:T(8,128)(2,1)S(1)} %collective-permute-done.4.refs_1_, ...), custom_call_target="tpu_custom_call" | custom-call | flops 1024 | bytes 1024 | tf_op jit(solution)/shard_map/gram/pallas_call | solution.py:371
  43.9 1.7 %collective-permute-start.10 = (s16[400,128]{1,0:T(8,128)(2,1)S(1)}, s16[400,128]{1,0:T(8,128)(2,1)S(1)}, u32[]{:S(2)}, u32[]{:S(2)}) collective-permute-start(s16[400,128]{1,0:T(8,128)(2,1)S(1)} %get-tuple-element.67), channel_id=1, source_target_pairs={{0,4},{4,0},{8,12},{12,8},{1,5},{5,1},{9,13},{13,9},{2,6},{6,2},{1... | collective-permute-start | bytes 307208 | tf_op jit(solution)/shard_map/ppermute | solution.py:671
  45.6 0.0 collective-permute-done.11.refs_1_
  45.6 3.9 %filters.3 = (s16[400,128]{1,0:T(8,128)(2,1)S(1)}, f32[8,128]{1,0:T(8,128)S(1)}) custom-call(s16[400,128]{1,0:T(8,128)(2,1)S(1)} %get-tuple-element.68.refs_0_, s16[400,128]{1,0:T(8,128)(2,1)S(1)} %collective-permute-done.11.refs_1_, f32[8,128]{1,0:T(8,128)S(1)} %get-tuple-element.69.refs_2_), custom_call_target="tpu_custom_call" | custom-call | flops 1024 | bytes 1024 | tf_op jit(solution)/shard_map/filters/pallas_call | solution.py:506
  49.5 0.5 collective-permute-start.16
  50.0 0.0 collective-permute-done.10.other
  50.0 1.3 %add.3 = (s16[400,128]{1,0:T(8,128)(2,1)S(1)}, f32[8,128]{1,0:T(8,128)S(1)}) custom-call(f32[12,64,128]{2,1,0:T(8,128)S(1)} %get-tuple-element.66.own, s16[400,128]{1,0:T(8,128)(2,1)S(1)} %collective-permute-done.10.other, f32[8,128]{1,0:T(8,128)S(1)} %get-tuple-element.70.refs_0_), custom_call_target="tpu_custom_call" | custom-call | flops 1024 | bytes 1024 | tf_op jit(solution)/shard_map/add/pallas_call | solution.py:395
  51.3 2.7 %collective-permute-start.15 = (s16[400,128]{1,0:T(8,128)(2,1)S(1)}, s16[400,128]{1,0:T(8,128)(2,1)S(1)}, u32[]{:S(2)}, u32[]{:S(2)}) collective-permute-start(s16[400,128]{1,0:T(8,128)(2,1)S(1)} %get-tuple-element.75.refs_0_), channel_id=1, source_target_pairs={{0,8},{4,12},{8,0},{12,4},{1,9},{5,13},{9,1},{13,5},{2,10},{6,14},... | collective-permute-start | bytes 307208 | tf_op jit(solution)/shard_map/ppermute | solution.py:671
  54.0 0.0 collective-permute-done.1.refs_1_
  54.0 0.0 collective-permute-done.2.refs_2_
  54.0 0.0 collective-permute-done.3.refs_3_
  54.0 1.5 %gram.5 = (bf16[16,64,512]{2,1,0:T(8,128)(2,1)S(1)}, f32[8,128]{1,0:T(8,128)S(1)}, s16[272,128]{1,0:T(8,128)(2,1)S(1)}, s16[272,128]{1,0:T(8,128)(2,1)S(1)}) custom-call(bf16[16,16,512]{2,1,0:T(8,128)(2,1)S(1)} %get-tuple-element.50.refs_0_, bf16[16,16,512]{2,1,0:T(8,128)(2,1)S(1)} %collective-permute-done.1.refs_1_, ...), custom_call_target="tpu_custom_call" | custom-call | flops 1024 | bytes 1024 | tf_op jit(solution)/shard_map/gram/pallas_call | solution.py:371
  55.5 2.7 %collective-permute-start.12 = (s16[272,128]{1,0:T(8,128)(2,1)S(1)}, s16[272,128]{1,0:T(8,128)(2,1)S(1)}, u32[]{:S(2)}, u32[]{:S(2)}) collective-permute-start(s16[272,128]{1,0:T(8,128)(2,1)S(1)} %get-tuple-element.73.refs_0_), channel_id=1, source_target_pairs={{0,8},{4,12},{8,0},{12,4},{1,9},{5,13},{9,1},{13,5},{2,10},{6,14},... | collective-permute-start | bytes 208904 | tf_op jit(solution)/shard_map/ppermute | solution.py:671
  58.2 1.3 %collective-permute-start.14 = (s16[272,128]{1,0:T(8,128)(2,1)S(1)}, s16[272,128]{1,0:T(8,128)(2,1)S(1)}, u32[]{:S(2)}, u32[]{:S(2)}) collective-permute-start(s16[272,128]{1,0:T(8,128)(2,1)S(1)} %get-tuple-element.74), channel_id=1, source_target_pairs={{0,12},{4,8},{8,4},{12,0},{1,13},{5,9},{9,5},{13,1},{2,14},{6,10},... | collective-permute-start | bytes 208904 | tf_op jit(solution)/shard_map/ppermute | solution.py:671
  59.5 0.2 collective-permute-start.13
  59.8 0.0 collective-permute-done.16.refs_2_
  59.8 2.1 %energy.3 = (f32[24,256]{1,0:T(8,128)S(1)}, f32[24,2,64,64]{3,2,1,0:T(8,128)S(1)}, f32[8,128]{1,0:T(8,128)S(1)}) custom-call(bf16[24,64,512]{2,1,0:T(8,128)(2,1)S(1)} %get-tuple-element.76.refs_0_, s16[400,128]{1,0:T(8,128)(2,1)S(1)} %get-tuple-element.77.refs_1_, s16[400,128]{1,0:T(8,128)(2,1)S(1)} %collective-permute-done.16.refs_2_, ...), custom_call_target="tpu_custom_call" | custom-call | flops 1024 | bytes 1024 | tf_op jit(solution)/shard_map/energy/pallas_call | solution.py:625
  61.8 0.0 collective-permute-done.15.refs_1_
  61.8 3.7 %filters.4 = (s16[400,128]{1,0:T(8,128)(2,1)S(1)}, f32[8,128]{1,0:T(8,128)S(1)}) custom-call(s16[400,128]{1,0:T(8,128)(2,1)S(1)} %get-tuple-element.75.refs_0_, s16[400,128]{1,0:T(8,128)(2,1)S(1)} %collective-permute-done.15.refs_1_, f32[8,128]{1,0:T(8,128)S(1)} %get-tuple-element.79.refs_2_), custom_call_target="tpu_custom_call" | custom-call | flops 1024 | bytes 1024 | tf_op jit(solution)/shard_map/filters/pallas_call | solution.py:506
  65.6 1.9 %collective-permute-start.18 = (s16[400,128]{1,0:T(8,128)(2,1)S(1)}, s16[400,128]{1,0:T(8,128)(2,1)S(1)}, u32[]{:S(2)}, u32[]{:S(2)}) collective-permute-start(s16[400,128]{1,0:T(8,128)(2,1)S(1)} %get-tuple-element.83.refs_1_), channel_id=1, source_target_pairs={{0,4},{4,0},{8,12},{12,8},{1,5},{5,1},{9,13},{13,9},{2,6},{6,2},{1... | collective-permute-start | bytes 307208 | tf_op jit(solution)/shard_map/ppermute | solution.py:671
  67.5 0.0 collective-permute-done.12.refs_1_
  67.5 0.0 collective-permute-done.14.refs_3_
  67.5 0.0 collective-permute-done.13.refs_2_
  67.5 3.4 %filters.5 = (s16[272,128]{1,0:T(8,128)(2,1)S(1)}, f32[8,128]{1,0:T(8,128)S(1)}) custom-call(s16[272,128]{1,0:T(8,128)(2,1)S(1)} %get-tuple-element.73.refs_0_, s16[272,128]{1,0:T(8,128)(2,1)S(1)} %collective-permute-done.12.refs_1_, s16[272,128]{1,0:T(8,128)(2,1)S(1)} %collective-permute-done.13.refs_2_, ...), custom_call_target="tpu_custom_call" | custom-call | flops 1024 | bytes 1024 | tf_op jit(solution)/shard_map/filters/pallas_call | solution.py:506
  70.9 0.3 collective-permute-start.17
  71.2 0.0 collective-permute-done.18.refs_2_
  71.2 3.1 %energy.4 = (f32[64,256]{1,0:T(8,128)}, f32[64,2,64,64]{3,2,1,0:T(8,128)}, f32[24,256]{1,0:T(8,128)S(1)}, f32[24,2,64,64]{3,2,1,0:T(8,128)S(1)}, f32[8,128]{1,0:T(8,128)S(1)}) custom-call(bf16[24,64,512]{2,1,0:T(8,128)(2,1)S(1)} %get-tuple-element.82.refs_0_, s16[400,128]{1,0:T(8,128)(2,1)S(1)} %get-tuple-element.83.refs_1_, ...), custom_call_target="tpu_custom_call" | custom-call | flops 1024 | bytes 1024 | tf_op jit(solution)/shard_map/energy/pallas_call | solution.py:625
  74.2 1.0 %collective-permute-done.17.refs_2_ = s16[272,128]{1,0:T(8,128)(2,1)S(1)} collective-permute-done((s16[272,128]{1,0:T(8,128)(2,1)S(1)}, s16[272,128]{1,0:T(8,128)(2,1)S(1)}, u32[]{:S(2)}, u32[]{:S(2)}) %collective-permute-start.17) | collective-permute-done | bytes 69664 | tf_op jit(solution)/shard_map/ppermute | solution.py:671
  75.2 2.7 %energy.5 = (f32[64,256]{1,0:T(8,128)}, f32[64,2,64,64]{3,2,1,0:T(8,128)}, f32[8,128]{1,0:T(8,128)}) custom-call(bf16[16,64,512]{2,1,0:T(8,128)(2,1)S(1)} %get-tuple-element.72.refs_0_, s16[272,128]{1,0:T(8,128)(2,1)S(1)} %get-tuple-element.81.refs_1_, ...), custom_call_target="tpu_custom_call", output_to_operand_aliasing={{0}: (5, {}), {1}: (6, {})} | custom-call | flops 1024 | bytes 1024 | tf_op jit(solution)/shard_map/energy/pallas_call | solution.py:625
Async XLA Ops:
  4.9 3.2 %collective-permute-start = (bf16[24,16,512]{2,1,0:T(8,128)(2,1)S(1)}, bf16[24,16,512]{2,1,0:T(8,128)(2,1)S(1)}, u32[]{:S(2)}, u32[]{:S(2)}) collective-permute-start(bf16[24,16,512]{2,1,0:T(8,128)(2,1)S(1)} %get-tuple-element.49), channel_id=1, source_target_pairs={{0,1},{1,0},{2,3},{3,2},{4,5},{5,4},{6,7},{7,6},{8,9},{9,8},{10,11... | collective-permute-start | bytes 1179656 | tf_op jit(solution)/shard_map/ppermute | solution.py:671
  5.5 12.5 %collective-permute-start.7 = (bf16[24,16,512]{2,1,0:T(8,128)(2,1)S(1)}, bf16[24,16,512]{2,1,0:T(8,128)(2,1)S(1)}, u32[]{:S(2)}, u32[]{:S(2)}) collective-permute-start(bf16[24,16,512]{2,1,0:T(8,128)(2,1)S(1)} %get-tuple-element.59), channel_id=1, source_target_pairs={{0,2},{1,3},{2,0},{3,1},{4,6},{5,7},{6,4},{7,5},{8,10},{9,11},{10,... | collective-permute-start | bytes 1179656 | tf_op jit(solution)/shard_map/ppermute | solution.py:671
  8.0 17.9 %collective-permute-start.8 = (bf16[24,16,512]{2,1,0:T(8,128)(2,1)S(1)}, bf16[24,16,512]{2,1,0:T(8,128)(2,1)S(1)}, u32[]{:S(2)}, u32[]{:S(2)}) collective-permute-start(bf16[24,16,512]{2,1,0:T(8,128)(2,1)S(1)} %get-tuple-element.60), channel_id=1, source_target_pairs={{0,3},{1,2},{2,1},{3,0},{4,7},{5,6},{6,5},{7,4},{8,11},{9,10},{10,... | collective-permute-start | bytes 1179656 | tf_op jit(solution)/shard_map/ppermute | solution.py:671
  13.5 20.7 %collective-permute-start.4 = (bf16[24,16,512]{2,1,0:T(8,128)(2,1)S(1)}, bf16[24,16,512]{2,1,0:T(8,128)(2,1)S(1)}, u32[]{:S(2)}, u32[]{:S(2)}) collective-permute-start(bf16[24,16,512]{2,1,0:T(8,128)(2,1)S(1)} %get-tuple-element.55), channel_id=1, source_target_pairs={{0,1},{1,0},{2,3},{3,2},{4,5},{5,4},{6,7},{7,6},{8,9},{9,8},{10,11... | collective-permute-start | bytes 1179656 | tf_op jit(solution)/shard_map/ppermute | solution.py:671
  13.7 21.8 %collective-permute-start.5 = (bf16[24,16,512]{2,1,0:T(8,128)(2,1)S(1)}, bf16[24,16,512]{2,1,0:T(8,128)(2,1)S(1)}, u32[]{:S(2)}, u32[]{:S(2)}) collective-permute-start(bf16[24,16,512]{2,1,0:T(8,128)(2,1)S(1)} %get-tuple-element.56), channel_id=1, source_target_pairs={{0,2},{1,3},{2,0},{3,1},{4,6},{5,7},{6,4},{7,5},{8,10},{9,11},{10,... | collective-permute-start | bytes 1179656 | tf_op jit(solution)/shard_map/ppermute | solution.py:671
  15.7 27.1 %collective-permute-start.6 = (bf16[24,16,512]{2,1,0:T(8,128)(2,1)S(1)}, bf16[24,16,512]{2,1,0:T(8,128)(2,1)S(1)}, u32[]{:S(2)}, u32[]{:S(2)}) collective-permute-start(bf16[24,16,512]{2,1,0:T(8,128)(2,1)S(1)} %get-tuple-element.57), channel_id=1, source_target_pairs={{0,3},{1,2},{2,1},{3,0},{4,7},{5,6},{6,5},{7,4},{8,11},{9,10},{10,... | collective-permute-start | bytes 1179656 | tf_op jit(solution)/shard_map/ppermute | solution.py:671
  27.0 5.5 %collective-permute-start.9 = (s16[400,128]{1,0:T(8,128)(2,1)S(1)}, s16[400,128]{1,0:T(8,128)(2,1)S(1)}, u32[]{:S(2)}, u32[]{:S(2)}) collective-permute-start(s16[400,128]{1,0:T(8,128)(2,1)S(1)} %get-tuple-element.63), channel_id=1, source_target_pairs={{0,4},{4,0},{8,12},{12,8},{1,5},{5,1},{9,13},{13,9},{2,6},{6,2},{1... | collective-permute-start | bytes 307208 | tf_op jit(solution)/shard_map/ppermute | solution.py:671
  28.7 25.3 %collective-permute-start.1 = (bf16[16,16,512]{2,1,0:T(8,128)(2,1)S(1)}, bf16[16,16,512]{2,1,0:T(8,128)(2,1)S(1)}, u32[]{:S(2)}, u32[]{:S(2)}) collective-permute-start(bf16[16,16,512]{2,1,0:T(8,128)(2,1)S(1)} %get-tuple-element.51), channel_id=1, source_target_pairs={{0,1},{1,0},{2,3},{3,2},{4,5},{5,4},{6,7},{7,6},{8,9},{9,8},{10,11... | collective-permute-start | bytes 786440 | tf_op jit(solution)/shard_map/ppermute | solution.py:671
  32.5 21.5 %collective-permute-start.2 = (bf16[16,16,512]{2,1,0:T(8,128)(2,1)S(1)}, bf16[16,16,512]{2,1,0:T(8,128)(2,1)S(1)}, u32[]{:S(2)}, u32[]{:S(2)}) collective-permute-start(bf16[16,16,512]{2,1,0:T(8,128)(2,1)S(1)} %get-tuple-element.52), channel_id=1, source_target_pairs={{0,2},{1,3},{2,0},{3,1},{4,6},{5,7},{6,4},{7,5},{8,10},{9,11},{10,... | collective-permute-start | bytes 786440 | tf_op jit(solution)/shard_map/ppermute | solution.py:671
  34.2 19.8 %collective-permute-start.3 = (bf16[16,16,512]{2,1,0:T(8,128)(2,1)S(1)}, bf16[16,16,512]{2,1,0:T(8,128)(2,1)S(1)}, u32[]{:S(2)}, u32[]{:S(2)}) collective-permute-start(bf16[16,16,512]{2,1,0:T(8,128)(2,1)S(1)} %get-tuple-element.53), channel_id=1, source_target_pairs={{0,3},{1,2},{2,1},{3,0},{4,7},{5,6},{6,5},{7,4},{8,11},{9,10},{10,... | collective-permute-start | bytes 786440 | tf_op jit(solution)/shard_map/ppermute | solution.py:671
  35.5 10.1 %collective-permute-start.11 = (s16[400,128]{1,0:T(8,128)(2,1)S(1)}, s16[400,128]{1,0:T(8,128)(2,1)S(1)}, u32[]{:S(2)}, u32[]{:S(2)}) collective-permute-start(s16[400,128]{1,0:T(8,128)(2,1)S(1)} %get-tuple-element.68.refs_0_), channel_id=1, source_target_pairs={{0,8},{4,12},{8,0},{12,4},{1,9},{5,13},{9,1},{13,5},{2,10},{6,14},... | collective-permute-start | bytes 307208 | tf_op jit(solution)/shard_map/ppermute | solution.py:671
  43.9 6.1 %collective-permute-start.10 = (s16[400,128]{1,0:T(8,128)(2,1)S(1)}, s16[400,128]{1,0:T(8,128)(2,1)S(1)}, u32[]{:S(2)}, u32[]{:S(2)}) collective-permute-start(s16[400,128]{1,0:T(8,128)(2,1)S(1)} %get-tuple-element.67), channel_id=1, source_target_pairs={{0,4},{4,0},{8,12},{12,8},{1,5},{5,1},{9,13},{13,9},{2,6},{6,2},{1... | collective-permute-start | bytes 307208 | tf_op jit(solution)/shard_map/ppermute | solution.py:671
  49.5 10.3 %collective-permute-start.16 = (s16[400,128]{1,0:T(8,128)(2,1)S(1)}, s16[400,128]{1,0:T(8,128)(2,1)S(1)}, u32[]{:S(2)}, u32[]{:S(2)}) collective-permute-start(s16[400,128]{1,0:T(8,128)(2,1)S(1)} %get-tuple-element.77.refs_1_), channel_id=1, source_target_pairs={{0,4},{4,0},{8,12},{12,8},{1,5},{5,1},{9,13},{13,9},{2,6},{6,2},{1... | collective-permute-start | bytes 307208 | tf_op jit(solution)/shard_map/ppermute | solution.py:671
  51.3 10.6 %collective-permute-start.15 = (s16[400,128]{1,0:T(8,128)(2,1)S(1)}, s16[400,128]{1,0:T(8,128)(2,1)S(1)}, u32[]{:S(2)}, u32[]{:S(2)}) collective-permute-start(s16[400,128]{1,0:T(8,128)(2,1)S(1)} %get-tuple-element.75.refs_0_), channel_id=1, source_target_pairs={{0,8},{4,12},{8,0},{12,4},{1,9},{5,13},{9,1},{13,5},{2,10},{6,14},... | collective-permute-start | bytes 307208 | tf_op jit(solution)/shard_map/ppermute | solution.py:671
  55.5 12.0 %collective-permute-start.12 = (s16[272,128]{1,0:T(8,128)(2,1)S(1)}, s16[272,128]{1,0:T(8,128)(2,1)S(1)}, u32[]{:S(2)}, u32[]{:S(2)}) collective-permute-start(s16[272,128]{1,0:T(8,128)(2,1)S(1)} %get-tuple-element.73.refs_0_), channel_id=1, source_target_pairs={{0,8},{4,12},{8,0},{12,4},{1,9},{5,13},{9,1},{13,5},{2,10},{6,14},... | collective-permute-start | bytes 208904 | tf_op jit(solution)/shard_map/ppermute | solution.py:671
  58.2 9.3 %collective-permute-start.14 = (s16[272,128]{1,0:T(8,128)(2,1)S(1)}, s16[272,128]{1,0:T(8,128)(2,1)S(1)}, u32[]{:S(2)}, u32[]{:S(2)}) collective-permute-start(s16[272,128]{1,0:T(8,128)(2,1)S(1)} %get-tuple-element.74), channel_id=1, source_target_pairs={{0,12},{4,8},{8,4},{12,0},{1,13},{5,9},{9,5},{13,1},{2,14},{6,10},... | collective-permute-start | bytes 208904 | tf_op jit(solution)/shard_map/ppermute | solution.py:671
  59.5 7.9 %collective-permute-start.13 = (s16[272,128]{1,0:T(8,128)(2,1)S(1)}, s16[272,128]{1,0:T(8,128)(2,1)S(1)}, u32[]{:S(2)}, u32[]{:S(2)}) collective-permute-start(s16[272,128]{1,0:T(8,128)(2,1)S(1)} %get-tuple-element.74), channel_id=1, source_target_pairs={{0,4},{4,0},{8,12},{12,8},{1,5},{5,1},{9,13},{13,9},{2,6},{6,2},{1... | collective-permute-start | bytes 208904 | tf_op jit(solution)/shard_map/ppermute | solution.py:671
  65.6 5.6 %collective-permute-start.18 = (s16[400,128]{1,0:T(8,128)(2,1)S(1)}, s16[400,128]{1,0:T(8,128)(2,1)S(1)}, u32[]{:S(2)}, u32[]{:S(2)}) collective-permute-start(s16[400,128]{1,0:T(8,128)(2,1)S(1)} %get-tuple-element.83.refs_1_), channel_id=1, source_target_pairs={{0,4},{4,0},{8,12},{12,8},{1,5},{5,1},{9,13},{13,9},{2,6},{6,2},{1... | collective-permute-start | bytes 307208 | tf_op jit(solution)/shard_map/ppermute | solution.py:671
  70.9 4.4 %collective-permute-start.17 = (s16[272,128]{1,0:T(8,128)(2,1)S(1)}, s16[272,128]{1,0:T(8,128)(2,1)S(1)}, u32[]{:S(2)}, u32[]{:S(2)}) collective-permute-start(s16[272,128]{1,0:T(8,128)(2,1)S(1)} %get-tuple-element.81.refs_1_), channel_id=1, source_target_pairs={{0,4},{4,0},{8,12},{12,8},{1,5},{5,1},{9,13},{13,9},{2,6},{6,2},{1... | collective-permute-start | bytes 208904 | tf_op jit(solution)/shard_map/ppermute | solution.py:671

commit v16 on v13

--- a/solution.py
+++ b/solution.py
@@ -626,8 +626,8 @@
 
 SIZES = [24, 24, 16]
 ORDER = (
-    ("T", 0), ("T", 1), ("G", 0), ("A", 0), ("G", 1), ("F", 0), ("A", 1), ("G", 2),
-    ("E", 0), ("F", 1), ("F", 2), ("E", 1), ("E", 2),
+    ("T", 0), ("T", 1), ("G", 0), ("F", 0), ("G", 1), ("E", 0), ("A", 1), ("G", 2),
+    ("F", 1), ("F", 2), ("E", 1), ("E", 2),
 )
 
 

time: 77.3 us -> 80.8 us (1.045)
  waiting for transfers between devices: 18.8 us -> 21.8 us
  starting transfers between devices: 23.3 us -> 24.4 us
    ppermute x19 -> x20, waiting for transfers between devices: 18.8 us -> 21.8 us  [permute(): return lax.ppermute(x, axis, pairs)]
    pallas_call x2 -> x1, Pallas kernels: 2.6 us -> 1.3 us  [add(): pl.pallas_call(add_kernel, in_specs=[whole_spec()] * 2 + [any_spec()] * l...]
    ppermute x19 -> x20, starting transfers between devices: 23.3 us -> 24.4 us  [permute(): return lax.ppermute(x, axis, pairs)]
  transfers between devices with their start and end apart: 19 -> 20, of which waited for: 5 -> 8; matrix products, arithmetic and copies ran while one was open for 0% -> 0% of each run, Pallas kernels for 36% -> 33%
where the time goes in v16:
time: 80.8 us; the launch traced here: 80.7 us
  Pallas kernels  33.6 us (42%)
  starting transfers between devices  24.4 us (30%)
  waiting for transfers between devices  21.8 us (27%)
  between operations  0.89 us (1%)
    ppermute x20, starting transfers between devices, permute(): return lax.ppermute(x, axis, pairs)  24.4 us
    ppermute x20, waiting for transfers between devices, permute(): return lax.ppermute(x, axis, pairs)  21.8 us
    pallas_call x3, Pallas kernels, solve(): pl.pallas_call(functools.partial(solve_kernel, shape, half_rows), in_spec...  11 us
    pallas_call x2, Pallas kernels, transform(): pl.pallas_call(functools.partial(transform_kernel, peers, parts, group),...  9.72 us
    pallas_call x3, Pallas kernels, filtered(): pl.pallas_call(functools.partial(energy_kernel, slots, direct, len(pieces...  7.03 us
    pallas_call x3, Pallas kernels, gram(): pl.pallas_call(functools.partial(gram_kernel, peers, slots, direct, len(a...  4.48 us
  transfers between devices with their start and end apart: 20, of which 8 were waited for; matrix products, arithmetic and copies ran while one was open for 0% of the time, Pallas kernels for 33%

profile of v16, /device:TPU:0, one launch (start us, length us, event | category | flops | bytes accessed | tf_op | source)
XLA Modules:
  0.0 80.7 jit_solution(12870760538332615139)
XLA Ops:
  0.6 4.3 %transform.2 = (bf16[24,16,512]{2,1,0:T(8,128)(2,1)S(1)}, bf16[24,16,512]{2,1,0:T(8,128)(2,1)S(1)}, bf16[24,16,512]{2,1,0:T(8,128)(2,1)S(1)}, bf16[24,16,512]{2,1,0:T(8,128)(2,1)S(1)}, f32[8,128]{1,0:T(8,128)S(1)}) custom-call(s32[256]{0:T(256)} %refs_0_.3, f32[1,256]{1,0:T(1,128)} %bitcast.1, bf16[16,512,256]{2,1,0:T(8,128)(2,1)} %refs_2_.3), custom_call_target="tpu_custom_call" | custom-call | flops 1024 | bytes 1024 | tf_op jit(solution)/shard_map/transform/pallas_call | solution.py:149
  4.9 0.5 collective-permute-start
  5.4 2.6 %collective-permute-start.7 = (bf16[24,16,512]{2,1,0:T(8,128)(2,1)S(1)}, bf16[24,16,512]{2,1,0:T(8,128)(2,1)S(1)}, u32[]{:S(2)}, u32[]{:S(2)}) collective-permute-start(bf16[24,16,512]{2,1,0:T(8,128)(2,1)S(1)} %get-tuple-element.55), channel_id=1, source_target_pairs={{0,2},{1,3},{2,0},{3,1},{4,6},{5,7},{6,4},{7,5},{8,10},{9,11},{10,... | collective-permute-start | bytes 1179656 | tf_op jit(solution)/shard_map/ppermute | solution.py:639
  8.0 0.1 collective-permute-start.8
  8.1 0.0 collective-permute-done.refs_4_.refs_1_
  8.1 5.4 %transform.3 = (bf16[24,16,512]{2,1,0:T(8,128)(2,1)S(1)}, bf16[24,16,512]{2,1,0:T(8,128)(2,1)S(1)}, bf16[24,16,512]{2,1,0:T(8,128)(2,1)S(1)}, bf16[24,16,512]{2,...) custom-call(s32[256]{0:T(256)} %refs_0_.3, ...), custom_call_target="tpu_custom_call" | custom-call | flops 1024 | bytes 1024 | tf_op jit(solution)/shard_map/transform/pallas_call | solution.py:149
  13.5 0.2 collective-permute-start.4
  13.7 1.9 %collective-permute-start.5 = (bf16[24,16,512]{2,1,0:T(8,128)(2,1)S(1)}, bf16[24,16,512]{2,1,0:T(8,128)(2,1)S(1)}, u32[]{:S(2)}, u32[]{:S(2)}) collective-permute-start(bf16[24,16,512]{2,1,0:T(8,128)(2,1)S(1)} %get-tuple-element.52), channel_id=1, source_target_pairs={{0,2},{1,3},{2,0},{3,1},{4,6},{5,7},{6,4},{7,5},{8,10},{9,11},{10,... | collective-permute-start | bytes 1179656 | tf_op jit(solution)/shard_map/ppermute | solution.py:639
  15.7 0.0 collective-permute-start.6
  15.7 2.3 %collective-permute-done.7.refs_2_ = bf16[24,16,512]{2,1,0:T(8,128)(2,1)S(1)} collective-permute-done((bf16[24,16,512]{2,1,0:T(8,128)(2,1)S(1)}, bf16[24,16,512]{2,1,0:T(8,128)(2,1)S(1)}, u32[]{:S(2)}, u32[]{:S(2)}) %collective-permute-start.7) | collective-permute-done | bytes 393248 | tf_op jit(solution)/shard_map/ppermute | solution.py:639
  18.0 7.9 %collective-permute-done.8.refs_3_ = bf16[24,16,512]{2,1,0:T(8,128)(2,1)S(1)} collective-permute-done((bf16[24,16,512]{2,1,0:T(8,128)(2,1)S(1)}, bf16[24,16,512]{2,1,0:T(8,128)(2,1)S(1)}, u32[]{:S(2)}, u32[]{:S(2)}) %collective-permute-start.8) | collective-permute-done | bytes 393248 | tf_op jit(solution)/shard_map/ppermute | solution.py:639
  25.9 1.7 %gram.3 = (bf16[24,64,512]{2,1,0:T(8,128)(2,1)S(1)}, f32[8,128]{1,0:T(8,128)S(1)}, s16[400,128]{1,0:T(8,128)(2,1)S(1)}, s16[400,128]{1,0:T(8,128)(2,1)S(1)}) custom-call(bf16[24,16,512]{2,1,0:T(8,128)(2,1)S(1)} %get-tuple-element.54.refs_0_, bf16[24,16,512]{2,1,0:T(8,128)(2,1)S(1)} %collective-permute-done.refs_4_.refs_1_, ...), custom_call_target="tpu_custom_call" | custom-call | flops 1024 | bytes 1024 | tf_op jit(solution)/shard_map/gram/pallas_call | solution.py:371
  27.6 1.7 %collective-permute-start.10 = (s16[400,128]{1,0:T(8,128)(2,1)S(1)}, s16[400,128]{1,0:T(8,128)(2,1)S(1)}, u32[]{:S(2)}, u32[]{:S(2)}) collective-permute-start(s16[400,128]{1,0:T(8,128)(2,1)S(1)} %get-tuple-element.59), channel_id=1, source_target_pairs={{0,4},{4,0},{8,12},{12,8},{1,5},{5,1},{9,13},{13,9},{2,6},{6,2},{1... | collective-permute-start | bytes 307208 | tf_op jit(solution)/shard_map/ppermute | solution.py:639
  29.3 2.5 %collective-permute-start.11 = (s16[400,128]{1,0:T(8,128)(2,1)S(1)}, s16[400,128]{1,0:T(8,128)(2,1)S(1)}, u32[]{:S(2)}, u32[]{:S(2)}) collective-permute-start(s16[400,128]{1,0:T(8,128)(2,1)S(1)} %get-tuple-element.59), channel_id=1, source_target_pairs={{0,12},{4,8},{8,4},{12,0},{1,13},{5,9},{9,5},{13,1},{2,14},{6,10},... | collective-permute-start | bytes 307208 | tf_op jit(solution)/shard_map/ppermute | solution.py:639
  31.8 1.3 %collective-permute-done.10.refs_2_ = s16[400,128]{1,0:T(8,128)(2,1)S(1)} collective-permute-done((s16[400,128]{1,0:T(8,128)(2,1)S(1)}, s16[400,128]{1,0:T(8,128)(2,1)S(1)}, u32[]{:S(2)}, u32[]{:S(2)}) %collective-permute-start.10) | collective-permute-done | bytes 102432 | tf_op jit(solution)/shard_map/ppermute | solution.py:639
  33.1 3.0 %collective-permute-start.9 = (s16[400,128]{1,0:T(8,128)(2,1)S(1)}, s16[400,128]{1,0:T(8,128)(2,1)S(1)}, u32[]{:S(2)}, u32[]{:S(2)}) collective-permute-start(s16[400,128]{1,0:T(8,128)(2,1)S(1)} %get-tuple-element.58.refs_0_), channel_id=1, source_target_pairs={{0,8},{4,12},{8,0},{12,4},{1,9},{5,13},{9,1},{13,5},{2,10},{6,14},... | collective-permute-start | bytes 307208 | tf_op jit(solution)/shard_map/ppermute | solution.py:639
  36.1 1.5 %collective-permute-done.11.refs_3_ = s16[400,128]{1,0:T(8,128)(2,1)S(1)} collective-permute-done((s16[400,128]{1,0:T(8,128)(2,1)S(1)}, s16[400,128]{1,0:T(8,128)(2,1)S(1)}, u32[]{:S(2)}, u32[]{:S(2)}) %collective-permute-start.11) | collective-permute-done | bytes 102432 | tf_op jit(solution)/shard_map/ppermute | solution.py:639
  37.6 0.0 collective-permute-start.1
  37.6 4.4 %collective-permute-done.9.refs_1_ = s16[400,128]{1,0:T(8,128)(2,1)S(1)} collective-permute-done((s16[400,128]{1,0:T(8,128)(2,1)S(1)}, s16[400,128]{1,0:T(8,128)(2,1)S(1)}, u32[]{:S(2)}, u32[]{:S(2)}) %collective-permute-start.9) | collective-permute-done | bytes 102432 | tf_op jit(solution)/shard_map/ppermute | solution.py:639
  42.0 1.5 %collective-permute-start.2 = (bf16[16,16,512]{2,1,0:T(8,128)(2,1)S(1)}, bf16[16,16,512]{2,1,0:T(8,128)(2,1)S(1)}, u32[]{:S(2)}, u32[]{:S(2)}) collective-permute-start(bf16[16,16,512]{2,1,0:T(8,128)(2,1)S(1)} %get-tuple-element.48), channel_id=1, source_target_pairs={{0,2},{1,3},{2,0},{3,1},{4,6},{5,7},{6,4},{7,5},{8,10},{9,11},{10,... | collective-permute-start | bytes 786440 | tf_op jit(solution)/shard_map/ppermute | solution.py:639
  43.5 0.0 collective-permute-done.4.refs_1_
  43.5 0.0 collective-permute-start.3
  43.5 3.9 %filters.3 = (s16[400,128]{1,0:T(8,128)(2,1)S(1)}, f32[8,128]{1,0:T(8,128)S(1)}) custom-call(s16[400,128]{1,0:T(8,128)(2,1)S(1)} %get-tuple-element.58.refs_0_, s16[400,128]{1,0:T(8,128)(2,1)S(1)} %collective-permute-done.9.refs_1_, s16[400,128]{1,0:T(8,128)(2,1)S(1)} %collective-permute-done.10.refs_2_, ...), custom_call_target="tpu_custom_call" | custom-call | flops 1024 | bytes 1024 | tf_op jit(solution)/shard_map/filters/pallas_call | solution.py:506
  47.4 0.0 collective-permute-done.5.refs_2_
  47.4 0.4 collective-permute-start.13
  47.9 0.0 collective-permute-done.6.refs_3_
  47.9 1.3 %gram.4 = (bf16[24,64,512]{2,1,0:T(8,128)(2,1)S(1)}, f32[8,128]{1,0:T(8,128)S(1)}, f32[12,64,128]{2,1,0:T(8,128)S(1)}, s16[400,128]{1,0:T(8,128)(2,1)S(1)}) custom-call(bf16[24,16,512]{2,1,0:T(8,128)(2,1)S(1)} %get-tuple-element.50.refs_0_, bf16[24,16,512]{2,1,0:T(8,128)(2,1)S(1)} %collective-permute-done.4.refs_1_, ...), custom_call_target="tpu_custom_call" | custom-call | flops 1024 | bytes 1024 | tf_op jit(solution)/shard_map/gram/pallas_call | solution.py:371
  49.2 1.7 %collective-permute-start.12 = (s16[400,128]{1,0:T(8,128)(2,1)S(1)}, s16[400,128]{1,0:T(8,128)(2,1)S(1)}, u32[]{:S(2)}, u32[]{:S(2)}) collective-permute-start(s16[400,128]{1,0:T(8,128)(2,1)S(1)} %get-tuple-element.63), channel_id=1, source_target_pairs={{0,4},{4,0},{8,12},{12,8},{1,5},{5,1},{9,13},{13,9},{2,6},{6,2},{1... | collective-permute-start | bytes 307208 | tf_op jit(solution)/shard_map/ppermute | solution.py:639
  50.9 2.3 %collective-permute-done.13.refs_2_ = s16[400,128]{1,0:T(8,128)(2,1)S(1)} collective-permute-done((s16[400,128]{1,0:T(8,128)(2,1)S(1)}, s16[400,128]{1,0:T(8,128)(2,1)S(1)}, u32[]{:S(2)}, u32[]{:S(2)}) %collective-permute-start.13) | collective-permute-done | bytes 102432 | tf_op jit(solution)/shard_map/ppermute | solution.py:639
  53.2 2.3 %energy.3 = (f32[64,256]{1,0:T(8,128)}, f32[64,2,64,64]{3,2,1,0:T(8,128)}, f32[8,128]{1,0:T(8,128)S(1)}) custom-call(bf16[24,64,512]{2,1,0:T(8,128)(2,1)S(1)} %get-tuple-element.64.refs_0_, s16[400,128]{1,0:T(8,128)(2,1)S(1)} %get-tuple-element.65.refs_1_, s16[400,128]{1,0:T(8,128)(2,1)S(1)} %collective-permute-done.13.refs_2_, ...), custom_call_target="tpu_custom_call" | custom-call | flops 1024 | bytes 1024 | tf_op jit(solution)/shard_map/energy/pallas_call | solution.py:588
  55.6 0.0 collective-permute-done.12.other
  55.6 1.3 %add.1 = (s16[400,128]{1,0:T(8,128)(2,1)S(1)}, f32[8,128]{1,0:T(8,128)S(1)}) custom-call(f32[12,64,128]{2,1,0:T(8,128)S(1)} %get-tuple-element.62.own, s16[400,128]{1,0:T(8,128)(2,1)S(1)} %collective-permute-done.12.other, f32[8,128]{1,0:T(8,128)S(1)} %get-tuple-element.67.refs_0_), custom_call_target="tpu_custom_call" | custom-call | flops 1024 | bytes 1024 | tf_op jit(solution)/shard_map/add/pallas_call | solution.py:395
  56.9 1.7 %collective-permute-start.17 = (s16[400,128]{1,0:T(8,128)(2,1)S(1)}, s16[400,128]{1,0:T(8,128)(2,1)S(1)}, u32[]{:S(2)}, u32[]{:S(2)}) collective-permute-start(s16[400,128]{1,0:T(8,128)(2,1)S(1)} %get-tuple-element.72.refs_0_), channel_id=1, source_target_pairs={{0,8},{4,12},{8,0},{12,4},{1,9},{5,13},{9,1},{13,5},{2,10},{6,14},... | collective-permute-start | bytes 307208 | tf_op jit(solution)/shard_map/ppermute | solution.py:639
  58.6 0.0 collective-permute-done.1.refs_1_
  58.6 0.0 collective-permute-done.2.refs_2_
  58.6 0.0 collective-permute-done.3.refs_3_
  58.6 1.5 %gram.5 = (bf16[16,64,512]{2,1,0:T(8,128)(2,1)S(1)}, f32[8,128]{1,0:T(8,128)S(1)}, s16[272,128]{1,0:T(8,128)(2,1)S(1)}, s16[272,128]{1,0:T(8,128)(2,1)S(1)}) custom-call(bf16[16,16,512]{2,1,0:T(8,128)(2,1)S(1)} %get-tuple-element.46.refs_0_, bf16[16,16,512]{2,1,0:T(8,128)(2,1)S(1)} %collective-permute-done.1.refs_1_, ...), custom_call_target="tpu_custom_call" | custom-call | flops 1024 | bytes 1024 | tf_op jit(solution)/shard_map/gram/pallas_call | solution.py:371
  60.1 1.4 %collective-permute-start.14 = (s16[272,128]{1,0:T(8,128)(2,1)S(1)}, s16[272,128]{1,0:T(8,128)(2,1)S(1)}, u32[]{:S(2)}, u32[]{:S(2)}) collective-permute-start(s16[272,128]{1,0:T(8,128)(2,1)S(1)} %get-tuple-element.70.refs_0_), channel_id=1, source_target_pairs={{0,8},{4,12},{8,0},{12,4},{1,9},{5,13},{9,1},{13,5},{2,10},{6,14},... | collective-permute-start | bytes 208904 | tf_op jit(solution)/shard_map/ppermute | solution.py:639
  61.4 0.4 collective-permute-start.15
  61.9 2.6 %collective-permute-start.16 = (s16[272,128]{1,0:T(8,128)(2,1)S(1)}, s16[272,128]{1,0:T(8,128)(2,1)S(1)}, u32[]{:S(2)}, u32[]{:S(2)}) collective-permute-start(s16[272,128]{1,0:T(8,128)(2,1)S(1)} %get-tuple-element.71), channel_id=1, source_target_pairs={{0,12},{4,8},{8,4},{12,0},{1,13},{5,9},{9,5},{13,1},{2,14},{6,10},... | collective-permute-start | bytes 208904 | tf_op jit(solution)/shard_map/ppermute | solution.py:639
  64.5 0.9 %collective-permute-done.17.refs_1_ = s16[400,128]{1,0:T(8,128)(2,1)S(1)} collective-permute-done((s16[400,128]{1,0:T(8,128)(2,1)S(1)}, s16[400,128]{1,0:T(8,128)(2,1)S(1)}, u32[]{:S(2)}, u32[]{:S(2)}) %collective-permute-start.17) | collective-permute-done | bytes 102432 | tf_op jit(solution)/shard_map/ppermute | solution.py:639
  65.4 3.7 %filters.4 = (s16[400,128]{1,0:T(8,128)(2,1)S(1)}, f32[8,128]{1,0:T(8,128)S(1)}) custom-call(s16[400,128]{1,0:T(8,128)(2,1)S(1)} %get-tuple-element.72.refs_0_, s16[400,128]{1,0:T(8,128)(2,1)S(1)} %collective-permute-done.17.refs_1_, f32[8,128]{1,0:T(8,128)S(1)} %get-tuple-element.73.refs_2_), custom_call_target="tpu_custom_call" | custom-call | flops 1024 | bytes 1024 | tf_op jit(solution)/shard_map/filters/pallas_call | solution.py:506
  69.1 1.2 %collective-permute-start.19 = (s16[400,128]{1,0:T(8,128)(2,1)S(1)}, s16[400,128]{1,0:T(8,128)(2,1)S(1)}, u32[]{:S(2)}, u32[]{:S(2)}) collective-permute-start(s16[400,128]{1,0:T(8,128)(2,1)S(1)} %get-tuple-element.77.refs_1_), channel_id=1, source_target_pairs={{0,4},{4,0},{8,12},{12,8},{1,5},{5,1},{9,13},{13,9},{2,6},{6,2},{1... | collective-permute-start | bytes 307208 | tf_op jit(solution)/shard_map/ppermute | solution.py:639
  70.4 0.0 collective-permute-done.14.refs_1_
  70.4 0.0 collective-permute-done.15.refs_2_
  70.4 0.0 collective-permute-done.16.refs_3_
  70.4 3.4 %filters.5 = (s16[272,128]{1,0:T(8,128)(2,1)S(1)}, f32[8,128]{1,0:T(8,128)S(1)}) custom-call(s16[272,128]{1,0:T(8,128)(2,1)S(1)} %get-tuple-element.70.refs_0_, s16[272,128]{1,0:T(8,128)(2,1)S(1)} %collective-permute-done.14.refs_1_, s16[272,128]{1,0:T(8,128)(2,1)S(1)} %collective-permute-done.15.refs_2_, ...), custom_call_target="tpu_custom_call" | custom-call | flops 1024 | bytes 1024 | tf_op jit(solution)/shard_map/filters/pallas_call | solution.py:506
  73.8 0.9 %collective-permute-start.18 = (s16[272,128]{1,0:T(8,128)(2,1)S(1)}, s16[272,128]{1,0:T(8,128)(2,1)S(1)}, u32[]{:S(2)}, u32[]{:S(2)}) collective-permute-start(s16[272,128]{1,0:T(8,128)(2,1)S(1)} %get-tuple-element.75.refs_1_), channel_id=1, source_target_pairs={{0,4},{4,0},{8,12},{12,8},{1,5},{5,1},{9,13},{13,9},{2,6},{6,2},{1... | collective-permute-start | bytes 208904 | tf_op jit(solution)/shard_map/ppermute | solution.py:639
  74.7 0.0 collective-permute-done.19.refs_2_
  74.7 2.3 %energy.4 = (f32[64,256]{1,0:T(8,128)}, f32[64,2,64,64]{3,2,1,0:T(8,128)}, f32[8,128]{1,0:T(8,128)S(1)}) custom-call(bf16[24,64,512]{2,1,0:T(8,128)(2,1)S(1)} %get-tuple-element.76.refs_0_, s16[400,128]{1,0:T(8,128)(2,1)S(1)} %get-tuple-element.77.refs_1_, ...), custom_call_target="tpu_custom_call", output_to_operand_aliasing={{0}: (3, {}), {1}: (4, {})} | custom-call | flops 1024 | bytes 1024 | tf_op jit(solution)/shard_map/energy/pallas_call | solution.py:588
  77.0 1.1 %collective-permute-done.18.refs_2_ = s16[272,128]{1,0:T(8,128)(2,1)S(1)} collective-permute-done((s16[272,128]{1,0:T(8,128)(2,1)S(1)}, s16[272,128]{1,0:T(8,128)(2,1)S(1)}, u32[]{:S(2)}, u32[]{:S(2)}) %collective-permute-start.18) | collective-permute-done | bytes 69664 | tf_op jit(solution)/shard_map/ppermute | solution.py:639
  78.1 2.4 %energy.5 = (f32[64,256]{1,0:T(8,128)}, f32[64,2,64,64]{3,2,1,0:T(8,128)}, f32[8,128]{1,0:T(8,128)}) custom-call(bf16[16,64,512]{2,1,0:T(8,128)(2,1)S(1)} %get-tuple-element.69.refs_0_, s16[272,128]{1,0:T(8,128)(2,1)S(1)} %get-tuple-element.75.refs_1_, ...), custom_call_target="tpu_custom_call", output_to_operand_aliasing={{0}: (3, {}), {1}: (4, {})} | custom-call | flops 1024 | bytes 1024 | tf_op jit(solution)/shard_map/energy/pallas_call | solution.py:588
Async XLA Ops:
  4.9 3.2 %collective-permute-start = (bf16[24,16,512]{2,1,0:T(8,128)(2,1)S(1)}, bf16[24,16,512]{2,1,0:T(8,128)(2,1)S(1)}, u32[]{:S(2)}, u32[]{:S(2)}) collective-permute-start(bf16[24,16,512]{2,1,0:T(8,128)(2,1)S(1)} %get-tuple-element.45), channel_id=1, source_target_pairs={{0,1},{1,0},{2,3},{3,2},{4,5},{5,4},{6,7},{7,6},{8,9},{9,8},{10,11... | collective-permute-start | bytes 1179656 | tf_op jit(solution)/shard_map/ppermute | solution.py:639
  5.4 12.5 %collective-permute-start.7 = (bf16[24,16,512]{2,1,0:T(8,128)(2,1)S(1)}, bf16[24,16,512]{2,1,0:T(8,128)(2,1)S(1)}, u32[]{:S(2)}, u32[]{:S(2)}) collective-permute-start(bf16[24,16,512]{2,1,0:T(8,128)(2,1)S(1)} %get-tuple-element.55), channel_id=1, source_target_pairs={{0,2},{1,3},{2,0},{3,1},{4,6},{5,7},{6,4},{7,5},{8,10},{9,11},{10,... | collective-permute-start | bytes 1179656 | tf_op jit(solution)/shard_map/ppermute | solution.py:639
  8.0 17.9 %collective-permute-start.8 = (bf16[24,16,512]{2,1,0:T(8,128)(2,1)S(1)}, bf16[24,16,512]{2,1,0:T(8,128)(2,1)S(1)}, u32[]{:S(2)}, u32[]{:S(2)}) collective-permute-start(bf16[24,16,512]{2,1,0:T(8,128)(2,1)S(1)} %get-tuple-element.56), channel_id=1, source_target_pairs={{0,3},{1,2},{2,1},{3,0},{4,7},{5,6},{6,5},{7,4},{8,11},{9,10},{10,... | collective-permute-start | bytes 1179656 | tf_op jit(solution)/shard_map/ppermute | solution.py:639
  13.5 30.0 %collective-permute-start.4 = (bf16[24,16,512]{2,1,0:T(8,128)(2,1)S(1)}, bf16[24,16,512]{2,1,0:T(8,128)(2,1)S(1)}, u32[]{:S(2)}, u32[]{:S(2)}) collective-permute-start(bf16[24,16,512]{2,1,0:T(8,128)(2,1)S(1)} %get-tuple-element.51), channel_id=1, source_target_pairs={{0,1},{1,0},{2,3},{3,2},{4,5},{5,4},{6,7},{7,6},{8,9},{9,8},{10,11... | collective-permute-start | bytes 1179656 | tf_op jit(solution)/shard_map/ppermute | solution.py:639
  13.7 33.7 %collective-permute-start.5 = (bf16[24,16,512]{2,1,0:T(8,128)(2,1)S(1)}, bf16[24,16,512]{2,1,0:T(8,128)(2,1)S(1)}, u32[]{:S(2)}, u32[]{:S(2)}) collective-permute-start(bf16[24,16,512]{2,1,0:T(8,128)(2,1)S(1)} %get-tuple-element.52), channel_id=1, source_target_pairs={{0,2},{1,3},{2,0},{3,1},{4,6},{5,7},{6,4},{7,5},{8,10},{9,11},{10,... | collective-permute-start | bytes 1179656 | tf_op jit(solution)/shard_map/ppermute | solution.py:639
  15.7 32.2 %collective-permute-start.6 = (bf16[24,16,512]{2,1,0:T(8,128)(2,1)S(1)}, bf16[24,16,512]{2,1,0:T(8,128)(2,1)S(1)}, u32[]{:S(2)}, u32[]{:S(2)}) collective-permute-start(bf16[24,16,512]{2,1,0:T(8,128)(2,1)S(1)} %get-tuple-element.53), channel_id=1, source_target_pairs={{0,3},{1,2},{2,1},{3,0},{4,7},{5,6},{6,5},{7,4},{8,11},{9,10},{10,... | collective-permute-start | bytes 1179656 | tf_op jit(solution)/shard_map/ppermute | solution.py:639
  27.6 5.5 %collective-permute-start.10 = (s16[400,128]{1,0:T(8,128)(2,1)S(1)}, s16[400,128]{1,0:T(8,128)(2,1)S(1)}, u32[]{:S(2)}, u32[]{:S(2)}) collective-permute-start(s16[400,128]{1,0:T(8,128)(2,1)S(1)} %get-tuple-element.59), channel_id=1, source_target_pairs={{0,4},{4,0},{8,12},{12,8},{1,5},{5,1},{9,13},{13,9},{2,6},{6,2},{1... | collective-permute-start | bytes 307208 | tf_op jit(solution)/shard_map/ppermute | solution.py:639
  29.3 8.3 %collective-permute-start.11 = (s16[400,128]{1,0:T(8,128)(2,1)S(1)}, s16[400,128]{1,0:T(8,128)(2,1)S(1)}, u32[]{:S(2)}, u32[]{:S(2)}) collective-permute-start(s16[400,128]{1,0:T(8,128)(2,1)S(1)} %get-tuple-element.59), channel_id=1, source_target_pairs={{0,12},{4,8},{8,4},{12,0},{1,13},{5,9},{9,5},{13,1},{2,14},{6,10},... | collective-permute-start | bytes 307208 | tf_op jit(solution)/shard_map/ppermute | solution.py:639
  33.1 8.9 %collective-permute-start.9 = (s16[400,128]{1,0:T(8,128)(2,1)S(1)}, s16[400,128]{1,0:T(8,128)(2,1)S(1)}, u32[]{:S(2)}, u32[]{:S(2)}) collective-permute-start(s16[400,128]{1,0:T(8,128)(2,1)S(1)} %get-tuple-element.58.refs_0_), channel_id=1, source_target_pairs={{0,8},{4,12},{8,0},{12,4},{1,9},{5,13},{9,1},{13,5},{2,10},{6,14},... | collective-permute-start | bytes 307208 | tf_op jit(solution)/shard_map/ppermute | solution.py:639
  37.6 21.0 %collective-permute-start.1 = (bf16[16,16,512]{2,1,0:T(8,128)(2,1)S(1)}, bf16[16,16,512]{2,1,0:T(8,128)(2,1)S(1)}, u32[]{:S(2)}, u32[]{:S(2)}) collective-permute-start(bf16[16,16,512]{2,1,0:T(8,128)(2,1)S(1)} %get-tuple-element.47), channel_id=1, source_target_pairs={{0,1},{1,0},{2,3},{3,2},{4,5},{5,4},{6,7},{7,6},{8,9},{9,8},{10,11... | collective-permute-start | bytes 786440 | tf_op jit(solution)/shard_map/ppermute | solution.py:639
  42.0 16.6 %collective-permute-start.2 = (bf16[16,16,512]{2,1,0:T(8,128)(2,1)S(1)}, bf16[16,16,512]{2,1,0:T(8,128)(2,1)S(1)}, u32[]{:S(2)}, u32[]{:S(2)}) collective-permute-start(bf16[16,16,512]{2,1,0:T(8,128)(2,1)S(1)} %get-tuple-element.48), channel_id=1, source_target_pairs={{0,2},{1,3},{2,0},{3,1},{4,6},{5,7},{6,4},{7,5},{8,10},{9,11},{10,... | collective-permute-start | bytes 786440 | tf_op jit(solution)/shard_map/ppermute | solution.py:639
  43.5 15.1 %collective-permute-start.3 = (bf16[16,16,512]{2,1,0:T(8,128)(2,1)S(1)}, bf16[16,16,512]{2,1,0:T(8,128)(2,1)S(1)}, u32[]{:S(2)}, u32[]{:S(2)}) collective-permute-start(bf16[16,16,512]{2,1,0:T(8,128)(2,1)S(1)} %get-tuple-element.49), channel_id=1, source_target_pairs={{0,3},{1,2},{2,1},{3,0},{4,7},{5,6},{6,5},{7,4},{8,11},{9,10},{10,... | collective-permute-start | bytes 786440 | tf_op jit(solution)/shard_map/ppermute | solution.py:639
  47.4 5.8 %collective-permute-start.13 = (s16[400,128]{1,0:T(8,128)(2,1)S(1)}, s16[400,128]{1,0:T(8,128)(2,1)S(1)}, u32[]{:S(2)}, u32[]{:S(2)}) collective-permute-start(s16[400,128]{1,0:T(8,128)(2,1)S(1)} %get-tuple-element.65.refs_1_), channel_id=1, source_target_pairs={{0,4},{4,0},{8,12},{12,8},{1,5},{5,1},{9,13},{13,9},{2,6},{6,2},{1... | collective-permute-start | bytes 307208 | tf_op jit(solution)/shard_map/ppermute | solution.py:639
  49.2 6.4 %collective-permute-start.12 = (s16[400,128]{1,0:T(8,128)(2,1)S(1)}, s16[400,128]{1,0:T(8,128)(2,1)S(1)}, u32[]{:S(2)}, u32[]{:S(2)}) collective-permute-start(s16[400,128]{1,0:T(8,128)(2,1)S(1)} %get-tuple-element.63), channel_id=1, source_target_pairs={{0,4},{4,0},{8,12},{12,8},{1,5},{5,1},{9,13},{13,9},{2,6},{6,2},{1... | collective-permute-start | bytes 307208 | tf_op jit(solution)/shard_map/ppermute | solution.py:639
  56.9 8.5 %collective-permute-start.17 = (s16[400,128]{1,0:T(8,128)(2,1)S(1)}, s16[400,128]{1,0:T(8,128)(2,1)S(1)}, u32[]{:S(2)}, u32[]{:S(2)}) collective-permute-start(s16[400,128]{1,0:T(8,128)(2,1)S(1)} %get-tuple-element.72.refs_0_), channel_id=1, source_target_pairs={{0,8},{4,12},{8,0},{12,4},{1,9},{5,13},{9,1},{13,5},{2,10},{6,14},... | collective-permute-start | bytes 307208 | tf_op jit(solution)/shard_map/ppermute | solution.py:639
  60.1 10.3 %collective-permute-start.14 = (s16[272,128]{1,0:T(8,128)(2,1)S(1)}, s16[272,128]{1,0:T(8,128)(2,1)S(1)}, u32[]{:S(2)}, u32[]{:S(2)}) collective-permute-start(s16[272,128]{1,0:T(8,128)(2,1)S(1)} %get-tuple-element.70.refs_0_), channel_id=1, source_target_pairs={{0,8},{4,12},{8,0},{12,4},{1,9},{5,13},{9,1},{13,5},{2,10},{6,14},... | collective-permute-start | bytes 208904 | tf_op jit(solution)/shard_map/ppermute | solution.py:639
  61.4 8.9 %collective-permute-start.15 = (s16[272,128]{1,0:T(8,128)(2,1)S(1)}, s16[272,128]{1,0:T(8,128)(2,1)S(1)}, u32[]{:S(2)}, u32[]{:S(2)}) collective-permute-start(s16[272,128]{1,0:T(8,128)(2,1)S(1)} %get-tuple-element.71), channel_id=1, source_target_pairs={{0,4},{4,0},{8,12},{12,8},{1,5},{5,1},{9,13},{13,9},{2,6},{6,2},{1... | collective-permute-start | bytes 208904 | tf_op jit(solution)/shard_map/ppermute | solution.py:639
  61.9 8.5 %collective-permute-start.16 = (s16[272,128]{1,0:T(8,128)(2,1)S(1)}, s16[272,128]{1,0:T(8,128)(2,1)S(1)}, u32[]{:S(2)}, u32[]{:S(2)}) collective-permute-start(s16[272,128]{1,0:T(8,128)(2,1)S(1)} %get-tuple-element.71), channel_id=1, source_target_pairs={{0,12},{4,8},{8,4},{12,0},{1,13},{5,9},{9,5},{13,1},{2,14},{6,10},... | collective-permute-start | bytes 208904 | tf_op jit(solution)/shard_map/ppermute | solution.py:639
  69.1 5.6 %collective-permute-start.19 = (s16[400,128]{1,0:T(8,128)(2,1)S(1)}, s16[400,128]{1,0:T(8,128)(2,1)S(1)}, u32[]{:S(2)}, u32[]{:S(2)}) collective-permute-start(s16[400,128]{1,0:T(8,128)(2,1)S(1)} %get-tuple-element.77.refs_1_), channel_id=1, source_target_pairs={{0,4},{4,0},{8,12},{12,8},{1,5},{5,1},{9,13},{13,9},{2,6},{6,2},{1... | collective-permute-start | bytes 307208 | tf_op jit(solution)/shard_map/ppermute | solution.py:639
  73.8 4.4 %collective-permute-start.18 = (s16[272,128]{1,0:T(8,128)(2,1)S(1)}, s16[272,128]{1,0:T(8,128)(2,1)S(1)}, u32[]{:S(2)}, u32[]{:S(2)}) collective-permute-start(s16[272,128]{1,0:T(8,128)(2,1)S(1)} %get-tuple-element.75.refs_1_), channel_id=1, source_target_pairs={{0,4},{4,0},{8,12},{12,8},{1,5},{5,1},{9,13},{13,9},{2,6},{6,2},{1... | collective-permute-start | bytes 208904 | tf_op jit(solution)/shard_map/ppermute | solution.py:639

commit v17 on v13

--- a/solution.py
+++ b/solution.py
@@ -269,7 +269,7 @@
     lane = lax.broadcasted_iota(jnp.int32, (half, width), 1)
     on = (lane == row) | (lane == row + half)
     diagonal = each(lambda b: jnp.sum(jnp.where(on, b, F32(0)), axis=0, keepdims=True), both)
-    root = jnp.sqrt(jnp.maximum(place(diagonal, pad_rows(len(both))), F32(1e-30)))
+    root = jnp.sqrt(jnp.maximum(place(diagonal, pad_rows(len(both))), F32(1e-36)))
     exponent = jnp.floor(jnp.log(root) * F32(1 / math.log(2.0)))
     part = jnp.maximum(jnp.ceil((root * jnp.exp2(-exponent) - 1) * 128), F32(0))
     codes = exponent * 256 + part
@@ -281,7 +281,7 @@
 
 def spread(values, codes):
     products = outer(scale_of(codes), len(values))
-    return each(lambda v, p: v * pack(p * F32(1 / TOP)), values, products)
+    return each(lambda v, p: (v * F32(1 / TOP)) * pack(p), values, products)
 
 
 def to_short(x):
@@ -478,7 +478,7 @@
         x = each(lambda v, m: F32(factor) * (v + m), xw, step)
     values, codes, scales = encode(each(lambda v: double(eye - v), x))
     products = outer(scales, number)
-    filters = each(lambda v, p: unpack(v, p * F32(0.5 / TOP)), values, products)
+    filters = each(lambda v, p: unpack(v * F32(0.5 / TOP), p), values, products)
     rounded = each(lambda c: c[0].astype(BF16), filters)
     turned = each(
         lambda c: jnp.concatenate([c[0].astype(BF16), c[1].astype(BF16)], 0), filters
@@ -490,7 +490,7 @@
         lambda c, h: jnp.sum(c.astype(F32) * h, keepdims=True) * F32(half), rounded, moved
     )
     energy = place([jnp.broadcast_to(e, (1, width)) for e in energy], codes.shape[0])
-    energy = jnp.maximum(energy, F32(1e-30))
+    energy = jnp.maximum(energy, F32(1e-36))
     whole = jnp.floor(jnp.log(energy) * F32(LOG_STEPS / math.log(2.0)))
     rest = jnp.round((energy * jnp.exp2(whole * F32(-1 / LOG_STEPS)) - 1.0) * F32(FINE))
     spot = lax.broadcasted_iota(jnp.int32, codes.shape, 1)
@@ -546,8 +546,8 @@
                 start = sum(counts[:chunk]) + owner * own + begin
                 some = range(base + begin, base + begin + size)
                 z = [merged[chunk][owner * own + begin + i] for i in range(size)]
-                scale = [products[i] * F32(0.5 / TOP) for i in some]
-                halves = each(unpack, [values[i] for i in some], scale)
+                scale = [products[i] for i in some]
+                halves = each(unpack, [values[i] * F32(0.5 / TOP) for i in some], scale)
                 both = each(
                     lambda h: jnp.concatenate([h[0].astype(BF16), h[1].astype(BF16)], 0), halves
                 )
@@ -609,15 +609,6 @@
     )(*args)
 
 
-def exchange(arrays, axis):
-    size = lax.axis_size(axis)
-    got = [arrays[0]]
-    for offset in range(1, size):
-        pairs = [(i, i ^ offset) for i in range(size)]
-        got.append(lax.ppermute(arrays[offset], axis, pairs))
-    return got
-
-
 def plan(owned, slots):
     if slots != 4 or owned != 64:
         return [owned], (("T", 0), ("G", 0), ("F", 0), ("E", 0))

time: 77.3 us -> 77.3 us (level)
  no operation moved by 1% of the time
where the time goes in v17:
time: 77.3 us; the launch traced here: 77.2 us
  Pallas kernels  34.3 us (44%)
  starting transfers between devices  23.3 us (30%)
  waiting for transfers between devices  18.7 us (24%)
  between operations  0.9 us (1%)
    ppermute x19, starting transfers between devices, permute(): return lax.ppermute(x, axis, pairs)  23.3 us
    ppermute x19, waiting for transfers between devices, permute(): return lax.ppermute(x, axis, pairs)  18.7 us
    pallas_call x3, Pallas kernels, solve(): pl.pallas_call(functools.partial(solve_kernel, shape, half_rows), in_spec...  11.1 us
    pallas_call x2, Pallas kernels, transform(): pl.pallas_call(functools.partial(transform_kernel, peers, parts, group),...  9.73 us
    pallas_call x3, Pallas kernels, filtered(): pl.pallas_call(functools.partial(energy_kernel, slots, direct, len(pieces...  7.11 us
    pallas_call x3, Pallas kernels, gram(): pl.pallas_call(functools.partial(gram_kernel, peers, slots, direct, len(a...  3.71 us
    pallas_call x2, Pallas kernels, add(): pl.pallas_call(add_kernel, in_specs=[whole_spec()] * 2 + [any_spec()] * l...  2.59 us
  transfers between devices with their start and end apart: 19, of which 5 were waited for; matrix products, arithmetic and copies ran while one was open for 0% of the time, Pallas kernels for 36%

profile of v17, /device:TPU:0, one launch (start us, length us, event | category | flops | bytes accessed | tf_op | source)
XLA Modules:
  0.0 77.2 jit_solution(4085174779436376302)
XLA Ops:
  0.6 4.3 %transform.2 = (bf16[24,16,512]{2,1,0:T(8,128)(2,1)S(1)}, bf16[24,16,512]{2,1,0:T(8,128)(2,1)S(1)}, bf16[24,16,512]{2,1,0:T(8,128)(2,1)S(1)}, bf16[24,16,512]{2,1,0:T(8,128)(2,1)S(1)}, f32[8,128]{1,0:T(8,128)S(1)}) custom-call(s32[256]{0:T(256)} %refs_0_.3, f32[1,256]{1,0:T(1,128)} %bitcast.1, bf16[16,512,256]{2,1,0:T(8,128)(2,1)} %refs_2_.3), custom_call_target="tpu_custom_call" | custom-call | flops 1024 | bytes 1024 | tf_op jit(solution)/shard_map/transform/pallas_call | solution.py:149
  4.9 0.5 collective-permute-start
  5.5 2.6 %collective-permute-start.7 = (bf16[24,16,512]{2,1,0:T(8,128)(2,1)S(1)}, bf16[24,16,512]{2,1,0:T(8,128)(2,1)S(1)}, u32[]{:S(2)}, u32[]{:S(2)}) collective-permute-start(bf16[24,16,512]{2,1,0:T(8,128)(2,1)S(1)} %get-tuple-element.57), channel_id=1, source_target_pairs={{0,2},{1,3},{2,0},{3,1},{4,6},{5,7},{6,4},{7,5},{8,10},{9,11},{10,... | collective-permute-start | bytes 1179656 | tf_op jit(solution)/shard_map/ppermute | solution.py:630
  8.0 0.1 collective-permute-start.8
  8.1 0.0 collective-permute-done.refs_4_.refs_1_
  8.1 5.4 %transform.3 = (bf16[24,16,512]{2,1,0:T(8,128)(2,1)S(1)}, bf16[24,16,512]{2,1,0:T(8,128)(2,1)S(1)}, bf16[24,16,512]{2,1,0:T(8,128)(2,1)S(1)}, bf16[24,16,512]{2,...) custom-call(s32[256]{0:T(256)} %refs_0_.3, ...), custom_call_target="tpu_custom_call" | custom-call | flops 1024 | bytes 1024 | tf_op jit(solution)/shard_map/transform/pallas_call | solution.py:149
  13.5 0.2 collective-permute-start.4
  13.7 1.9 %collective-permute-start.5 = (bf16[24,16,512]{2,1,0:T(8,128)(2,1)S(1)}, bf16[24,16,512]{2,1,0:T(8,128)(2,1)S(1)}, u32[]{:S(2)}, u32[]{:S(2)}) collective-permute-start(bf16[24,16,512]{2,1,0:T(8,128)(2,1)S(1)} %get-tuple-element.54), channel_id=1, source_target_pairs={{0,2},{1,3},{2,0},{3,1},{4,6},{5,7},{6,4},{7,5},{8,10},{9,11},{10,... | collective-permute-start | bytes 1179656 | tf_op jit(solution)/shard_map/ppermute | solution.py:630
  15.7 0.0 collective-permute-start.6
  15.7 2.3 %collective-permute-done.7.refs_2_ = bf16[24,16,512]{2,1,0:T(8,128)(2,1)S(1)} collective-permute-done((bf16[24,16,512]{2,1,0:T(8,128)(2,1)S(1)}, bf16[24,16,512]{2,1,0:T(8,128)(2,1)S(1)}, u32[]{:S(2)}, u32[]{:S(2)}) %collective-permute-start.7) | collective-permute-done | bytes 393248 | tf_op jit(solution)/shard_map/ppermute | solution.py:630
  18.0 7.9 %collective-permute-done.8.refs_3_ = bf16[24,16,512]{2,1,0:T(8,128)(2,1)S(1)} collective-permute-done((bf16[24,16,512]{2,1,0:T(8,128)(2,1)S(1)}, bf16[24,16,512]{2,1,0:T(8,128)(2,1)S(1)}, u32[]{:S(2)}, u32[]{:S(2)}) %collective-permute-start.8) | collective-permute-done | bytes 393248 | tf_op jit(solution)/shard_map/ppermute | solution.py:630
  25.9 1.1 %gram.3 = (bf16[24,64,512]{2,1,0:T(8,128)(2,1)S(1)}, f32[8,128]{1,0:T(8,128)S(1)}, f32[12,64,128]{2,1,0:T(8,128)S(1)}, s16[400,128]{1,0:T(8,128)(2,1)S(1)}) custom-call(bf16[24,16,512]{2,1,0:T(8,128)(2,1)S(1)} %get-tuple-element.56.refs_0_, bf16[24,16,512]{2,1,0:T(8,128)(2,1)S(1)} %collective-permute-done.refs_4_.refs_1_, ...), custom_call_target="tpu_custom_call" | custom-call | flops 1024 | bytes 1024 | tf_op jit(solution)/shard_map/gram/pallas_call | solution.py:371
  27.0 1.7 %collective-permute-start.9 = (s16[400,128]{1,0:T(8,128)(2,1)S(1)}, s16[400,128]{1,0:T(8,128)(2,1)S(1)}, u32[]{:S(2)}, u32[]{:S(2)}) collective-permute-start(s16[400,128]{1,0:T(8,128)(2,1)S(1)} %get-tuple-element.61), channel_id=1, source_target_pairs={{0,4},{4,0},{8,12},{12,8},{1,5},{5,1},{9,13},{13,9},{2,6},{6,2},{1... | collective-permute-start | bytes 307208 | tf_op jit(solution)/shard_map/ppermute | solution.py:630
  28.7 0.5 collective-permute-start.1
  29.2 3.3 %collective-permute-done.9.other = s16[400,128]{1,0:T(8,128)(2,1)S(1)} collective-permute-done((s16[400,128]{1,0:T(8,128)(2,1)S(1)}, s16[400,128]{1,0:T(8,128)(2,1)S(1)}, u32[]{:S(2)}, u32[]{:S(2)}) %collective-permute-start.9) | collective-permute-done | bytes 102432 | tf_op jit(solution)/shard_map/ppermute | solution.py:630
  32.5 1.7 %collective-permute-start.2 = (bf16[16,16,512]{2,1,0:T(8,128)(2,1)S(1)}, bf16[16,16,512]{2,1,0:T(8,128)(2,1)S(1)}, u32[]{:S(2)}, u32[]{:S(2)}) collective-permute-start(bf16[16,16,512]{2,1,0:T(8,128)(2,1)S(1)} %get-tuple-element.50), channel_id=1, source_target_pairs={{0,2},{1,3},{2,0},{3,1},{4,6},{5,7},{6,4},{7,5},{8,10},{9,11},{10,... | collective-permute-start | bytes 786440 | tf_op jit(solution)/shard_map/ppermute | solution.py:630
  34.2 0.0 collective-permute-done.4.refs_1_
  34.2 0.0 collective-permute-start.3
  34.2 1.3 %add.2 = (s16[400,128]{1,0:T(8,128)(2,1)S(1)}, f32[8,128]{1,0:T(8,128)S(1)}) custom-call(f32[12,64,128]{2,1,0:T(8,128)S(1)} %get-tuple-element.60.own, s16[400,128]{1,0:T(8,128)(2,1)S(1)} %collective-permute-done.9.other, f32[8,128]{1,0:T(8,128)S(1)} %get-tuple-element.62.refs_0_), custom_call_target="tpu_custom_call" | custom-call | flops 1024 | bytes 1024 | tf_op jit(solution)/shard_map/add/pallas_call | solution.py:395
  35.5 0.0 collective-permute-done.5.refs_2_
  35.5 2.7 %collective-permute-start.11 = (s16[400,128]{1,0:T(8,128)(2,1)S(1)}, s16[400,128]{1,0:T(8,128)(2,1)S(1)}, u32[]{:S(2)}, u32[]{:S(2)}) collective-permute-start(s16[400,128]{1,0:T(8,128)(2,1)S(1)} %get-tuple-element.66.refs_0_), channel_id=1, source_target_pairs={{0,8},{4,12},{8,0},{12,4},{1,9},{5,13},{9,1},{13,5},{2,10},{6,14},... | collective-permute-start | bytes 307208 | tf_op jit(solution)/shard_map/ppermute | solution.py:630
  38.2 4.6 %collective-permute-done.6.refs_3_ = bf16[24,16,512]{2,1,0:T(8,128)(2,1)S(1)} collective-permute-done((bf16[24,16,512]{2,1,0:T(8,128)(2,1)S(1)}, bf16[24,16,512]{2,1,0:T(8,128)(2,1)S(1)}, u32[]{:S(2)}, u32[]{:S(2)}) %collective-permute-start.6) | collective-permute-done | bytes 393248 | tf_op jit(solution)/shard_map/ppermute | solution.py:630
  42.7 1.1 %gram.4 = (bf16[24,64,512]{2,1,0:T(8,128)(2,1)S(1)}, f32[8,128]{1,0:T(8,128)S(1)}, f32[12,64,128]{2,1,0:T(8,128)S(1)}, s16[400,128]{1,0:T(8,128)(2,1)S(1)}) custom-call(bf16[24,16,512]{2,1,0:T(8,128)(2,1)S(1)} %get-tuple-element.52.refs_0_, bf16[24,16,512]{2,1,0:T(8,128)(2,1)S(1)} %collective-permute-done.4.refs_1_, ...), custom_call_target="tpu_custom_call" | custom-call | flops 1024 | bytes 1024 | tf_op jit(solution)/shard_map/gram/pallas_call | solution.py:371
  43.9 1.7 %collective-permute-start.10 = (s16[400,128]{1,0:T(8,128)(2,1)S(1)}, s16[400,128]{1,0:T(8,128)(2,1)S(1)}, u32[]{:S(2)}, u32[]{:S(2)}) collective-permute-start(s16[400,128]{1,0:T(8,128)(2,1)S(1)} %get-tuple-element.65), channel_id=1, source_target_pairs={{0,4},{4,0},{8,12},{12,8},{1,5},{5,1},{9,13},{13,9},{2,6},{6,2},{1... | collective-permute-start | bytes 307208 | tf_op jit(solution)/shard_map/ppermute | solution.py:630
  45.6 0.0 collective-permute-done.11.refs_1_
  45.6 3.9 %filters.3 = (s16[400,128]{1,0:T(8,128)(2,1)S(1)}, f32[8,128]{1,0:T(8,128)S(1)}) custom-call(s16[400,128]{1,0:T(8,128)(2,1)S(1)} %get-tuple-element.66.refs_0_, s16[400,128]{1,0:T(8,128)(2,1)S(1)} %collective-permute-done.11.refs_1_, f32[8,128]{1,0:T(8,128)S(1)} %get-tuple-element.67.refs_2_), custom_call_target="tpu_custom_call" | custom-call | flops 1024 | bytes 1024 | tf_op jit(solution)/shard_map/filters/pallas_call | solution.py:506
  49.5 0.5 collective-permute-start.16
  50.0 0.0 collective-permute-done.10.other
  50.0 1.3 %add.3 = (s16[400,128]{1,0:T(8,128)(2,1)S(1)}, f32[8,128]{1,0:T(8,128)S(1)}) custom-call(f32[12,64,128]{2,1,0:T(8,128)S(1)} %get-tuple-element.64.own, s16[400,128]{1,0:T(8,128)(2,1)S(1)} %collective-permute-done.10.other, f32[8,128]{1,0:T(8,128)S(1)} %get-tuple-element.68.refs_0_), custom_call_target="tpu_custom_call" | custom-call | flops 1024 | bytes 1024 | tf_op jit(solution)/shard_map/add/pallas_call | solution.py:395
  51.3 2.7 %collective-permute-start.15 = (s16[400,128]{1,0:T(8,128)(2,1)S(1)}, s16[400,128]{1,0:T(8,128)(2,1)S(1)}, u32[]{:S(2)}, u32[]{:S(2)}) collective-permute-start(s16[400,128]{1,0:T(8,128)(2,1)S(1)} %get-tuple-element.73.refs_0_), channel_id=1, source_target_pairs={{0,8},{4,12},{8,0},{12,4},{1,9},{5,13},{9,1},{13,5},{2,10},{6,14},... | collective-permute-start | bytes 307208 | tf_op jit(solution)/shard_map/ppermute | solution.py:630
  54.0 0.0 collective-permute-done.1.refs_1_
  54.0 0.0 collective-permute-done.2.refs_2_
  54.0 0.0 collective-permute-done.3.refs_3_
  54.0 1.5 %gram.5 = (bf16[16,64,512]{2,1,0:T(8,128)(2,1)S(1)}, f32[8,128]{1,0:T(8,128)S(1)}, s16[272,128]{1,0:T(8,128)(2,1)S(1)}, s16[272,128]{1,0:T(8,128)(2,1)S(1)}) custom-call(bf16[16,16,512]{2,1,0:T(8,128)(2,1)S(1)} %get-tuple-element.48.refs_0_, bf16[16,16,512]{2,1,0:T(8,128)(2,1)S(1)} %collective-permute-done.1.refs_1_, ...), custom_call_target="tpu_custom_call" | custom-call | flops 1024 | bytes 1024 | tf_op jit(solution)/shard_map/gram/pallas_call | solution.py:371
  55.5 2.6 %collective-permute-start.12 = (s16[272,128]{1,0:T(8,128)(2,1)S(1)}, s16[272,128]{1,0:T(8,128)(2,1)S(1)}, u32[]{:S(2)}, u32[]{:S(2)}) collective-permute-start(s16[272,128]{1,0:T(8,128)(2,1)S(1)} %get-tuple-element.71.refs_0_), channel_id=1, source_target_pairs={{0,8},{4,12},{8,0},{12,4},{1,9},{5,13},{9,1},{13,5},{2,10},{6,14},... | collective-permute-start | bytes 208904 | tf_op jit(solution)/shard_map/ppermute | solution.py:630
  58.2 1.6 %collective-permute-start.13 = (s16[272,128]{1,0:T(8,128)(2,1)S(1)}, s16[272,128]{1,0:T(8,128)(2,1)S(1)}, u32[]{:S(2)}, u32[]{:S(2)}) collective-permute-start(s16[272,128]{1,0:T(8,128)(2,1)S(1)} %get-tuple-element.72), channel_id=1, source_target_pairs={{0,4},{4,0},{8,12},{12,8},{1,5},{5,1},{9,13},{13,9},{2,6},{6,2},{1... | collective-permute-start | bytes 208904 | tf_op jit(solution)/shard_map/ppermute | solution.py:630
  59.7 0.2 collective-permute-start.14
  60.0 0.0 collective-permute-done.16.refs_2_
  60.0 2.4 %energy.3 = (f32[64,256]{1,0:T(8,128)}, f32[64,2,64,64]{3,2,1,0:T(8,128)}, f32[8,128]{1,0:T(8,128)S(1)}) custom-call(bf16[24,64,512]{2,1,0:T(8,128)(2,1)S(1)} %get-tuple-element.74.refs_0_, s16[400,128]{1,0:T(8,128)(2,1)S(1)} %get-tuple-element.75.refs_1_, s16[400,128]{1,0:T(8,128)(2,1)S(1)} %collective-permute-done.16.refs_2_, ...), custom_call_target="tpu_custom_call" | custom-call | flops 1024 | bytes 1024 | tf_op jit(solution)/shard_map/energy/pallas_call | solution.py:588
  62.4 0.0 collective-permute-done.15.refs_1_
  62.4 3.8 %filters.4 = (s16[400,128]{1,0:T(8,128)(2,1)S(1)}, f32[8,128]{1,0:T(8,128)S(1)}) custom-call(s16[400,128]{1,0:T(8,128)(2,1)S(1)} %get-tuple-element.73.refs_0_, s16[400,128]{1,0:T(8,128)(2,1)S(1)} %collective-permute-done.15.refs_1_, f32[8,128]{1,0:T(8,128)S(1)} %get-tuple-element.77.refs_2_), custom_call_target="tpu_custom_call" | custom-call | flops 1024 | bytes 1024 | tf_op jit(solution)/shard_map/filters/pallas_call | solution.py:506
  66.2 0.7 collective-permute-start.18
  66.9 0.0 collective-permute-done.12.refs_1_
  66.9 0.0 collective-permute-done.13.refs_2_
  66.9 0.0 collective-permute-done.14.refs_3_
  66.9 3.4 %filters.5 = (s16[272,128]{1,0:T(8,128)(2,1)S(1)}, f32[8,128]{1,0:T(8,128)S(1)}) custom-call(s16[272,128]{1,0:T(8,128)(2,1)S(1)} %get-tuple-element.71.refs_0_, s16[272,128]{1,0:T(8,128)(2,1)S(1)} %collective-permute-done.12.refs_1_, s16[272,128]{1,0:T(8,128)(2,1)S(1)} %collective-permute-done.13.refs_2_, ...), custom_call_target="tpu_custom_call" | custom-call | flops 1024 | bytes 1024 | tf_op jit(solution)/shard_map/filters/pallas_call | solution.py:506
  70.3 1.4 %collective-permute-start.17 = (s16[272,128]{1,0:T(8,128)(2,1)S(1)}, s16[272,128]{1,0:T(8,128)(2,1)S(1)}, u32[]{:S(2)}, u32[]{:S(2)}) collective-permute-start(s16[272,128]{1,0:T(8,128)(2,1)S(1)} %get-tuple-element.79.refs_1_), channel_id=1, source_target_pairs={{0,4},{4,0},{8,12},{12,8},{1,5},{5,1},{9,13},{13,9},{2,6},{6,2},{1... | collective-permute-start | bytes 208904 | tf_op jit(solution)/shard_map/ppermute | solution.py:630
  71.7 0.0 collective-permute-done.18.refs_2_
  71.7 2.4 %energy.4 = (f32[64,256]{1,0:T(8,128)}, f32[64,2,64,64]{3,2,1,0:T(8,128)}, f32[8,128]{1,0:T(8,128)S(1)}) custom-call(bf16[24,64,512]{2,1,0:T(8,128)(2,1)S(1)} %get-tuple-element.80.refs_0_, s16[400,128]{1,0:T(8,128)(2,1)S(1)} %get-tuple-element.81.refs_1_, ...), custom_call_target="tpu_custom_call", output_to_operand_aliasing={{0}: (3, {}), {1}: (4, {})} | custom-call | flops 1024 | bytes 1024 | tf_op jit(solution)/shard_map/energy/pallas_call | solution.py:588
  74.1 0.6 collective-permute-done.17.refs_2_
  74.7 2.4 %energy.5 = (f32[64,256]{1,0:T(8,128)}, f32[64,2,64,64]{3,2,1,0:T(8,128)}, f32[8,128]{1,0:T(8,128)}) custom-call(bf16[16,64,512]{2,1,0:T(8,128)(2,1)S(1)} %get-tuple-element.70.refs_0_, s16[272,128]{1,0:T(8,128)(2,1)S(1)} %get-tuple-element.79.refs_1_, ...), custom_call_target="tpu_custom_call", output_to_operand_aliasing={{0}: (3, {}), {1}: (4, {})} | custom-call | flops 1024 | bytes 1024 | tf_op jit(solution)/shard_map/energy/pallas_call | solution.py:588
Async XLA Ops:
  4.9 3.2 %collective-permute-start = (bf16[24,16,512]{2,1,0:T(8,128)(2,1)S(1)}, bf16[24,16,512]{2,1,0:T(8,128)(2,1)S(1)}, u32[]{:S(2)}, u32[]{:S(2)}) collective-permute-start(bf16[24,16,512]{2,1,0:T(8,128)(2,1)S(1)} %get-tuple-element.47), channel_id=1, source_target_pairs={{0,1},{1,0},{2,3},{3,2},{4,5},{5,4},{6,7},{7,6},{8,9},{9,8},{10,11... | collective-permute-start | bytes 1179656 | tf_op jit(solution)/shard_map/ppermute | solution.py:630
  5.5 12.5 %collective-permute-start.7 = (bf16[24,16,512]{2,1,0:T(8,128)(2,1)S(1)}, bf16[24,16,512]{2,1,0:T(8,128)(2,1)S(1)}, u32[]{:S(2)}, u32[]{:S(2)}) collective-permute-start(bf16[24,16,512]{2,1,0:T(8,128)(2,1)S(1)} %get-tuple-element.57), channel_id=1, source_target_pairs={{0,2},{1,3},{2,0},{3,1},{4,6},{5,7},{6,4},{7,5},{8,10},{9,11},{10,... | collective-permute-start | bytes 1179656 | tf_op jit(solution)/shard_map/ppermute | solution.py:630
  8.0 17.9 %collective-permute-start.8 = (bf16[24,16,512]{2,1,0:T(8,128)(2,1)S(1)}, bf16[24,16,512]{2,1,0:T(8,128)(2,1)S(1)}, u32[]{:S(2)}, u32[]{:S(2)}) collective-permute-start(bf16[24,16,512]{2,1,0:T(8,128)(2,1)S(1)} %get-tuple-element.58), channel_id=1, source_target_pairs={{0,3},{1,2},{2,1},{3,0},{4,7},{5,6},{6,5},{7,4},{8,11},{9,10},{10,... | collective-permute-start | bytes 1179656 | tf_op jit(solution)/shard_map/ppermute | solution.py:630
  13.5 20.7 %collective-permute-start.4 = (bf16[24,16,512]{2,1,0:T(8,128)(2,1)S(1)}, bf16[24,16,512]{2,1,0:T(8,128)(2,1)S(1)}, u32[]{:S(2)}, u32[]{:S(2)}) collective-permute-start(bf16[24,16,512]{2,1,0:T(8,128)(2,1)S(1)} %get-tuple-element.53), channel_id=1, source_target_pairs={{0,1},{1,0},{2,3},{3,2},{4,5},{5,4},{6,7},{7,6},{8,9},{9,8},{10,11... | collective-permute-start | bytes 1179656 | tf_op jit(solution)/shard_map/ppermute | solution.py:630
  13.7 21.8 %collective-permute-start.5 = (bf16[24,16,512]{2,1,0:T(8,128)(2,1)S(1)}, bf16[24,16,512]{2,1,0:T(8,128)(2,1)S(1)}, u32[]{:S(2)}, u32[]{:S(2)}) collective-permute-start(bf16[24,16,512]{2,1,0:T(8,128)(2,1)S(1)} %get-tuple-element.54), channel_id=1, source_target_pairs={{0,2},{1,3},{2,0},{3,1},{4,6},{5,7},{6,4},{7,5},{8,10},{9,11},{10,... | collective-permute-start | bytes 1179656 | tf_op jit(solution)/shard_map/ppermute | solution.py:630
  15.7 27.1 %collective-permute-start.6 = (bf16[24,16,512]{2,1,0:T(8,128)(2,1)S(1)}, bf16[24,16,512]{2,1,0:T(8,128)(2,1)S(1)}, u32[]{:S(2)}, u32[]{:S(2)}) collective-permute-start(bf16[24,16,512]{2,1,0:T(8,128)(2,1)S(1)} %get-tuple-element.55), channel_id=1, source_target_pairs={{0,3},{1,2},{2,1},{3,0},{4,7},{5,6},{6,5},{7,4},{8,11},{9,10},{10,... | collective-permute-start | bytes 1179656 | tf_op jit(solution)/shard_map/ppermute | solution.py:630
  27.0 5.5 %collective-permute-start.9 = (s16[400,128]{1,0:T(8,128)(2,1)S(1)}, s16[400,128]{1,0:T(8,128)(2,1)S(1)}, u32[]{:S(2)}, u32[]{:S(2)}) collective-permute-start(s16[400,128]{1,0:T(8,128)(2,1)S(1)} %get-tuple-element.61), channel_id=1, source_target_pairs={{0,4},{4,0},{8,12},{12,8},{1,5},{5,1},{9,13},{13,9},{2,6},{6,2},{1... | collective-permute-start | bytes 307208 | tf_op jit(solution)/shard_map/ppermute | solution.py:630
  28.7 25.3 %collective-permute-start.1 = (bf16[16,16,512]{2,1,0:T(8,128)(2,1)S(1)}, bf16[16,16,512]{2,1,0:T(8,128)(2,1)S(1)}, u32[]{:S(2)}, u32[]{:S(2)}) collective-permute-start(bf16[16,16,512]{2,1,0:T(8,128)(2,1)S(1)} %get-tuple-element.49), channel_id=1, source_target_pairs={{0,1},{1,0},{2,3},{3,2},{4,5},{5,4},{6,7},{7,6},{8,9},{9,8},{10,11... | collective-permute-start | bytes 786440 | tf_op jit(solution)/shard_map/ppermute | solution.py:630
  32.5 21.5 %collective-permute-start.2 = (bf16[16,16,512]{2,1,0:T(8,128)(2,1)S(1)}, bf16[16,16,512]{2,1,0:T(8,128)(2,1)S(1)}, u32[]{:S(2)}, u32[]{:S(2)}) collective-permute-start(bf16[16,16,512]{2,1,0:T(8,128)(2,1)S(1)} %get-tuple-element.50), channel_id=1, source_target_pairs={{0,2},{1,3},{2,0},{3,1},{4,6},{5,7},{6,4},{7,5},{8,10},{9,11},{10,... | collective-permute-start | bytes 786440 | tf_op jit(solution)/shard_map/ppermute | solution.py:630
  34.2 19.8 %collective-permute-start.3 = (bf16[16,16,512]{2,1,0:T(8,128)(2,1)S(1)}, bf16[16,16,512]{2,1,0:T(8,128)(2,1)S(1)}, u32[]{:S(2)}, u32[]{:S(2)}) collective-permute-start(bf16[16,16,512]{2,1,0:T(8,128)(2,1)S(1)} %get-tuple-element.51), channel_id=1, source_target_pairs={{0,3},{1,2},{2,1},{3,0},{4,7},{5,6},{6,5},{7,4},{8,11},{9,10},{10,... | collective-permute-start | bytes 786440 | tf_op jit(solution)/shard_map/ppermute | solution.py:630
  35.5 10.1 %collective-permute-start.11 = (s16[400,128]{1,0:T(8,128)(2,1)S(1)}, s16[400,128]{1,0:T(8,128)(2,1)S(1)}, u32[]{:S(2)}, u32[]{:S(2)}) collective-permute-start(s16[400,128]{1,0:T(8,128)(2,1)S(1)} %get-tuple-element.66.refs_0_), channel_id=1, source_target_pairs={{0,8},{4,12},{8,0},{12,4},{1,9},{5,13},{9,1},{13,5},{2,10},{6,14},... | collective-permute-start | bytes 307208 | tf_op jit(solution)/shard_map/ppermute | solution.py:630
  43.9 6.1 %collective-permute-start.10 = (s16[400,128]{1,0:T(8,128)(2,1)S(1)}, s16[400,128]{1,0:T(8,128)(2,1)S(1)}, u32[]{:S(2)}, u32[]{:S(2)}) collective-permute-start(s16[400,128]{1,0:T(8,128)(2,1)S(1)} %get-tuple-element.65), channel_id=1, source_target_pairs={{0,4},{4,0},{8,12},{12,8},{1,5},{5,1},{9,13},{13,9},{2,6},{6,2},{1... | collective-permute-start | bytes 307208 | tf_op jit(solution)/shard_map/ppermute | solution.py:630
  49.5 10.4 %collective-permute-start.16 = (s16[400,128]{1,0:T(8,128)(2,1)S(1)}, s16[400,128]{1,0:T(8,128)(2,1)S(1)}, u32[]{:S(2)}, u32[]{:S(2)}) collective-permute-start(s16[400,128]{1,0:T(8,128)(2,1)S(1)} %get-tuple-element.75.refs_1_), channel_id=1, source_target_pairs={{0,4},{4,0},{8,12},{12,8},{1,5},{5,1},{9,13},{13,9},{2,6},{6,2},{1... | collective-permute-start | bytes 307208 | tf_op jit(solution)/shard_map/ppermute | solution.py:630
  51.3 11.1 %collective-permute-start.15 = (s16[400,128]{1,0:T(8,128)(2,1)S(1)}, s16[400,128]{1,0:T(8,128)(2,1)S(1)}, u32[]{:S(2)}, u32[]{:S(2)}) collective-permute-start(s16[400,128]{1,0:T(8,128)(2,1)S(1)} %get-tuple-element.73.refs_0_), channel_id=1, source_target_pairs={{0,8},{4,12},{8,0},{12,4},{1,9},{5,13},{9,1},{13,5},{2,10},{6,14},... | collective-permute-start | bytes 307208 | tf_op jit(solution)/shard_map/ppermute | solution.py:630
  55.5 11.4 %collective-permute-start.12 = (s16[272,128]{1,0:T(8,128)(2,1)S(1)}, s16[272,128]{1,0:T(8,128)(2,1)S(1)}, u32[]{:S(2)}, u32[]{:S(2)}) collective-permute-start(s16[272,128]{1,0:T(8,128)(2,1)S(1)} %get-tuple-element.71.refs_0_), channel_id=1, source_target_pairs={{0,8},{4,12},{8,0},{12,4},{1,9},{5,13},{9,1},{13,5},{2,10},{6,14},... | collective-permute-start | bytes 208904 | tf_op jit(solution)/shard_map/ppermute | solution.py:630
  58.2 8.7 %collective-permute-start.13 = (s16[272,128]{1,0:T(8,128)(2,1)S(1)}, s16[272,128]{1,0:T(8,128)(2,1)S(1)}, u32[]{:S(2)}, u32[]{:S(2)}) collective-permute-start(s16[272,128]{1,0:T(8,128)(2,1)S(1)} %get-tuple-element.72), channel_id=1, source_target_pairs={{0,4},{4,0},{8,12},{12,8},{1,5},{5,1},{9,13},{13,9},{2,6},{6,2},{1... | collective-permute-start | bytes 208904 | tf_op jit(solution)/shard_map/ppermute | solution.py:630
  59.7 7.2 %collective-permute-start.14 = (s16[272,128]{1,0:T(8,128)(2,1)S(1)}, s16[272,128]{1,0:T(8,128)(2,1)S(1)}, u32[]{:S(2)}, u32[]{:S(2)}) collective-permute-start(s16[272,128]{1,0:T(8,128)(2,1)S(1)} %get-tuple-element.72), channel_id=1, source_target_pairs={{0,12},{4,8},{8,4},{12,0},{1,13},{5,9},{9,5},{13,1},{2,14},{6,10},... | collective-permute-start | bytes 208904 | tf_op jit(solution)/shard_map/ppermute | solution.py:630
  66.2 5.6 %collective-permute-start.18 = (s16[400,128]{1,0:T(8,128)(2,1)S(1)}, s16[400,128]{1,0:T(8,128)(2,1)S(1)}, u32[]{:S(2)}, u32[]{:S(2)}) collective-permute-start(s16[400,128]{1,0:T(8,128)(2,1)S(1)} %get-tuple-element.81.refs_1_), channel_id=1, source_target_pairs={{0,4},{4,0},{8,12},{12,8},{1,5},{5,1},{9,13},{13,9},{2,6},{6,2},{1... | collective-permute-start | bytes 307208 | tf_op jit(solution)/shard_map/ppermute | solution.py:630
  70.3 4.4 %collective-permute-start.17 = (s16[272,128]{1,0:T(8,128)(2,1)S(1)}, s16[272,128]{1,0:T(8,128)(2,1)S(1)}, u32[]{:S(2)}, u32[]{:S(2)}) collective-permute-start(s16[272,128]{1,0:T(8,128)(2,1)S(1)} %get-tuple-element.79.refs_1_), channel_id=1, source_target_pairs={{0,4},{4,0},{8,12},{12,8},{1,5},{5,1},{9,13},{13,9},{2,6},{6,2},{1... | collective-permute-start | bytes 208904 | tf_op jit(solution)/shard_map/ppermute | solution.py:630

commit v18 on v14

--- a/solution.py
+++ b/solution.py
@@ -269,7 +269,7 @@
     lane = lax.broadcasted_iota(jnp.int32, (half, width), 1)
     on = (lane == row) | (lane == row + half)
     diagonal = each(lambda b: jnp.sum(jnp.where(on, b, F32(0)), axis=0, keepdims=True), both)
-    root = jnp.sqrt(jnp.maximum(place(diagonal, pad_rows(len(both))), F32(1e-30)))
+    root = jnp.sqrt(jnp.maximum(place(diagonal, pad_rows(len(both))), F32(1e-36)))
     exponent = jnp.floor(jnp.log(root) * F32(1 / math.log(2.0)))
     part = jnp.maximum(jnp.ceil((root * jnp.exp2(-exponent) - 1) * 128), F32(0))
     codes = exponent * 256 + part
@@ -281,7 +281,7 @@
 
 def spread(values, codes):
     products = outer(scale_of(codes), len(values))
-    return each(lambda v, p: v * pack(p * F32(1 / TOP)), values, products)
+    return each(lambda v, p: (v * F32(1 / TOP)) * pack(p), values, products)
 
 
 def to_short(x):
@@ -408,8 +408,19 @@
     return high, (x - high.astype(F32)).astype(BF16)
 
 
-def solve_kernel(chunks, half_rows, *refs):
+def solve_kernel(chunks, half_rows, before, *refs):
     out, token = refs[-2:]
+    puts = []
+    if before is not None:
+        energies_out, filters_out, out, token, sem = refs[-5:]
+        inputs = sum(parts for parts, _ in chunks)
+        for i, target in enumerate((energies_out, filters_out)):
+            source = refs[inputs + i]
+            put = pltpu.make_async_copy(
+                source, target.at[pl.ds(before, source.shape[0])], sem.at[i]
+            )
+            put.start()
+            puts.append(put)
     token[...] = jnp.zeros_like(token)
     width = out.shape[1]
     half = width // 2
@@ -478,7 +489,7 @@
         x = each(lambda v, m: F32(factor) * (v + m), xw, step)
     values, codes, scales = encode(each(lambda v: double(eye - v), x))
     products = outer(scales, number)
-    filters = each(lambda v, p: unpack(v, p * F32(0.5 / TOP)), values, products)
+    filters = each(lambda v, p: unpack(v * F32(0.5 / TOP), p), values, products)
     rounded = each(lambda c: c[0].astype(BF16), filters)
     turned = each(
         lambda c: jnp.concatenate([c[0].astype(BF16), c[1].astype(BF16)], 0), filters
@@ -490,31 +501,38 @@
         lambda c, h: jnp.sum(c.astype(F32) * h, keepdims=True) * F32(half), rounded, moved
     )
     energy = place([jnp.broadcast_to(e, (1, width)) for e in energy], codes.shape[0])
-    energy = jnp.maximum(energy, F32(1e-30))
+    energy = jnp.maximum(energy, F32(1e-36))
     whole = jnp.floor(jnp.log(energy) * F32(LOG_STEPS / math.log(2.0)))
     rest = jnp.round((energy * jnp.exp2(whole * F32(-1 / LOG_STEPS)) - 1.0) * F32(FINE))
     spot = lax.broadcasted_iota(jnp.int32, codes.shape, 1)
     codes = jnp.where(spot == half, whole, jnp.where(spot == half + 1, rest, codes))
     write_coded(out, values, codes)
-
-
-def solve(chunks, half_rows, after):
+    for put in puts:
+        put.wait()
+
+
+def solve(chunks, half_rows, earlier, owned, after):
     args = [x for parts, _ in chunks for x in parts]
     width = args[0].shape[-1]
     number = sum(count for _, count in chunks)
     shape = [(len(parts), count) for parts, count in chunks]
-    return pl.pallas_call(
-        functools.partial(solve_kernel, shape, half_rows),
-        in_specs=[whole_spec()] * len(args) + [any_spec()] * len(after),
-        out_specs=[whole_spec()] * 2,
-        out_shape=[
+    results = list(earlier[:2]) if earlier else []
+    hbm = pl.BlockSpec(memory_space=pltpu.HBM)
+    out = pl.pallas_call(
+        functools.partial(solve_kernel, shape, half_rows, earlier[2] if earlier else None),
+        in_specs=[whole_spec()] * (len(args) + len(results)) + [any_spec()] * len(after),
+        out_specs=[hbm] * len(results) + [whole_spec()] * 2,
+        out_shape=[jax.ShapeDtypeStruct((owned, *r.shape[1:]), F32) for r in results]
+        + [
             jax.ShapeDtypeStruct((coded_rows(number, half_rows), width), jnp.int16),
             TOKEN,
         ],
+        scratch_shapes=[pltpu.SemaphoreType.DMA((2,))] if results else [],
         compiler_params=params(),
         cost_estimate=light(),
         name="filters",
-    )(*args, *after)
+    )(*args, *results, *after)
+    return out[-2], out[-1], list(out[:2]) if results else None
 
 
 def energy_kernel(slots, direct, number, chunks, first, before, last, *refs):
@@ -561,8 +579,8 @@
                 start = sum(counts[:chunk]) + owner * own + begin
                 some = range(base + begin, base + begin + size)
                 z = [merged[chunk][owner * own + begin + i] for i in range(size)]
-                scale = [products[i] * F32(0.5 / TOP) for i in some]
-                halves = each(unpack, [values[i] for i in some], scale)
+                scale = [products[i] for i in some]
+                halves = each(unpack, [values[i] * F32(0.5 / TOP) for i in some], scale)
                 both = each(
                     lambda h: jnp.concatenate([h[0].astype(BF16), h[1].astype(BF16)], 0), halves
                 )
@@ -718,9 +736,11 @@
         return range(c, last)
 
     def do_solve(c):
-        nonlocal token
+        nonlocal token, carry, earlier
         work = [(parts[k], sizes[k] // halves) for k in joined("F", c)]
-        own, done = solve(work, merged[c].shape[1] // 2, token)
+        own, done, written = solve(work, merged[c].shape[1] // 2, earlier, owned, token)
+        if written:
+            carry, earlier = written, None
         token = [done]
         if paired:
             pieces[c] = [own, permute(own, "space", 1)]
@@ -730,9 +750,10 @@
     def do_energy(c):
         nonlocal token, carry, earlier
         chunks = joined("E", c)
+        copies = c > 0 or len(sizes) == 1
         carry, earlier, done = filtered(
             [merged[k] for k in chunks], pieces[c], halves, paired, earlier, carry, owned,
-            starts[c], chunks[-1] == len(sizes) - 1, token,
+            starts[c], copies, token,
         )
         token = [done]
 

time: 77.7 us -> 76.8 us (0.988)
  waiting for transfers between devices: 19.5 us -> 18.7 us
    ppermute x19, waiting for transfers between devices: 19.5 us -> 18.7 us  [permute(): return lax.ppermute(x, axis, pairs)]
where the time goes in v18:
time: 76.8 us; the launch traced here: 76.7 us
  Pallas kernels  33.7 us (44%)
  starting transfers between devices  23.3 us (30%)
  waiting for transfers between devices  18.7 us (24%)
  between operations  0.91 us (1%)
    ppermute x19, starting transfers between devices, permute(): return lax.ppermute(x, axis, pairs)  23.3 us
    ppermute x19, waiting for transfers between devices, permute(): return lax.ppermute(x, axis, pairs)  18.7 us
    pallas_call x3, Pallas kernels, solve(): pl.pallas_call(functools.partial(solve_kernel, shape, half_rows, earlier[...  11.2 us
    pallas_call x2, Pallas kernels, transform(): pl.pallas_call(functools.partial(transform_kernel, peers, parts, group),...  9.73 us
    pallas_call x3, Pallas kernels, filtered(): pl.pallas_call(functools.partial(energy_kernel, slots, direct, len(pieces...  6.56 us
    pallas_call x3, Pallas kernels, gram(): pl.pallas_call(functools.partial(gram_kernel, peers, slots, direct, len(a...  3.71 us
    pallas_call x2, Pallas kernels, add(): pl.pallas_call(add_kernel, in_specs=[whole_spec()] * 2 + [any_spec()] * l...  2.6 us
  transfers between devices with their start and end apart: 19, of which 5 were waited for; matrix products, arithmetic and copies ran while one was open for 0% of the time, Pallas kernels for 35%

profile of v18, /device:TPU:0, one launch (start us, length us, event | category | flops | bytes accessed | tf_op | source)
XLA Modules:
  0.0 76.7 jit_solution(15493289636226731649)
XLA Ops:
  0.6 4.3 %transform.2 = (bf16[24,16,512]{2,1,0:T(8,128)(2,1)S(1)}, bf16[24,16,512]{2,1,0:T(8,128)(2,1)S(1)}, bf16[24,16,512]{2,1,0:T(8,128)(2,1)S(1)}, bf16[24,16,512]{2,1,0:T(8,128)(2,1)S(1)}, f32[8,128]{1,0:T(8,128)S(1)}) custom-call(s32[256]{0:T(256)} %refs_0_.3, f32[1,256]{1,0:T(1,128)} %bitcast.1, bf16[16,512,256]{2,1,0:T(8,128)(2,1)} %refs_2_.3), custom_call_target="tpu_custom_call" | custom-call | flops 1024 | bytes 1024 | tf_op jit(solution)/shard_map/transform/pallas_call | solution.py:149
  4.9 0.5 collective-permute-start
  5.5 2.6 %collective-permute-start.7 = (bf16[24,16,512]{2,1,0:T(8,128)(2,1)S(1)}, bf16[24,16,512]{2,1,0:T(8,128)(2,1)S(1)}, u32[]{:S(2)}, u32[]{:S(2)}) collective-permute-start(bf16[24,16,512]{2,1,0:T(8,128)(2,1)S(1)} %get-tuple-element.59), channel_id=1, source_target_pairs={{0,2},{1,3},{2,0},{3,1},{4,6},{5,7},{6,4},{7,5},{8,10},{9,11},{10,... | collective-permute-start | bytes 1179656 | tf_op jit(solution)/shard_map/ppermute | solution.py:681
  8.0 0.1 collective-permute-start.8
  8.1 0.0 collective-permute-done.refs_4_.refs_1_
  8.1 5.4 %transform.3 = (bf16[24,16,512]{2,1,0:T(8,128)(2,1)S(1)}, bf16[24,16,512]{2,1,0:T(8,128)(2,1)S(1)}, bf16[24,16,512]{2,1,0:T(8,128)(2,1)S(1)}, bf16[24,16,512]{2,...) custom-call(s32[256]{0:T(256)} %refs_0_.3, ...), custom_call_target="tpu_custom_call" | custom-call | flops 1024 | bytes 1024 | tf_op jit(solution)/shard_map/transform/pallas_call | solution.py:149
  13.5 0.2 collective-permute-start.4
  13.7 1.9 %collective-permute-start.5 = (bf16[24,16,512]{2,1,0:T(8,128)(2,1)S(1)}, bf16[24,16,512]{2,1,0:T(8,128)(2,1)S(1)}, u32[]{:S(2)}, u32[]{:S(2)}) collective-permute-start(bf16[24,16,512]{2,1,0:T(8,128)(2,1)S(1)} %get-tuple-element.56), channel_id=1, source_target_pairs={{0,2},{1,3},{2,0},{3,1},{4,6},{5,7},{6,4},{7,5},{8,10},{9,11},{10,... | collective-permute-start | bytes 1179656 | tf_op jit(solution)/shard_map/ppermute | solution.py:681
  15.7 0.0 collective-permute-start.6
  15.7 2.3 %collective-permute-done.7.refs_2_ = bf16[24,16,512]{2,1,0:T(8,128)(2,1)S(1)} collective-permute-done((bf16[24,16,512]{2,1,0:T(8,128)(2,1)S(1)}, bf16[24,16,512]{2,1,0:T(8,128)(2,1)S(1)}, u32[]{:S(2)}, u32[]{:S(2)}) %collective-permute-start.7) | collective-permute-done | bytes 393248 | tf_op jit(solution)/shard_map/ppermute | solution.py:681
  18.0 7.9 %collective-permute-done.8.refs_3_ = bf16[24,16,512]{2,1,0:T(8,128)(2,1)S(1)} collective-permute-done((bf16[24,16,512]{2,1,0:T(8,128)(2,1)S(1)}, bf16[24,16,512]{2,1,0:T(8,128)(2,1)S(1)}, u32[]{:S(2)}, u32[]{:S(2)}) %collective-permute-start.8) | collective-permute-done | bytes 393248 | tf_op jit(solution)/shard_map/ppermute | solution.py:681
  25.9 1.1 %gram.3 = (bf16[24,64,512]{2,1,0:T(8,128)(2,1)S(1)}, f32[8,128]{1,0:T(8,128)S(1)}, f32[12,64,128]{2,1,0:T(8,128)S(1)}, s16[400,128]{1,0:T(8,128)(2,1)S(1)}) custom-call(bf16[24,16,512]{2,1,0:T(8,128)(2,1)S(1)} %get-tuple-element.58.refs_0_, bf16[24,16,512]{2,1,0:T(8,128)(2,1)S(1)} %collective-permute-done.refs_4_.refs_1_, ...), custom_call_target="tpu_custom_call" | custom-call | flops 1024 | bytes 1024 | tf_op jit(solution)/shard_map/gram/pallas_call | solution.py:371
  27.0 1.7 %collective-permute-start.9 = (s16[400,128]{1,0:T(8,128)(2,1)S(1)}, s16[400,128]{1,0:T(8,128)(2,1)S(1)}, u32[]{:S(2)}, u32[]{:S(2)}) collective-permute-start(s16[400,128]{1,0:T(8,128)(2,1)S(1)} %get-tuple-element.63), channel_id=1, source_target_pairs={{0,4},{4,0},{8,12},{12,8},{1,5},{5,1},{9,13},{13,9},{2,6},{6,2},{1... | collective-permute-start | bytes 307208 | tf_op jit(solution)/shard_map/ppermute | solution.py:681
  28.7 0.5 collective-permute-start.1
  29.2 3.3 %collective-permute-done.9.other = s16[400,128]{1,0:T(8,128)(2,1)S(1)} collective-permute-done((s16[400,128]{1,0:T(8,128)(2,1)S(1)}, s16[400,128]{1,0:T(8,128)(2,1)S(1)}, u32[]{:S(2)}, u32[]{:S(2)}) %collective-permute-start.9) | collective-permute-done | bytes 102432 | tf_op jit(solution)/shard_map/ppermute | solution.py:681
  32.5 1.7 %collective-permute-start.2 = (bf16[16,16,512]{2,1,0:T(8,128)(2,1)S(1)}, bf16[16,16,512]{2,1,0:T(8,128)(2,1)S(1)}, u32[]{:S(2)}, u32[]{:S(2)}) collective-permute-start(bf16[16,16,512]{2,1,0:T(8,128)(2,1)S(1)} %get-tuple-element.52), channel_id=1, source_target_pairs={{0,2},{1,3},{2,0},{3,1},{4,6},{5,7},{6,4},{7,5},{8,10},{9,11},{10,... | collective-permute-start | bytes 786440 | tf_op jit(solution)/shard_map/ppermute | solution.py:681
  34.2 0.0 collective-permute-done.4.refs_1_
  34.2 0.0 collective-permute-start.3
  34.2 1.3 %add.2 = (s16[400,128]{1,0:T(8,128)(2,1)S(1)}, f32[8,128]{1,0:T(8,128)S(1)}) custom-call(f32[12,64,128]{2,1,0:T(8,128)S(1)} %get-tuple-element.62.own, s16[400,128]{1,0:T(8,128)(2,1)S(1)} %collective-permute-done.9.other, f32[8,128]{1,0:T(8,128)S(1)} %get-tuple-element.64.refs_0_), custom_call_target="tpu_custom_call" | custom-call | flops 1024 | bytes 1024 | tf_op jit(solution)/shard_map/add/pallas_call | solution.py:395
  35.5 0.0 collective-permute-done.5.refs_2_
  35.5 2.7 %collective-permute-start.11 = (s16[400,128]{1,0:T(8,128)(2,1)S(1)}, s16[400,128]{1,0:T(8,128)(2,1)S(1)}, u32[]{:S(2)}, u32[]{:S(2)}) collective-permute-start(s16[400,128]{1,0:T(8,128)(2,1)S(1)} %get-tuple-element.68.refs_0_), channel_id=1, source_target_pairs={{0,8},{4,12},{8,0},{12,4},{1,9},{5,13},{9,1},{13,5},{2,10},{6,14},... | collective-permute-start | bytes 307208 | tf_op jit(solution)/shard_map/ppermute | solution.py:681
  38.2 4.6 %collective-permute-done.6.refs_3_ = bf16[24,16,512]{2,1,0:T(8,128)(2,1)S(1)} collective-permute-done((bf16[24,16,512]{2,1,0:T(8,128)(2,1)S(1)}, bf16[24,16,512]{2,1,0:T(8,128)(2,1)S(1)}, u32[]{:S(2)}, u32[]{:S(2)}) %collective-permute-start.6) | collective-permute-done | bytes 393248 | tf_op jit(solution)/shard_map/ppermute | solution.py:681
  42.7 1.1 %gram.4 = (bf16[24,64,512]{2,1,0:T(8,128)(2,1)S(1)}, f32[8,128]{1,0:T(8,128)S(1)}, f32[12,64,128]{2,1,0:T(8,128)S(1)}, s16[400,128]{1,0:T(8,128)(2,1)S(1)}) custom-call(bf16[24,16,512]{2,1,0:T(8,128)(2,1)S(1)} %get-tuple-element.54.refs_0_, bf16[24,16,512]{2,1,0:T(8,128)(2,1)S(1)} %collective-permute-done.4.refs_1_, ...), custom_call_target="tpu_custom_call" | custom-call | flops 1024 | bytes 1024 | tf_op jit(solution)/shard_map/gram/pallas_call | solution.py:371
  43.9 1.7 %collective-permute-start.10 = (s16[400,128]{1,0:T(8,128)(2,1)S(1)}, s16[400,128]{1,0:T(8,128)(2,1)S(1)}, u32[]{:S(2)}, u32[]{:S(2)}) collective-permute-start(s16[400,128]{1,0:T(8,128)(2,1)S(1)} %get-tuple-element.67), channel_id=1, source_target_pairs={{0,4},{4,0},{8,12},{12,8},{1,5},{5,1},{9,13},{13,9},{2,6},{6,2},{1... | collective-permute-start | bytes 307208 | tf_op jit(solution)/shard_map/ppermute | solution.py:681
  45.6 0.0 collective-permute-done.11.refs_1_
  45.6 3.9 %filters.3 = (s16[400,128]{1,0:T(8,128)(2,1)S(1)}, f32[8,128]{1,0:T(8,128)S(1)}) custom-call(s16[400,128]{1,0:T(8,128)(2,1)S(1)} %get-tuple-element.68.refs_0_, s16[400,128]{1,0:T(8,128)(2,1)S(1)} %collective-permute-done.11.refs_1_, f32[8,128]{1,0:T(8,128)S(1)} %get-tuple-element.69.refs_2_), custom_call_target="tpu_custom_call" | custom-call | flops 1024 | bytes 1024 | tf_op jit(solution)/shard_map/filters/pallas_call | solution.py:521
  49.5 0.5 collective-permute-start.16
  50.0 0.0 collective-permute-done.10.other
  50.0 1.3 %add.3 = (s16[400,128]{1,0:T(8,128)(2,1)S(1)}, f32[8,128]{1,0:T(8,128)S(1)}) custom-call(f32[12,64,128]{2,1,0:T(8,128)S(1)} %get-tuple-element.66.own, s16[400,128]{1,0:T(8,128)(2,1)S(1)} %collective-permute-done.10.other, f32[8,128]{1,0:T(8,128)S(1)} %get-tuple-element.70.refs_0_), custom_call_target="tpu_custom_call" | custom-call | flops 1024 | bytes 1024 | tf_op jit(solution)/shard_map/add/pallas_call | solution.py:395
  51.3 2.7 %collective-permute-start.15 = (s16[400,128]{1,0:T(8,128)(2,1)S(1)}, s16[400,128]{1,0:T(8,128)(2,1)S(1)}, u32[]{:S(2)}, u32[]{:S(2)}) collective-permute-start(s16[400,128]{1,0:T(8,128)(2,1)S(1)} %get-tuple-element.75.refs_0_), channel_id=1, source_target_pairs={{0,8},{4,12},{8,0},{12,4},{1,9},{5,13},{9,1},{13,5},{2,10},{6,14},... | collective-permute-start | bytes 307208 | tf_op jit(solution)/shard_map/ppermute | solution.py:681
  54.0 0.0 collective-permute-done.1.refs_1_
  54.0 0.0 collective-permute-done.2.refs_2_
  54.0 0.0 collective-permute-done.3.refs_3_
  54.0 1.5 %gram.5 = (bf16[16,64,512]{2,1,0:T(8,128)(2,1)S(1)}, f32[8,128]{1,0:T(8,128)S(1)}, s16[272,128]{1,0:T(8,128)(2,1)S(1)}, s16[272,128]{1,0:T(8,128)(2,1)S(1)}) custom-call(bf16[16,16,512]{2,1,0:T(8,128)(2,1)S(1)} %get-tuple-element.50.refs_0_, bf16[16,16,512]{2,1,0:T(8,128)(2,1)S(1)} %collective-permute-done.1.refs_1_, ...), custom_call_target="tpu_custom_call" | custom-call | flops 1024 | bytes 1024 | tf_op jit(solution)/shard_map/gram/pallas_call | solution.py:371
  55.5 2.7 %collective-permute-start.12 = (s16[272,128]{1,0:T(8,128)(2,1)S(1)}, s16[272,128]{1,0:T(8,128)(2,1)S(1)}, u32[]{:S(2)}, u32[]{:S(2)}) collective-permute-start(s16[272,128]{1,0:T(8,128)(2,1)S(1)} %get-tuple-element.73.refs_0_), channel_id=1, source_target_pairs={{0,8},{4,12},{8,0},{12,4},{1,9},{5,13},{9,1},{13,5},{2,10},{6,14},... | collective-permute-start | bytes 208904 | tf_op jit(solution)/shard_map/ppermute | solution.py:681
  58.2 1.6 %collective-permute-start.13 = (s16[272,128]{1,0:T(8,128)(2,1)S(1)}, s16[272,128]{1,0:T(8,128)(2,1)S(1)}, u32[]{:S(2)}, u32[]{:S(2)}) collective-permute-start(s16[272,128]{1,0:T(8,128)(2,1)S(1)} %get-tuple-element.74), channel_id=1, source_target_pairs={{0,4},{4,0},{8,12},{12,8},{1,5},{5,1},{9,13},{13,9},{2,6},{6,2},{1... | collective-permute-start | bytes 208904 | tf_op jit(solution)/shard_map/ppermute | solution.py:681
  59.7 0.2 collective-permute-start.14
  60.0 0.0 collective-permute-done.16.refs_2_
  60.0 1.8 %energy.3 = (f32[24,256]{1,0:T(8,128)S(1)}, f32[24,2,64,64]{3,2,1,0:T(8,128)S(1)}, f32[8,128]{1,0:T(8,128)S(1)}) custom-call(bf16[24,64,512]{2,1,0:T(8,128)(2,1)S(1)} %get-tuple-element.76.refs_0_, s16[400,128]{1,0:T(8,128)(2,1)S(1)} %get-tuple-element.77.refs_1_, s16[400,128]{1,0:T(8,128)(2,1)S(1)} %collective-permute-done.16.refs_2_, ...), custom_call_target="tpu_custom_call" | custom-call | flops 1024 | bytes 1024 | tf_op jit(solution)/shard_map/energy/pallas_call | solution.py:635
  61.8 0.0 collective-permute-done.15.refs_1_
  61.8 3.8 %filters.4 = (f32[64,256]{1,0:T(8,128)}, f32[64,2,64,64]{3,2,1,0:T(8,128)}, s16[400,128]{1,0:T(8,128)(2,1)S(1)}, f32[8,128]{1,0:T(8,128)S(1)}) custom-call(s16[400,128]{1,0:T(8,128)(2,1)S(1)} %get-tuple-element.75.refs_0_, s16[400,128]{1,0:T(8,128)(2,1)S(1)} %collective-permute-done.15.refs_1_, f32[24,256]{1,0:T(8,128)S(1)} %get-tuple-element.79.refs_2_, ...), custom_call_target="tpu_custom_call" | custom-call | flops 1024 | bytes 1024 | tf_op jit(solution)/shard_map/filters/pallas_call | solution.py:521
  65.6 0.7 collective-permute-start.18
  66.3 0.0 collective-permute-done.12.refs_1_
  66.3 0.0 collective-permute-done.13.refs_2_
  66.3 0.0 collective-permute-done.14.refs_3_
  66.3 3.4 %filters.5 = (s16[272,128]{1,0:T(8,128)(2,1)S(1)}, f32[8,128]{1,0:T(8,128)S(1)}) custom-call(s16[272,128]{1,0:T(8,128)(2,1)S(1)} %get-tuple-element.73.refs_0_, s16[272,128]{1,0:T(8,128)(2,1)S(1)} %collective-permute-done.12.refs_1_, s16[272,128]{1,0:T(8,128)(2,1)S(1)} %collective-permute-done.13.refs_2_, ...), custom_call_target="tpu_custom_call" | custom-call | flops 1024 | bytes 1024 | tf_op jit(solution)/shard_map/filters/pallas_call | solution.py:521
  69.7 1.4 %collective-permute-start.17 = (s16[272,128]{1,0:T(8,128)(2,1)S(1)}, s16[272,128]{1,0:T(8,128)(2,1)S(1)}, u32[]{:S(2)}, u32[]{:S(2)}) collective-permute-start(s16[272,128]{1,0:T(8,128)(2,1)S(1)} %get-tuple-element.83.refs_1_), channel_id=1, source_target_pairs={{0,4},{4,0},{8,12},{12,8},{1,5},{5,1},{9,13},{13,9},{2,6},{6,2},{1... | collective-permute-start | bytes 208904 | tf_op jit(solution)/shard_map/ppermute | solution.py:681
  71.2 0.0 collective-permute-done.18.refs_2_
  71.2 2.4 %energy.4 = (f32[64,256]{1,0:T(8,128)}, f32[64,2,64,64]{3,2,1,0:T(8,128)}, f32[8,128]{1,0:T(8,128)S(1)}) custom-call(bf16[24,64,512]{2,1,0:T(8,128)(2,1)S(1)} %get-tuple-element.84.refs_0_, s16[400,128]{1,0:T(8,128)(2,1)S(1)} %get-tuple-element.85.refs_1_, ...), custom_call_target="tpu_custom_call", output_to_operand_aliasing={{0}: (3, {}), {1}: (4, {})} | custom-call | flops 1024 | bytes 1024 | tf_op jit(solution)/shard_map/energy/pallas_call | solution.py:635
  73.6 0.5 collective-permute-done.17.refs_2_
  74.1 2.4 %energy.5 = (f32[64,256]{1,0:T(8,128)}, f32[64,2,64,64]{3,2,1,0:T(8,128)}, f32[8,128]{1,0:T(8,128)}) custom-call(bf16[16,64,512]{2,1,0:T(8,128)(2,1)S(1)} %get-tuple-element.72.refs_0_, s16[272,128]{1,0:T(8,128)(2,1)S(1)} %get-tuple-element.83.refs_1_, ...), custom_call_target="tpu_custom_call", output_to_operand_aliasing={{0}: (3, {}), {1}: (4, {})} | custom-call | flops 1024 | bytes 1024 | tf_op jit(solution)/shard_map/energy/pallas_call | solution.py:635
Async XLA Ops:
  4.9 3.2 %collective-permute-start = (bf16[24,16,512]{2,1,0:T(8,128)(2,1)S(1)}, bf16[24,16,512]{2,1,0:T(8,128)(2,1)S(1)}, u32[]{:S(2)}, u32[]{:S(2)}) collective-permute-start(bf16[24,16,512]{2,1,0:T(8,128)(2,1)S(1)} %get-tuple-element.49), channel_id=1, source_target_pairs={{0,1},{1,0},{2,3},{3,2},{4,5},{5,4},{6,7},{7,6},{8,9},{9,8},{10,11... | collective-permute-start | bytes 1179656 | tf_op jit(solution)/shard_map/ppermute | solution.py:681
  5.5 12.5 %collective-permute-start.7 = (bf16[24,16,512]{2,1,0:T(8,128)(2,1)S(1)}, bf16[24,16,512]{2,1,0:T(8,128)(2,1)S(1)}, u32[]{:S(2)}, u32[]{:S(2)}) collective-permute-start(bf16[24,16,512]{2,1,0:T(8,128)(2,1)S(1)} %get-tuple-element.59), channel_id=1, source_target_pairs={{0,2},{1,3},{2,0},{3,1},{4,6},{5,7},{6,4},{7,5},{8,10},{9,11},{10,... | collective-permute-start | bytes 1179656 | tf_op jit(solution)/shard_map/ppermute | solution.py:681
  8.0 17.9 %collective-permute-start.8 = (bf16[24,16,512]{2,1,0:T(8,128)(2,1)S(1)}, bf16[24,16,512]{2,1,0:T(8,128)(2,1)S(1)}, u32[]{:S(2)}, u32[]{:S(2)}) collective-permute-start(bf16[24,16,512]{2,1,0:T(8,128)(2,1)S(1)} %get-tuple-element.60), channel_id=1, source_target_pairs={{0,3},{1,2},{2,1},{3,0},{4,7},{5,6},{6,5},{7,4},{8,11},{9,10},{10,... | collective-permute-start | bytes 1179656 | tf_op jit(solution)/shard_map/ppermute | solution.py:681
  13.5 20.7 %collective-permute-start.4 = (bf16[24,16,512]{2,1,0:T(8,128)(2,1)S(1)}, bf16[24,16,512]{2,1,0:T(8,128)(2,1)S(1)}, u32[]{:S(2)}, u32[]{:S(2)}) collective-permute-start(bf16[24,16,512]{2,1,0:T(8,128)(2,1)S(1)} %get-tuple-element.55), channel_id=1, source_target_pairs={{0,1},{1,0},{2,3},{3,2},{4,5},{5,4},{6,7},{7,6},{8,9},{9,8},{10,11... | collective-permute-start | bytes 1179656 | tf_op jit(solution)/shard_map/ppermute | solution.py:681
  13.7 21.8 %collective-permute-start.5 = (bf16[24,16,512]{2,1,0:T(8,128)(2,1)S(1)}, bf16[24,16,512]{2,1,0:T(8,128)(2,1)S(1)}, u32[]{:S(2)}, u32[]{:S(2)}) collective-permute-start(bf16[24,16,512]{2,1,0:T(8,128)(2,1)S(1)} %get-tuple-element.56), channel_id=1, source_target_pairs={{0,2},{1,3},{2,0},{3,1},{4,6},{5,7},{6,4},{7,5},{8,10},{9,11},{10,... | collective-permute-start | bytes 1179656 | tf_op jit(solution)/shard_map/ppermute | solution.py:681
  15.7 27.1 %collective-permute-start.6 = (bf16[24,16,512]{2,1,0:T(8,128)(2,1)S(1)}, bf16[24,16,512]{2,1,0:T(8,128)(2,1)S(1)}, u32[]{:S(2)}, u32[]{:S(2)}) collective-permute-start(bf16[24,16,512]{2,1,0:T(8,128)(2,1)S(1)} %get-tuple-element.57), channel_id=1, source_target_pairs={{0,3},{1,2},{2,1},{3,0},{4,7},{5,6},{6,5},{7,4},{8,11},{9,10},{10,... | collective-permute-start | bytes 1179656 | tf_op jit(solution)/shard_map/ppermute | solution.py:681
  27.0 5.5 %collective-permute-start.9 = (s16[400,128]{1,0:T(8,128)(2,1)S(1)}, s16[400,128]{1,0:T(8,128)(2,1)S(1)}, u32[]{:S(2)}, u32[]{:S(2)}) collective-permute-start(s16[400,128]{1,0:T(8,128)(2,1)S(1)} %get-tuple-element.63), channel_id=1, source_target_pairs={{0,4},{4,0},{8,12},{12,8},{1,5},{5,1},{9,13},{13,9},{2,6},{6,2},{1... | collective-permute-start | bytes 307208 | tf_op jit(solution)/shard_map/ppermute | solution.py:681
  28.7 25.3 %collective-permute-start.1 = (bf16[16,16,512]{2,1,0:T(8,128)(2,1)S(1)}, bf16[16,16,512]{2,1,0:T(8,128)(2,1)S(1)}, u32[]{:S(2)}, u32[]{:S(2)}) collective-permute-start(bf16[16,16,512]{2,1,0:T(8,128)(2,1)S(1)} %get-tuple-element.51), channel_id=1, source_target_pairs={{0,1},{1,0},{2,3},{3,2},{4,5},{5,4},{6,7},{7,6},{8,9},{9,8},{10,11... | collective-permute-start | bytes 786440 | tf_op jit(solution)/shard_map/ppermute | solution.py:681
  32.5 21.5 %collective-permute-start.2 = (bf16[16,16,512]{2,1,0:T(8,128)(2,1)S(1)}, bf16[16,16,512]{2,1,0:T(8,128)(2,1)S(1)}, u32[]{:S(2)}, u32[]{:S(2)}) collective-permute-start(bf16[16,16,512]{2,1,0:T(8,128)(2,1)S(1)} %get-tuple-element.52), channel_id=1, source_target_pairs={{0,2},{1,3},{2,0},{3,1},{4,6},{5,7},{6,4},{7,5},{8,10},{9,11},{10,... | collective-permute-start | bytes 786440 | tf_op jit(solution)/shard_map/ppermute | solution.py:681
  34.2 19.8 %collective-permute-start.3 = (bf16[16,16,512]{2,1,0:T(8,128)(2,1)S(1)}, bf16[16,16,512]{2,1,0:T(8,128)(2,1)S(1)}, u32[]{:S(2)}, u32[]{:S(2)}) collective-permute-start(bf16[16,16,512]{2,1,0:T(8,128)(2,1)S(1)} %get-tuple-element.53), channel_id=1, source_target_pairs={{0,3},{1,2},{2,1},{3,0},{4,7},{5,6},{6,5},{7,4},{8,11},{9,10},{10,... | collective-permute-start | bytes 786440 | tf_op jit(solution)/shard_map/ppermute | solution.py:681
  35.5 10.1 %collective-permute-start.11 = (s16[400,128]{1,0:T(8,128)(2,1)S(1)}, s16[400,128]{1,0:T(8,128)(2,1)S(1)}, u32[]{:S(2)}, u32[]{:S(2)}) collective-permute-start(s16[400,128]{1,0:T(8,128)(2,1)S(1)} %get-tuple-element.68.refs_0_), channel_id=1, source_target_pairs={{0,8},{4,12},{8,0},{12,4},{1,9},{5,13},{9,1},{13,5},{2,10},{6,14},... | collective-permute-start | bytes 307208 | tf_op jit(solution)/shard_map/ppermute | solution.py:681
  43.9 6.1 %collective-permute-start.10 = (s16[400,128]{1,0:T(8,128)(2,1)S(1)}, s16[400,128]{1,0:T(8,128)(2,1)S(1)}, u32[]{:S(2)}, u32[]{:S(2)}) collective-permute-start(s16[400,128]{1,0:T(8,128)(2,1)S(1)} %get-tuple-element.67), channel_id=1, source_target_pairs={{0,4},{4,0},{8,12},{12,8},{1,5},{5,1},{9,13},{13,9},{2,6},{6,2},{1... | collective-permute-start | bytes 307208 | tf_op jit(solution)/shard_map/ppermute | solution.py:681
  49.5 10.4 %collective-permute-start.16 = (s16[400,128]{1,0:T(8,128)(2,1)S(1)}, s16[400,128]{1,0:T(8,128)(2,1)S(1)}, u32[]{:S(2)}, u32[]{:S(2)}) collective-permute-start(s16[400,128]{1,0:T(8,128)(2,1)S(1)} %get-tuple-element.77.refs_1_), channel_id=1, source_target_pairs={{0,4},{4,0},{8,12},{12,8},{1,5},{5,1},{9,13},{13,9},{2,6},{6,2},{1... | collective-permute-start | bytes 307208 | tf_op jit(solution)/shard_map/ppermute | solution.py:681
  51.3 10.4 %collective-permute-start.15 = (s16[400,128]{1,0:T(8,128)(2,1)S(1)}, s16[400,128]{1,0:T(8,128)(2,1)S(1)}, u32[]{:S(2)}, u32[]{:S(2)}) collective-permute-start(s16[400,128]{1,0:T(8,128)(2,1)S(1)} %get-tuple-element.75.refs_0_), channel_id=1, source_target_pairs={{0,8},{4,12},{8,0},{12,4},{1,9},{5,13},{9,1},{13,5},{2,10},{6,14},... | collective-permute-start | bytes 307208 | tf_op jit(solution)/shard_map/ppermute | solution.py:681
  55.5 10.8 %collective-permute-start.12 = (s16[272,128]{1,0:T(8,128)(2,1)S(1)}, s16[272,128]{1,0:T(8,128)(2,1)S(1)}, u32[]{:S(2)}, u32[]{:S(2)}) collective-permute-start(s16[272,128]{1,0:T(8,128)(2,1)S(1)} %get-tuple-element.73.refs_0_), channel_id=1, source_target_pairs={{0,8},{4,12},{8,0},{12,4},{1,9},{5,13},{9,1},{13,5},{2,10},{6,14},... | collective-permute-start | bytes 208904 | tf_op jit(solution)/shard_map/ppermute | solution.py:681
  58.2 8.2 %collective-permute-start.13 = (s16[272,128]{1,0:T(8,128)(2,1)S(1)}, s16[272,128]{1,0:T(8,128)(2,1)S(1)}, u32[]{:S(2)}, u32[]{:S(2)}) collective-permute-start(s16[272,128]{1,0:T(8,128)(2,1)S(1)} %get-tuple-element.74), channel_id=1, source_target_pairs={{0,4},{4,0},{8,12},{12,8},{1,5},{5,1},{9,13},{13,9},{2,6},{6,2},{1... | collective-permute-start | bytes 208904 | tf_op jit(solution)/shard_map/ppermute | solution.py:681
  59.7 6.6 %collective-permute-start.14 = (s16[272,128]{1,0:T(8,128)(2,1)S(1)}, s16[272,128]{1,0:T(8,128)(2,1)S(1)}, u32[]{:S(2)}, u32[]{:S(2)}) collective-permute-start(s16[272,128]{1,0:T(8,128)(2,1)S(1)} %get-tuple-element.74), channel_id=1, source_target_pairs={{0,12},{4,8},{8,4},{12,0},{1,13},{5,9},{9,5},{13,1},{2,14},{6,10},... | collective-permute-start | bytes 208904 | tf_op jit(solution)/shard_map/ppermute | solution.py:681
  65.6 5.6 %collective-permute-start.18 = (s16[400,128]{1,0:T(8,128)(2,1)S(1)}, s16[400,128]{1,0:T(8,128)(2,1)S(1)}, u32[]{:S(2)}, u32[]{:S(2)}) collective-permute-start(s16[400,128]{1,0:T(8,128)(2,1)S(1)} %get-tuple-element.85.refs_1_), channel_id=1, source_target_pairs={{0,4},{4,0},{8,12},{12,8},{1,5},{5,1},{9,13},{13,9},{2,6},{6,2},{1... | collective-permute-start | bytes 307208 | tf_op jit(solution)/shard_map/ppermute | solution.py:681
  69.7 4.4 %collective-permute-start.17 = (s16[272,128]{1,0:T(8,128)(2,1)S(1)}, s16[272,128]{1,0:T(8,128)(2,1)S(1)}, u32[]{:S(2)}, u32[]{:S(2)}) collective-permute-start(s16[272,128]{1,0:T(8,128)(2,1)S(1)} %get-tuple-element.83.refs_1_), channel_id=1, source_target_pairs={{0,4},{4,0},{8,12},{12,8},{1,5},{5,1},{9,13},{13,9},{2,6},{6,2},{1... | collective-permute-start | bytes 208904 | tf_op jit(solution)/shard_map/ppermute | solution.py:681

commit v19 on v18

--- a/solution.py
+++ b/solution.py
@@ -750,11 +750,12 @@
     def do_energy(c):
         nonlocal token, carry, earlier
         chunks = joined("E", c)
-        copies = c > 0 or len(sizes) == 1
-        carry, earlier, done = filtered(
-            [merged[k] for k in chunks], pieces[c], halves, paired, earlier, carry, owned,
-            starts[c], copies, token,
+        copies = chunks[-1] == len(sizes) - 1
+        written, earlier, done = filtered(
+            [merged[k] for k in chunks], pieces[c], halves, paired, earlier,
+            carry if copies or earlier else None, owned, starts[c], copies, token,
         )
+        carry = written or carry
         token = [done]
 
     stages = {"T": do_transform, "G": do_gram, "A": do_add, "F": do_solve, "E": do_energy}

time: 76.8 us -> 77.8 us (1.013)
  waiting for transfers between devices: 18.7 us -> 20.4 us
    ppermute x19, waiting for transfers between devices: 18.7 us -> 20.4 us  [permute(): return lax.ppermute(x, axis, pairs)]
  transfers between devices with their start and end apart: 19 -> 19, of which waited for: 5 -> 5; matrix products, arithmetic and copies ran while one was open for 0% -> 0% of each run, Pallas kernels for 35% -> 34%
where the time goes in v19:
time: 77.8 us; the launch traced here: 77.6 us
  Pallas kernels  33.2 us (43%)
  starting transfers between devices  23.1 us (30%)
  waiting for transfers between devices  20.4 us (26%)
  between operations  0.91 us (1%)
    ppermute x19, starting transfers between devices, permute(): return lax.ppermute(x, axis, pairs)  23.1 us
    ppermute x19, waiting for transfers between devices, permute(): return lax.ppermute(x, axis, pairs)  20.4 us
    pallas_call x3, Pallas kernels, solve(): pl.pallas_call(functools.partial(solve_kernel, shape, half_rows, earlier[...  11.2 us
    pallas_call x2, Pallas kernels, transform(): pl.pallas_call(functools.partial(transform_kernel, peers, parts, group),...  9.73 us
    pallas_call x3, Pallas kernels, filtered(): pl.pallas_call(functools.partial(energy_kernel, slots, direct, len(pieces...  5.97 us
    pallas_call x3, Pallas kernels, gram(): pl.pallas_call(functools.partial(gram_kernel, peers, slots, direct, len(a...  3.72 us
    pallas_call x2, Pallas kernels, add(): pl.pallas_call(add_kernel, in_specs=[whole_spec()] * 2 + [any_spec()] * l...  2.59 us
  transfers between devices with their start and end apart: 19, of which 5 were waited for; matrix products, arithmetic and copies ran while one was open for 0% of the time, Pallas kernels for 34%

profile of v19, /device:TPU:0, one launch (start us, length us, event | category | flops | bytes accessed | tf_op | source)
XLA Modules:
  0.0 77.6 jit_solution(14488950332199522316)
XLA Ops:
  0.6 4.3 %transform.2 = (bf16[24,16,512]{2,1,0:T(8,128)(2,1)S(1)}, bf16[24,16,512]{2,1,0:T(8,128)(2,1)S(1)}, bf16[24,16,512]{2,1,0:T(8,128)(2,1)S(1)}, bf16[24,16,512]{2,1,0:T(8,128)(2,1)S(1)}, f32[8,128]{1,0:T(8,128)S(1)}) custom-call(s32[256]{0:T(256)} %refs_0_.3, f32[1,256]{1,0:T(1,128)} %bitcast.1, bf16[16,512,256]{2,1,0:T(8,128)(2,1)} %refs_2_.3), custom_call_target="tpu_custom_call" | custom-call | flops 1024 | bytes 1024 | tf_op jit(solution)/shard_map/transform/pallas_call | solution.py:149
  4.9 0.5 collective-permute-start
  5.5 2.6 %collective-permute-start.7 = (bf16[24,16,512]{2,1,0:T(8,128)(2,1)S(1)}, bf16[24,16,512]{2,1,0:T(8,128)(2,1)S(1)}, u32[]{:S(2)}, u32[]{:S(2)}) collective-permute-start(bf16[24,16,512]{2,1,0:T(8,128)(2,1)S(1)} %get-tuple-element.59), channel_id=1, source_target_pairs={{0,2},{1,3},{2,0},{3,1},{4,6},{5,7},{6,4},{7,5},{8,10},{9,11},{10,... | collective-permute-start | bytes 1179656 | tf_op jit(solution)/shard_map/ppermute | solution.py:681
  8.0 0.1 collective-permute-start.8
  8.1 0.0 collective-permute-done.refs_4_.refs_1_
  8.1 5.4 %transform.3 = (bf16[24,16,512]{2,1,0:T(8,128)(2,1)S(1)}, bf16[24,16,512]{2,1,0:T(8,128)(2,1)S(1)}, bf16[24,16,512]{2,1,0:T(8,128)(2,1)S(1)}, bf16[24,16,512]{2,...) custom-call(s32[256]{0:T(256)} %refs_0_.3, ...), custom_call_target="tpu_custom_call" | custom-call | flops 1024 | bytes 1024 | tf_op jit(solution)/shard_map/transform/pallas_call | solution.py:149
  13.5 0.2 collective-permute-start.4
  13.7 1.9 %collective-permute-start.5 = (bf16[24,16,512]{2,1,0:T(8,128)(2,1)S(1)}, bf16[24,16,512]{2,1,0:T(8,128)(2,1)S(1)}, u32[]{:S(2)}, u32[]{:S(2)}) collective-permute-start(bf16[24,16,512]{2,1,0:T(8,128)(2,1)S(1)} %get-tuple-element.56), channel_id=1, source_target_pairs={{0,2},{1,3},{2,0},{3,1},{4,6},{5,7},{6,4},{7,5},{8,10},{9,11},{10,... | collective-permute-start | bytes 1179656 | tf_op jit(solution)/shard_map/ppermute | solution.py:681
  15.7 0.0 collective-permute-start.6
  15.7 2.3 %collective-permute-done.7.refs_2_ = bf16[24,16,512]{2,1,0:T(8,128)(2,1)S(1)} collective-permute-done((bf16[24,16,512]{2,1,0:T(8,128)(2,1)S(1)}, bf16[24,16,512]{2,1,0:T(8,128)(2,1)S(1)}, u32[]{:S(2)}, u32[]{:S(2)}) %collective-permute-start.7) | collective-permute-done | bytes 393248 | tf_op jit(solution)/shard_map/ppermute | solution.py:681
  18.0 7.9 %collective-permute-done.8.refs_3_ = bf16[24,16,512]{2,1,0:T(8,128)(2,1)S(1)} collective-permute-done((bf16[24,16,512]{2,1,0:T(8,128)(2,1)S(1)}, bf16[24,16,512]{2,1,0:T(8,128)(2,1)S(1)}, u32[]{:S(2)}, u32[]{:S(2)}) %collective-permute-start.8) | collective-permute-done | bytes 393248 | tf_op jit(solution)/shard_map/ppermute | solution.py:681
  25.9 1.1 %gram.3 = (bf16[24,64,512]{2,1,0:T(8,128)(2,1)S(1)}, f32[8,128]{1,0:T(8,128)S(1)}, f32[12,64,128]{2,1,0:T(8,128)S(1)}, s16[400,128]{1,0:T(8,128)(2,1)S(1)}) custom-call(bf16[24,16,512]{2,1,0:T(8,128)(2,1)S(1)} %get-tuple-element.58.refs_0_, bf16[24,16,512]{2,1,0:T(8,128)(2,1)S(1)} %collective-permute-done.refs_4_.refs_1_, ...), custom_call_target="tpu_custom_call" | custom-call | flops 1024 | bytes 1024 | tf_op jit(solution)/shard_map/gram/pallas_call | solution.py:371
  27.0 1.7 %collective-permute-start.9 = (s16[400,128]{1,0:T(8,128)(2,1)S(1)}, s16[400,128]{1,0:T(8,128)(2,1)S(1)}, u32[]{:S(2)}, u32[]{:S(2)}) collective-permute-start(s16[400,128]{1,0:T(8,128)(2,1)S(1)} %get-tuple-element.63), channel_id=1, source_target_pairs={{0,4},{4,0},{8,12},{12,8},{1,5},{5,1},{9,13},{13,9},{2,6},{6,2},{1... | collective-permute-start | bytes 307208 | tf_op jit(solution)/shard_map/ppermute | solution.py:681
  28.7 0.5 collective-permute-start.1
  29.2 3.3 %collective-permute-done.9.other = s16[400,128]{1,0:T(8,128)(2,1)S(1)} collective-permute-done((s16[400,128]{1,0:T(8,128)(2,1)S(1)}, s16[400,128]{1,0:T(8,128)(2,1)S(1)}, u32[]{:S(2)}, u32[]{:S(2)}) %collective-permute-start.9) | collective-permute-done | bytes 102432 | tf_op jit(solution)/shard_map/ppermute | solution.py:681
  32.5 1.7 %collective-permute-start.2 = (bf16[16,16,512]{2,1,0:T(8,128)(2,1)S(1)}, bf16[16,16,512]{2,1,0:T(8,128)(2,1)S(1)}, u32[]{:S(2)}, u32[]{:S(2)}) collective-permute-start(bf16[16,16,512]{2,1,0:T(8,128)(2,1)S(1)} %get-tuple-element.52), channel_id=1, source_target_pairs={{0,2},{1,3},{2,0},{3,1},{4,6},{5,7},{6,4},{7,5},{8,10},{9,11},{10,... | collective-permute-start | bytes 786440 | tf_op jit(solution)/shard_map/ppermute | solution.py:681
  34.2 0.0 collective-permute-done.4.refs_1_
  34.2 0.0 collective-permute-start.3
  34.2 1.3 %add.2 = (s16[400,128]{1,0:T(8,128)(2,1)S(1)}, f32[8,128]{1,0:T(8,128)S(1)}) custom-call(f32[12,64,128]{2,1,0:T(8,128)S(1)} %get-tuple-element.62.own, s16[400,128]{1,0:T(8,128)(2,1)S(1)} %collective-permute-done.9.other, f32[8,128]{1,0:T(8,128)S(1)} %get-tuple-element.64.refs_0_), custom_call_target="tpu_custom_call" | custom-call | flops 1024 | bytes 1024 | tf_op jit(solution)/shard_map/add/pallas_call | solution.py:395
  35.5 0.0 collective-permute-done.5.refs_2_
  35.5 2.7 %collective-permute-start.11 = (s16[400,128]{1,0:T(8,128)(2,1)S(1)}, s16[400,128]{1,0:T(8,128)(2,1)S(1)}, u32[]{:S(2)}, u32[]{:S(2)}) collective-permute-start(s16[400,128]{1,0:T(8,128)(2,1)S(1)} %get-tuple-element.68.refs_0_), channel_id=1, source_target_pairs={{0,8},{4,12},{8,0},{12,4},{1,9},{5,13},{9,1},{13,5},{2,10},{6,14},... | collective-permute-start | bytes 307208 | tf_op jit(solution)/shard_map/ppermute | solution.py:681
  38.2 4.6 %collective-permute-done.6.refs_3_ = bf16[24,16,512]{2,1,0:T(8,128)(2,1)S(1)} collective-permute-done((bf16[24,16,512]{2,1,0:T(8,128)(2,1)S(1)}, bf16[24,16,512]{2,1,0:T(8,128)(2,1)S(1)}, u32[]{:S(2)}, u32[]{:S(2)}) %collective-permute-start.6) | collective-permute-done | bytes 393248 | tf_op jit(solution)/shard_map/ppermute | solution.py:681
  42.7 1.1 %gram.4 = (bf16[24,64,512]{2,1,0:T(8,128)(2,1)S(1)}, f32[8,128]{1,0:T(8,128)S(1)}, f32[12,64,128]{2,1,0:T(8,128)S(1)}, s16[400,128]{1,0:T(8,128)(2,1)S(1)}) custom-call(bf16[24,16,512]{2,1,0:T(8,128)(2,1)S(1)} %get-tuple-element.54.refs_0_, bf16[24,16,512]{2,1,0:T(8,128)(2,1)S(1)} %collective-permute-done.4.refs_1_, ...), custom_call_target="tpu_custom_call" | custom-call | flops 1024 | bytes 1024 | tf_op jit(solution)/shard_map/gram/pallas_call | solution.py:371
  43.9 1.7 %collective-permute-start.10 = (s16[400,128]{1,0:T(8,128)(2,1)S(1)}, s16[400,128]{1,0:T(8,128)(2,1)S(1)}, u32[]{:S(2)}, u32[]{:S(2)}) collective-permute-start(s16[400,128]{1,0:T(8,128)(2,1)S(1)} %get-tuple-element.67), channel_id=1, source_target_pairs={{0,4},{4,0},{8,12},{12,8},{1,5},{5,1},{9,13},{13,9},{2,6},{6,2},{1... | collective-permute-start | bytes 307208 | tf_op jit(solution)/shard_map/ppermute | solution.py:681
  45.6 0.0 collective-permute-done.11.refs_1_
  45.6 3.9 %filters.3 = (s16[400,128]{1,0:T(8,128)(2,1)S(1)}, f32[8,128]{1,0:T(8,128)S(1)}) custom-call(s16[400,128]{1,0:T(8,128)(2,1)S(1)} %get-tuple-element.68.refs_0_, s16[400,128]{1,0:T(8,128)(2,1)S(1)} %collective-permute-done.11.refs_1_, f32[8,128]{1,0:T(8,128)S(1)} %get-tuple-element.69.refs_2_), custom_call_target="tpu_custom_call" | custom-call | flops 1024 | bytes 1024 | tf_op jit(solution)/shard_map/filters/pallas_call | solution.py:521
  49.5 0.5 collective-permute-start.16
  50.0 0.0 collective-permute-done.10.other
  50.0 1.3 %add.3 = (s16[400,128]{1,0:T(8,128)(2,1)S(1)}, f32[8,128]{1,0:T(8,128)S(1)}) custom-call(f32[12,64,128]{2,1,0:T(8,128)S(1)} %get-tuple-element.66.own, s16[400,128]{1,0:T(8,128)(2,1)S(1)} %collective-permute-done.10.other, f32[8,128]{1,0:T(8,128)S(1)} %get-tuple-element.70.refs_0_), custom_call_target="tpu_custom_call" | custom-call | flops 1024 | bytes 1024 | tf_op jit(solution)/shard_map/add/pallas_call | solution.py:395
  51.3 2.7 %collective-permute-start.15 = (s16[400,128]{1,0:T(8,128)(2,1)S(1)}, s16[400,128]{1,0:T(8,128)(2,1)S(1)}, u32[]{:S(2)}, u32[]{:S(2)}) collective-permute-start(s16[400,128]{1,0:T(8,128)(2,1)S(1)} %get-tuple-element.75.refs_0_), channel_id=1, source_target_pairs={{0,8},{4,12},{8,0},{12,4},{1,9},{5,13},{9,1},{13,5},{2,10},{6,14},... | collective-permute-start | bytes 307208 | tf_op jit(solution)/shard_map/ppermute | solution.py:681
  54.0 0.0 collective-permute-done.1.refs_1_
  54.0 0.0 collective-permute-done.2.refs_2_
  54.0 0.0 collective-permute-done.3.refs_3_
  54.0 1.5 %gram.5 = (bf16[16,64,512]{2,1,0:T(8,128)(2,1)S(1)}, f32[8,128]{1,0:T(8,128)S(1)}, s16[272,128]{1,0:T(8,128)(2,1)S(1)}, s16[272,128]{1,0:T(8,128)(2,1)S(1)}) custom-call(bf16[16,16,512]{2,1,0:T(8,128)(2,1)S(1)} %get-tuple-element.50.refs_0_, bf16[16,16,512]{2,1,0:T(8,128)(2,1)S(1)} %collective-permute-done.1.refs_1_, ...), custom_call_target="tpu_custom_call" | custom-call | flops 1024 | bytes 1024 | tf_op jit(solution)/shard_map/gram/pallas_call | solution.py:371
  55.5 2.6 %collective-permute-start.12 = (s16[272,128]{1,0:T(8,128)(2,1)S(1)}, s16[272,128]{1,0:T(8,128)(2,1)S(1)}, u32[]{:S(2)}, u32[]{:S(2)}) collective-permute-start(s16[272,128]{1,0:T(8,128)(2,1)S(1)} %get-tuple-element.73.refs_0_), channel_id=1, source_target_pairs={{0,8},{4,12},{8,0},{12,4},{1,9},{5,13},{9,1},{13,5},{2,10},{6,14},... | collective-permute-start | bytes 208904 | tf_op jit(solution)/shard_map/ppermute | solution.py:681
  58.2 1.3 %collective-permute-start.14 = (s16[272,128]{1,0:T(8,128)(2,1)S(1)}, s16[272,128]{1,0:T(8,128)(2,1)S(1)}, u32[]{:S(2)}, u32[]{:S(2)}) collective-permute-start(s16[272,128]{1,0:T(8,128)(2,1)S(1)} %get-tuple-element.74), channel_id=1, source_target_pairs={{0,12},{4,8},{8,4},{12,0},{1,13},{5,9},{9,5},{13,1},{2,14},{6,10},... | collective-permute-start | bytes 208904 | tf_op jit(solution)/shard_map/ppermute | solution.py:681
  59.5 0.2 collective-permute-start.13
  59.8 0.0 collective-permute-done.16.refs_2_
  59.8 1.8 %energy.3 = (f32[24,256]{1,0:T(8,128)S(1)}, f32[24,2,64,64]{3,2,1,0:T(8,128)S(1)}, f32[8,128]{1,0:T(8,128)S(1)}) custom-call(bf16[24,64,512]{2,1,0:T(8,128)(2,1)S(1)} %get-tuple-element.76.refs_0_, s16[400,128]{1,0:T(8,128)(2,1)S(1)} %get-tuple-element.77.refs_1_, s16[400,128]{1,0:T(8,128)(2,1)S(1)} %collective-permute-done.16.refs_2_, ...), custom_call_target="tpu_custom_call" | custom-call | flops 1024 | bytes 1024 | tf_op jit(solution)/shard_map/energy/pallas_call | solution.py:635
  61.5 0.0 collective-permute-done.15.refs_1_
  61.6 3.8 %filters.4 = (f32[64,256]{1,0:T(8,128)}, f32[64,2,64,64]{3,2,1,0:T(8,128)}, s16[400,128]{1,0:T(8,128)(2,1)S(1)}, f32[8,128]{1,0:T(8,128)S(1)}) custom-call(s16[400,128]{1,0:T(8,128)(2,1)S(1)} %get-tuple-element.75.refs_0_, s16[400,128]{1,0:T(8,128)(2,1)S(1)} %collective-permute-done.15.refs_1_, f32[24,256]{1,0:T(8,128)S(1)} %get-tuple-element.79.refs_2_, ...), custom_call_target="tpu_custom_call" | custom-call | flops 1024 | bytes 1024 | tf_op jit(solution)/shard_map/filters/pallas_call | solution.py:521
  65.4 1.9 %collective-permute-start.18 = (s16[400,128]{1,0:T(8,128)(2,1)S(1)}, s16[400,128]{1,0:T(8,128)(2,1)S(1)}, u32[]{:S(2)}, u32[]{:S(2)}) collective-permute-start(s16[400,128]{1,0:T(8,128)(2,1)S(1)} %get-tuple-element.85.refs_1_), channel_id=1, source_target_pairs={{0,4},{4,0},{8,12},{12,8},{1,5},{5,1},{9,13},{13,9},{2,6},{6,2},{1... | collective-permute-start | bytes 307208 | tf_op jit(solution)/shard_map/ppermute | solution.py:681
  67.2 0.0 collective-permute-done.12.refs_1_
  67.2 0.0 collective-permute-done.14.refs_3_
  67.2 0.0 collective-permute-done.13.refs_2_
  67.2 3.4 %filters.5 = (s16[272,128]{1,0:T(8,128)(2,1)S(1)}, f32[8,128]{1,0:T(8,128)S(1)}) custom-call(s16[272,128]{1,0:T(8,128)(2,1)S(1)} %get-tuple-element.73.refs_0_, s16[272,128]{1,0:T(8,128)(2,1)S(1)} %collective-permute-done.12.refs_1_, s16[272,128]{1,0:T(8,128)(2,1)S(1)} %collective-permute-done.13.refs_2_, ...), custom_call_target="tpu_custom_call" | custom-call | flops 1024 | bytes 1024 | tf_op jit(solution)/shard_map/filters/pallas_call | solution.py:521
  70.7 0.3 collective-permute-start.17
  70.9 0.0 collective-permute-done.18.refs_2_
  71.0 1.8 %energy.4 = (f32[24,256]{1,0:T(8,128)S(1)}, f32[24,2,64,64]{3,2,1,0:T(8,128)S(1)}, f32[8,128]{1,0:T(8,128)S(1)}) custom-call(bf16[24,64,512]{2,1,0:T(8,128)(2,1)S(1)} %get-tuple-element.84.refs_0_, s16[400,128]{1,0:T(8,128)(2,1)S(1)} %get-tuple-element.85.refs_1_, s16[400,128]{1,0:T(8,128)(2,1)S(1)} %collective-permute-done.18.refs_2_, ...), custom_call_target="tpu_custom_call" | custom-call | flops 1024 | bytes 1024 | tf_op jit(solution)/shard_map/energy/pallas_call | solution.py:635
  72.7 2.3 %collective-permute-done.17.refs_2_ = s16[272,128]{1,0:T(8,128)(2,1)S(1)} collective-permute-done((s16[272,128]{1,0:T(8,128)(2,1)S(1)}, s16[272,128]{1,0:T(8,128)(2,1)S(1)}, u32[]{:S(2)}, u32[]{:S(2)}) %collective-permute-start.17) | collective-permute-done | bytes 69664 | tf_op jit(solution)/shard_map/ppermute | solution.py:681
  75.0 2.4 %energy.5 = (f32[64,256]{1,0:T(8,128)}, f32[64,2,64,64]{3,2,1,0:T(8,128)}, f32[8,128]{1,0:T(8,128)}) custom-call(bf16[16,64,512]{2,1,0:T(8,128)(2,1)S(1)} %get-tuple-element.72.refs_0_, s16[272,128]{1,0:T(8,128)(2,1)S(1)} %get-tuple-element.83.refs_1_, ...), custom_call_target="tpu_custom_call", output_to_operand_aliasing={{0}: (5, {}), {1}: (6, {})} | custom-call | flops 1024 | bytes 1024 | tf_op jit(solution)/shard_map/energy/pallas_call | solution.py:635
Async XLA Ops:
  4.9 3.2 %collective-permute-start = (bf16[24,16,512]{2,1,0:T(8,128)(2,1)S(1)}, bf16[24,16,512]{2,1,0:T(8,128)(2,1)S(1)}, u32[]{:S(2)}, u32[]{:S(2)}) collective-permute-start(bf16[24,16,512]{2,1,0:T(8,128)(2,1)S(1)} %get-tuple-element.49), channel_id=1, source_target_pairs={{0,1},{1,0},{2,3},{3,2},{4,5},{5,4},{6,7},{7,6},{8,9},{9,8},{10,11... | collective-permute-start | bytes 1179656 | tf_op jit(solution)/shard_map/ppermute | solution.py:681
  5.5 12.5 %collective-permute-start.7 = (bf16[24,16,512]{2,1,0:T(8,128)(2,1)S(1)}, bf16[24,16,512]{2,1,0:T(8,128)(2,1)S(1)}, u32[]{:S(2)}, u32[]{:S(2)}) collective-permute-start(bf16[24,16,512]{2,1,0:T(8,128)(2,1)S(1)} %get-tuple-element.59), channel_id=1, source_target_pairs={{0,2},{1,3},{2,0},{3,1},{4,6},{5,7},{6,4},{7,5},{8,10},{9,11},{10,... | collective-permute-start | bytes 1179656 | tf_op jit(solution)/shard_map/ppermute | solution.py:681
  8.0 17.9 %collective-permute-start.8 = (bf16[24,16,512]{2,1,0:T(8,128)(2,1)S(1)}, bf16[24,16,512]{2,1,0:T(8,128)(2,1)S(1)}, u32[]{:S(2)}, u32[]{:S(2)}) collective-permute-start(bf16[24,16,512]{2,1,0:T(8,128)(2,1)S(1)} %get-tuple-element.60), channel_id=1, source_target_pairs={{0,3},{1,2},{2,1},{3,0},{4,7},{5,6},{6,5},{7,4},{8,11},{9,10},{10,... | collective-permute-start | bytes 1179656 | tf_op jit(solution)/shard_map/ppermute | solution.py:681
  13.5 20.7 %collective-permute-start.4 = (bf16[24,16,512]{2,1,0:T(8,128)(2,1)S(1)}, bf16[24,16,512]{2,1,0:T(8,128)(2,1)S(1)}, u32[]{:S(2)}, u32[]{:S(2)}) collective-permute-start(bf16[24,16,512]{2,1,0:T(8,128)(2,1)S(1)} %get-tuple-element.55), channel_id=1, source_target_pairs={{0,1},{1,0},{2,3},{3,2},{4,5},{5,4},{6,7},{7,6},{8,9},{9,8},{10,11... | collective-permute-start | bytes 1179656 | tf_op jit(solution)/shard_map/ppermute | solution.py:681
  13.7 21.8 %collective-permute-start.5 = (bf16[24,16,512]{2,1,0:T(8,128)(2,1)S(1)}, bf16[24,16,512]{2,1,0:T(8,128)(2,1)S(1)}, u32[]{:S(2)}, u32[]{:S(2)}) collective-permute-start(bf16[24,16,512]{2,1,0:T(8,128)(2,1)S(1)} %get-tuple-element.56), channel_id=1, source_target_pairs={{0,2},{1,3},{2,0},{3,1},{4,6},{5,7},{6,4},{7,5},{8,10},{9,11},{10,... | collective-permute-start | bytes 1179656 | tf_op jit(solution)/shard_map/ppermute | solution.py:681
  15.7 27.1 %collective-permute-start.6 = (bf16[24,16,512]{2,1,0:T(8,128)(2,1)S(1)}, bf16[24,16,512]{2,1,0:T(8,128)(2,1)S(1)}, u32[]{:S(2)}, u32[]{:S(2)}) collective-permute-start(bf16[24,16,512]{2,1,0:T(8,128)(2,1)S(1)} %get-tuple-element.57), channel_id=1, source_target_pairs={{0,3},{1,2},{2,1},{3,0},{4,7},{5,6},{6,5},{7,4},{8,11},{9,10},{10,... | collective-permute-start | bytes 1179656 | tf_op jit(solution)/shard_map/ppermute | solution.py:681
  27.0 5.5 %collective-permute-start.9 = (s16[400,128]{1,0:T(8,128)(2,1)S(1)}, s16[400,128]{1,0:T(8,128)(2,1)S(1)}, u32[]{:S(2)}, u32[]{:S(2)}) collective-permute-start(s16[400,128]{1,0:T(8,128)(2,1)S(1)} %get-tuple-element.63), channel_id=1, source_target_pairs={{0,4},{4,0},{8,12},{12,8},{1,5},{5,1},{9,13},{13,9},{2,6},{6,2},{1... | collective-permute-start | bytes 307208 | tf_op jit(solution)/shard_map/ppermute | solution.py:681
  28.7 25.3 %collective-permute-start.1 = (bf16[16,16,512]{2,1,0:T(8,128)(2,1)S(1)}, bf16[16,16,512]{2,1,0:T(8,128)(2,1)S(1)}, u32[]{:S(2)}, u32[]{:S(2)}) collective-permute-start(bf16[16,16,512]{2,1,0:T(8,128)(2,1)S(1)} %get-tuple-element.51), channel_id=1, source_target_pairs={{0,1},{1,0},{2,3},{3,2},{4,5},{5,4},{6,7},{7,6},{8,9},{9,8},{10,11... | collective-permute-start | bytes 786440 | tf_op jit(solution)/shard_map/ppermute | solution.py:681
  32.5 21.5 %collective-permute-start.2 = (bf16[16,16,512]{2,1,0:T(8,128)(2,1)S(1)}, bf16[16,16,512]{2,1,0:T(8,128)(2,1)S(1)}, u32[]{:S(2)}, u32[]{:S(2)}) collective-permute-start(bf16[16,16,512]{2,1,0:T(8,128)(2,1)S(1)} %get-tuple-element.52), channel_id=1, source_target_pairs={{0,2},{1,3},{2,0},{3,1},{4,6},{5,7},{6,4},{7,5},{8,10},{9,11},{10,... | collective-permute-start | bytes 786440 | tf_op jit(solution)/shard_map/ppermute | solution.py:681
  34.2 19.8 %collective-permute-start.3 = (bf16[16,16,512]{2,1,0:T(8,128)(2,1)S(1)}, bf16[16,16,512]{2,1,0:T(8,128)(2,1)S(1)}, u32[]{:S(2)}, u32[]{:S(2)}) collective-permute-start(bf16[16,16,512]{2,1,0:T(8,128)(2,1)S(1)} %get-tuple-element.53), channel_id=1, source_target_pairs={{0,3},{1,2},{2,1},{3,0},{4,7},{5,6},{6,5},{7,4},{8,11},{9,10},{10,... | collective-permute-start | bytes 786440 | tf_op jit(solution)/shard_map/ppermute | solution.py:681
  35.5 10.1 %collective-permute-start.11 = (s16[400,128]{1,0:T(8,128)(2,1)S(1)}, s16[400,128]{1,0:T(8,128)(2,1)S(1)}, u32[]{:S(2)}, u32[]{:S(2)}) collective-permute-start(s16[400,128]{1,0:T(8,128)(2,1)S(1)} %get-tuple-element.68.refs_0_), channel_id=1, source_target_pairs={{0,8},{4,12},{8,0},{12,4},{1,9},{5,13},{9,1},{13,5},{2,10},{6,14},... | collective-permute-start | bytes 307208 | tf_op jit(solution)/shard_map/ppermute | solution.py:681
  43.9 6.1 %collective-permute-start.10 = (s16[400,128]{1,0:T(8,128)(2,1)S(1)}, s16[400,128]{1,0:T(8,128)(2,1)S(1)}, u32[]{:S(2)}, u32[]{:S(2)}) collective-permute-start(s16[400,128]{1,0:T(8,128)(2,1)S(1)} %get-tuple-element.67), channel_id=1, source_target_pairs={{0,4},{4,0},{8,12},{12,8},{1,5},{5,1},{9,13},{13,9},{2,6},{6,2},{1... | collective-permute-start | bytes 307208 | tf_op jit(solution)/shard_map/ppermute | solution.py:681
  49.5 10.2 %collective-permute-start.16 = (s16[400,128]{1,0:T(8,128)(2,1)S(1)}, s16[400,128]{1,0:T(8,128)(2,1)S(1)}, u32[]{:S(2)}, u32[]{:S(2)}) collective-permute-start(s16[400,128]{1,0:T(8,128)(2,1)S(1)} %get-tuple-element.77.refs_1_), channel_id=1, source_target_pairs={{0,4},{4,0},{8,12},{12,8},{1,5},{5,1},{9,13},{13,9},{2,6},{6,2},{1... | collective-permute-start | bytes 307208 | tf_op jit(solution)/shard_map/ppermute | solution.py:681
  51.3 10.2 %collective-permute-start.15 = (s16[400,128]{1,0:T(8,128)(2,1)S(1)}, s16[400,128]{1,0:T(8,128)(2,1)S(1)}, u32[]{:S(2)}, u32[]{:S(2)}) collective-permute-start(s16[400,128]{1,0:T(8,128)(2,1)S(1)} %get-tuple-element.75.refs_0_), channel_id=1, source_target_pairs={{0,8},{4,12},{8,0},{12,4},{1,9},{5,13},{9,1},{13,5},{2,10},{6,14},... | collective-permute-start | bytes 307208 | tf_op jit(solution)/shard_map/ppermute | solution.py:681
  55.5 11.7 %collective-permute-start.12 = (s16[272,128]{1,0:T(8,128)(2,1)S(1)}, s16[272,128]{1,0:T(8,128)(2,1)S(1)}, u32[]{:S(2)}, u32[]{:S(2)}) collective-permute-start(s16[272,128]{1,0:T(8,128)(2,1)S(1)} %get-tuple-element.73.refs_0_), channel_id=1, source_target_pairs={{0,8},{4,12},{8,0},{12,4},{1,9},{5,13},{9,1},{13,5},{2,10},{6,14},... | collective-permute-start | bytes 208904 | tf_op jit(solution)/shard_map/ppermute | solution.py:681
  58.2 9.1 %collective-permute-start.14 = (s16[272,128]{1,0:T(8,128)(2,1)S(1)}, s16[272,128]{1,0:T(8,128)(2,1)S(1)}, u32[]{:S(2)}, u32[]{:S(2)}) collective-permute-start(s16[272,128]{1,0:T(8,128)(2,1)S(1)} %get-tuple-element.74), channel_id=1, source_target_pairs={{0,12},{4,8},{8,4},{12,0},{1,13},{5,9},{9,5},{13,1},{2,14},{6,10},... | collective-permute-start | bytes 208904 | tf_op jit(solution)/shard_map/ppermute | solution.py:681
  59.5 7.7 %collective-permute-start.13 = (s16[272,128]{1,0:T(8,128)(2,1)S(1)}, s16[272,128]{1,0:T(8,128)(2,1)S(1)}, u32[]{:S(2)}, u32[]{:S(2)}) collective-permute-start(s16[272,128]{1,0:T(8,128)(2,1)S(1)} %get-tuple-element.74), channel_id=1, source_target_pairs={{0,4},{4,0},{8,12},{12,8},{1,5},{5,1},{9,13},{13,9},{2,6},{6,2},{1... | collective-permute-start | bytes 208904 | tf_op jit(solution)/shard_map/ppermute | solution.py:681
  65.4 5.6 %collective-permute-start.18 = (s16[400,128]{1,0:T(8,128)(2,1)S(1)}, s16[400,128]{1,0:T(8,128)(2,1)S(1)}, u32[]{:S(2)}, u32[]{:S(2)}) collective-permute-start(s16[400,128]{1,0:T(8,128)(2,1)S(1)} %get-tuple-element.85.refs_1_), channel_id=1, source_target_pairs={{0,4},{4,0},{8,12},{12,8},{1,5},{5,1},{9,13},{13,9},{2,6},{6,2},{1... | collective-permute-start | bytes 307208 | tf_op jit(solution)/shard_map/ppermute | solution.py:681
  70.7 4.4 %collective-permute-start.17 = (s16[272,128]{1,0:T(8,128)(2,1)S(1)}, s16[272,128]{1,0:T(8,128)(2,1)S(1)}, u32[]{:S(2)}, u32[]{:S(2)}) collective-permute-start(s16[272,128]{1,0:T(8,128)(2,1)S(1)} %get-tuple-element.83.refs_1_), channel_id=1, source_target_pairs={{0,4},{4,0},{8,12},{12,8},{1,5},{5,1},{9,13},{13,9},{2,6},{6,2},{1... | collective-permute-start | bytes 208904 | tf_op jit(solution)/shard_map/ppermute | solution.py:681
